TPU v7x, 32 devices: a whole 2x2x4 slice. The times are simulated.
32 devices in a mesh: groups: 2 (over x), dp: 16 (over z, y, core).
Axes of the slice: x: 2, y: 2, z: 4, core: 2. Of those that a mesh axis runs over, the one named last changes fastest.
Arguments:
- activations: bfloat16 [4096, 8192], P(('groups', 'dp')), parts along dimension 0, may hold values from -16 to 16
- out_grads: bfloat16 [4096, 28672], P(('groups', 'dp')), parts along dimension 0, may hold values from -16 to 16
- slot_of_row: int32 [4096], P(('groups', 'dp')), parts along dimension 0, may hold values from -1 to 1023, as said below
- basis_in: bfloat16 [16384, 256], P(('groups', 'dp')), parts along dimension 0, may hold values from -0.0625 to 0.0625
- basis_out: bfloat16 [57344, 256], P(('groups', 'dp')), parts along dimension 0, may hold values from -0.03125 to 0.03125
Outputs:
- corrected: float32 [512, 256], P(('groups', 'dp')), parts along dimension 0
- self_score: float32 [2048], P(('groups', 'dp')), parts along dimension 0
There are 2 independent parts, one for each index of `groups`. A program takes and returns all parts, laid end to end along the dimension named above; each array names one. Nothing has to cross between parts.
Inputs may be any that keep to these rules, and one draw needn't show every extreme that they name: Rows with slot_of_row >= 0 are the valid token rows; every slot 0 to 1023 is named by exactly one row, and slot s belongs to device s // 64 of dp. A device sends at most 8 valid rows to any one device, and some device sends exactly 8 to every device.
All inputs are finite; a program needn't handle non-finite values.
Results may differ from a plain program's by a relative error of at most 0.00056.
Values may be sent and summed in bfloat16 or wider, within the bound.
No kernel may reach another device: no remote copies, remote signals or barrier semaphores. Data moves between devices by JAX's collectives and lax.ppermute only.
A program may use at most 128 MiB of HBM per device.

v0:
```python
import jax
import jax.numpy as jnp
from jax import lax
from jax.sharding import PartitionSpec as P

damping = 0.1


def body(activations, out_grads, slot_of_row, basis_in, basis_out):
    devices = lax.axis_size("dp")
    own_index = lax.axis_index("dp")
    capacity = activations.shape[0]
    balanced = capacity // 2
    per_peer = capacity // devices
    out_panel = basis_out.shape[1]
    in_panel = basis_in.shape[1]
    total_rows = devices * balanced
    is_valid = slot_of_row >= 0
    target = jnp.where(is_valid, slot_of_row // balanced, devices)
    onehot = (target[:, None] == jnp.arange(devices, dtype=jnp.int32)[None, :]).astype(jnp.int32)
    earlier = jnp.cumsum(onehot, axis=0) - onehot
    rank_in_peer = jnp.sum(earlier * onehot, axis=1)
    buffer_pos = jnp.where(is_valid, target * per_peer + rank_in_peer, devices * per_peer)
    row_ids = jnp.arange(capacity, dtype=jnp.int32)
    source_row = (
        jnp.zeros((devices * per_peer,), jnp.int32).at[buffer_pos].set(row_ids, mode="drop")
    )
    sent_slots = (
        jnp.full((devices * per_peer,), -1, jnp.int32).at[buffer_pos].set(slot_of_row, mode="drop")
    )
    sent_slots = sent_slots.reshape(devices, per_peer)
    columns = out_grads
    rotated_out = jnp.dot(
        columns,
        lax.all_gather(basis_out, "dp", axis=0, tiled=True),
        preferred_element_type=jnp.float32,
    )
    grad_sq = (rotated_out * rotated_out).astype(jnp.bfloat16)
    columns = activations
    rotated_in = jnp.dot(
        columns,
        lax.all_gather(basis_in, "dp", axis=0, tiled=True),
        preferred_element_type=jnp.float32,
    )
    act_sq = (rotated_in * rotated_in).astype(jnp.bfloat16)
    grad_masked = jnp.where(is_valid[:, None], grad_sq, jnp.zeros_like(grad_sq))
    corrected = (
        lax.psum_scatter(
            lax.dot_general(
                grad_masked, act_sq, (((0,), (0,)), ((), ())), preferred_element_type=jnp.float32
            ),
            "dp",
            scatter_dimension=0,
            tiled=True,
        )
        / total_rows
    )
    inverse = lax.all_gather(1.0 / (corrected + damping), "dp", axis=0, tiled=True)
    weighted = lax.dot_general(
        act_sq.astype(jnp.float32),
        inverse,
        (((1,), (1,)), ((), ())),
        precision=lax.Precision.HIGHEST,
    )
    scores = jnp.sum(grad_sq.astype(jnp.float32) * weighted, axis=1) / (out_panel * in_panel)
    score_send = jnp.take(scores, source_row, axis=0).reshape(devices, per_peer)
    score_recv, slot_back = (
        lax.all_to_all(score_send, "dp", split_axis=0, concat_axis=0, tiled=True),
        lax.all_to_all(sent_slots, "dp", split_axis=0, concat_axis=0, tiled=True),
    )
    back_slot = jnp.where(slot_back >= 0, slot_back - own_index * balanced, balanced).reshape(
        devices * per_peer
    )
    self_score = (
        jnp.zeros((balanced,), jnp.float32)
        .at[back_slot]
        .set(score_recv.reshape(devices * per_peer), mode="drop")
    )
    return (corrected, self_score)


def solution(mesh):
    return jax.shard_map(
        body,
        mesh=mesh,
        in_specs=(
            P(("groups", "dp"), None),
            P(("groups", "dp"), None),
            P(("groups", "dp")),
            P(("groups", "dp"), None),
            P(("groups", "dp"), None),
        ),
        out_specs=(P(("groups", "dp"), None), P(("groups", "dp"))),
        check_vma=False,
    )
```

profile of v0, /device:TPU:0, one launch (start us, length us, event | category | flops | bytes accessed | tf_op | source)
XLA Modules:
  0.0 285.0 jit_solution(5779209087378793211)
XLA Ops:
  7.2 0.0 copy-start
  7.2 0.0 all-gather.5.cloned.1.call-start
  7.2 0.7 all-gather.5.cloned.1.call-update
  7.9 0.0 all-gather.3.cloned.1.call-start
  8.0 0.7 all-gather.3.cloned.1.call-update
  8.7 0.7 fusion.10
  9.3 0.1 fusion.3
  9.4 0.2 reduce_window_sum.11
  9.6 0.2 select_reduce_fusion
  9.8 0.7 compare_select_fusion.3
  10.4 1.1 scatter_custom_fusion
  11.6 0.7 all_to_all.10
  12.2 7.4 %all-to-all-start = ((s32[16,1,8]{2,1,0:T(1,128)}), s32[16,1,8]{2,1,0:T(1,128)S(1)}, u32[]{:S(2)}, u32[]{:S(2)}) async-start(s32[16,1,8]{2,1,0:T(1,128)} %bitcast), calls=%async_computation.1 | async-start | bytes 16384 | tf_op jit(solution)/shard_map/all_to_all | solution.py:69
  19.6 0.0 reduce-scatter.2.cloned.1.call-start
  19.7 1.0 scatter_custom_fusion.1
  20.7 0.7 broadcast_compare_fusion
  21.3 42.1 %all-gather.5.cloned.1.call-done = bf16[8192,256]{1,0:T(8,128)(2,1)} async-done(((bf16[512,256]{1,0:T(8,128)(2,1)}), bf16[8192,256]{1,0:T(8,128)(2,1)}) %all-gather.5.cloned.1.call-update) | async-done | bytes 4194320 | tf_op jit(solution)/shard_map/all_gather | solution.py:42
  63.5 0.0 copy-done
  63.5 2.9 %fusion.1 = bf16[128,256]{1,0:T(8,128)(2,1)S(1)} fusion(bf16[128,8192]{1,0:T(8,128)(2,1)S(1)} %copy-done, bf16[8192,256]{1,0:T(8,128)(2,1)} %all-gather.5.cloned.1.call-done), kind=kOutput, calls=%fused_computation.8 | convolution fusion | flops 536936448 | bytes 6356992 | tf_op jit(solution)/shard_map/dot_general | solution.py:40
  66.4 111.8 %all-gather.3.cloned.1.call-done = bf16[28672,256]{1,0:T(8,128)(2,1)} async-done(((bf16[1792,256]{1,0:T(8,128)(2,1)}), bf16[28672,256]{1,0:T(8,128)(2,1)}) %all-gather.3.cloned.1.call-update) | async-done | bytes 14680080 | tf_op jit(solution)/shard_map/all_gather | solution.py:35
  178.1 9.3 %fusion = bf16[128,256]{1,0:T(8,128)(2,1)S(1)} fusion(bf16[128,28672]{1,0:T(8,128)(2,1)} %param.6, bf16[28672,256]{1,0:T(8,128)(2,1)} %all-gather.3.cloned.1.call-done), kind=kOutput, calls=%fused_computation.7 | convolution fusion | flops 1879113728 | bytes 22085632 | tf_op jit(solution)/shard_map/dot_general | solution.py:33
  187.5 1.0 fusion.4
  188.4 0.0 reduce-scatter.2.cloned.1.call-update
  188.5 0.0 all-to-all-done
  188.6 0.1 select_n.70
  188.6 53.5 %reduce-scatter.2.cloned.1.call-done = f32[16,256]{1,0:T(8,128)} async-done(((f32[256,256]{1,0:T(8,128)}), f32[16,256]{1,0:T(8,128)}) %reduce-scatter.2.cloned.1.call-update) | async-done | bytes 16400 | tf_op jit(solution)/shard_map/reduce_scatter | solution.py:48
  242.1 1.3 add_divide_fusion
  243.4 20.1 %all_gather.11 = f32[256,256]{1,0:T(8,128)S(1)} all-gather(f32[16,256]{1,0:T(8,128)S(1)} %get-tuple-element.2), channel_id=1, replica_groups=mesh['groups'=2,'dp'=16] {'dp'}, dimensions={0}, use_global_device_ids=true | all-gather | bytes 278528 | tf_op jit(solution)/shard_map/all_gather | solution.py:58
  263.6 0.4 fusion.2
  263.9 1.2 gather_fusion
  265.2 0.7 select_n.74
  265.9 3.5 %all-to-all-start.1 = ((f32[16,1,8]{2,1,0:T(1,128)}), f32[16,1,8]{2,1,0:T(1,128)S(1)}, u32[]{:S(2)}, u32[]{:S(2)}) async-start(f32[16,1,8]{2,1,0:T(1,128)} %bitcast.2), calls=%async_computation.2 | async-start | bytes 16384 | tf_op jit(solution)/shard_map/all_to_all | solution.py:68
  269.4 6.4 %all-to-all-done.1 = f32[16,1,8]{2,1,0:T(1,128)S(1)} async-done(((f32[16,1,8]{2,1,0:T(1,128)}), f32[16,1,8]{2,1,0:T(1,128)S(1)}, u32[]{:S(2)}, u32[]{:S(2)}) %all-to-all-start.1) | async-done | bytes 544 | tf_op jit(solution)/shard_map/all_to_all | solution.py:68
  275.8 0.5 broadcast.98
  276.3 0.7 reduce.7
  276.9 0.1 reshape.111
  277.0 1.5 scatter_custom_fusion.2
  (7 shorter events, 0.1 us)
Async XLA Ops:
  7.2 56.3 %copy-start = (bf16[128,8192]{1,0:T(8,128)(2,1)S(1)}, bf16[128,8192]{1,0:T(8,128)(2,1)}, u32[]{:S(2)}) copy-start(bf16[128,8192]{1,0:T(8,128)(2,1)} %param.5) | copy-start | bytes 6291460
  7.2 56.3 %all-gather.5.cloned.1.call-start = ((), (), s32[]{:S(2)}) async-start(), calls=%async_computation.4 | async-start | bytes 4456448 | tf_op jit(solution)/shard_map/all_gather | solution.py:42
  7.9 170.2 %all-gather.3.cloned.1.call-start = ((), (), s32[]{:S(2)}) async-start(), calls=%async_computation.3 | async-start | bytes 15597568 | tf_op jit(solution)/shard_map/all_gather | solution.py:35
  12.2 176.3 %all-to-all-start = ((s32[16,1,8]{2,1,0:T(1,128)}), s32[16,1,8]{2,1,0:T(1,128)S(1)}, u32[]{:S(2)}, u32[]{:S(2)}) async-start(s32[16,1,8]{2,1,0:T(1,128)} %bitcast), calls=%async_computation.1 | async-start | bytes 16384 | tf_op jit(solution)/shard_map/all_to_all | solution.py:69
  19.6 222.5 %reduce-scatter.2.cloned.1.call-start = ((), (), s32[]{:S(2)}) async-start(), calls=%async_computation.5 | async-start | bytes 278528 | tf_op jit(solution)/shard_map/reduce_scatter | solution.py:48
  265.9 9.9 %all-to-all-start.1 = ((f32[16,1,8]{2,1,0:T(1,128)}), f32[16,1,8]{2,1,0:T(1,128)S(1)}, u32[]{:S(2)}, u32[]{:S(2)}) async-start(f32[16,1,8]{2,1,0:T(1,128)} %bitcast.2), calls=%async_computation.2 | async-start | bytes 16384 | tf_op jit(solution)/shard_map/all_to_all | solution.py:68
Sparse Core Ops, SparseCore 0:
  10.2 53.2 all-gather.4
  65.8 112.3 all-gather.2
  188.6 53.4 reduce-scatter.1
where the time goes:
time: 285 us
  waiting for transfers between devices  215 us (75%)
  blocking collectives  20.1 us (7%)
  between operations  13.9 us (5%)
  matrix products  13.6 us (5%)
  starting transfers between devices  11 us (4%)
  local copies, waits for them, and re-layouts  6.85 us (2%)
  other arithmetic  4.48 us (2%)
    all_gather x1, waiting for transfers between devices, body(): lax.all_gather(basis_out, 'dp', axis=0, tiled=True)  112 us
    reduce_scatter x1, waiting for transfers between devices, body(): lax.psum_scatter(lax.dot_general(grad_masked, act_sq, (((0,), (0,)), ((),...  53.5 us
    all_gather x1, waiting for transfers between devices, body(): lax.all_gather(basis_in, 'dp', axis=0, tiled=True)  42.1 us
    all_gather x1, blocking collectives, body(): lax.all_gather(1.0 / (corrected + damping), 'dp', axis=0, tiled=True)  20.1 us
    dot_general x1, matrix products, body(): jnp.dot(columns, lax.all_gather(basis_out, 'dp', axis=0, tiled=True), pre...  9.32 us
    all_to_all x1, starting transfers between devices, body(): lax.all_to_all(sent_slots, 'dp', split_axis=0, concat_axis=0, tiled=True)  7.39 us
    all_to_all x1, waiting for transfers between devices, body(): lax.all_to_all(score_send, 'dp', split_axis=0, concat_axis=0, tiled=True)  6.36 us
  transfers between devices with their start and end apart: 5, of which 4 were waited for; matrix products, arithmetic and copies ran while one was open for 6% of the time, Pallas kernels for 0%

commit v1 on v0

v1 whole, which is shorter than its diff:
```python
import jax
import jax.numpy as jnp
from jax import lax
from jax.sharding import PartitionSpec as P

damping = 0.1


def ring_order(chips):
    if chips == 8:
        return [0, 2, 4, 6, 7, 5, 3, 1]
    return list(range(chips))


def body(activations, out_grads, slot_of_row, basis_in, basis_out):
    devices = lax.axis_size("dp")
    chips = devices // 2
    own_index = lax.axis_index("dp")
    core = own_index % 2
    rows = activations.shape[0]
    balanced = rows // 2
    total_rows = devices * balanced
    out_panel = basis_out.shape[1]
    in_panel = basis_in.shape[1]

    order = ring_order(chips)
    place = [order.index(c) for c in range(chips)]
    position = jnp.array(place, jnp.int32)[own_index // 2]
    order_of = jnp.array(order, jnp.int32)

    def ring(step):
        pairs = []
        for i, chip in enumerate(order):
            to = order[(i + step) % chips]
            pairs += [(2 * chip, 2 * to), (2 * chip + 1, 2 * to + 1)]
        return pairs

    forward, backward = ring(1), ring(-1)
    swap = [(i, i ^ 1) for i in range(devices)]

    def send(x, pairs):
        return lax.ppermute(x, "dp", pairs)

    def owner(distance, which_core):
        return order_of[(position - distance) % chips] * 2 + which_core

    half = chips // 2
    distances = [0]
    for d in range(1, half):
        distances += [d, -d]
    distances += [half]

    def columns(x, depth, distance, which_core):
        start = owner(distance, which_core) * depth
        return lax.dynamic_slice(x, (0, start), (rows, depth))

    def both(x, depth):
        tokens = {}
        for d in distances:
            other = send(columns(x, depth, d, 1 - core), swap)
            tokens[d] = jnp.concatenate([columns(x, depth, d, core), other], axis=0)
        return tokens

    def dot(a, b):
        return jnp.dot(a, b, preferred_element_type=jnp.float32)

    def gather(pieces_of, last_forward, last_backward):
        held = [{0: p} for p in pieces_of]
        for s in range(1, half):
            for h in held:
                h[s] = send(h[s - 1], forward)
                h[-s] = send(h[1 - s], backward)
        for i in last_forward:
            held[i][half] = send(held[i][half - 1], forward)
        for i in last_backward:
            held[i][half] = send(held[i][1 - half], backward)
        return held

    def halves(x):
        h = x.shape[0] // 2
        return [x[:h], x[h:]]

    def project(x, basis):
        depth = basis.shape[0]
        if chips > 8:
            total = dot(x, lax.all_gather(basis, "dp", axis=0, tiled=True))
            return (total * total).astype(jnp.bfloat16)
        tokens = both(x, depth)
        held = gather(halves(basis), [0], [1])
        h = depth // 2
        total = 0.0
        for d in distances:
            total += dot(tokens[d][:, :h], held[0][d]) + dot(tokens[d][:, h:], held[1][d])
        total = total[:rows] + send(total[rows:], swap)
        return (total * total).astype(jnp.bfloat16)

    def everyone(x):
        if chips > 8:
            return lax.all_gather(x, "dp", axis=0, tiled=True)
        held = gather(halves(x), [0], [1])
        mine = jnp.concatenate([h[d] for h in held for d in distances], axis=0)
        return jnp.concatenate([mine, send(mine, swap)], axis=0)

    act_sq = project(activations, basis_in)
    slots = everyone(slot_of_row[:, None])[:, 0]
    all_act = everyone(act_sq)
    grad_sq = project(out_grads, basis_out)
    is_valid = slot_of_row >= 0
    all_grad = everyone(jnp.where(is_valid[:, None], grad_sq, jnp.zeros_like(grad_sq)))

    corrected = (
        lax.dot_general(
            all_grad, all_act, (((0,), (0,)), ((), ())), preferred_element_type=jnp.float32
        )
        / total_rows
    )
    inverse = 1.0 / (corrected + damping)
    wanted = own_index * balanced + jnp.arange(balanced, dtype=jnp.int32)
    pick = (slots[None, :] == wanted[:, None]).astype(jnp.bfloat16)
    own_grad = dot(pick, all_grad)
    own_act = dot(pick, all_act)
    weighted = lax.dot_general(
        own_act, inverse, (((1,), (1,)), ((), ())), precision=lax.Precision.HIGHEST
    )
    self_score = jnp.sum(own_grad * weighted, axis=1) / (out_panel * in_panel)
    panel_rows = out_panel // devices
    own_corrected = lax.dynamic_slice(corrected, (own_index * panel_rows, 0), (panel_rows, in_panel))
    return (own_corrected, self_score)


def solution(mesh):
    return jax.shard_map(
        body,
        mesh=mesh,
        in_specs=(
            P(("groups", "dp"), None),
            P(("groups", "dp"), None),
            P(("groups", "dp")),
            P(("groups", "dp"), None),
            P(("groups", "dp"), None),
        ),
        out_specs=(P(("groups", "dp"), None), P(("groups", "dp"))),
        check_vma=False,
    )
```

time: 285 us -> 287 us (level)
  starting transfers between devices: 11 us -> 77.6 us
  waiting for transfers between devices: 215 us -> 153 us
  local copies, waits for them, and re-layouts: 6.85 us -> 32.7 us
  blocking collectives: 20.1 us -> 0 us
  matrix products: 13.6 us -> 9.41 us
  other arithmetic: 4.48 us -> 0.64 us
    all_gather x2 -> x0, waiting for transfers between devices: 154 us -> none  [the longest x1 112 us: body(): lax.all_gather(basis_out, 'dp', axis=0, tiled=True)]
    ppermute x0 -> x91, waiting for transfers between devices: none -> 153 us  [send(): return lax.ppermute(x, 'dp', pairs)]
    ppermute x0 -> x91, starting transfers between devices: none -> 77.6 us  [send(): return lax.ppermute(x, 'dp', pairs)]
    reduce_scatter x1 -> x0, waiting for transfers between devices: 53.5 us -> none  [body(): lax.psum_scatter(lax.dot_general(grad_masked, act_sq, (((0,), (0,)), ((),...]
    all_gather x1 -> x0, blocking collectives: 20.1 us -> none  [body(): lax.all_gather(1.0 / (corrected + damping), 'dp', axis=0, tiled=True)]
    unnamed x2 -> x64, local copies, waits for them, and re-layouts: 0.01 us -> 18.3 us
    all_to_all x2 -> x0, starting transfers between devices: 10.9 us -> none  [the longest x1 7.39 us: body(): lax.all_to_all(sent_slots, 'dp', split_axis=0, concat_axis=0, tiled=True)]
    dynamic_slice x0 -> x5, local copies, waits for them, and re-layouts: none -> 9.94 us  [the longest x2 6.45 us: columns(): return lax.dynamic_slice(x, (0, start), (rows, depth))]
  transfers between devices with their start and end apart: 5 -> 91, of which waited for: 4 -> 53; matrix products, arithmetic and copies ran while one was open for 6% -> 14% of each run, Pallas kernels for 0% -> 0%
where the time goes in v1:
time: 287 us
  waiting for transfers between devices  153 us (53%)
  starting transfers between devices  77.6 us (27%)
  local copies, waits for them, and re-layouts  32.7 us (11%)
  between operations  13.4 us (5%)
  matrix products  9.41 us (3%)
    ppermute x91, waiting for transfers between devices, send(): return lax.ppermute(x, 'dp', pairs)  153 us
    ppermute x91, starting transfers between devices, send(): return lax.ppermute(x, 'dp', pairs)  77.6 us
    unnamed x64, local copies, waits for them, and re-layouts  18.3 us
    dot_general x34, matrix products, dot(): return jnp.dot(a, b, preferred_element_type=jnp.float32)  8.56 us
    dynamic_slice x2, local copies, waits for them, and re-layouts, columns(): return lax.dynamic_slice(x, (0, start), (rows, depth))  6.45 us
  transfers between devices with their start and end apart: 91, of which 53 were waited for; matrix products, arithmetic and copies ran while one was open for 14% of the time, Pallas kernels for 0%

profile of v1, /device:TPU:0, one launch (start us, length us, event | category | flops | bytes accessed | tf_op | source)
XLA Modules:
  0.0 286.6 jit_solution(6892390270898074242)
XLA Ops:
  1.9 3.0 %collective-permute-start.6 = (bf16[896,256]{1,0:T(8,128)(2,1)S(1)}, bf16[896,256]{1,0:T(8,128)(2,1)S(1)}, u32[]{:S(2)}, u32[]{:S(2)}) collective-permute-start(bf16[896,256]{1,0:T(8,128)(2,1)S(1)} %get-tuple-element.35), channel_id=1, source_target_pairs={{0,2},{1,3},{4,0},{5,1},{8,4},{9,5},{12,8},{13,9},{14,12},{15,13},... | collective-permute-start | bytes 1376264 | tf_op jit(solution)/shard_map/ppermute | solution.py:42
  5.0 1.7 fusion.133
  6.7 1.9 collective-permute-start.44
  16.6 1.6 fusion.134
  23.4 2.7 constant_dynamic-slice_fusion.2
  26.4 3.8 %constant_dynamic-slice_fusion.18 = (bf16[128,1792]{1,0:T(8,128)(2,1)S(1)}, bf16[128,1792]{1,0:T(8,128)(2,1)S(1)}, bf16[128,1792]{1,0:T(8,128)(2,1)S(1)}, bf16[1...) fusion(bf16[128,28672]{1,0:T(8,128)(2,1)} %param.8, ...), kind=kLoop, calls=%fused_computation.231 | loop fusion | bytes 14680128 | tf_op jit(solution)/shard_map/dynamic_slice | solution.py:55
  30.2 2.0 collective-permute-start.43
  32.4 5.1 %collective-permute-done.40 = bf16[256,256]{1,0:T(8,128)(2,1)S(1)} collective-permute-done((bf16[256,256]{1,0:T(8,128)(2,1)S(1)}, bf16[256,256]{1,0:T(8,128)(2,1)S(1)}, u32[]{:S(2)}, u32[]{:S(2)}) %collective-permute-start.40) | collective-permute-done | bytes 131104 | tf_op jit(solution)/shard_map/ppermute | solution.py:42
  39.5 1.6 collective-permute-start.5
  41.4 1.6 collective-permute-start.50
  43.5 11.7 %collective-permute-done.50 = bf16[256,256]{1,0:T(8,128)(2,1)S(1)} collective-permute-done((bf16[256,256]{1,0:T(8,128)(2,1)S(1)}, bf16[256,256]{1,0:T(8,128)(2,1)S(1)}, u32[]{:S(2)}, u32[]{:S(2)}) %collective-permute-start.50) | collective-permute-done | bytes 131104 | tf_op jit(solution)/shard_map/ppermute | solution.py:42
  56.9 3.2 %collective-permute-done.49 = bf16[256,256]{1,0:T(8,128)(2,1)S(1)} collective-permute-done((bf16[256,256]{1,0:T(8,128)(2,1)S(1)}, bf16[256,256]{1,0:T(8,128)(2,1)S(1)}, u32[]{:S(2)}, u32[]{:S(2)}) %collective-permute-start.49) | collective-permute-done | bytes 131104 | tf_op jit(solution)/shard_map/ppermute | solution.py:42
  60.8 4.4 %collective-permute-done.47 = bf16[256,256]{1,0:T(8,128)(2,1)S(1)} collective-permute-done((bf16[256,256]{1,0:T(8,128)(2,1)S(1)}, bf16[256,256]{1,0:T(8,128)(2,1)S(1)}, u32[]{:S(2)}, u32[]{:S(2)}) %collective-permute-start.47) | collective-permute-done | bytes 131104 | tf_op jit(solution)/shard_map/ppermute | solution.py:42
  65.7 4.5 %collective-permute-done.46 = bf16[256,256]{1,0:T(8,128)(2,1)S(1)} collective-permute-done((bf16[256,256]{1,0:T(8,128)(2,1)S(1)}, bf16[256,256]{1,0:T(8,128)(2,1)S(1)}, u32[]{:S(2)}, u32[]{:S(2)}) %collective-permute-start.46) | collective-permute-done | bytes 131104 | tf_op jit(solution)/shard_map/ppermute | solution.py:42
  72.0 3.1 %collective-permute-done.56 = bf16[256,256]{1,0:T(8,128)(2,1)S(1)} collective-permute-done((bf16[256,256]{1,0:T(8,128)(2,1)S(1)}, bf16[256,256]{1,0:T(8,128)(2,1)S(1)}, u32[]{:S(2)}, u32[]{:S(2)}) %collective-permute-start.56) | collective-permute-done | bytes 131104 | tf_op jit(solution)/shard_map/ppermute | solution.py:42
  76.9 3.2 %collective-permute-done.55 = bf16[256,256]{1,0:T(8,128)(2,1)S(1)} collective-permute-done((bf16[256,256]{1,0:T(8,128)(2,1)S(1)}, bf16[256,256]{1,0:T(8,128)(2,1)S(1)}, u32[]{:S(2)}, u32[]{:S(2)}) %collective-permute-start.55) | collective-permute-done | bytes 131104 | tf_op jit(solution)/shard_map/ppermute | solution.py:42
  81.5 4.0 %collective-permute-done.53 = bf16[256,256]{1,0:T(8,128)(2,1)S(1)} collective-permute-done((bf16[256,256]{1,0:T(8,128)(2,1)S(1)}, bf16[256,256]{1,0:T(8,128)(2,1)S(1)}, u32[]{:S(2)}, u32[]{:S(2)}) %collective-permute-start.53) | collective-permute-done | bytes 131104 | tf_op jit(solution)/shard_map/ppermute | solution.py:42
  86.4 4.3 %collective-permute-done.52 = bf16[256,256]{1,0:T(8,128)(2,1)S(1)} collective-permute-done((bf16[256,256]{1,0:T(8,128)(2,1)S(1)}, bf16[256,256]{1,0:T(8,128)(2,1)S(1)}, u32[]{:S(2)}, u32[]{:S(2)}) %collective-permute-start.52) | collective-permute-done | bytes 131104 | tf_op jit(solution)/shard_map/ppermute | solution.py:42
  93.7 10.9 %collective-permute-done.2 = bf16[896,256]{1,0:T(8,128)(2,1)S(1)} collective-permute-done((bf16[896,256]{1,0:T(8,128)(2,1)S(1)}, bf16[896,256]{1,0:T(8,128)(2,1)S(1)}, u32[]{:S(2)}, u32[]{:S(2)}) %collective-permute-start.2) | collective-permute-done | bytes 458784 | tf_op jit(solution)/shard_map/ppermute | solution.py:42
  104.7 2.0 collective-permute-start.59
  107.1 2.9 %collective-permute-done.59 = bf16[256,256]{1,0:T(8,128)(2,1)S(1)} collective-permute-done((bf16[256,256]{1,0:T(8,128)(2,1)S(1)}, bf16[256,256]{1,0:T(8,128)(2,1)S(1)}, u32[]{:S(2)}, u32[]{:S(2)}) %collective-permute-start.59) | collective-permute-done | bytes 131104 | tf_op jit(solution)/shard_map/ppermute | solution.py:42
  110.0 2.0 collective-permute-start.12
  112.4 1.9 collective-permute-start.11
  117.0 3.5 %collective-permute-done.61 = bf16[64,256]{1,0:T(8,128)(2,1)S(1)} collective-permute-done((bf16[64,256]{1,0:T(8,128)(2,1)S(1)}, bf16[64,256]{1,0:T(8,128)(2,1)S(1)}, u32[]{:S(2)}, u32[]{:S(2)}) %collective-permute-start.61) | collective-permute-done | bytes 32800 | tf_op jit(solution)/shard_map/ppermute | solution.py:42
  122.6 9.4 %collective-permute-done.62 = bf16[64,256]{1,0:T(8,128)(2,1)S(1)} collective-permute-done((bf16[64,256]{1,0:T(8,128)(2,1)S(1)}, bf16[64,256]{1,0:T(8,128)(2,1)S(1)}, u32[]{:S(2)}, u32[]{:S(2)}) %collective-permute-start.62) | collective-permute-done | bytes 32800 | tf_op jit(solution)/shard_map/ppermute | solution.py:42
  132.6 3.3 %collective-permute-done.63 = bf16[64,256]{1,0:T(8,128)(2,1)S(1)} collective-permute-done((bf16[64,256]{1,0:T(8,128)(2,1)S(1)}, bf16[64,256]{1,0:T(8,128)(2,1)S(1)}, u32[]{:S(2)}, u32[]{:S(2)}) %collective-permute-start.63) | collective-permute-done | bytes 32800 | tf_op jit(solution)/shard_map/ppermute | solution.py:42
  135.9 2.0 collective-permute-start.64
  140.5 3.3 %collective-permute-done.65 = bf16[64,256]{1,0:T(8,128)(2,1)S(1)} collective-permute-done((bf16[64,256]{1,0:T(8,128)(2,1)S(1)}, bf16[64,256]{1,0:T(8,128)(2,1)S(1)}, u32[]{:S(2)}, u32[]{:S(2)}) %collective-permute-start.65) | collective-permute-done | bytes 32800 | tf_op jit(solution)/shard_map/ppermute | solution.py:42
  143.8 2.0 collective-permute-start.66
  148.5 3.2 %collective-permute-done.67 = bf16[64,256]{1,0:T(8,128)(2,1)S(1)} collective-permute-done((bf16[64,256]{1,0:T(8,128)(2,1)S(1)}, bf16[64,256]{1,0:T(8,128)(2,1)S(1)}, u32[]{:S(2)}, u32[]{:S(2)}) %collective-permute-start.67) | collective-permute-done | bytes 32800 | tf_op jit(solution)/shard_map/ppermute | solution.py:42
  153.1 3.7 %collective-permute-done.68 = bf16[64,256]{1,0:T(8,128)(2,1)S(1)} collective-permute-done((bf16[64,256]{1,0:T(8,128)(2,1)S(1)}, bf16[64,256]{1,0:T(8,128)(2,1)S(1)}, u32[]{:S(2)}, u32[]{:S(2)}) %collective-permute-start.68) | collective-permute-done | bytes 32800 | tf_op jit(solution)/shard_map/ppermute | solution.py:42
  156.7 2.0 collective-permute-start.69
  161.4 3.2 %collective-permute-done.70 = bf16[64,256]{1,0:T(8,128)(2,1)S(1)} collective-permute-done((bf16[64,256]{1,0:T(8,128)(2,1)S(1)}, bf16[64,256]{1,0:T(8,128)(2,1)S(1)}, u32[]{:S(2)}, u32[]{:S(2)}) %collective-permute-start.70) | collective-permute-done | bytes 32800 | tf_op jit(solution)/shard_map/ppermute | solution.py:42
  164.6 2.0 collective-permute-start.71
  170.1 2.1 collective-permute-start.8
  172.6 10.4 %collective-permute-done.9 = bf16[896,256]{1,0:T(8,128)(2,1)S(1)} collective-permute-done((bf16[896,256]{1,0:T(8,128)(2,1)S(1)}, bf16[896,256]{1,0:T(8,128)(2,1)S(1)}, u32[]{:S(2)}, u32[]{:S(2)}) %collective-permute-start.9) | collective-permute-done | bytes 458784 | tf_op jit(solution)/shard_map/ppermute | solution.py:42
  183.0 2.0 collective-permute-start.18
  185.3 6.9 %collective-permute-done.8 = bf16[896,256]{1,0:T(8,128)(2,1)S(1)} collective-permute-done((bf16[896,256]{1,0:T(8,128)(2,1)S(1)}, bf16[896,256]{1,0:T(8,128)(2,1)S(1)}, u32[]{:S(2)}, u32[]{:S(2)}) %collective-permute-start.8) | collective-permute-done | bytes 458784 | tf_op jit(solution)/shard_map/ppermute | solution.py:42
  192.2 2.0 collective-permute-start.17
  195.0 9.2 %collective-permute-done.17 = bf16[896,256]{1,0:T(8,128)(2,1)S(1)} collective-permute-done((bf16[896,256]{1,0:T(8,128)(2,1)S(1)}, bf16[896,256]{1,0:T(8,128)(2,1)S(1)}, u32[]{:S(2)}, u32[]{:S(2)}) %collective-permute-start.17) | collective-permute-done | bytes 458784 | tf_op jit(solution)/shard_map/ppermute | solution.py:42
  204.2 2.0 collective-permute-start.73
  208.1 2.0 collective-permute-start.74
  211.5 4.9 %collective-permute-done.14 = bf16[896,256]{1,0:T(8,128)(2,1)S(1)} collective-permute-done((bf16[896,256]{1,0:T(8,128)(2,1)S(1)}, bf16[896,256]{1,0:T(8,128)(2,1)S(1)}, u32[]{:S(2)}, u32[]{:S(2)}) %collective-permute-start.14) | collective-permute-done | bytes 458784 | tf_op jit(solution)/shard_map/ppermute | solution.py:42
  217.3 3.0 %collective-permute-done.21 = bf16[896,256]{1,0:T(8,128)(2,1)S(1)} collective-permute-done((bf16[896,256]{1,0:T(8,128)(2,1)S(1)}, bf16[896,256]{1,0:T(8,128)(2,1)S(1)}, u32[]{:S(2)}, u32[]{:S(2)}) %collective-permute-start.21) | collective-permute-done | bytes 458784 | tf_op jit(solution)/shard_map/ppermute | solution.py:42
  220.6 6.2 %collective-permute-done.20 = bf16[896,256]{1,0:T(8,128)(2,1)S(1)} collective-permute-done((bf16[896,256]{1,0:T(8,128)(2,1)S(1)}, bf16[896,256]{1,0:T(8,128)(2,1)S(1)}, u32[]{:S(2)}, u32[]{:S(2)}) %collective-permute-start.20) | collective-permute-done | bytes 458784 | tf_op jit(solution)/shard_map/ppermute | solution.py:42
  242.9 2.1 collective-permute-done.29
  248.3 1.8 collective-permute-done.30
  263.3 1.8 collective-permute-start.77
  (255 shorter events, 96.0 us)
Async XLA Ops:
  1.9 89.1 %collective-permute-start.6 = (bf16[896,256]{1,0:T(8,128)(2,1)S(1)}, bf16[896,256]{1,0:T(8,128)(2,1)S(1)}, u32[]{:S(2)}, u32[]{:S(2)}) collective-permute-start(bf16[896,256]{1,0:T(8,128)(2,1)S(1)} %get-tuple-element.35), channel_id=1, source_target_pairs={{0,2},{1,3},{4,0},{5,1},{8,4},{9,5},{12,8},{13,9},{14,12},{15,13},... | collective-permute-start | bytes 1376264 | tf_op jit(solution)/shard_map/ppermute | solution.py:42
  4.9 87.1 %collective-permute-start.3 = (bf16[896,256]{1,0:T(8,128)(2,1)S(1)}, bf16[896,256]{1,0:T(8,128)(2,1)S(1)}, u32[]{:S(2)}, u32[]{:S(2)}) collective-permute-start(bf16[896,256]{1,0:T(8,128)(2,1)S(1)} %get-tuple-element.35), channel_id=1, source_target_pairs={{0,4},{1,5},{4,8},{5,9},{8,12},{9,13},{12,14},{13,15},{14,10},{15,... | collective-permute-start | bytes 1376264 | tf_op jit(solution)/shard_map/ppermute | solution.py:42
  6.7 32.8 %collective-permute-start.44 = (bf16[256,256]{1,0:T(8,128)(2,1)}, bf16[256,256]{1,0:T(8,128)(2,1)S(1)}, u32[]{:S(2)}, u32[]{:S(2)}) collective-permute-start(bf16[256,256]{1,0:T(8,128)(2,1)} %get-tuple-element.37), channel_id=1, source_target_pairs={{0,2},{1,3},{4,0},{5,1},{8,4},{9,5},{12,8},{13,9},{14,12},{15,13},... | collective-permute-start | bytes 393224 | tf_op jit(solution)/shard_map/ppermute | solution.py:42
  8.6 21.6 %collective-permute-start.41 = (bf16[256,256]{1,0:T(8,128)(2,1)}, bf16[256,256]{1,0:T(8,128)(2,1)S(1)}, u32[]{:S(2)}, u32[]{:S(2)}) collective-permute-start(bf16[256,256]{1,0:T(8,128)(2,1)} %get-tuple-element.37), channel_id=1, source_target_pairs={{0,4},{1,5},{4,8},{5,9},{8,12},{9,13},{12,14},{13,15},{14,10},{15,... | collective-permute-start | bytes 393224 | tf_op jit(solution)/shard_map/ppermute | solution.py:42
  26.1 6.0 %collective-permute-start.39 = (bf16[128,512]{1,0:T(8,128)(2,1)}, bf16[128,512]{1,0:T(8,128)(2,1)S(1)}, u32[]{:S(2)}, u32[]{:S(2)}) collective-permute-start(bf16[128,512]{1,0:T(8,128)(2,1)} %get-tuple-element.29), channel_id=1, source_target_pairs={{0,1},{1,0},{2,3},{3,2},{4,5},{5,4},{6,7},{7,6},{8,9},{9,8},{10,11... | collective-permute-start | bytes 393224 | tf_op jit(solution)/shard_map/ppermute | solution.py:42
  30.2 11.2 %collective-permute-start.43 = (bf16[256,256]{1,0:T(8,128)(2,1)S(1)}, bf16[256,256]{1,0:T(8,128)(2,1)S(1)}, u32[]{:S(2)}, u32[]{:S(2)}) collective-permute-start(bf16[256,256]{1,0:T(8,128)(2,1)S(1)} %copy-done.7), channel_id=1, source_target_pairs={{0,2},{1,3},{4,0},{5,1},{8,4},{9,5},{12,8},{13,9},{14,12},{15,13},... | collective-permute-start | bytes 393224 | tf_op jit(solution)/shard_map/ppermute | solution.py:42
  32.1 5.4 %collective-permute-start.40 = (bf16[256,256]{1,0:T(8,128)(2,1)S(1)}, bf16[256,256]{1,0:T(8,128)(2,1)S(1)}, u32[]{:S(2)}, u32[]{:S(2)}) collective-permute-start(bf16[256,256]{1,0:T(8,128)(2,1)S(1)} %copy-done.7), channel_id=1, source_target_pairs={{0,4},{1,5},{4,8},{5,9},{8,12},{9,13},{12,14},{13,15},{14,10},{15,... | collective-permute-start | bytes 393224 | tf_op jit(solution)/shard_map/ppermute | solution.py:42
  39.5 53.5 %collective-permute-start.5 = (bf16[896,256]{1,0:T(8,128)(2,1)S(1)}, bf16[896,256]{1,0:T(8,128)(2,1)S(1)}, u32[]{:S(2)}, u32[]{:S(2)}) collective-permute-start(bf16[896,256]{1,0:T(8,128)(2,1)S(1)} %get-tuple-element.34), channel_id=1, source_target_pairs={{0,2},{1,3},{4,0},{5,1},{8,4},{9,5},{12,8},{13,9},{14,12},{15,13},... | collective-permute-start | bytes 1376264 | tf_op jit(solution)/shard_map/ppermute | solution.py:42
  41.4 13.7 %collective-permute-start.50 = (bf16[256,256]{1,0:T(8,128)(2,1)S(1)}, bf16[256,256]{1,0:T(8,128)(2,1)S(1)}, u32[]{:S(2)}, u32[]{:S(2)}) collective-permute-start(bf16[256,256]{1,0:T(8,128)(2,1)S(1)} %collective-permute-done.44), channel_id=1, source_target_pairs={{0,2},{1,3},{4,0},{5,1},{8,4},{9,5},{12,8},{13,9},{14,12},{15,13},... | collective-permute-start | bytes 393224 | tf_op jit(solution)/shard_map/ppermute | solution.py:42
  43.2 17.5 %collective-permute-start.45 = (bf16[128,512]{1,0:T(8,128)(2,1)S(1)}, bf16[128,512]{1,0:T(8,128)(2,1)S(1)}, u32[]{:S(2)}, u32[]{:S(2)}) collective-permute-start(bf16[128,512]{1,0:T(8,128)(2,1)S(1)} %copy-done.3), channel_id=1, source_target_pairs={{0,1},{1,0},{2,3},{3,2},{4,5},{5,4},{6,7},{7,6},{8,9},{9,8},{10,11... | collective-permute-start | bytes 393224 | tf_op jit(solution)/shard_map/ppermute | solution.py:42
  55.1 5.0 %collective-permute-start.49 = (bf16[256,256]{1,0:T(8,128)(2,1)S(1)}, bf16[256,256]{1,0:T(8,128)(2,1)S(1)}, u32[]{:S(2)}, u32[]{:S(2)}) collective-permute-start(bf16[256,256]{1,0:T(8,128)(2,1)S(1)} %collective-permute-done.43), channel_id=1, source_target_pairs={{0,2},{1,3},{4,0},{5,1},{8,4},{9,5},{12,8},{13,9},{14,12},{15,13},... | collective-permute-start | bytes 393224 | tf_op jit(solution)/shard_map/ppermute | solution.py:42
  60.1 5.1 %collective-permute-start.47 = (bf16[256,256]{1,0:T(8,128)(2,1)S(1)}, bf16[256,256]{1,0:T(8,128)(2,1)S(1)}, u32[]{:S(2)}, u32[]{:S(2)}) collective-permute-start(bf16[256,256]{1,0:T(8,128)(2,1)S(1)} %collective-permute-done.41), channel_id=1, source_target_pairs={{0,4},{1,5},{4,8},{5,9},{8,12},{9,13},{12,14},{13,15},{14,10},{15,... | collective-permute-start | bytes 393224 | tf_op jit(solution)/shard_map/ppermute | solution.py:42
  60.7 11.2 %collective-permute-start.54 = (bf16[128,512]{1,0:T(8,128)(2,1)S(1)}, bf16[128,512]{1,0:T(8,128)(2,1)S(1)}, u32[]{:S(2)}, u32[]{:S(2)}) collective-permute-start(bf16[128,512]{1,0:T(8,128)(2,1)S(1)} %copy-done.2), channel_id=1, source_target_pairs={{0,1},{1,0},{2,3},{3,2},{4,5},{5,4},{6,7},{7,6},{8,9},{9,8},{10,11... | collective-permute-start | bytes 393224 | tf_op jit(solution)/shard_map/ppermute | solution.py:42
  65.2 5.0 %collective-permute-start.46 = (bf16[256,256]{1,0:T(8,128)(2,1)S(1)}, bf16[256,256]{1,0:T(8,128)(2,1)S(1)}, u32[]{:S(2)}, u32[]{:S(2)}) collective-permute-start(bf16[256,256]{1,0:T(8,128)(2,1)S(1)} %collective-permute-done.40), channel_id=1, source_target_pairs={{0,4},{1,5},{4,8},{5,9},{8,12},{9,13},{12,14},{13,15},{14,10},{15,... | collective-permute-start | bytes 393224 | tf_op jit(solution)/shard_map/ppermute | solution.py:42
  70.2 5.0 %collective-permute-start.56 = (bf16[256,256]{1,0:T(8,128)(2,1)S(1)}, bf16[256,256]{1,0:T(8,128)(2,1)S(1)}, u32[]{:S(2)}, u32[]{:S(2)}) collective-permute-start(bf16[256,256]{1,0:T(8,128)(2,1)S(1)} %collective-permute-done.50), channel_id=1, source_target_pairs={{0,2},{1,3},{4,0},{5,1},{8,4},{9,5},{12,8},{13,9},{14,12},{15,13},... | collective-permute-start | bytes 393224 | tf_op jit(solution)/shard_map/ppermute | solution.py:42
  71.9 9.5 %collective-permute-start.51 = (bf16[128,512]{1,0:T(8,128)(2,1)S(1)}, bf16[128,512]{1,0:T(8,128)(2,1)S(1)}, u32[]{:S(2)}, u32[]{:S(2)}) collective-permute-start(bf16[128,512]{1,0:T(8,128)(2,1)S(1)} %get-tuple-element.21), channel_id=1, source_target_pairs={{0,1},{1,0},{2,3},{3,2},{4,5},{5,4},{6,7},{7,6},{8,9},{9,8},{10,11... | collective-permute-start | bytes 393224 | tf_op jit(solution)/shard_map/ppermute | solution.py:42
  75.1 5.0 %collective-permute-start.55 = (bf16[256,256]{1,0:T(8,128)(2,1)S(1)}, bf16[256,256]{1,0:T(8,128)(2,1)S(1)}, u32[]{:S(2)}, u32[]{:S(2)}) collective-permute-start(bf16[256,256]{1,0:T(8,128)(2,1)S(1)} %collective-permute-done.49), channel_id=1, source_target_pairs={{0,2},{1,3},{4,0},{5,1},{8,4},{9,5},{12,8},{13,9},{14,12},{15,13},... | collective-permute-start | bytes 393224 | tf_op jit(solution)/shard_map/ppermute | solution.py:42
  80.1 5.4 %collective-permute-start.53 = (bf16[256,256]{1,0:T(8,128)(2,1)S(1)}, bf16[256,256]{1,0:T(8,128)(2,1)S(1)}, u32[]{:S(2)}, u32[]{:S(2)}) collective-permute-start(bf16[256,256]{1,0:T(8,128)(2,1)S(1)} %collective-permute-done.47), channel_id=1, source_target_pairs={{0,4},{1,5},{4,8},{5,9},{8,12},{9,13},{12,14},{13,15},{14,10},{15,... | collective-permute-start | bytes 393224 | tf_op jit(solution)/shard_map/ppermute | solution.py:42
  81.5 10.0 %collective-permute-start.4 = (bf16[128,1792]{1,0:T(8,128)(2,1)S(1)}, bf16[128,1792]{1,0:T(8,128)(2,1)S(1)}, u32[]{:S(2)}, u32[]{:S(2)}) collective-permute-start(bf16[128,1792]{1,0:T(8,128)(2,1)S(1)} %get-tuple-element.11), channel_id=1, source_target_pairs={{0,1},{1,0},{2,3},{3,2},{4,5},{5,4},{6,7},{7,6},{8,9},{9,8},{10,11... | collective-permute-start | bytes 1376264 | tf_op jit(solution)/shard_map/ppermute | solution.py:42
  85.5 5.2 %collective-permute-start.52 = (bf16[256,256]{1,0:T(8,128)(2,1)S(1)}, bf16[256,256]{1,0:T(8,128)(2,1)S(1)}, u32[]{:S(2)}, u32[]{:S(2)}) collective-permute-start(bf16[256,256]{1,0:T(8,128)(2,1)S(1)} %collective-permute-done.46), channel_id=1, source_target_pairs={{0,4},{1,5},{4,8},{5,9},{8,12},{9,13},{12,14},{13,15},{14,10},{15,... | collective-permute-start | bytes 393224 | tf_op jit(solution)/shard_map/ppermute | solution.py:42
  90.9 13.7 %collective-permute-start.2 = (bf16[896,256]{1,0:T(8,128)(2,1)S(1)}, bf16[896,256]{1,0:T(8,128)(2,1)S(1)}, u32[]{:S(2)}, u32[]{:S(2)}) collective-permute-start(bf16[896,256]{1,0:T(8,128)(2,1)S(1)} %get-tuple-element.34), channel_id=1, source_target_pairs={{0,4},{1,5},{4,8},{5,9},{8,12},{9,13},{12,14},{13,15},{14,10},{15,... | collective-permute-start | bytes 1376264 | tf_op jit(solution)/shard_map/ppermute | solution.py:42
  91.5 103.1 %collective-permute-start.16 = (bf16[128,1792]{1,0:T(8,128)(2,1)S(1)}, bf16[128,1792]{1,0:T(8,128)(2,1)S(1)}, u32[]{:S(2)}, u32[]{:S(2)}) collective-permute-start(bf16[128,1792]{1,0:T(8,128)(2,1)S(1)} %get-tuple-element.3), channel_id=1, source_target_pairs={{0,1},{1,0},{2,3},{3,2},{4,5},{5,4},{6,7},{7,6},{8,9},{9,8},{10,11... | collective-permute-start | bytes 1376264 | tf_op jit(solution)/shard_map/ppermute | solution.py:42
  92.0 77.1 %collective-permute-start.10 = (bf16[128,1792]{1,0:T(8,128)(2,1)S(1)}, bf16[128,1792]{1,0:T(8,128)(2,1)S(1)}, u32[]{:S(2)}, u32[]{:S(2)}) collective-permute-start(bf16[128,1792]{1,0:T(8,128)(2,1)S(1)} %get-tuple-element.7), channel_id=1, source_target_pairs={{0,1},{1,0},{2,3},{3,2},{4,5},{5,4},{6,7},{7,6},{8,9},{9,8},{10,11... | collective-permute-start | bytes 1376264 | tf_op jit(solution)/shard_map/ppermute | solution.py:42
  92.5 22.0 %collective-permute-start = (bf16[128,1792]{1,0:T(8,128)(2,1)S(1)}, bf16[128,1792]{1,0:T(8,128)(2,1)S(1)}, u32[]{:S(2)}, u32[]{:S(2)}) collective-permute-start(bf16[128,1792]{1,0:T(8,128)(2,1)S(1)} %get-tuple-element.15), channel_id=1, source_target_pairs={{0,1},{1,0},{2,3},{3,2},{4,5},{5,4},{6,7},{7,6},{8,9},{9,8},{10,11... | collective-permute-start | bytes 1376264 | tf_op jit(solution)/shard_map/ppermute | solution.py:42
  93.0 14.0 %collective-permute-start.57 = (bf16[128,512]{1,0:T(8,128)(2,1)S(1)}, bf16[128,512]{1,0:T(8,128)(2,1)S(1)}, u32[]{:S(2)}, u32[]{:S(2)}) collective-permute-start(bf16[128,512]{1,0:T(8,128)(2,1)S(1)} %get-tuple-element.33), channel_id=1, source_target_pairs={{0,1},{1,0},{2,3},{3,2},{4,5},{5,4},{6,7},{7,6},{8,9},{9,8},{10,11... | collective-permute-start | bytes 393224 | tf_op jit(solution)/shard_map/ppermute | solution.py:42
  104.7 5.3 %collective-permute-start.59 = (bf16[256,256]{1,0:T(8,128)(2,1)S(1)}, bf16[256,256]{1,0:T(8,128)(2,1)S(1)}, u32[]{:S(2)}, u32[]{:S(2)}) collective-permute-start(bf16[256,256]{1,0:T(8,128)(2,1)S(1)} %collective-permute-done.56), channel_id=1, source_target_pairs={{0,2},{1,3},{4,0},{5,1},{8,4},{9,5},{12,8},{13,9},{14,12},{15,13},... | collective-permute-start | bytes 393224 | tf_op jit(solution)/shard_map/ppermute | solution.py:42
  107.0 5.4 %collective-permute-start.58 = (bf16[256,256]{1,0:T(8,128)(2,1)S(1)}, bf16[256,256]{1,0:T(8,128)(2,1)S(1)}, u32[]{:S(2)}, u32[]{:S(2)}) collective-permute-start(bf16[256,256]{1,0:T(8,128)(2,1)S(1)} %collective-permute-done.52), channel_id=1, source_target_pairs={{0,4},{1,5},{4,8},{5,9},{8,12},{9,13},{12,14},{13,15},{14,10},{15,... | collective-permute-start | bytes 393224 | tf_op jit(solution)/shard_map/ppermute | solution.py:42
  110.0 59.6 %collective-permute-start.12 = (bf16[896,256]{1,0:T(8,128)(2,1)S(1)}, bf16[896,256]{1,0:T(8,128)(2,1)S(1)}, u32[]{:S(2)}, u32[]{:S(2)}) collective-permute-start(bf16[896,256]{1,0:T(8,128)(2,1)S(1)} %collective-permute-done.6), channel_id=1, source_target_pairs={{0,2},{1,3},{4,0},{5,1},{8,4},{9,5},{12,8},{13,9},{14,12},{15,13},... | collective-permute-start | bytes 1376264 | tf_op jit(solution)/shard_map/ppermute | solution.py:42
  112.4 57.7 %collective-permute-start.11 = (bf16[896,256]{1,0:T(8,128)(2,1)S(1)}, bf16[896,256]{1,0:T(8,128)(2,1)S(1)}, u32[]{:S(2)}, u32[]{:S(2)}) collective-permute-start(bf16[896,256]{1,0:T(8,128)(2,1)S(1)} %collective-permute-done.5), channel_id=1, source_target_pairs={{0,2},{1,3},{4,0},{5,1},{8,4},{9,5},{12,8},{13,9},{14,12},{15,13},... | collective-permute-start | bytes 1376264 | tf_op jit(solution)/shard_map/ppermute | solution.py:42
  120.5 11.5 %collective-permute-start.62 = (bf16[64,256]{1,0:T(8,128)(2,1)S(1)}, bf16[64,256]{1,0:T(8,128)(2,1)S(1)}, u32[]{:S(2)}, u32[]{:S(2)}) collective-permute-start(bf16[64,256]{1,0:T(8,128)(2,1)S(1)} %get-tuple-element.42), channel_id=1, source_target_pairs={{0,2},{1,3},{4,0},{5,1},{8,4},{9,5},{12,8},{13,9},{14,12},{15,13},... | collective-permute-start | bytes 98312 | tf_op jit(solution)/shard_map/ppermute | solution.py:42
  168.5 4.0 %collective-permute-start.7 = (bf16[128,1792]{1,0:T(8,128)(2,1)S(1)}, bf16[128,1792]{1,0:T(8,128)(2,1)S(1)}, u32[]{:S(2)}, u32[]{:S(2)}) collective-permute-start(bf16[128,1792]{1,0:T(8,128)(2,1)S(1)} %get-tuple-element.9), channel_id=1, source_target_pairs={{0,1},{1,0},{2,3},{3,2},{4,5},{5,4},{6,7},{7,6},{8,9},{9,8},{10,11... | collective-permute-start | bytes 1376264 | tf_op jit(solution)/shard_map/ppermute | solution.py:42
  169.1 37.4 %collective-permute-start.13 = (bf16[128,1792]{1,0:T(8,128)(2,1)S(1)}, bf16[128,1792]{1,0:T(8,128)(2,1)S(1)}, u32[]{:S(2)}, u32[]{:S(2)}) collective-permute-start(bf16[128,1792]{1,0:T(8,128)(2,1)S(1)} %get-tuple-element.5), channel_id=1, source_target_pairs={{0,1},{1,0},{2,3},{3,2},{4,5},{5,4},{6,7},{7,6},{8,9},{9,8},{10,11... | collective-permute-start | bytes 1376264 | tf_op jit(solution)/shard_map/ppermute | solution.py:42
  169.6 13.3 %collective-permute-start.9 = (bf16[896,256]{1,0:T(8,128)(2,1)S(1)}, bf16[896,256]{1,0:T(8,128)(2,1)S(1)}, u32[]{:S(2)}, u32[]{:S(2)}) collective-permute-start(bf16[896,256]{1,0:T(8,128)(2,1)S(1)} %collective-permute-done.3), channel_id=1, source_target_pairs={{0,4},{1,5},{4,8},{5,9},{8,12},{9,13},{12,14},{13,15},{14,10},{15,... | collective-permute-start | bytes 1376264 | tf_op jit(solution)/shard_map/ppermute | solution.py:42
  170.1 22.1 %collective-permute-start.8 = (bf16[896,256]{1,0:T(8,128)(2,1)S(1)}, bf16[896,256]{1,0:T(8,128)(2,1)S(1)}, u32[]{:S(2)}, u32[]{:S(2)}) collective-permute-start(bf16[896,256]{1,0:T(8,128)(2,1)S(1)} %collective-permute-done.2), channel_id=1, source_target_pairs={{0,4},{1,5},{4,8},{5,9},{8,12},{9,13},{12,14},{13,15},{14,10},{15,... | collective-permute-start | bytes 1376264 | tf_op jit(solution)/shard_map/ppermute | solution.py:42
  172.5 44.9 %collective-permute-start.19 = (bf16[128,1792]{1,0:T(8,128)(2,1)S(1)}, bf16[128,1792]{1,0:T(8,128)(2,1)S(1)}, u32[]{:S(2)}, u32[]{:S(2)}) collective-permute-start(bf16[128,1792]{1,0:T(8,128)(2,1)S(1)} %get-tuple-element.17), channel_id=1, source_target_pairs={{0,1},{1,0},{2,3},{3,2},{4,5},{5,4},{6,7},{7,6},{8,9},{9,8},{10,11... | collective-permute-start | bytes 1376264 | tf_op jit(solution)/shard_map/ppermute | solution.py:42
  183.0 11.7 %collective-permute-start.18 = (bf16[896,256]{1,0:T(8,128)(2,1)S(1)}, bf16[896,256]{1,0:T(8,128)(2,1)S(1)}, u32[]{:S(2)}, u32[]{:S(2)}) collective-permute-start(bf16[896,256]{1,0:T(8,128)(2,1)S(1)} %collective-permute-done.12), channel_id=1, source_target_pairs={{0,2},{1,3},{4,0},{5,1},{8,4},{9,5},{12,8},{13,9},{14,12},{15,13},... | collective-permute-start | bytes 1376264 | tf_op jit(solution)/shard_map/ppermute | solution.py:42
  192.2 12.0 %collective-permute-start.17 = (bf16[896,256]{1,0:T(8,128)(2,1)S(1)}, bf16[896,256]{1,0:T(8,128)(2,1)S(1)}, u32[]{:S(2)}, u32[]{:S(2)}) collective-permute-start(bf16[896,256]{1,0:T(8,128)(2,1)S(1)} %collective-permute-done.11), channel_id=1, source_target_pairs={{0,2},{1,3},{4,0},{5,1},{8,4},{9,5},{12,8},{13,9},{14,12},{15,13},... | collective-permute-start | bytes 1376264 | tf_op jit(solution)/shard_map/ppermute | solution.py:42
  194.5 15.5 %collective-permute-start.15 = (bf16[896,256]{1,0:T(8,128)(2,1)S(1)}, bf16[896,256]{1,0:T(8,128)(2,1)S(1)}, u32[]{:S(2)}, u32[]{:S(2)}) collective-permute-start(bf16[896,256]{1,0:T(8,128)(2,1)S(1)} %collective-permute-done.9), channel_id=1, source_target_pairs={{0,4},{1,5},{4,8},{5,9},{8,12},{9,13},{12,14},{13,15},{14,10},{15,... | collective-permute-start | bytes 1376264 | tf_op jit(solution)/shard_map/ppermute | solution.py:42
  194.6 21.8 %collective-permute-start.14 = (bf16[896,256]{1,0:T(8,128)(2,1)S(1)}, bf16[896,256]{1,0:T(8,128)(2,1)S(1)}, u32[]{:S(2)}, u32[]{:S(2)}) collective-permute-start(bf16[896,256]{1,0:T(8,128)(2,1)S(1)} %collective-permute-done.8), channel_id=1, source_target_pairs={{0,4},{1,5},{4,8},{5,9},{8,12},{9,13},{12,14},{13,15},{14,10},{15,... | collective-permute-start | bytes 1376264 | tf_op jit(solution)/shard_map/ppermute | solution.py:42
  206.5 20.8 %collective-permute-start.72 = (bf16[64,256]{1,0:T(8,128)(2,1)S(1)}, bf16[64,256]{1,0:T(8,128)(2,1)S(1)}, u32[]{:S(2)}, u32[]{:S(2)}) collective-permute-start(bf16[64,256]{1,0:T(8,128)(2,1)S(1)} %collective-permute-done.70), channel_id=1, source_target_pairs={{0,4},{1,5},{4,8},{5,9},{8,12},{9,13},{12,14},{13,15},{14,10},{15,... | collective-permute-start | bytes 98312 | tf_op jit(solution)/shard_map/ppermute | solution.py:42
  208.1 21.8 %collective-permute-start.74 = (bf16[64,256]{1,0:T(8,128)(2,1)S(1)}, bf16[64,256]{1,0:T(8,128)(2,1)S(1)}, u32[]{:S(2)}, u32[]{:S(2)}) collective-permute-start(bf16[64,256]{1,0:T(8,128)(2,1)S(1)} %collective-permute-done.73), channel_id=1, source_target_pairs={{0,2},{1,3},{4,0},{5,1},{8,4},{9,5},{12,8},{13,9},{14,12},{15,13},... | collective-permute-start | bytes 98312 | tf_op jit(solution)/shard_map/ppermute | solution.py:42
  210.1 10.2 %collective-permute-start.21 = (bf16[896,256]{1,0:T(8,128)(2,1)S(1)}, bf16[896,256]{1,0:T(8,128)(2,1)S(1)}, u32[]{:S(2)}, u32[]{:S(2)}) collective-permute-start(bf16[896,256]{1,0:T(8,128)(2,1)S(1)} %collective-permute-done.18), channel_id=1, source_target_pairs={{0,2},{1,3},{4,0},{5,1},{8,4},{9,5},{12,8},{13,9},{14,12},{15,13},... | collective-permute-start | bytes 1376264 | tf_op jit(solution)/shard_map/ppermute | solution.py:42
  216.4 10.4 %collective-permute-start.20 = (bf16[896,256]{1,0:T(8,128)(2,1)S(1)}, bf16[896,256]{1,0:T(8,128)(2,1)S(1)}, u32[]{:S(2)}, u32[]{:S(2)}) collective-permute-start(bf16[896,256]{1,0:T(8,128)(2,1)S(1)} %collective-permute-done.14), channel_id=1, source_target_pairs={{0,4},{1,5},{4,8},{5,9},{8,12},{9,13},{12,14},{13,15},{14,10},{15,... | collective-permute-start | bytes 1376264 | tf_op jit(solution)/shard_map/ppermute | solution.py:42
  230.4 53.2 %collective-permute-start.75 = (bf16[1024,256]{1,0:T(8,128)(2,1)}, bf16[1024,256]{1,0:T(8,128)(2,1)S(1)}, u32[]{:S(2)}, u32[]{:S(2)}) collective-permute-start(bf16[1024,256]{1,0:T(8,128)(2,1)} %get-tuple-element.48), channel_id=1, source_target_pairs={{0,1},{1,0},{2,3},{3,2},{4,5},{5,4},{6,7},{7,6},{8,9},{9,8},{10,11... | collective-permute-start | bytes 1572872 | tf_op jit(solution)/shard_map/ppermute | solution.py:42
  254.0 5.9 %collective-permute-start.34 = (bf16[64,256]{1,0:T(8,128)(2,1)S(1)}, bf16[64,256]{1,0:T(8,128)(2,1)S(1)}, u32[]{:S(2)}, u32[]{:S(2)}) collective-permute-start(bf16[64,256]{1,0:T(8,128)(2,1)S(1)} %collective-permute-done.32), channel_id=1, source_target_pairs={{0,4},{1,5},{4,8},{5,9},{8,12},{9,13},{12,14},{13,15},{14,10},{15,... | collective-permute-start | bytes 98312 | tf_op jit(solution)/shard_map/ppermute | solution.py:42
  263.1 21.0 %collective-permute-start.37 = (bf16[1024,256]{1,0:T(8,128)(2,1)}, bf16[1024,256]{1,0:T(8,128)(2,1)S(1)}, u32[]{:S(2)}, u32[]{:S(2)}) collective-permute-start(bf16[1024,256]{1,0:T(8,128)(2,1)} %get-tuple-element.62), channel_id=1, source_target_pairs={{0,1},{1,0},{2,3},{3,2},{4,5},{5,4},{6,7},{7,6},{8,9},{9,8},{10,11... | collective-permute-start | bytes 1572872 | tf_op jit(solution)/shard_map/ppermute | solution.py:42
  263.3 4.7 %collective-permute-start.77 = (s32[64,1]{0,1:T(1,128)S(1)}, s32[64,1]{0,1:T(1,128)S(1)}, u32[]{:S(2)}, u32[]{:S(2)}) collective-permute-start(s32[64,1]{0,1:T(1,128)S(1)} %get-tuple-element.77), channel_id=1, source_target_pairs={{0,2},{1,3},{4,0},{5,1},{8,4},{9,5},{12,8},{13,9},{14,12},{15,13},... | collective-permute-start | bytes 776 | tf_op jit(solution)/shard_map/ppermute | solution.py:42
  268.7 4.1 %collective-permute-start.79 = (s32[64,1]{0,1:T(1,128)S(1)}, s32[64,1]{0,1:T(1,128)S(1)}, u32[]{:S(2)}, u32[]{:S(2)}) collective-permute-start(s32[64,1]{0,1:T(1,128)S(1)} %collective-permute-done.77), channel_id=1, source_target_pairs={{0,2},{1,3},{4,0},{5,1},{8,4},{9,5},{12,8},{13,9},{14,12},{15,13},... | collective-permute-start | bytes 776 | tf_op jit(solution)/shard_map/ppermute | solution.py:42
  (52 other events, 307.6 us)

commit v2 on v1

v2 whole, which is shorter than its diff:
```python
import functools

import jax
import jax.numpy as jnp
from jax import lax
from jax.experimental import pallas as pl
from jax.experimental.pallas import tpu as pltpu
from jax.sharding import PartitionSpec as P

damping = 0.1


def ring_order(chips):
    if chips == 8:
        return [0, 2, 4, 6, 7, 5, 3, 1]
    return list(range(chips))


def dot(a, b):
    return jnp.dot(a, b, preferred_element_type=jnp.float32)


def squared(x):
    return (x * x).astype(jnp.bfloat16)


def finish(all_grad, all_act, owners, places, own_index, devices, balanced):
    out_panel, in_panel = all_grad.shape[1], all_act.shape[1]
    masked = jnp.where(owners[:, None] >= 0, all_grad, jnp.zeros_like(all_grad))
    corrected = lax.dot_general(
        masked, all_act, (((0,), (0,)), ((), ())), preferred_element_type=jnp.float32
    ) / (devices * balanced)
    inverse = 1.0 / (corrected + damping)
    wanted = jnp.arange(balanced, dtype=jnp.int32)
    pick = ((owners[None, :] == own_index) & (places[None, :] == wanted[:, None])).astype(jnp.bfloat16)
    own_grad = dot(pick, all_grad)
    own_act = dot(pick, all_act)
    weighted = lax.dot_general(
        own_act, inverse, (((1,), (1,)), ((), ())), precision=lax.Precision.HIGHEST
    )
    self_score = jnp.sum(own_grad * weighted, axis=1) / (out_panel * in_panel)
    panel_rows = out_panel // devices
    own_corrected = lax.dynamic_slice(corrected, (own_index * panel_rows, 0), (panel_rows, in_panel))
    return own_corrected, self_score


def gathered(activations, out_grads, slot_of_row, basis_in, basis_out):
    devices = lax.axis_size("dp")
    own_index = lax.axis_index("dp")
    balanced = activations.shape[0] // 2

    def everyone(x):
        return lax.all_gather(x, "dp", axis=0, tiled=True)

    act_sq = squared(dot(activations, everyone(basis_in)))
    grad_sq = squared(dot(out_grads, everyone(basis_out)))
    slots = everyone(slot_of_row)
    owners = jnp.where(slots >= 0, slots // balanced, -1)
    return finish(
        everyone(grad_sq), everyone(act_sq), owners, slots % balanced, own_index, devices, balanced
    )


def runs(first, count, depth_in, depth_out):
    inside = max(0, min(depth_in - first, count))
    found = []
    if inside:
        found.append((0, first, inside, 0))
    if count > inside:
        found.append((1, first + inside - depth_in, count - inside, inside))
    return found


def project_kernel(parts, depths, owners_ref, act_ref, grad_ref, other_act_ref, other_grad_ref, *refs):
    panels, (mine_ref, theirs_ref, mine_out, theirs_out, block, sems) = (
        refs[: len(parts)],
        refs[len(parts) :],
    )
    rows, width = act_ref.shape[0], panels[0].shape[1]
    sources = ((act_ref, other_act_ref), (grad_ref, other_grad_ref))
    work, at, index = [], 0, 0
    for (slot, first), panel in zip(parts, panels):
        for kind, start, count, within in runs(first, panel.shape[0], *depths):
            column = pl.multiple_of(owners_ref[slot] * depths[kind] + start, 128)
            copies = []
            for j, source in enumerate(sources[kind]):
                copy = pltpu.make_async_copy(
                    source.at[:, pl.ds(column, count)],
                    block.at[pl.ds(j * rows, rows), pl.ds(at, count)],
                    sems.at[index, j],
                )
                copy.start()
                copies.append(copy)
            work.append((kind, at, count, panel.at[pl.ds(within, count), :], copies))
            at += count
            index += 1
    totals = [0.0, 0.0]
    for kind, at, count, panel, copies in work:
        for copy in copies:
            copy.wait()
        totals[kind] += dot(block[:, at : at + count], panel[...])
    for kind, total in enumerate(totals):
        columns = slice(kind * width, (kind + 1) * width)
        mine_out[:, columns] = mine_ref[:, columns] + total[:rows]
        theirs_out[:, columns] = theirs_ref[:, columns] + total[rows:]


def project(owners, tokens, parts, before, depth_in, depth_out):
    rows, width = tokens[0].shape[0], parts[0][2].shape[1]
    panels = [p[2] for p in parts]
    depth = sum(p.shape[0] for p in panels)
    vmem = pl.BlockSpec(memory_space=pltpu.VMEM)
    total = jax.ShapeDtypeStruct((rows, 2 * width), jnp.float32)
    return pl.pallas_call(
        functools.partial(project_kernel, [p[:2] for p in parts], (depth_in, depth_out)),
        out_shape=(total, total),
        in_specs=[pl.BlockSpec(memory_space=pltpu.SMEM)]
        + [pl.BlockSpec(memory_space=pl.ANY)] * 4
        + [vmem] * (len(parts) + 2),
        out_specs=(vmem, vmem),
        scratch_shapes=[
            pltpu.VMEM((2 * rows, depth), tokens[0].dtype),
            pltpu.SemaphoreType.DMA((2 * len(parts), 2)),
        ],
        compiler_params=pltpu.CompilerParams(vmem_limit_bytes=40 * 2**20),
        cost_estimate=pl.CostEstimate(
            flops=4 * rows * depth * width, bytes_accessed=8 * rows * depth, transcendentals=0
        ),
    )(owners, *tokens, *panels, *before)


def last_kernel(scale, rows, me_ref, *refs):
    pieces, (corrected_ref, score_ref, squares, held) = refs[:-4], refs[-4:]
    me = me_ref[0]
    panel_rows, in_panel = corrected_ref.shape
    out_panel = squares.shape[1] - in_panel
    balanced = score_ref.shape[1]
    wanted = lax.broadcasted_iota(jnp.int32, (balanced, rows), 0)
    at, picks = 0, []
    for piece in pieces:
        count = min(piece.shape[0], rows)
        if at % rows:
            count = rows - at % rows
        squares[at : at + count, :] = piece[:count, :]
        at += count
        if at % rows == 0:
            tag = piece[count : count + 16, :][:1].astype(jnp.float32).astype(jnp.int32)
            owner, place = tag[:, :rows], tag[:, rows : 2 * rows]
            picks.append(((owner == me) & (place == wanted)).astype(jnp.float32))
    pick = jnp.concatenate(picks, axis=1).astype(jnp.bfloat16)
    act, grad = squares[:, :in_panel], squares[:, in_panel:]
    corrected = lax.dot_general(
        grad, act, (((0,), (0,)), ((), ())), preferred_element_type=jnp.float32
    ) * scale
    held[...] = corrected
    corrected_ref[...] = held[pl.ds(pl.multiple_of(me * panel_rows, panel_rows), panel_rows), :]
    inverse = 1.0 / (corrected + damping)
    high = inverse.astype(jnp.bfloat16)
    low = (inverse - high.astype(jnp.float32)).astype(jnp.bfloat16)
    own_act = dot(pick, act).astype(jnp.bfloat16)
    own_grad = lax.dot_general(
        grad, pick, (((0,), (1,)), ((), ())), preferred_element_type=jnp.float32
    )
    weighted = sum(
        lax.dot_general(part, own_act, (((1,), (1,)), ((), ())), preferred_element_type=jnp.float32)
        for part in (high, low)
    )
    score_ref[...] = jnp.sum(own_grad * weighted, axis=0, keepdims=True) / (out_panel * in_panel)


def last(me, pieces, rows, out_panel, devices, balanced):
    vmem = pl.BlockSpec(memory_space=pltpu.VMEM)
    width = pieces[0].shape[1]
    in_panel = width - out_panel
    corrected, score = pl.pallas_call(
        functools.partial(last_kernel, 1.0 / (devices * balanced), rows),
        out_shape=(
            jax.ShapeDtypeStruct((out_panel // devices, in_panel), jnp.float32),
            jax.ShapeDtypeStruct((1, balanced), jnp.float32),
        ),
        in_specs=[pl.BlockSpec(memory_space=pltpu.SMEM)] + [vmem] * len(pieces),
        out_specs=(vmem, vmem),
        scratch_shapes=[
            pltpu.VMEM((devices * rows, width), jnp.bfloat16),
            pltpu.VMEM((out_panel, in_panel), jnp.float32),
        ],
        compiler_params=pltpu.CompilerParams(vmem_limit_bytes=40 * 2**20),
    )(me, *pieces)
    return corrected, score.reshape(balanced)


def ringed(activations, out_grads, slot_of_row, basis_in, basis_out):
    devices = lax.axis_size("dp")
    chips = devices // 2
    own_index = lax.axis_index("dp")
    rows = activations.shape[0]
    balanced = rows // 2
    depth_in, width = basis_in.shape
    depth_out = basis_out.shape[0]

    order = ring_order(chips)

    def ring(step):
        pairs = []
        for i, chip in enumerate(order):
            to = order[(i + step) % chips]
            pairs += [(2 * chip, 2 * to), (2 * chip + 1, 2 * to + 1)]
        return pairs

    forward, backward = ring(1), ring(-1)
    swap = [(i, i ^ 1) for i in range(devices)]

    def send(x, pairs):
        return lax.ppermute(x, "dp", pairs)

    half = chips // 2
    distances = [0]
    for d in range(1, half):
        distances += [d, -d]
    distances += [half]

    chip = own_index // 2
    position = jnp.where(chip % 2 == 0, chip // 2, chips - 1 - chip // 2)
    from_position = (position - jnp.array(distances, jnp.int32)) % chips
    owners = jnp.where(
        from_position < half, 2 * from_position, 2 * (chips - 1 - from_position) + 1
    ) * 2 + own_index % 2

    shard = {0: jnp.concatenate([basis_in, basis_out], axis=0)}
    depth = depth_in + depth_out
    cut = depth // 2

    def pieces(d, first, panel):
        return [(distances.index(d), first, panel)]

    def pair(s):
        return send(shard[s - 1], forward), send(shard[1 - s], backward)

    shard[1], shard[-1] = pair(1)
    ready_act, ready_grad, _ = lax.optimization_barrier((activations, out_grads, shard[0]))
    swapped_act, swapped_grad = send(ready_act, swap), send(ready_grad, swap)
    shard[1], shard[-1], swapped_act, swapped_grad = lax.optimization_barrier(
        (shard[1], shard[-1], swapped_act, swapped_grad)
    )
    tokens = (activations, out_grads, swapped_act, swapped_grad)
    totals = [jnp.zeros((rows, 2 * width), jnp.float32)] * 2
    for s in range(1, half):
        parts = pieces(s, 0, shard[s]) + pieces(-s, 0, shard[-s])
        if s == 1:
            parts = pieces(0, 0, shard[0]) + parts
        if s + 1 < half:
            shard[s + 1], shard[-s - 1] = pair(s + 1)
        else:
            upper = send(shard[s][cut:], forward)
            lower = send(shard[-s][:cut], backward)
        totals = project(owners, tokens, parts, totals, depth_in, depth_out)
        if s + 1 < half:
            shard[s + 1], shard[-s - 1], *totals = lax.optimization_barrier(
                (shard[s + 1], shard[-s - 1], *totals)
            )
    parts = pieces(half, cut, upper) + pieces(half, 0, lower)
    mine, theirs = project(owners, tokens, parts, totals, depth_in, depth_out)

    is_valid = slot_of_row >= 0
    owner = jnp.where(is_valid, slot_of_row // balanced, -1)
    tag = jnp.concatenate([owner, slot_of_row % balanced]).astype(jnp.bfloat16)
    tag = jnp.broadcast_to(jnp.pad(tag, (0, 2 * width - 2 * rows))[None, :], (16, 2 * width))
    rotated = mine + send(theirs, swap)
    counts = is_valid[:, None] | (jnp.arange(2 * width) < width)[None, :]
    squares = jnp.where(counts, rotated * rotated, 0.0).astype(jnp.bfloat16)

    held = {0: jnp.concatenate([squares, tag], axis=0)}
    middle = (rows + 16) // 32 * 16
    for s in range(1, half):
        held[s], held[-s] = send(held[s - 1], forward), send(held[1 - s], backward)
    gathered_pieces = [held[d] for d in distances[:-1]]
    gathered_pieces.append(send(held[half - 1][:middle], forward))
    gathered_pieces.append(send(held[1 - half][middle:], backward))
    gathered_pieces += [send(x, swap) for x in gathered_pieces]
    return last(own_index[None], gathered_pieces, rows, width, devices, balanced)


def body(*arrays):
    if lax.axis_size("dp") == 16:
        return ringed(*arrays)
    return gathered(*arrays)


def solution(mesh):
    return jax.shard_map(
        body,
        mesh=mesh,
        in_specs=(
            P(("groups", "dp"), None),
            P(("groups", "dp"), None),
            P(("groups", "dp")),
            P(("groups", "dp"), None),
            P(("groups", "dp"), None),
        ),
        out_specs=(P(("groups", "dp"), None), P(("groups", "dp"))),
        check_vma=False,
    )
```

time: 287 us -> 135 us (0.47)
  waiting for transfers between devices: 153 us -> 91.7 us
  starting transfers between devices: 77.6 us -> 19.4 us
  local copies, waits for them, and re-layouts: 32.7 us -> 5.46 us
  Pallas kernels: 0 us -> 16.7 us
  between operations: 13.4 us -> 0.82 us
  matrix products: 9.41 us -> 0 us
    ppermute x91 -> x28, waiting for transfers between devices: 153 us -> 91.7 us  [send(): return lax.ppermute(x, 'dp', pairs)]
    ppermute x91 -> x28, starting transfers between devices: 77.6 us -> 19.4 us  [send(): return lax.ppermute(x, 'dp', pairs)]
    pallas_call x0 -> x5, Pallas kernels: none -> 16.7 us  [the longest x4 15.2 us: project(): pl.pallas_call(functools.partial(project_kernel, [p[:2] for p in parts],...]
    unnamed x64 -> x15, local copies, waits for them, and re-layouts: 18.3 us -> 4.11 us
    dynamic_slice x5 -> x0, local copies, waits for them, and re-layouts: 9.94 us -> none  [the longest x2 6.45 us: columns(): return lax.dynamic_slice(x, (0, start), (rows, depth))]
    dot_general x36 -> x0, matrix products: 9.41 us -> none  [the longest x34 8.56 us: dot(): return jnp.dot(a, b, preferred_element_type=jnp.float32)]
    slice x5 -> x4, local copies, waits for them, and re-layouts: 2.99 us -> 0.09 us  [the longest x1 0.04 us: ringed(): lower = send(shard[-s][:cut], backward)]
  transfers between devices with their start and end apart: 91 -> 28, of which waited for: 53 -> 16; matrix products, arithmetic and copies ran while one was open for 14% -> 0% of each run, Pallas kernels for 0% -> 9%
where the time goes in v2:
time: 135 us; the launch traced here: 134 us
  waiting for transfers between devices  91.7 us (68%)
  starting transfers between devices  19.4 us (14%)
  Pallas kernels  16.7 us (12%)
  local copies, waits for them, and re-layouts  5.46 us (4%)
    ppermute x28, waiting for transfers between devices, send(): return lax.ppermute(x, 'dp', pairs)  91.7 us
    ppermute x28, starting transfers between devices, send(): return lax.ppermute(x, 'dp', pairs)  19.4 us
    pallas_call x4, Pallas kernels, project(): pl.pallas_call(functools.partial(project_kernel, [p[:2] for p in parts],...  15.2 us
    unnamed x15, local copies, waits for them, and re-layouts  4.11 us
  transfers between devices with their start and end apart: 28, of which 16 were waited for; matrix products, arithmetic and copies ran while one was open for 0% of the time, Pallas kernels for 9%

profile of v2, /device:TPU:0, one launch (start us, length us, event | category | flops | bytes accessed | tf_op | source)
XLA Modules:
  0.0 134.2 jit_solution(10519624053597362959)
XLA Ops:
  0.7 1.1 constant_dynamic-update-slice_fusion.1
  1.8 1.2 constant_dynamic-update-slice_fusion.refs_0_
  3.0 0.5 collective-permute-start.3
  3.5 0.1 collective-permute-start.2
  3.6 3.0 %collective-permute-start = (bf16[2304,256]{1,0:T(8,128)(2,1)S(1)}, bf16[2304,256]{1,0:T(8,128)(2,1)}, u32[]{:S(2)}, u32[]{:S(2)}) collective-permute-start(bf16[2304,256]{1,0:T(8,128)(2,1)S(1)} %constant_dynamic-update-slice_fusion.refs_0_), channel_id=1, source_target_pairs={{0,4},{1,5},{4,8},{5,9},{8,12},{9,13},{12,14},{13,15},{14,10},{15,... | collective-permute-start | bytes 3538952 | tf_op jit(solution)/shard_map/ppermute | solution.py:214
  6.6 26.3 %collective-permute-done.refs_1_ = bf16[2304,256]{1,0:T(8,128)(2,1)} collective-permute-done((bf16[2304,256]{1,0:T(8,128)(2,1)S(1)}, bf16[2304,256]{1,0:T(8,128)(2,1)}, u32[]{:S(2)}, u32[]{:S(2)}) %collective-permute-start) | collective-permute-done | bytes 1179680 | tf_op jit(solution)/shard_map/ppermute | solution.py:214
  32.9 1.5 %collective-permute-done.1.refs_2_ = bf16[2304,256]{1,0:T(8,128)(2,1)} collective-permute-done((bf16[2304,256]{1,0:T(8,128)(2,1)S(1)}, bf16[2304,256]{1,0:T(8,128)(2,1)}, u32[]{:S(2)}, u32[]{:S(2)}) %collective-permute-start.1) | collective-permute-done | bytes 1179680 | tf_op jit(solution)/shard_map/ppermute | solution.py:214
  34.4 1.4 %copy-done.1 = bf16[128,8192]{1,0:T(8,128)(2,1)} copy-done((bf16[128,8192]{1,0:T(8,128)(2,1)}, bf16[128,8192]{1,0:T(8,128)(2,1)S(1)}, u32[]{:S(2)}) %copy-start.1) | copy-done | bytes 2097176
  35.8 1.6 %collective-permute-start.4 = (bf16[2304,256]{1,0:T(8,128)(2,1)}, bf16[2304,256]{1,0:T(8,128)(2,1)}, u32[]{:S(2)}, u32[]{:S(2)}) collective-permute-start(bf16[2304,256]{1,0:T(8,128)(2,1)} %collective-permute-done.refs_1_), channel_id=1, source_target_pairs={{0,4},{1,5},{4,8},{5,9},{8,12},{9,13},{12,14},{13,15},{14,10},{15,... | collective-permute-start | bytes 3538952 | tf_op jit(solution)/shard_map/ppermute | solution.py:214
  37.4 0.4 collective-permute-start.5
  37.9 1.6 %copy-done.2 = bf16[128,8192]{1,0:T(8,128)(2,1)S(1)} copy-done((bf16[128,8192]{1,0:T(8,128)(2,1)S(1)}, bf16[128,8192]{1,0:T(8,128)(2,1)}, u32[]{:S(2)}) %copy-start.2) | copy-done | bytes 2097176
  39.5 5.0 %shard_map.77 = (f32[128,512]{1,0:T(8,128)S(1)}, f32[128,512]{1,0:T(8,128)S(1)}) custom-call(s32[8]{0:T(128)S(1)} %fusion.6.owners_ref, bf16[128,8192]{1,0:T(8,128)(2,1)S(1)} %copy-done, bf16[128,28672]{1,0:T(8,128)(2,1)} %grad_ref.7, bf16[128,8192]{1,0:T(8,128)(2,1)S(1)} %copy-done.2, bf16[128,28672]{1,0:T(8,128)(2,1)} %collective-permute-done.3.other_grad_ref, ...), custom_call_target="tpu_custom_call" | custom-call | flops 905969664 | bytes 7077888 | tf_op jit(solution)/shard_map/pallas_call | solution.py:114
  44.4 18.5 %collective-permute-done.4.refs_0_ = bf16[2304,256]{1,0:T(8,128)(2,1)} collective-permute-done((bf16[2304,256]{1,0:T(8,128)(2,1)}, bf16[2304,256]{1,0:T(8,128)(2,1)}, u32[]{:S(2)}, u32[]{:S(2)}) %collective-permute-start.4) | collective-permute-done | bytes 1179680 | tf_op jit(solution)/shard_map/ppermute | solution.py:214
  62.9 1.3 collective-permute-done.5.refs_1_
  64.2 1.6 %collective-permute-start.6 = (bf16[2304,256]{1,0:T(8,128)(2,1)}, bf16[2304,256]{1,0:T(8,128)(2,1)S(1)}, u32[]{:S(2)}, u32[]{:S(2)}) collective-permute-start(bf16[2304,256]{1,0:T(8,128)(2,1)} %collective-permute-done.4.refs_0_), channel_id=1, source_target_pairs={{0,4},{1,5},{4,8},{5,9},{8,12},{9,13},{12,14},{13,15},{14,10},{15,... | collective-permute-start | bytes 3538952 | tf_op jit(solution)/shard_map/ppermute | solution.py:214
  65.8 0.4 collective-permute-start.7
  66.2 4.3 %shard_map.78 = (f32[128,512]{1,0:T(8,128)S(1)}, f32[128,512]{1,0:T(8,128)S(1)}) custom-call(s32[8]{0:T(128)S(1)} %fusion.6.owners_ref, bf16[128,8192]{1,0:T(8,128)(2,1)S(1)} %copy-done, bf16[128,28672]{1,0:T(8,128)(2,1)} %grad_ref.7, bf16[128,8192]{1,0:T(8,128)(2,1)S(1)} %copy-done.2, bf16[128,28672]{1,0:T(8,128)(2,1)} %collective-permute-done.3.other_grad_ref, ...), custom_call_target="tpu_custom_call" | custom-call | flops 603979776 | bytes 4718592 | tf_op jit(solution)/shard_map/pallas_call | solution.py:114
  70.5 19.5 %collective-permute-done.6.refs_0_ = bf16[2304,256]{1,0:T(8,128)(2,1)S(1)} collective-permute-done((bf16[2304,256]{1,0:T(8,128)(2,1)}, bf16[2304,256]{1,0:T(8,128)(2,1)S(1)}, u32[]{:S(2)}, u32[]{:S(2)}) %collective-permute-start.6) | collective-permute-done | bytes 1179680 | tf_op jit(solution)/shard_map/ppermute | solution.py:214
  90.0 1.3 collective-permute-done.7.refs_1_
  91.4 1.6 %collective-permute-start.8 = (bf16[1152,256]{1,0:T(8,128)(2,1)S(1)}, bf16[1152,256]{1,0:T(8,128)(2,1)S(1)}, u32[]{:S(2)}, u32[]{:S(2)}) collective-permute-start(bf16[1152,256]{1,0:T(8,128)(2,1)S(1)} %slice.12), channel_id=1, source_target_pairs={{0,4},{1,5},{4,8},{5,9},{8,12},{9,13},{12,14},{13,15},{14,10},{15,... | collective-permute-start | bytes 1769480 | tf_op jit(solution)/shard_map/ppermute | solution.py:214
  93.0 0.6 collective-permute-start.9
  93.6 0.0 slice-start.1
  93.6 3.5 %shard_map.79 = (f32[128,512]{1,0:T(8,128)S(1)}, f32[128,512]{1,0:T(8,128)S(1)}) custom-call(s32[8]{0:T(128)S(1)} %fusion.6.owners_ref, bf16[128,8192]{1,0:T(8,128)(2,1)S(1)} %copy-done, bf16[128,28672]{1,0:T(8,128)(2,1)} %grad_ref.7, bf16[128,8192]{1,0:T(8,128)(2,1)S(1)} %copy-done.2, bf16[128,28672]{1,0:T(8,128)(2,1)} %collective-permute-done.3.other_grad_ref, ...), custom_call_target="tpu_custom_call" | custom-call | flops 603979776 | bytes 4718592 | tf_op jit(solution)/shard_map/pallas_call | solution.py:114
  97.1 6.1 %collective-permute-done.8.refs_0_ = bf16[1152,256]{1,0:T(8,128)(2,1)S(1)} collective-permute-done((bf16[1152,256]{1,0:T(8,128)(2,1)S(1)}, bf16[1152,256]{1,0:T(8,128)(2,1)S(1)}, u32[]{:S(2)}, u32[]{:S(2)}) %collective-permute-start.8) | collective-permute-done | bytes 589856 | tf_op jit(solution)/shard_map/ppermute | solution.py:214
  103.2 1.3 collective-permute-done.9.refs_1_
  104.5 2.5 %shard_map.80 = (f32[128,512]{1,0:T(8,128)S(1)}, f32[128,512]{1,0:T(8,128)S(1)}) custom-call(s32[8]{0:T(128)S(1)} %fusion.6.owners_ref, bf16[128,8192]{1,0:T(8,128)(2,1)S(1)} %copy-done, bf16[128,28672]{1,0:T(8,128)(2,1)S(1)} %bitcast.3, bf16[128,8192]{1,0:T(8,128)(2,1)S(1)} %copy-done.2, bf16[128,28672]{1,0:T(8,128)(2,1)} %collective-permute-done.3.other_grad_ref, ...), custom_call_target="tpu_custom_call" | custom-call | flops 301989888 | bytes 2359296 | tf_op jit(solution)/shard_map/pallas_call | solution.py:114
  107.0 0.1 collective-permute-start.10
  107.1 1.5 %collective-permute-done.10 = f32[128,512]{1,0:T(8,128)S(1)} collective-permute-done((f32[128,512]{1,0:T(8,128)S(1)}, f32[128,512]{1,0:T(8,128)S(1)}, u32[]{:S(2)}, u32[]{:S(2)}) %collective-permute-start.10) | collective-permute-done | bytes 262176 | tf_op jit(solution)/shard_map/ppermute | solution.py:214
  108.6 0.1 select_convert_fusion
  108.8 0.6 collective-permute-start.12
  109.3 1.5 %collective-permute-start.11 = (bf16[144,512]{1,0:T(8,128)(2,1)S(1)}, bf16[144,512]{1,0:T(8,128)(2,1)S(1)}, u32[]{:S(2)}, u32[]{:S(2)}) collective-permute-start(bf16[144,512]{1,0:T(8,128)(2,1)S(1)} %pad_maximum_fusion.refs_0_), channel_id=1, source_target_pairs={{0,4},{1,5},{4,8},{5,9},{8,12},{9,13},{12,14},{13,15},{14,10},{15,... | collective-permute-start | bytes 442376 | tf_op jit(solution)/shard_map/ppermute | solution.py:214
  110.8 3.9 %collective-permute-done.12.refs_2_ = bf16[144,512]{1,0:T(8,128)(2,1)S(1)} collective-permute-done((bf16[144,512]{1,0:T(8,128)(2,1)S(1)}, bf16[144,512]{1,0:T(8,128)(2,1)S(1)}, u32[]{:S(2)}, u32[]{:S(2)}) %collective-permute-start.12) | collective-permute-done | bytes 147488 | tf_op jit(solution)/shard_map/ppermute | solution.py:214
  114.7 0.5 collective-permute-start.14
  115.2 1.5 %collective-permute-start.13 = (bf16[144,512]{1,0:T(8,128)(2,1)S(1)}, bf16[144,512]{1,0:T(8,128)(2,1)S(1)}, u32[]{:S(2)}, u32[]{:S(2)}) collective-permute-start(bf16[144,512]{1,0:T(8,128)(2,1)S(1)} %collective-permute-done.11.refs_1_), channel_id=1, source_target_pairs={{0,4},{1,5},{4,8},{5,9},{8,12},{9,13},{12,14},{13,15},{14,10},{15,... | collective-permute-start | bytes 442376 | tf_op jit(solution)/shard_map/ppermute | solution.py:214
  116.7 3.1 %collective-permute-done.14.refs_4_ = bf16[144,512]{1,0:T(8,128)(2,1)S(1)} collective-permute-done((bf16[144,512]{1,0:T(8,128)(2,1)S(1)}, bf16[144,512]{1,0:T(8,128)(2,1)S(1)}, u32[]{:S(2)}, u32[]{:S(2)}) %collective-permute-start.14) | collective-permute-done | bytes 147488 | tf_op jit(solution)/shard_map/ppermute | solution.py:214
  119.8 0.5 collective-permute-start.16
  120.3 0.5 collective-permute-start.20
  120.9 1.5 %collective-permute-start.15 = (bf16[144,512]{1,0:T(8,128)(2,1)S(1)}, bf16[144,512]{1,0:T(8,128)(2,1)S(1)}, u32[]{:S(2)}, u32[]{:S(2)}) collective-permute-start(bf16[144,512]{1,0:T(8,128)(2,1)S(1)} %collective-permute-done.13.refs_3_), channel_id=1, source_target_pairs={{0,4},{1,5},{4,8},{5,9},{8,12},{9,13},{12,14},{13,15},{14,10},{15,... | collective-permute-start | bytes 442376 | tf_op jit(solution)/shard_map/ppermute | solution.py:214
  122.4 2.6 %collective-permute-done.16.refs_6_ = bf16[144,512]{1,0:T(8,128)(2,1)S(1)} collective-permute-done((bf16[144,512]{1,0:T(8,128)(2,1)S(1)}, bf16[144,512]{1,0:T(8,128)(2,1)S(1)}, u32[]{:S(2)}, u32[]{:S(2)}) %collective-permute-start.16) | collective-permute-done | bytes 147488 | tf_op jit(solution)/shard_map/ppermute | solution.py:214
  125.0 0.6 collective-permute-start.18
  125.6 0.2 collective-permute-start.23
  125.8 0.8 collective-permute-done.15.refs_5_
  126.6 0.5 collective-permute-start.25
  127.1 1.6 %collective-permute-start.17 = (bf16[64,512]{1,0:T(8,128)(2,1)S(1)}, bf16[64,512]{1,0:T(8,128)(2,1)S(1)}, u32[]{:S(2)}, u32[]{:S(2)}) collective-permute-start(bf16[64,512]{1,0:T(8,128)(2,1)S(1)} %slice.16), channel_id=1, source_target_pairs={{0,4},{1,5},{4,8},{5,9},{8,12},{9,13},{12,14},{13,15},{14,10},{15,... | collective-permute-start | bytes 196616 | tf_op jit(solution)/shard_map/ppermute | solution.py:214
  128.7 1.2 collective-permute-done.18.refs_8_
  129.9 1.6 %collective-permute-done.17.refs_7_ = bf16[64,512]{1,0:T(8,128)(2,1)S(1)} collective-permute-done((bf16[64,512]{1,0:T(8,128)(2,1)S(1)}, bf16[64,512]{1,0:T(8,128)(2,1)S(1)}, u32[]{:S(2)}, u32[]{:S(2)}) %collective-permute-start.17) | collective-permute-done | bytes 65568 | tf_op jit(solution)/shard_map/ppermute | solution.py:214
  131.5 1.2 collective-permute-done.26.refs_16_
  132.7 1.5 %shard_map.81 = (f32[16,256]{1,0:T(8,128)}, f32[1,64]{1,0:T(1,128)}) custom-call(s32[1]{0:T(128)} %bitcast.me_ref, bf16[144,512]{1,0:T(8,128)(2,1)S(1)} %pad_maximum_fusion.refs_0_, bf16[144,512]{1,0:T(8,128)(2,1)S(1)} %collective-permute-done.11.refs_1_, bf16[144,512]{1,0:T(8,128)(2,1)S(1)} %collective-permute-done.12.refs_2_, ...), custom_call_target="tpu_custom_call" | custom-call | tf_op jit(solution)/shard_map/pallas_call | solution.py:175
  (43 shorter events, 0.3 us)
Async XLA Ops:
  0.6 37.2 %copy-start.3 = (s32[8]{0:T(128)S(1)}, s32[8]{0:T(128)}, u32[]{:S(2)}) copy-start(s32[8]{0:T(128)} %constant.101) | copy-start | bytes 100
  0.6 2.9 %copy-start = (bf16[128,8192]{1,0:T(8,128)(2,1)S(1)}, bf16[128,8192]{1,0:T(8,128)(2,1)}, u32[]{:S(2)}) copy-start(bf16[128,8192]{1,0:T(8,128)(2,1)} %act_ref.7) | copy-start | bytes 6291460
  3.0 32.8 %collective-permute-start.3 = (bf16[128,28672]{1,0:T(8,128)(2,1)}, bf16[128,28672]{1,0:T(8,128)(2,1)}, u32[]{:S(2)}, u32[]{:S(2)}) collective-permute-start(bf16[128,28672]{1,0:T(8,128)(2,1)} %grad_ref.7), channel_id=1, source_target_pairs={{0,1},{1,0},{2,3},{3,2},{4,5},{5,4},{6,7},{7,6},{8,9},{9,8},{10,11... | collective-permute-start | bytes 22020104 | tf_op jit(solution)/shard_map/ppermute | solution.py:214
  3.5 30.9 %collective-permute-start.2 = (bf16[128,8192]{1,0:T(8,128)(2,1)S(1)}, bf16[128,8192]{1,0:T(8,128)(2,1)S(1)}, u32[]{:S(2)}, u32[]{:S(2)}) collective-permute-start(bf16[128,8192]{1,0:T(8,128)(2,1)S(1)} %copy-done), channel_id=1, source_target_pairs={{0,1},{1,0},{2,3},{3,2},{4,5},{5,4},{6,7},{7,6},{8,9},{9,8},{10,11... | collective-permute-start | bytes 6291464 | tf_op jit(solution)/shard_map/ppermute | solution.py:214
  3.6 29.3 %collective-permute-start = (bf16[2304,256]{1,0:T(8,128)(2,1)S(1)}, bf16[2304,256]{1,0:T(8,128)(2,1)}, u32[]{:S(2)}, u32[]{:S(2)}) collective-permute-start(bf16[2304,256]{1,0:T(8,128)(2,1)S(1)} %constant_dynamic-update-slice_fusion.refs_0_), channel_id=1, source_target_pairs={{0,4},{1,5},{4,8},{5,9},{8,12},{9,13},{12,14},{13,15},{14,10},{15,... | collective-permute-start | bytes 3538952 | tf_op jit(solution)/shard_map/ppermute | solution.py:214
  6.6 27.8 %collective-permute-start.1 = (bf16[2304,256]{1,0:T(8,128)(2,1)S(1)}, bf16[2304,256]{1,0:T(8,128)(2,1)}, u32[]{:S(2)}, u32[]{:S(2)}) collective-permute-start(bf16[2304,256]{1,0:T(8,128)(2,1)S(1)} %constant_dynamic-update-slice_fusion.refs_0_), channel_id=1, source_target_pairs={{0,2},{1,3},{4,0},{5,1},{8,4},{9,5},{12,8},{13,9},{14,12},{15,13},... | collective-permute-start | bytes 3538952 | tf_op jit(solution)/shard_map/ppermute | solution.py:214
  34.4 1.4 %copy-start.1 = (bf16[128,8192]{1,0:T(8,128)(2,1)}, bf16[128,8192]{1,0:T(8,128)(2,1)S(1)}, u32[]{:S(2)}) copy-start(bf16[128,8192]{1,0:T(8,128)(2,1)S(1)} %collective-permute-done.2.other_act_ref) | copy-start | bytes 6291460
  35.8 27.1 %collective-permute-start.4 = (bf16[2304,256]{1,0:T(8,128)(2,1)}, bf16[2304,256]{1,0:T(8,128)(2,1)}, u32[]{:S(2)}, u32[]{:S(2)}) collective-permute-start(bf16[2304,256]{1,0:T(8,128)(2,1)} %collective-permute-done.refs_1_), channel_id=1, source_target_pairs={{0,4},{1,5},{4,8},{5,9},{8,12},{9,13},{12,14},{13,15},{14,10},{15,... | collective-permute-start | bytes 3538952 | tf_op jit(solution)/shard_map/ppermute | solution.py:214
  37.4 26.8 %collective-permute-start.5 = (bf16[2304,256]{1,0:T(8,128)(2,1)}, bf16[2304,256]{1,0:T(8,128)(2,1)}, u32[]{:S(2)}, u32[]{:S(2)}) collective-permute-start(bf16[2304,256]{1,0:T(8,128)(2,1)} %collective-permute-done.1.refs_2_), channel_id=1, source_target_pairs={{0,2},{1,3},{4,0},{5,1},{8,4},{9,5},{12,8},{13,9},{14,12},{15,13},... | collective-permute-start | bytes 3538952 | tf_op jit(solution)/shard_map/ppermute | solution.py:214
  37.9 1.6 %copy-start.2 = (bf16[128,8192]{1,0:T(8,128)(2,1)S(1)}, bf16[128,8192]{1,0:T(8,128)(2,1)}, u32[]{:S(2)}) copy-start(bf16[128,8192]{1,0:T(8,128)(2,1)} %copy-done.1) | copy-start | bytes 6291460
  64.2 25.8 %collective-permute-start.6 = (bf16[2304,256]{1,0:T(8,128)(2,1)}, bf16[2304,256]{1,0:T(8,128)(2,1)S(1)}, u32[]{:S(2)}, u32[]{:S(2)}) collective-permute-start(bf16[2304,256]{1,0:T(8,128)(2,1)} %collective-permute-done.4.refs_0_), channel_id=1, source_target_pairs={{0,4},{1,5},{4,8},{5,9},{8,12},{9,13},{12,14},{13,15},{14,10},{15,... | collective-permute-start | bytes 3538952 | tf_op jit(solution)/shard_map/ppermute | solution.py:214
  65.8 25.5 %collective-permute-start.7 = (bf16[2304,256]{1,0:T(8,128)(2,1)}, bf16[2304,256]{1,0:T(8,128)(2,1)S(1)}, u32[]{:S(2)}, u32[]{:S(2)}) collective-permute-start(bf16[2304,256]{1,0:T(8,128)(2,1)} %collective-permute-done.5.refs_1_), channel_id=1, source_target_pairs={{0,2},{1,3},{4,0},{5,1},{8,4},{9,5},{12,8},{13,9},{14,12},{15,13},... | collective-permute-start | bytes 3538952 | tf_op jit(solution)/shard_map/ppermute | solution.py:214
  91.3 2.2 %copy-start.4 = (s32[128]{0:T(128)S(1)}, s32[128]{0:T(128)}, u32[]{:S(2)}) copy-start(s32[128]{0:T(128)} %param.8) | copy-start | bytes 1540
  91.4 11.8 %collective-permute-start.8 = (bf16[1152,256]{1,0:T(8,128)(2,1)S(1)}, bf16[1152,256]{1,0:T(8,128)(2,1)S(1)}, u32[]{:S(2)}, u32[]{:S(2)}) collective-permute-start(bf16[1152,256]{1,0:T(8,128)(2,1)S(1)} %slice.12), channel_id=1, source_target_pairs={{0,4},{1,5},{4,8},{5,9},{8,12},{9,13},{12,14},{13,15},{14,10},{15,... | collective-permute-start | bytes 1769480 | tf_op jit(solution)/shard_map/ppermute | solution.py:214
  93.0 11.5 %collective-permute-start.9 = (bf16[1152,256]{1,0:T(8,128)(2,1)S(1)}, bf16[1152,256]{1,0:T(8,128)(2,1)S(1)}, u32[]{:S(2)}, u32[]{:S(2)}) collective-permute-start(bf16[1152,256]{1,0:T(8,128)(2,1)S(1)} %slice.13), channel_id=1, source_target_pairs={{0,2},{1,3},{4,0},{5,1},{8,4},{9,5},{12,8},{13,9},{14,12},{15,13},... | collective-permute-start | bytes 1769480 | tf_op jit(solution)/shard_map/ppermute | solution.py:214
  93.6 11.0 %slice-start = ((s8[7340032]{0:T(1024)(128)(4,1)}), s8[4194304]{0:T(1024)(128)(4,1)S(1)}, s32[]{:S(2)}) async-start(s8[7340032]{0:T(1024)(128)(4,1)} %bitcast.2), calls=%async_computation | async-start | bytes 8388608
  93.6 10.9 %slice-start.1 = ((s8[7340032]{0:T(1024)(128)(4,1)}), s8[3145728]{0:T(1024)(128)(4,1)S(1)}, s32[]{:S(2)}) async-start(s8[7340032]{0:T(1024)(128)(4,1)} %bitcast.2), calls=%async_computation.1 | async-start | bytes 6291456
  107.0 1.6 %collective-permute-start.10 = (f32[128,512]{1,0:T(8,128)S(1)}, f32[128,512]{1,0:T(8,128)S(1)}, u32[]{:S(2)}, u32[]{:S(2)}) collective-permute-start(f32[128,512]{1,0:T(8,128)S(1)} %get-tuple-element.47), channel_id=1, source_target_pairs={{0,1},{1,0},{2,3},{3,2},{4,5},{5,4},{6,7},{7,6},{8,9},{9,8},{10,11... | collective-permute-start | bytes 786440 | tf_op jit(solution)/shard_map/ppermute | solution.py:214
  108.8 5.9 %collective-permute-start.12 = (bf16[144,512]{1,0:T(8,128)(2,1)S(1)}, bf16[144,512]{1,0:T(8,128)(2,1)S(1)}, u32[]{:S(2)}, u32[]{:S(2)}) collective-permute-start(bf16[144,512]{1,0:T(8,128)(2,1)S(1)} %pad_maximum_fusion.refs_0_), channel_id=1, source_target_pairs={{0,2},{1,3},{4,0},{5,1},{8,4},{9,5},{12,8},{13,9},{14,12},{15,13},... | collective-permute-start | bytes 442376 | tf_op jit(solution)/shard_map/ppermute | solution.py:214
  109.3 5.9 %collective-permute-start.11 = (bf16[144,512]{1,0:T(8,128)(2,1)S(1)}, bf16[144,512]{1,0:T(8,128)(2,1)S(1)}, u32[]{:S(2)}, u32[]{:S(2)}) collective-permute-start(bf16[144,512]{1,0:T(8,128)(2,1)S(1)} %pad_maximum_fusion.refs_0_), channel_id=1, source_target_pairs={{0,4},{1,5},{4,8},{5,9},{8,12},{9,13},{12,14},{13,15},{14,10},{15,... | collective-permute-start | bytes 442376 | tf_op jit(solution)/shard_map/ppermute | solution.py:214
  114.7 5.1 %collective-permute-start.14 = (bf16[144,512]{1,0:T(8,128)(2,1)S(1)}, bf16[144,512]{1,0:T(8,128)(2,1)S(1)}, u32[]{:S(2)}, u32[]{:S(2)}) collective-permute-start(bf16[144,512]{1,0:T(8,128)(2,1)S(1)} %collective-permute-done.12.refs_2_), channel_id=1, source_target_pairs={{0,2},{1,3},{4,0},{5,1},{8,4},{9,5},{12,8},{13,9},{14,12},{15,13},... | collective-permute-start | bytes 442376 | tf_op jit(solution)/shard_map/ppermute | solution.py:214
  115.2 5.7 %collective-permute-start.13 = (bf16[144,512]{1,0:T(8,128)(2,1)S(1)}, bf16[144,512]{1,0:T(8,128)(2,1)S(1)}, u32[]{:S(2)}, u32[]{:S(2)}) collective-permute-start(bf16[144,512]{1,0:T(8,128)(2,1)S(1)} %collective-permute-done.11.refs_1_), channel_id=1, source_target_pairs={{0,4},{1,5},{4,8},{5,9},{8,12},{9,13},{12,14},{13,15},{14,10},{15,... | collective-permute-start | bytes 442376 | tf_op jit(solution)/shard_map/ppermute | solution.py:214
  119.8 5.1 %collective-permute-start.16 = (bf16[144,512]{1,0:T(8,128)(2,1)S(1)}, bf16[144,512]{1,0:T(8,128)(2,1)S(1)}, u32[]{:S(2)}, u32[]{:S(2)}) collective-permute-start(bf16[144,512]{1,0:T(8,128)(2,1)S(1)} %collective-permute-done.14.refs_4_), channel_id=1, source_target_pairs={{0,2},{1,3},{4,0},{5,1},{8,4},{9,5},{12,8},{13,9},{14,12},{15,13},... | collective-permute-start | bytes 442376 | tf_op jit(solution)/shard_map/ppermute | solution.py:214
  120.3 4.7 %collective-permute-start.19 = (bf16[144,512]{1,0:T(8,128)(2,1)S(1)}, bf16[144,512]{1,0:T(8,128)(2,1)S(1)}, u32[]{:S(2)}, u32[]{:S(2)}) collective-permute-start(bf16[144,512]{1,0:T(8,128)(2,1)S(1)} %pad_maximum_fusion.refs_0_), channel_id=1, source_target_pairs={{0,1},{1,0},{2,3},{3,2},{4,5},{5,4},{6,7},{7,6},{8,9},{9,8},{10,11... | collective-permute-start | bytes 442376 | tf_op jit(solution)/shard_map/ppermute | solution.py:214
  120.3 5.2 %collective-permute-start.20 = (bf16[144,512]{1,0:T(8,128)(2,1)S(1)}, bf16[144,512]{1,0:T(8,128)(2,1)S(1)}, u32[]{:S(2)}, u32[]{:S(2)}) collective-permute-start(bf16[144,512]{1,0:T(8,128)(2,1)S(1)} %collective-permute-done.11.refs_1_), channel_id=1, source_target_pairs={{0,1},{1,0},{2,3},{3,2},{4,5},{5,4},{6,7},{7,6},{8,9},{9,8},{10,11... | collective-permute-start | bytes 442376 | tf_op jit(solution)/shard_map/ppermute | solution.py:214
  120.9 5.8 %collective-permute-start.15 = (bf16[144,512]{1,0:T(8,128)(2,1)S(1)}, bf16[144,512]{1,0:T(8,128)(2,1)S(1)}, u32[]{:S(2)}, u32[]{:S(2)}) collective-permute-start(bf16[144,512]{1,0:T(8,128)(2,1)S(1)} %collective-permute-done.13.refs_3_), channel_id=1, source_target_pairs={{0,4},{1,5},{4,8},{5,9},{8,12},{9,13},{12,14},{13,15},{14,10},{15,... | collective-permute-start | bytes 442376 | tf_op jit(solution)/shard_map/ppermute | solution.py:214
  122.4 4.2 %collective-permute-start.21 = (bf16[144,512]{1,0:T(8,128)(2,1)S(1)}, bf16[144,512]{1,0:T(8,128)(2,1)S(1)}, u32[]{:S(2)}, u32[]{:S(2)}) collective-permute-start(bf16[144,512]{1,0:T(8,128)(2,1)S(1)} %collective-permute-done.12.refs_2_), channel_id=1, source_target_pairs={{0,1},{1,0},{2,3},{3,2},{4,5},{5,4},{6,7},{7,6},{8,9},{9,8},{10,11... | collective-permute-start | bytes 442376 | tf_op jit(solution)/shard_map/ppermute | solution.py:214
  125.0 2.2 %collective-permute-start.22 = (bf16[144,512]{1,0:T(8,128)(2,1)S(1)}, bf16[144,512]{1,0:T(8,128)(2,1)S(1)}, u32[]{:S(2)}, u32[]{:S(2)}) collective-permute-start(bf16[144,512]{1,0:T(8,128)(2,1)S(1)} %collective-permute-done.13.refs_3_), channel_id=1, source_target_pairs={{0,1},{1,0},{2,3},{3,2},{4,5},{5,4},{6,7},{7,6},{8,9},{9,8},{10,11... | collective-permute-start | bytes 442376 | tf_op jit(solution)/shard_map/ppermute | solution.py:214
  125.0 4.9 %collective-permute-start.18 = (bf16[80,512]{1,0:T(8,128)(2,1)S(1)}, bf16[80,512]{1,0:T(8,128)(2,1)S(1)}, u32[]{:S(2)}, u32[]{:S(2)}) collective-permute-start(bf16[80,512]{1,0:T(8,128)(2,1)S(1)} %slice.17), channel_id=1, source_target_pairs={{0,2},{1,3},{4,0},{5,1},{8,4},{9,5},{12,8},{13,9},{14,12},{15,13},... | collective-permute-start | bytes 245768 | tf_op jit(solution)/shard_map/ppermute | solution.py:214
  125.6 5.9 %collective-permute-start.23 = (bf16[144,512]{1,0:T(8,128)(2,1)S(1)}, bf16[144,512]{1,0:T(8,128)(2,1)S(1)}, u32[]{:S(2)}, u32[]{:S(2)}) collective-permute-start(bf16[144,512]{1,0:T(8,128)(2,1)S(1)} %collective-permute-done.14.refs_4_), channel_id=1, source_target_pairs={{0,1},{1,0},{2,3},{3,2},{4,5},{5,4},{6,7},{7,6},{8,9},{9,8},{10,11... | collective-permute-start | bytes 442376 | tf_op jit(solution)/shard_map/ppermute | solution.py:214
  126.6 6.1 %collective-permute-start.24 = (bf16[144,512]{1,0:T(8,128)(2,1)S(1)}, bf16[144,512]{1,0:T(8,128)(2,1)S(1)}, u32[]{:S(2)}, u32[]{:S(2)}) collective-permute-start(bf16[144,512]{1,0:T(8,128)(2,1)S(1)} %collective-permute-done.15.refs_5_), channel_id=1, source_target_pairs={{0,1},{1,0},{2,3},{3,2},{4,5},{5,4},{6,7},{7,6},{8,9},{9,8},{10,11... | collective-permute-start | bytes 442376 | tf_op jit(solution)/shard_map/ppermute | solution.py:214
  126.6 6.1 %collective-permute-start.25 = (bf16[144,512]{1,0:T(8,128)(2,1)S(1)}, bf16[144,512]{1,0:T(8,128)(2,1)S(1)}, u32[]{:S(2)}, u32[]{:S(2)}) collective-permute-start(bf16[144,512]{1,0:T(8,128)(2,1)S(1)} %collective-permute-done.16.refs_6_), channel_id=1, source_target_pairs={{0,1},{1,0},{2,3},{3,2},{4,5},{5,4},{6,7},{7,6},{8,9},{9,8},{10,11... | collective-permute-start | bytes 442376 | tf_op jit(solution)/shard_map/ppermute | solution.py:214
  127.1 4.3 %collective-permute-start.17 = (bf16[64,512]{1,0:T(8,128)(2,1)S(1)}, bf16[64,512]{1,0:T(8,128)(2,1)S(1)}, u32[]{:S(2)}, u32[]{:S(2)}) collective-permute-start(bf16[64,512]{1,0:T(8,128)(2,1)S(1)} %slice.16), channel_id=1, source_target_pairs={{0,4},{1,5},{4,8},{5,9},{8,12},{9,13},{12,14},{13,15},{14,10},{15,... | collective-permute-start | bytes 196616 | tf_op jit(solution)/shard_map/ppermute | solution.py:214
  129.9 2.8 %collective-permute-start.27 = (bf16[80,512]{1,0:T(8,128)(2,1)S(1)}, bf16[80,512]{1,0:T(8,128)(2,1)S(1)}, u32[]{:S(2)}, u32[]{:S(2)}) collective-permute-start(bf16[80,512]{1,0:T(8,128)(2,1)S(1)} %collective-permute-done.18.refs_8_), channel_id=1, source_target_pairs={{0,1},{1,0},{2,3},{3,2},{4,5},{5,4},{6,7},{7,6},{8,9},{9,8},{10,11... | collective-permute-start | bytes 245768 | tf_op jit(solution)/shard_map/ppermute | solution.py:214
  131.5 1.3 collective-permute-start.26

commit v3 on v2

--- a/solution.py
+++ b/solution.py
@@ -71,62 +71,67 @@
     return found
 
 
-def project_kernel(parts, depths, owners_ref, act_ref, grad_ref, other_act_ref, other_grad_ref, *refs):
-    panels, (mine_ref, theirs_ref, mine_out, theirs_out, block, sems) = (
-        refs[: len(parts)],
-        refs[len(parts) :],
-    )
-    rows, width = act_ref.shape[0], panels[0].shape[1]
-    sources = ((act_ref, other_act_ref), (grad_ref, other_grad_ref))
-    work, at, index = [], 0, 0
+def project_kernel(kinds, parts, depths, owners_ref, *refs):
+    sources, refs = refs[: 2 * len(kinds)], refs[2 * len(kinds) :]
+    panels, refs = refs[: len(parts)], refs[len(parts) :]
+    before, (mine_out, theirs_out, block, sems) = refs[: 2 * len(kinds)], refs[2 * len(kinds) :]
+    rows, width = sources[0].shape[0], panels[0].shape[1]
+    work, at = [], 0
     for (slot, first), panel in zip(parts, panels):
         for kind, start, count, within in runs(first, panel.shape[0], *depths):
+            if kind not in kinds:
+                continue
             column = pl.multiple_of(owners_ref[slot] * depths[kind] + start, 128)
             copies = []
-            for j, source in enumerate(sources[kind]):
+            for j in range(2):
                 copy = pltpu.make_async_copy(
-                    source.at[:, pl.ds(column, count)],
+                    sources[2 * kinds.index(kind) + j].at[:, pl.ds(column, count)],
                     block.at[pl.ds(j * rows, rows), pl.ds(at, count)],
-                    sems.at[index, j],
+                    sems.at[len(work), j],
                 )
                 copy.start()
                 copies.append(copy)
             work.append((kind, at, count, panel.at[pl.ds(within, count), :], copies))
             at += count
-            index += 1
-    totals = [0.0, 0.0]
+    totals = {}
     for kind, at, count, panel, copies in work:
         for copy in copies:
             copy.wait()
-        totals[kind] += dot(block[:, at : at + count], panel[...])
-    for kind, total in enumerate(totals):
-        columns = slice(kind * width, (kind + 1) * width)
-        mine_out[:, columns] = mine_ref[:, columns] + total[:rows]
-        theirs_out[:, columns] = theirs_ref[:, columns] + total[rows:]
-
-
-def project(owners, tokens, parts, before, depth_in, depth_out):
-    rows, width = tokens[0].shape[0], parts[0][2].shape[1]
+        totals[kind] = totals.get(kind, 0.0) + dot(block[:, at : at + count], panel[...])
+    for i, kind in enumerate(kinds):
+        columns = slice(i * width, (i + 1) * width)
+        mine_out[:, columns] = before[2 * i][...] + totals[kind][:rows]
+        theirs_out[:, columns] = before[2 * i + 1][...] + totals[kind][rows:]
+
+
+def project(owners, kinds, tokens, parts, before, depths):
+    sources = [x for kind in kinds for x in tokens[kind]]
+    rows, width = sources[0].shape[0], parts[0][2].shape[1]
     panels = [p[2] for p in parts]
-    depth = sum(p.shape[0] for p in panels)
+    counts = [
+        run[2] for p in parts for run in runs(p[1], p[2].shape[0], *depths) if run[0] in kinds
+    ]
     vmem = pl.BlockSpec(memory_space=pltpu.VMEM)
-    total = jax.ShapeDtypeStruct((rows, 2 * width), jnp.float32)
+    total = jax.ShapeDtypeStruct((rows, len(kinds) * width), jnp.float32)
     return pl.pallas_call(
-        functools.partial(project_kernel, [p[:2] for p in parts], (depth_in, depth_out)),
+        functools.partial(project_kernel, kinds, [p[:2] for p in parts], depths),
         out_shape=(total, total),
         in_specs=[pl.BlockSpec(memory_space=pltpu.SMEM)]
-        + [pl.BlockSpec(memory_space=pl.ANY)] * 4
-        + [vmem] * (len(parts) + 2),
+        + [pl.BlockSpec(memory_space=pl.ANY)] * len(sources)
+        + [vmem] * (len(parts) + len(before)),
         out_specs=(vmem, vmem),
         scratch_shapes=[
-            pltpu.VMEM((2 * rows, depth), tokens[0].dtype),
-            pltpu.SemaphoreType.DMA((2 * len(parts), 2)),
+            pltpu.VMEM((2 * rows, sum(counts)), sources[0].dtype),
+            pltpu.SemaphoreType.DMA((len(counts), 2)),
         ],
-        compiler_params=pltpu.CompilerParams(vmem_limit_bytes=40 * 2**20),
-        cost_estimate=pl.CostEstimate(
-            flops=4 * rows * depth * width, bytes_accessed=8 * rows * depth, transcendentals=0
-        ),
-    )(owners, *tokens, *panels, *before)
+        compiler_params=pltpu.CompilerParams(vmem_limit_bytes=16 * 2**20),
+        cost_estimate=pl.CostEstimate(flops=1, bytes_accessed=1, transcendentals=0),
+    )(
+        owners,
+        *[pltpu.with_memory_space_constraint(x, pltpu.HBM) for x in sources],
+        *[pltpu.with_memory_space_constraint(x, pltpu.VMEM) for x in panels],
+        *before,
+    )
 
 
 def last_kernel(scale, rows, me_ref, *refs):
@@ -184,7 +189,7 @@
             pltpu.VMEM((devices * rows, width), jnp.bfloat16),
             pltpu.VMEM((out_panel, in_panel), jnp.float32),
         ],
-        compiler_params=pltpu.CompilerParams(vmem_limit_bytes=40 * 2**20),
+        compiler_params=pltpu.CompilerParams(vmem_limit_bytes=16 * 2**20),
     )(me, *pieces)
     return corrected, score.reshape(balanced)
 
@@ -226,40 +231,48 @@
         from_position < half, 2 * from_position, 2 * (chips - 1 - from_position) + 1
     ) * 2 + own_index % 2
 
-    shard = {0: jnp.concatenate([basis_in, basis_out], axis=0)}
-    depth = depth_in + depth_out
-    cut = depth // 2
-
-    def pieces(d, first, panel):
-        return [(distances.index(d), first, panel)]
-
-    def pair(s):
-        return send(shard[s - 1], forward), send(shard[1 - s], backward)
-
-    shard[1], shard[-1] = pair(1)
-    ready_act, ready_grad, _ = lax.optimization_barrier((activations, out_grads, shard[0]))
-    swapped_act, swapped_grad = send(ready_act, swap), send(ready_grad, swap)
-    shard[1], shard[-1], swapped_act, swapped_grad = lax.optimization_barrier(
-        (shard[1], shard[-1], swapped_act, swapped_grad)
-    )
-    tokens = (activations, out_grads, swapped_act, swapped_grad)
-    totals = [jnp.zeros((rows, 2 * width), jnp.float32)] * 2
+    cut = (depth_in + depth_out) // 2
+    first = {0: jnp.concatenate([basis_in, basis_out[: cut - depth_in]], axis=0)}
+    second = {0: basis_out[cut - depth_in :]}
+
+    def hop(ahead, behind, s):
+        ahead[s] = send(ahead[s - 1], forward)
+        behind[-s] = send(behind[1 - s], backward)
+
+    def pieces(held, at):
+        return [(distances.index(d), 0 if held is first else cut, held[d]) for d in at]
+
+    def add(kinds, parts, totals):
+        tokens = [(activations, swapped_act), (out_grads, swapped_grad)]
+        return list(project(owners, kinds, tokens, parts, totals, (depth_in, depth_out)))
+
+    def after(held, at, totals):
+        got = lax.optimization_barrier(tuple(held[d] for d in at) + tuple(totals))
+        for d, x in zip(at, got):
+            held[d] = x
+        return list(got[len(at) :])
+
+    hop(first, second, 1)
+    hop(second, first, 1)
+    swapped_grad, swapped_act = send(out_grads, swap), None
+    zero = jnp.zeros((rows, width), jnp.float32)
+    grad = [zero, zero]
     for s in range(1, half):
-        parts = pieces(s, 0, shard[s]) + pieces(-s, 0, shard[-s])
-        if s == 1:
-            parts = pieces(0, 0, shard[0]) + parts
+        own = pieces(first, [0]) + pieces(second, [0]) if s == 1 else []
         if s + 1 < half:
-            shard[s + 1], shard[-s - 1] = pair(s + 1)
+            hop(first, second, s + 1)
         else:
-            upper = send(shard[s][cut:], forward)
-            lower = send(shard[-s][:cut], backward)
-        totals = project(owners, tokens, parts, totals, depth_in, depth_out)
+            first[half], second[half] = send(first[s], forward), send(second[-s], backward)
+        grad = add((1,), own + pieces(first, [s]) + pieces(second, [-s]), grad)
+        grad = after(second, [s], after(first, [-s], grad))
         if s + 1 < half:
-            shard[s + 1], shard[-s - 1], *totals = lax.optimization_barrier(
-                (shard[s + 1], shard[-s - 1], *totals)
-            )
-    parts = pieces(half, cut, upper) + pieces(half, 0, lower)
-    mine, theirs = project(owners, tokens, parts, totals, depth_in, depth_out)
+            hop(second, first, s + 1)
+        grad = add((1,), pieces(second, [s]) + pieces(first, [-s]), grad)
+        if s + 1 < half:
+            grad = after(first, [s + 1], after(second, [-s - 1], grad))
+    swapped_act = send(activations, swap)
+    act = add((0,), pieces(first, distances[:-1]), [zero, zero])
+    mine, theirs = add((0, 1), pieces(first, [half]) + pieces(second, [half]), act + grad)
 
     is_valid = slot_of_row >= 0
     owner = jnp.where(is_valid, slot_of_row // balanced, -1)

time: 135 us -> 129 us (0.956)
  waiting for transfers between devices: 91.7 us -> 77.2 us
  starting transfers between devices: 19.4 us -> 26.4 us
  Pallas kernels: 16.7 us -> 22.2 us
  local copies, waits for them, and re-layouts: 5.46 us -> 1.07 us
    ppermute x28 -> x34, waiting for transfers between devices: 91.7 us -> 77.2 us  [send(): return lax.ppermute(x, 'dp', pairs)]
    ppermute x28 -> x34, starting transfers between devices: 19.4 us -> 26.4 us  [send(): return lax.ppermute(x, 'dp', pairs)]
    pallas_call x4 -> x8, Pallas kernels: 15.2 us -> 20.7 us  [project(): pl.pallas_call(functools.partial(project_kernel, kinds, [p[:2] for p in p...]
    unnamed x15 -> x6, local copies, waits for them, and re-layouts: 4.11 us -> 0.01 us
  transfers between devices with their start and end apart: 28 -> 34, of which waited for: 16 -> 20; matrix products, arithmetic and copies ran while one was open for 0% -> 2% of each run, Pallas kernels for 9% -> 14%
where the time goes in v3:
time: 129 us
  waiting for transfers between devices  77.2 us (60%)
  starting transfers between devices  26.4 us (20%)
  Pallas kernels  22.2 us (17%)
    ppermute x34, waiting for transfers between devices, send(): return lax.ppermute(x, 'dp', pairs)  77.2 us
    ppermute x34, starting transfers between devices, send(): return lax.ppermute(x, 'dp', pairs)  26.4 us
    pallas_call x8, Pallas kernels, project(): pl.pallas_call(functools.partial(project_kernel, kinds, [p[:2] for p in p...  20.7 us
  transfers between devices with their start and end apart: 34, of which 20 were waited for; matrix products, arithmetic and copies ran while one was open for 2% of the time, Pallas kernels for 14%

profile of v3, /device:TPU:0, one launch (start us, length us, event | category | flops | bytes accessed | tf_op | source)
XLA Modules:
  0.0 128.9 jit_solution(1623362911933054961)
XLA Ops:
  0.7 0.5 collective-permute-start.1
  1.2 1.0 slice.12
  2.2 1.0 pad_maximum_fusion.refs_2_
  3.2 2.7 %collective-permute-start.2 = (bf16[1152,256]{1,0:T(8,128)(2,1)S(1)}, bf16[1152,256]{1,0:T(8,128)(2,1)S(1)}, u32[]{:S(2)}, u32[]{:S(2)}) collective-permute-start(bf16[1152,256]{1,0:T(8,128)(2,1)S(1)} %pad_maximum_fusion.refs_2_), channel_id=1, source_target_pairs={{0,4},{1,5},{4,8},{5,9},{8,12},{9,13},{12,14},{13,15},{14,10},{15,... | collective-permute-start | bytes 1769480 | tf_op jit(solution)/shard_map/ppermute | solution.py:219
  6.2 1.7 %collective-permute-start.7 = (bf16[1152,256]{1,0:T(8,128)(2,1)S(1)}, bf16[1152,256]{1,0:T(8,128)(2,1)S(1)}, u32[]{:S(2)}, u32[]{:S(2)}) collective-permute-start(bf16[1152,256]{1,0:T(8,128)(2,1)S(1)} %pad_maximum_fusion.refs_2_), channel_id=1, source_target_pairs={{0,2},{1,3},{4,0},{5,1},{8,4},{9,5},{12,8},{13,9},{14,12},{15,13},... | collective-permute-start | bytes 1769480 | tf_op jit(solution)/shard_map/ppermute | solution.py:219
  7.9 11.8 %collective-permute-done.2.refs_4_.refs_3_ = bf16[1152,256]{1,0:T(8,128)(2,1)S(1)} collective-permute-done((bf16[1152,256]{1,0:T(8,128)(2,1)S(1)}, bf16[1152,256]{1,0:T(8,128)(2,1)S(1)}, u32[]{:S(2)}, u32[]{:S(2)}) %collective-permute-start.2) | collective-permute-done | bytes 589856 | tf_op jit(solution)/shard_map/ppermute | solution.py:219
  19.7 1.8 %collective-permute-start.6 = (bf16[1152,256]{1,0:T(8,128)(2,1)S(1)}, bf16[1152,256]{1,0:T(8,128)(2,1)}, u32[]{:S(2)}, u32[]{:S(2)}) collective-permute-start(bf16[1152,256]{1,0:T(8,128)(2,1)S(1)} %slice.13.refs_3_), channel_id=1, source_target_pairs={{0,4},{1,5},{4,8},{5,9},{8,12},{9,13},{12,14},{13,15},{14,10},{15,... | collective-permute-start | bytes 1769480 | tf_op jit(solution)/shard_map/ppermute | solution.py:219
  21.5 0.7 collective-permute-done.4.refs_5_
  22.3 2.0 %collective-permute-start.3 = (bf16[1152,256]{1,0:T(8,128)(2,1)S(1)}, bf16[1152,256]{1,0:T(8,128)(2,1)S(1)}, u32[]{:S(2)}, u32[]{:S(2)}) collective-permute-start(bf16[1152,256]{1,0:T(8,128)(2,1)S(1)} %collective-permute-done.2.refs_4_.refs_3_), channel_id=1, source_target_pairs={{0,4},{1,5},{4,8},{5,9},{8,12},{9,13},{12,14},{13,15},{14,10},{15,... | collective-permute-start | bytes 1769480 | tf_op jit(solution)/shard_map/ppermute | solution.py:219
  24.3 3.7 %shard_map.77 = (f32[128,256]{1,0:T(8,128)S(1)}, f32[128,256]{1,0:T(8,128)S(1)}) custom-call(s32[8]{0:T(128)S(1)} %fusion.6.owners_ref, bf16[128,28672]{1,0:T(8,128)(2,1)} %refs_2_.1, bf16[128,28672]{1,0:T(8,128)(2,1)} %collective-permute-done.1.refs_1_.refs_3_, bf16[1152,256]{1,0:T(8,128)(2,1)S(1)} %pad_maximum_fusion.refs_2_, ...), custom_call_target="tpu_custom_call" | custom-call | flops 1 | bytes 1 | tf_op jit(solution)/shard_map/pallas_call | solution.py:116
  28.0 6.8 %collective-permute-done.7.refs_3_.refs_4_ = bf16[1152,256]{1,0:T(8,128)(2,1)S(1)} collective-permute-done((bf16[1152,256]{1,0:T(8,128)(2,1)S(1)}, bf16[1152,256]{1,0:T(8,128)(2,1)S(1)}, u32[]{:S(2)}, u32[]{:S(2)}) %collective-permute-start.7) | collective-permute-done | bytes 589856 | tf_op jit(solution)/shard_map/ppermute | solution.py:219
  34.8 1.3 collective-permute-done.6.refs_2_
  36.0 1.8 %collective-permute-start.10 = (bf16[1152,256]{1,0:T(8,128)(2,1)}, bf16[1152,256]{1,0:T(8,128)(2,1)S(1)}, u32[]{:S(2)}, u32[]{:S(2)}) collective-permute-start(bf16[1152,256]{1,0:T(8,128)(2,1)} %collective-permute-done.6.refs_2_), channel_id=1, source_target_pairs={{0,4},{1,5},{4,8},{5,9},{8,12},{9,13},{12,14},{13,15},{14,10},{15,... | collective-permute-start | bytes 1769480 | tf_op jit(solution)/shard_map/ppermute | solution.py:219
  37.9 2.7 %shard_map.78 = (f32[128,256]{1,0:T(8,128)S(1)}, f32[128,256]{1,0:T(8,128)S(1)}) custom-call(s32[8]{0:T(128)S(1)} %fusion.6.owners_ref, bf16[128,28672]{1,0:T(8,128)(2,1)} %refs_2_.1, bf16[128,28672]{1,0:T(8,128)(2,1)} %collective-permute-done.1.refs_1_.refs_3_, bf16[1152,256]{1,0:T(8,128)(2,1)} %collective-permute-done.6.refs_2_, ...), custom_call_target="tpu_custom_call" | custom-call | flops 1 | bytes 1 | tf_op jit(solution)/shard_map/pallas_call | solution.py:116
  40.6 6.8 %collective-permute-done.5.refs_3_ = bf16[1152,256]{1,0:T(8,128)(2,1)S(1)} collective-permute-done((bf16[1152,256]{1,0:T(8,128)(2,1)}, bf16[1152,256]{1,0:T(8,128)(2,1)S(1)}, u32[]{:S(2)}, u32[]{:S(2)}) %collective-permute-start.5) | collective-permute-done | bytes 589856 | tf_op jit(solution)/shard_map/ppermute | solution.py:219
  47.4 1.1 collective-permute-done.3.refs_2_.refs_5_
  48.6 1.8 %collective-permute-start.8 = (bf16[1152,256]{1,0:T(8,128)(2,1)S(1)}, bf16[1152,256]{1,0:T(8,128)(2,1)S(1)}, u32[]{:S(2)}, u32[]{:S(2)}) collective-permute-start(bf16[1152,256]{1,0:T(8,128)(2,1)S(1)} %collective-permute-done.3.refs_2_.refs_5_), channel_id=1, source_target_pairs={{0,4},{1,5},{4,8},{5,9},{8,12},{9,13},{12,14},{13,15},{14,10},{15,... | collective-permute-start | bytes 1769480 | tf_op jit(solution)/shard_map/ppermute | solution.py:219
  50.4 2.2 %shard_map.79 = (f32[128,256]{1,0:T(8,128)S(1)}, f32[128,256]{1,0:T(8,128)S(1)}) custom-call(s32[8]{0:T(128)S(1)} %fusion.6.owners_ref, bf16[128,28672]{1,0:T(8,128)(2,1)} %refs_2_.1, bf16[128,28672]{1,0:T(8,128)(2,1)} %collective-permute-done.1.refs_1_.refs_3_, bf16[1152,256]{1,0:T(8,128)(2,1)S(1)} %collective-permute-done.3.refs_2_.refs_5_, ...), custom_call_target="tpu_custom_call" | custom-call | flops 1 | bytes 1 | tf_op jit(solution)/shard_map/pallas_call | solution.py:116
  52.7 7.4 %collective-permute-done.11.refs_3_.refs_6_ = bf16[1152,256]{1,0:T(8,128)(2,1)S(1)} collective-permute-done((bf16[1152,256]{1,0:T(8,128)(2,1)S(1)}, bf16[1152,256]{1,0:T(8,128)(2,1)S(1)}, u32[]{:S(2)}, u32[]{:S(2)}) %collective-permute-start.11) | collective-permute-done | bytes 589856 | tf_op jit(solution)/shard_map/ppermute | solution.py:219
  60.1 1.1 collective-permute-done.10.refs_2_
  61.2 1.8 %collective-permute-start.14 = (bf16[1152,256]{1,0:T(8,128)(2,1)S(1)}, bf16[1152,256]{1,0:T(8,128)(2,1)S(1)}, u32[]{:S(2)}, u32[]{:S(2)}) collective-permute-start(bf16[1152,256]{1,0:T(8,128)(2,1)S(1)} %collective-permute-done.11.refs_3_.refs_6_), channel_id=1, source_target_pairs={{0,2},{1,3},{4,0},{5,1},{8,4},{9,5},{12,8},{13,9},{14,12},{15,13},... | collective-permute-start | bytes 1769480 | tf_op jit(solution)/shard_map/ppermute | solution.py:219
  63.2 2.2 %shard_map.80 = (f32[128,256]{1,0:T(8,128)S(1)}, f32[128,256]{1,0:T(8,128)S(1)}) custom-call(s32[8]{0:T(128)S(1)} %fusion.6.owners_ref, bf16[128,28672]{1,0:T(8,128)(2,1)} %refs_2_.1, bf16[128,28672]{1,0:T(8,128)(2,1)} %collective-permute-done.1.refs_1_.refs_3_, bf16[1152,256]{1,0:T(8,128)(2,1)S(1)} %collective-permute-done.10.refs_2_, ...), custom_call_target="tpu_custom_call" | custom-call | flops 1 | bytes 1 | tf_op jit(solution)/shard_map/pallas_call | solution.py:116
  65.4 7.3 %collective-permute-done.9.refs_3_ = bf16[1152,256]{1,0:T(8,128)(2,1)S(1)} collective-permute-done((bf16[1152,256]{1,0:T(8,128)(2,1)S(1)}, bf16[1152,256]{1,0:T(8,128)(2,1)S(1)}, u32[]{:S(2)}, u32[]{:S(2)}) %collective-permute-start.9) | collective-permute-done | bytes 589856 | tf_op jit(solution)/shard_map/ppermute | solution.py:219
  72.7 1.2 collective-permute-done.8.refs_2_.refs_7_
  73.9 1.8 %collective-permute-start.12 = (bf16[1152,256]{1,0:T(8,128)(2,1)S(1)}, bf16[1152,256]{1,0:T(8,128)(2,1)S(1)}, u32[]{:S(2)}, u32[]{:S(2)}) collective-permute-start(bf16[1152,256]{1,0:T(8,128)(2,1)S(1)} %collective-permute-done.8.refs_2_.refs_7_), channel_id=1, source_target_pairs={{0,4},{1,5},{4,8},{5,9},{8,12},{9,13},{12,14},{13,15},{14,10},{15,... | collective-permute-start | bytes 1769480 | tf_op jit(solution)/shard_map/ppermute | solution.py:219
  75.9 2.2 %shard_map.81 = (f32[128,256]{1,0:T(8,128)S(1)}, f32[128,256]{1,0:T(8,128)S(1)}) custom-call(s32[8]{0:T(128)S(1)} %fusion.6.owners_ref, bf16[128,28672]{1,0:T(8,128)(2,1)} %refs_2_.1, bf16[128,28672]{1,0:T(8,128)(2,1)} %collective-permute-done.1.refs_1_.refs_3_, bf16[1152,256]{1,0:T(8,128)(2,1)S(1)} %collective-permute-done.8.refs_2_.refs_7_, ...), custom_call_target="tpu_custom_call" | custom-call | flops 1 | bytes 1 | tf_op jit(solution)/shard_map/pallas_call | solution.py:116
  78.2 7.2 %collective-permute-done.14.refs_8_.refs_3_ = bf16[1152,256]{1,0:T(8,128)(2,1)S(1)} collective-permute-done((bf16[1152,256]{1,0:T(8,128)(2,1)S(1)}, bf16[1152,256]{1,0:T(8,128)(2,1)S(1)}, u32[]{:S(2)}, u32[]{:S(2)}) %collective-permute-start.14) | collective-permute-done | bytes 589856 | tf_op jit(solution)/shard_map/ppermute | solution.py:219
  85.3 3.1 %shard_map.82 = (f32[128,256]{1,0:T(8,128)S(1)}, f32[128,256]{1,0:T(8,128)S(1)}) custom-call(s32[8]{0:T(128)S(1)} %fusion.6.owners_ref, bf16[128,8192]{1,0:T(8,128)(2,1)} %refs_0_.15, bf16[128,8192]{1,0:T(8,128)(2,1)} %collective-permute-done.refs_1_, bf16[1152,256]{1,0:T(8,128)(2,1)S(1)} %pad_maximum_fusion.refs_2_, ...), custom_call_target="tpu_custom_call" | custom-call | flops 1 | bytes 1 | tf_op jit(solution)/shard_map/pallas_call | solution.py:116
  88.5 2.2 %shard_map.83 = (f32[128,256]{1,0:T(8,128)S(1)}, f32[128,256]{1,0:T(8,128)S(1)}) custom-call(s32[8]{0:T(128)S(1)} %fusion.6.owners_ref, bf16[128,28672]{1,0:T(8,128)(2,1)} %refs_2_.1, bf16[128,28672]{1,0:T(8,128)(2,1)} %collective-permute-done.1.refs_1_.refs_3_, bf16[1152,256]{1,0:T(8,128)(2,1)S(1)} %collective-permute-done.15.refs_2_, ...), custom_call_target="tpu_custom_call" | custom-call | flops 1 | bytes 1 | tf_op jit(solution)/shard_map/pallas_call | solution.py:116
  90.6 7.5 %collective-permute-done.12.refs_4_ = bf16[1152,256]{1,0:T(8,128)(2,1)S(1)} collective-permute-done((bf16[1152,256]{1,0:T(8,128)(2,1)S(1)}, bf16[1152,256]{1,0:T(8,128)(2,1)S(1)}, u32[]{:S(2)}, u32[]{:S(2)}) %collective-permute-start.12) | collective-permute-done | bytes 589856 | tf_op jit(solution)/shard_map/ppermute | solution.py:219
  98.1 2.5 %shard_map.84 = (f32[128,512]{1,0:T(8,128)S(1)}, f32[128,512]{1,0:T(8,128)S(1)}) custom-call(s32[8]{0:T(128)S(1)} %fusion.6.owners_ref, bf16[128,8192]{1,0:T(8,128)(2,1)} %refs_0_.15, bf16[128,8192]{1,0:T(8,128)(2,1)} %collective-permute-done.refs_1_, bf16[128,28672]{1,0:T(8,128)(2,1)} %refs_2_.1, bf16[128,28672]{1,0:T(8,128)(2,1)} %collective-permute-done.1.refs_1_.refs_3_, ...), custom_call_target="tpu_custom_call" | custom-call | flops 1 | bytes 1 | tf_op jit(solution)/shard_map/pallas_call | solution.py:116
  100.7 1.5 %collective-permute-done.16 = f32[128,512]{1,0:T(8,128)S(1)} collective-permute-done((f32[128,512]{1,0:T(8,128)S(1)}, f32[128,512]{1,0:T(8,128)S(1)}, u32[]{:S(2)}, u32[]{:S(2)}) %collective-permute-start.16) | collective-permute-done | bytes 262176 | tf_op jit(solution)/shard_map/ppermute | solution.py:219
  102.3 1.6 %collective-permute-start.18 = (bf16[144,512]{1,0:T(8,128)(2,1)S(1)}, bf16[144,512]{1,0:T(8,128)(2,1)S(1)}, u32[]{:S(2)}, u32[]{:S(2)}) collective-permute-start(bf16[144,512]{1,0:T(8,128)(2,1)S(1)} %pad_maximum_fusion.1.refs_0_), channel_id=1, source_target_pairs={{0,2},{1,3},{4,0},{5,1},{8,4},{9,5},{12,8},{13,9},{14,12},{15,13},... | collective-permute-start | bytes 442376 | tf_op jit(solution)/shard_map/ppermute | solution.py:219
  104.4 3.9 %collective-permute-done.18.refs_2_ = bf16[144,512]{1,0:T(8,128)(2,1)S(1)} collective-permute-done((bf16[144,512]{1,0:T(8,128)(2,1)S(1)}, bf16[144,512]{1,0:T(8,128)(2,1)S(1)}, u32[]{:S(2)}, u32[]{:S(2)}) %collective-permute-start.18) | collective-permute-done | bytes 147488 | tf_op jit(solution)/shard_map/ppermute | solution.py:219
  108.3 1.6 %collective-permute-start.20 = (bf16[144,512]{1,0:T(8,128)(2,1)S(1)}, bf16[144,512]{1,0:T(8,128)(2,1)S(1)}, u32[]{:S(2)}, u32[]{:S(2)}) collective-permute-start(bf16[144,512]{1,0:T(8,128)(2,1)S(1)} %collective-permute-done.18.refs_2_), channel_id=1, source_target_pairs={{0,2},{1,3},{4,0},{5,1},{8,4},{9,5},{12,8},{13,9},{14,12},{15,13},... | collective-permute-start | bytes 442376 | tf_op jit(solution)/shard_map/ppermute | solution.py:219
  109.8 0.5 collective-permute-start.19
  110.3 3.1 %collective-permute-done.20.refs_4_ = bf16[144,512]{1,0:T(8,128)(2,1)S(1)} collective-permute-done((bf16[144,512]{1,0:T(8,128)(2,1)S(1)}, bf16[144,512]{1,0:T(8,128)(2,1)S(1)}, u32[]{:S(2)}, u32[]{:S(2)}) %collective-permute-start.20) | collective-permute-done | bytes 147488 | tf_op jit(solution)/shard_map/ppermute | solution.py:219
  113.4 1.6 %collective-permute-start.22 = (bf16[144,512]{1,0:T(8,128)(2,1)S(1)}, bf16[144,512]{1,0:T(8,128)(2,1)S(1)}, u32[]{:S(2)}, u32[]{:S(2)}) collective-permute-start(bf16[144,512]{1,0:T(8,128)(2,1)S(1)} %collective-permute-done.20.refs_4_), channel_id=1, source_target_pairs={{0,2},{1,3},{4,0},{5,1},{8,4},{9,5},{12,8},{13,9},{14,12},{15,13},... | collective-permute-start | bytes 442376 | tf_op jit(solution)/shard_map/ppermute | solution.py:219
  115.0 0.5 collective-permute-start.26
  116.0 2.6 %collective-permute-done.22.refs_6_ = bf16[144,512]{1,0:T(8,128)(2,1)S(1)} collective-permute-done((bf16[144,512]{1,0:T(8,128)(2,1)S(1)}, bf16[144,512]{1,0:T(8,128)(2,1)S(1)}, u32[]{:S(2)}, u32[]{:S(2)}) %collective-permute-start.22) | collective-permute-done | bytes 147488 | tf_op jit(solution)/shard_map/ppermute | solution.py:219
  118.6 1.6 %collective-permute-start.24 = (bf16[80,512]{1,0:T(8,128)(2,1)S(1)}, bf16[80,512]{1,0:T(8,128)(2,1)S(1)}, u32[]{:S(2)}, u32[]{:S(2)}) collective-permute-start(bf16[80,512]{1,0:T(8,128)(2,1)S(1)} %slice.17), channel_id=1, source_target_pairs={{0,2},{1,3},{4,0},{5,1},{8,4},{9,5},{12,8},{13,9},{14,12},{15,13},... | collective-permute-start | bytes 245768 | tf_op jit(solution)/shard_map/ppermute | solution.py:219
  120.4 0.8 collective-permute-done.21.refs_5_
  121.3 0.5 collective-permute-start.31
  121.8 0.5 collective-permute-start.23
  122.3 1.2 collective-permute-done.24.refs_8_
  123.5 2.6 %collective-permute-done.23.refs_7_ = bf16[64,512]{1,0:T(8,128)(2,1)S(1)} collective-permute-done((bf16[64,512]{1,0:T(8,128)(2,1)S(1)}, bf16[64,512]{1,0:T(8,128)(2,1)S(1)}, u32[]{:S(2)}, u32[]{:S(2)}) %collective-permute-start.23) | collective-permute-done | bytes 65568 | tf_op jit(solution)/shard_map/ppermute | solution.py:219
  126.1 1.2 collective-permute-done.32.refs_16_
  127.4 1.5 %shard_map.85 = (f32[16,256]{1,0:T(8,128)}, f32[1,64]{1,0:T(1,128)}) custom-call(s32[1]{0:T(128)} %bitcast.me_ref, bf16[144,512]{1,0:T(8,128)(2,1)S(1)} %pad_maximum_fusion.1.refs_0_, bf16[144,512]{1,0:T(8,128)(2,1)S(1)} %collective-permute-done.17.refs_1_, bf16[144,512]{1,0:T(8,128)(2,1)S(1)} %collective-permute-done.18.refs_2_, ...), custom_call_target="tpu_custom_call" | custom-call | tf_op jit(solution)/shard_map/pallas_call | solution.py:180
  (49 shorter events, 2.3 us)
Async XLA Ops:
  0.6 23.6 %copy-start.1 = (s32[8]{0:T(128)S(1)}, s32[8]{0:T(128)}, u32[]{:S(2)}) copy-start(s32[8]{0:T(128)} %constant.101) | copy-start | bytes 100
  0.6 5.2 %copy-start = (bf16[1792,256]{1,0:T(8,128)(2,1)S(1)}, bf16[1792,256]{1,0:T(8,128)(2,1)}, u32[]{:S(2)}) copy-start(bf16[1792,256]{1,0:T(8,128)(2,1)} %param.10) | copy-start | bytes 2752516
  0.7 21.6 %collective-permute-start.1 = (bf16[128,28672]{1,0:T(8,128)(2,1)}, bf16[128,28672]{1,0:T(8,128)(2,1)}, u32[]{:S(2)}, u32[]{:S(2)}) collective-permute-start(bf16[128,28672]{1,0:T(8,128)(2,1)} %refs_2_.1), channel_id=1, source_target_pairs={{0,1},{1,0},{2,3},{3,2},{4,5},{5,4},{6,7},{7,6},{8,9},{9,8},{10,11... | collective-permute-start | bytes 22020104 | tf_op jit(solution)/shard_map/ppermute | solution.py:219
  3.2 16.6 %collective-permute-start.2 = (bf16[1152,256]{1,0:T(8,128)(2,1)S(1)}, bf16[1152,256]{1,0:T(8,128)(2,1)S(1)}, u32[]{:S(2)}, u32[]{:S(2)}) collective-permute-start(bf16[1152,256]{1,0:T(8,128)(2,1)S(1)} %pad_maximum_fusion.refs_2_), channel_id=1, source_target_pairs={{0,4},{1,5},{4,8},{5,9},{8,12},{9,13},{12,14},{13,15},{14,10},{15,... | collective-permute-start | bytes 1769480 | tf_op jit(solution)/shard_map/ppermute | solution.py:219
  5.9 16.3 %collective-permute-start.4 = (bf16[1152,256]{1,0:T(8,128)(2,1)S(1)}, bf16[1152,256]{1,0:T(8,128)(2,1)}, u32[]{:S(2)}, u32[]{:S(2)}) collective-permute-start(bf16[1152,256]{1,0:T(8,128)(2,1)S(1)} %slice.13.refs_3_), channel_id=1, source_target_pairs={{0,2},{1,3},{4,0},{5,1},{8,4},{9,5},{12,8},{13,9},{14,12},{15,13},... | collective-permute-start | bytes 1769480 | tf_op jit(solution)/shard_map/ppermute | solution.py:219
  6.0 79.4 %collective-permute-start = (bf16[128,8192]{1,0:T(8,128)(2,1)}, bf16[128,8192]{1,0:T(8,128)(2,1)}, u32[]{:S(2)}, u32[]{:S(2)}) collective-permute-start(bf16[128,8192]{1,0:T(8,128)(2,1)} %refs_0_.15), channel_id=1, source_target_pairs={{0,1},{1,0},{2,3},{3,2},{4,5},{5,4},{6,7},{7,6},{8,9},{9,8},{10,11... | collective-permute-start | bytes 6291464 | tf_op jit(solution)/shard_map/ppermute | solution.py:219
  6.2 28.6 %collective-permute-start.7 = (bf16[1152,256]{1,0:T(8,128)(2,1)S(1)}, bf16[1152,256]{1,0:T(8,128)(2,1)S(1)}, u32[]{:S(2)}, u32[]{:S(2)}) collective-permute-start(bf16[1152,256]{1,0:T(8,128)(2,1)S(1)} %pad_maximum_fusion.refs_2_), channel_id=1, source_target_pairs={{0,2},{1,3},{4,0},{5,1},{8,4},{9,5},{12,8},{13,9},{14,12},{15,13},... | collective-permute-start | bytes 1769480 | tf_op jit(solution)/shard_map/ppermute | solution.py:219
  19.7 16.3 %collective-permute-start.6 = (bf16[1152,256]{1,0:T(8,128)(2,1)S(1)}, bf16[1152,256]{1,0:T(8,128)(2,1)}, u32[]{:S(2)}, u32[]{:S(2)}) collective-permute-start(bf16[1152,256]{1,0:T(8,128)(2,1)S(1)} %slice.13.refs_3_), channel_id=1, source_target_pairs={{0,4},{1,5},{4,8},{5,9},{8,12},{9,13},{12,14},{13,15},{14,10},{15,... | collective-permute-start | bytes 1769480 | tf_op jit(solution)/shard_map/ppermute | solution.py:219
  22.2 25.2 %collective-permute-start.5 = (bf16[1152,256]{1,0:T(8,128)(2,1)}, bf16[1152,256]{1,0:T(8,128)(2,1)S(1)}, u32[]{:S(2)}, u32[]{:S(2)}) collective-permute-start(bf16[1152,256]{1,0:T(8,128)(2,1)} %collective-permute-done.4.refs_5_), channel_id=1, source_target_pairs={{0,2},{1,3},{4,0},{5,1},{8,4},{9,5},{12,8},{13,9},{14,12},{15,13},... | collective-permute-start | bytes 1769480 | tf_op jit(solution)/shard_map/ppermute | solution.py:219
  22.3 26.3 %collective-permute-start.3 = (bf16[1152,256]{1,0:T(8,128)(2,1)S(1)}, bf16[1152,256]{1,0:T(8,128)(2,1)S(1)}, u32[]{:S(2)}, u32[]{:S(2)}) collective-permute-start(bf16[1152,256]{1,0:T(8,128)(2,1)S(1)} %collective-permute-done.2.refs_4_.refs_3_), channel_id=1, source_target_pairs={{0,4},{1,5},{4,8},{5,9},{8,12},{9,13},{12,14},{13,15},{14,10},{15,... | collective-permute-start | bytes 1769480 | tf_op jit(solution)/shard_map/ppermute | solution.py:219
  34.8 25.3 %collective-permute-start.11 = (bf16[1152,256]{1,0:T(8,128)(2,1)S(1)}, bf16[1152,256]{1,0:T(8,128)(2,1)S(1)}, u32[]{:S(2)}, u32[]{:S(2)}) collective-permute-start(bf16[1152,256]{1,0:T(8,128)(2,1)S(1)} %collective-permute-done.7.refs_3_.refs_4_), channel_id=1, source_target_pairs={{0,2},{1,3},{4,0},{5,1},{8,4},{9,5},{12,8},{13,9},{14,12},{15,13},... | collective-permute-start | bytes 1769480 | tf_op jit(solution)/shard_map/ppermute | solution.py:219
  36.0 25.2 %collective-permute-start.10 = (bf16[1152,256]{1,0:T(8,128)(2,1)}, bf16[1152,256]{1,0:T(8,128)(2,1)S(1)}, u32[]{:S(2)}, u32[]{:S(2)}) collective-permute-start(bf16[1152,256]{1,0:T(8,128)(2,1)} %collective-permute-done.6.refs_2_), channel_id=1, source_target_pairs={{0,4},{1,5},{4,8},{5,9},{8,12},{9,13},{12,14},{13,15},{14,10},{15,... | collective-permute-start | bytes 1769480 | tf_op jit(solution)/shard_map/ppermute | solution.py:219
  47.4 25.3 %collective-permute-start.9 = (bf16[1152,256]{1,0:T(8,128)(2,1)S(1)}, bf16[1152,256]{1,0:T(8,128)(2,1)S(1)}, u32[]{:S(2)}, u32[]{:S(2)}) collective-permute-start(bf16[1152,256]{1,0:T(8,128)(2,1)S(1)} %collective-permute-done.5.refs_3_), channel_id=1, source_target_pairs={{0,2},{1,3},{4,0},{5,1},{8,4},{9,5},{12,8},{13,9},{14,12},{15,13},... | collective-permute-start | bytes 1769480 | tf_op jit(solution)/shard_map/ppermute | solution.py:219
  48.6 25.3 %collective-permute-start.8 = (bf16[1152,256]{1,0:T(8,128)(2,1)S(1)}, bf16[1152,256]{1,0:T(8,128)(2,1)S(1)}, u32[]{:S(2)}, u32[]{:S(2)}) collective-permute-start(bf16[1152,256]{1,0:T(8,128)(2,1)S(1)} %collective-permute-done.3.refs_2_.refs_5_), channel_id=1, source_target_pairs={{0,4},{1,5},{4,8},{5,9},{8,12},{9,13},{12,14},{13,15},{14,10},{15,... | collective-permute-start | bytes 1769480 | tf_op jit(solution)/shard_map/ppermute | solution.py:219
  60.1 15.8 %copy-start.2 = (s32[128]{0:T(128)S(1)}, s32[128]{0:T(128)}, u32[]{:S(2)}) copy-start(s32[128]{0:T(128)} %param.8) | copy-start | bytes 1540
  61.2 24.1 %collective-permute-start.14 = (bf16[1152,256]{1,0:T(8,128)(2,1)S(1)}, bf16[1152,256]{1,0:T(8,128)(2,1)S(1)}, u32[]{:S(2)}, u32[]{:S(2)}) collective-permute-start(bf16[1152,256]{1,0:T(8,128)(2,1)S(1)} %collective-permute-done.11.refs_3_.refs_6_), channel_id=1, source_target_pairs={{0,2},{1,3},{4,0},{5,1},{8,4},{9,5},{12,8},{13,9},{14,12},{15,13},... | collective-permute-start | bytes 1769480 | tf_op jit(solution)/shard_map/ppermute | solution.py:219
  63.0 25.5 %collective-permute-start.15 = (bf16[1152,256]{1,0:T(8,128)(2,1)S(1)}, bf16[1152,256]{1,0:T(8,128)(2,1)S(1)}, u32[]{:S(2)}, u32[]{:S(2)}) collective-permute-start(bf16[1152,256]{1,0:T(8,128)(2,1)S(1)} %collective-permute-done.10.refs_2_), channel_id=1, source_target_pairs={{0,4},{1,5},{4,8},{5,9},{8,12},{9,13},{12,14},{13,15},{14,10},{15,... | collective-permute-start | bytes 1769480 | tf_op jit(solution)/shard_map/ppermute | solution.py:219
  73.9 24.3 %collective-permute-start.12 = (bf16[1152,256]{1,0:T(8,128)(2,1)S(1)}, bf16[1152,256]{1,0:T(8,128)(2,1)S(1)}, u32[]{:S(2)}, u32[]{:S(2)}) collective-permute-start(bf16[1152,256]{1,0:T(8,128)(2,1)S(1)} %collective-permute-done.8.refs_2_.refs_7_), channel_id=1, source_target_pairs={{0,4},{1,5},{4,8},{5,9},{8,12},{9,13},{12,14},{13,15},{14,10},{15,... | collective-permute-start | bytes 1769480 | tf_op jit(solution)/shard_map/ppermute | solution.py:219
  75.7 22.4 %collective-permute-start.13 = (bf16[1152,256]{1,0:T(8,128)(2,1)S(1)}, bf16[1152,256]{1,0:T(8,128)(2,1)S(1)}, u32[]{:S(2)}, u32[]{:S(2)}) collective-permute-start(bf16[1152,256]{1,0:T(8,128)(2,1)S(1)} %collective-permute-done.9.refs_3_), channel_id=1, source_target_pairs={{0,2},{1,3},{4,0},{5,1},{8,4},{9,5},{12,8},{13,9},{14,12},{15,13},... | collective-permute-start | bytes 1769480 | tf_op jit(solution)/shard_map/ppermute | solution.py:219
  100.6 1.6 %collective-permute-start.16 = (f32[128,512]{1,0:T(8,128)S(1)}, f32[128,512]{1,0:T(8,128)S(1)}, u32[]{:S(2)}, u32[]{:S(2)}) collective-permute-start(f32[128,512]{1,0:T(8,128)S(1)} %get-tuple-element.95), channel_id=1, source_target_pairs={{0,1},{1,0},{2,3},{3,2},{4,5},{5,4},{6,7},{7,6},{8,9},{9,8},{10,11... | collective-permute-start | bytes 786440 | tf_op jit(solution)/shard_map/ppermute | solution.py:219
  102.3 5.9 %collective-permute-start.18 = (bf16[144,512]{1,0:T(8,128)(2,1)S(1)}, bf16[144,512]{1,0:T(8,128)(2,1)S(1)}, u32[]{:S(2)}, u32[]{:S(2)}) collective-permute-start(bf16[144,512]{1,0:T(8,128)(2,1)S(1)} %pad_maximum_fusion.1.refs_0_), channel_id=1, source_target_pairs={{0,2},{1,3},{4,0},{5,1},{8,4},{9,5},{12,8},{13,9},{14,12},{15,13},... | collective-permute-start | bytes 442376 | tf_op jit(solution)/shard_map/ppermute | solution.py:219
  104.0 5.9 %collective-permute-start.17 = (bf16[144,512]{1,0:T(8,128)(2,1)S(1)}, bf16[144,512]{1,0:T(8,128)(2,1)S(1)}, u32[]{:S(2)}, u32[]{:S(2)}) collective-permute-start(bf16[144,512]{1,0:T(8,128)(2,1)S(1)} %pad_maximum_fusion.1.refs_0_), channel_id=1, source_target_pairs={{0,4},{1,5},{4,8},{5,9},{8,12},{9,13},{12,14},{13,15},{14,10},{15,... | collective-permute-start | bytes 442376 | tf_op jit(solution)/shard_map/ppermute | solution.py:219
  108.3 5.1 %collective-permute-start.20 = (bf16[144,512]{1,0:T(8,128)(2,1)S(1)}, bf16[144,512]{1,0:T(8,128)(2,1)S(1)}, u32[]{:S(2)}, u32[]{:S(2)}) collective-permute-start(bf16[144,512]{1,0:T(8,128)(2,1)S(1)} %collective-permute-done.18.refs_2_), channel_id=1, source_target_pairs={{0,2},{1,3},{4,0},{5,1},{8,4},{9,5},{12,8},{13,9},{14,12},{15,13},... | collective-permute-start | bytes 442376 | tf_op jit(solution)/shard_map/ppermute | solution.py:219
  109.8 5.7 %collective-permute-start.19 = (bf16[144,512]{1,0:T(8,128)(2,1)S(1)}, bf16[144,512]{1,0:T(8,128)(2,1)S(1)}, u32[]{:S(2)}, u32[]{:S(2)}) collective-permute-start(bf16[144,512]{1,0:T(8,128)(2,1)S(1)} %collective-permute-done.17.refs_1_), channel_id=1, source_target_pairs={{0,4},{1,5},{4,8},{5,9},{8,12},{9,13},{12,14},{13,15},{14,10},{15,... | collective-permute-start | bytes 442376 | tf_op jit(solution)/shard_map/ppermute | solution.py:219
  113.4 5.1 %collective-permute-start.22 = (bf16[144,512]{1,0:T(8,128)(2,1)S(1)}, bf16[144,512]{1,0:T(8,128)(2,1)S(1)}, u32[]{:S(2)}, u32[]{:S(2)}) collective-permute-start(bf16[144,512]{1,0:T(8,128)(2,1)S(1)} %collective-permute-done.20.refs_4_), channel_id=1, source_target_pairs={{0,2},{1,3},{4,0},{5,1},{8,4},{9,5},{12,8},{13,9},{14,12},{15,13},... | collective-permute-start | bytes 442376 | tf_op jit(solution)/shard_map/ppermute | solution.py:219
  115.0 3.6 %collective-permute-start.25 = (bf16[144,512]{1,0:T(8,128)(2,1)S(1)}, bf16[144,512]{1,0:T(8,128)(2,1)S(1)}, u32[]{:S(2)}, u32[]{:S(2)}) collective-permute-start(bf16[144,512]{1,0:T(8,128)(2,1)S(1)} %pad_maximum_fusion.1.refs_0_), channel_id=1, source_target_pairs={{0,1},{1,0},{2,3},{3,2},{4,5},{5,4},{6,7},{7,6},{8,9},{9,8},{10,11... | collective-permute-start | bytes 442376 | tf_op jit(solution)/shard_map/ppermute | solution.py:219
  115.0 5.2 %collective-permute-start.26 = (bf16[144,512]{1,0:T(8,128)(2,1)S(1)}, bf16[144,512]{1,0:T(8,128)(2,1)S(1)}, u32[]{:S(2)}, u32[]{:S(2)}) collective-permute-start(bf16[144,512]{1,0:T(8,128)(2,1)S(1)} %collective-permute-done.17.refs_1_), channel_id=1, source_target_pairs={{0,1},{1,0},{2,3},{3,2},{4,5},{5,4},{6,7},{7,6},{8,9},{9,8},{10,11... | collective-permute-start | bytes 442376 | tf_op jit(solution)/shard_map/ppermute | solution.py:219
  115.5 5.8 %collective-permute-start.21 = (bf16[144,512]{1,0:T(8,128)(2,1)S(1)}, bf16[144,512]{1,0:T(8,128)(2,1)S(1)}, u32[]{:S(2)}, u32[]{:S(2)}) collective-permute-start(bf16[144,512]{1,0:T(8,128)(2,1)S(1)} %collective-permute-done.19.refs_3_), channel_id=1, source_target_pairs={{0,4},{1,5},{4,8},{5,9},{8,12},{9,13},{12,14},{13,15},{14,10},{15,... | collective-permute-start | bytes 442376 | tf_op jit(solution)/shard_map/ppermute | solution.py:219
  116.0 5.3 %collective-permute-start.27 = (bf16[144,512]{1,0:T(8,128)(2,1)S(1)}, bf16[144,512]{1,0:T(8,128)(2,1)S(1)}, u32[]{:S(2)}, u32[]{:S(2)}) collective-permute-start(bf16[144,512]{1,0:T(8,128)(2,1)S(1)} %collective-permute-done.18.refs_2_), channel_id=1, source_target_pairs={{0,1},{1,0},{2,3},{3,2},{4,5},{5,4},{6,7},{7,6},{8,9},{9,8},{10,11... | collective-permute-start | bytes 442376 | tf_op jit(solution)/shard_map/ppermute | solution.py:219
  118.6 3.2 %collective-permute-start.28 = (bf16[144,512]{1,0:T(8,128)(2,1)S(1)}, bf16[144,512]{1,0:T(8,128)(2,1)S(1)}, u32[]{:S(2)}, u32[]{:S(2)}) collective-permute-start(bf16[144,512]{1,0:T(8,128)(2,1)S(1)} %collective-permute-done.19.refs_3_), channel_id=1, source_target_pairs={{0,1},{1,0},{2,3},{3,2},{4,5},{5,4},{6,7},{7,6},{8,9},{9,8},{10,11... | collective-permute-start | bytes 442376 | tf_op jit(solution)/shard_map/ppermute | solution.py:219
  118.6 4.9 %collective-permute-start.24 = (bf16[80,512]{1,0:T(8,128)(2,1)S(1)}, bf16[80,512]{1,0:T(8,128)(2,1)S(1)}, u32[]{:S(2)}, u32[]{:S(2)}) collective-permute-start(bf16[80,512]{1,0:T(8,128)(2,1)S(1)} %slice.17), channel_id=1, source_target_pairs={{0,2},{1,3},{4,0},{5,1},{8,4},{9,5},{12,8},{13,9},{14,12},{15,13},... | collective-permute-start | bytes 245768 | tf_op jit(solution)/shard_map/ppermute | solution.py:219
  120.2 5.9 %collective-permute-start.29 = (bf16[144,512]{1,0:T(8,128)(2,1)S(1)}, bf16[144,512]{1,0:T(8,128)(2,1)S(1)}, u32[]{:S(2)}, u32[]{:S(2)}) collective-permute-start(bf16[144,512]{1,0:T(8,128)(2,1)S(1)} %collective-permute-done.20.refs_4_), channel_id=1, source_target_pairs={{0,1},{1,0},{2,3},{3,2},{4,5},{5,4},{6,7},{7,6},{8,9},{9,8},{10,11... | collective-permute-start | bytes 442376 | tf_op jit(solution)/shard_map/ppermute | solution.py:219
  121.3 6.1 %collective-permute-start.30 = (bf16[144,512]{1,0:T(8,128)(2,1)S(1)}, bf16[144,512]{1,0:T(8,128)(2,1)S(1)}, u32[]{:S(2)}, u32[]{:S(2)}) collective-permute-start(bf16[144,512]{1,0:T(8,128)(2,1)S(1)} %collective-permute-done.21.refs_5_), channel_id=1, source_target_pairs={{0,1},{1,0},{2,3},{3,2},{4,5},{5,4},{6,7},{7,6},{8,9},{9,8},{10,11... | collective-permute-start | bytes 442376 | tf_op jit(solution)/shard_map/ppermute | solution.py:219
  121.3 6.1 %collective-permute-start.31 = (bf16[144,512]{1,0:T(8,128)(2,1)S(1)}, bf16[144,512]{1,0:T(8,128)(2,1)S(1)}, u32[]{:S(2)}, u32[]{:S(2)}) collective-permute-start(bf16[144,512]{1,0:T(8,128)(2,1)S(1)} %collective-permute-done.22.refs_6_), channel_id=1, source_target_pairs={{0,1},{1,0},{2,3},{3,2},{4,5},{5,4},{6,7},{7,6},{8,9},{9,8},{10,11... | collective-permute-start | bytes 442376 | tf_op jit(solution)/shard_map/ppermute | solution.py:219
  121.8 4.3 %collective-permute-start.23 = (bf16[64,512]{1,0:T(8,128)(2,1)S(1)}, bf16[64,512]{1,0:T(8,128)(2,1)S(1)}, u32[]{:S(2)}, u32[]{:S(2)}) collective-permute-start(bf16[64,512]{1,0:T(8,128)(2,1)S(1)} %slice.16), channel_id=1, source_target_pairs={{0,4},{1,5},{4,8},{5,9},{8,12},{9,13},{12,14},{13,15},{14,10},{15,... | collective-permute-start | bytes 196616 | tf_op jit(solution)/shard_map/ppermute | solution.py:219
  123.5 3.9 %collective-permute-start.33 = (bf16[80,512]{1,0:T(8,128)(2,1)S(1)}, bf16[80,512]{1,0:T(8,128)(2,1)S(1)}, u32[]{:S(2)}, u32[]{:S(2)}) collective-permute-start(bf16[80,512]{1,0:T(8,128)(2,1)S(1)} %collective-permute-done.24.refs_8_), channel_id=1, source_target_pairs={{0,1},{1,0},{2,3},{3,2},{4,5},{5,4},{6,7},{7,6},{8,9},{9,8},{10,11... | collective-permute-start | bytes 245768 | tf_op jit(solution)/shard_map/ppermute | solution.py:219
  126.1 1.3 collective-permute-start.32

commit v4 on v3

--- a/solution.py
+++ b/solution.py
@@ -134,6 +134,98 @@
     )
 
 
+def copy_all(copies):
+    for copy in copies:
+        copy.start()
+    for copy in copies:
+        copy.wait()
+
+
+def halves_kernel(upper_ref, lower_ref, first_ref, second_ref, sems):
+    above, rest = upper_ref.shape[0], first_ref.shape[0] - upper_ref.shape[0]
+    copy_all([
+        pltpu.make_async_copy(
+            lower_ref.at[pl.ds(rest, second_ref.shape[0]), :], second_ref, sems.at[0]
+        ),
+        pltpu.make_async_copy(upper_ref, first_ref.at[pl.ds(0, above), :], sems.at[1]),
+        pltpu.make_async_copy(
+            lower_ref.at[pl.ds(0, rest), :], first_ref.at[pl.ds(above, rest), :], sems.at[2]
+        ),
+    ])
+
+
+def halves(upper, lower, cut):
+    total, width = upper.shape[0] + lower.shape[0], upper.shape[1]
+    vmem = pl.BlockSpec(memory_space=pltpu.VMEM)
+    return pl.pallas_call(
+        halves_kernel,
+        out_shape=(
+            jax.ShapeDtypeStruct((cut, width), upper.dtype),
+            jax.ShapeDtypeStruct((total - cut, width), upper.dtype),
+        ),
+        in_specs=[pl.BlockSpec(memory_space=pl.ANY)] * 2,
+        out_specs=(vmem, vmem),
+        scratch_shapes=[pltpu.SemaphoreType.DMA((3,))],
+        compiler_params=pltpu.CompilerParams(vmem_limit_bytes=16 * 2**20),
+    )(*[pltpu.with_memory_space_constraint(x, pltpu.HBM) for x in (upper, lower)])
+
+
+def fetch_kernel(slot, depths, owners_ref, *refs):
+    sources, (own_ref, sibling_ref, sems) = refs[:4], refs[4:7]
+    copies, at = [], 0
+    for kind, depth in enumerate(depths):
+        column = pl.multiple_of(owners_ref[slot] * depth, 128)
+        for j, block in enumerate((own_ref, sibling_ref)):
+            copies.append(
+                pltpu.make_async_copy(
+                    sources[2 * j + kind].at[:, pl.ds(column, depth)],
+                    block.at[:, pl.ds(at, depth)],
+                    sems.at[kind, j],
+                )
+            )
+        at += depth
+    copy_all(copies)
+
+
+def fetch(owners, slot, tokens, depth_in, depth_out, after):
+    rows = tokens[0].shape[0]
+    vmem = pl.BlockSpec(memory_space=pltpu.VMEM)
+    block = jax.ShapeDtypeStruct((rows, depth_in + depth_out), tokens[0].dtype)
+    got = pl.pallas_call(
+        functools.partial(fetch_kernel, slot, (depth_in, depth_out)),
+        out_shape=(block, block),
+        in_specs=[pl.BlockSpec(memory_space=pltpu.SMEM)] + [pl.BlockSpec(memory_space=pl.ANY)] * 4,
+        out_specs=(vmem, vmem),
+        scratch_shapes=[pltpu.SemaphoreType.DMA((2, 2))],
+        compiler_params=pltpu.CompilerParams(vmem_limit_bytes=16 * 2**20),
+        cost_estimate=pl.CostEstimate(flops=1, bytes_accessed=1, transcendentals=0),
+    )(owners, *[pltpu.with_memory_space_constraint(x, pltpu.HBM) for x in tokens])
+    return [list(got), *after]
+
+
+def finish_dots_kernel(depth_in, block_ref, first_ref, second_ref, act_ref, grad_ref, out_ref):
+    cut, width = first_ref.shape
+    out_ref[:, :width] = act_ref[...] + dot(block_ref[:, :depth_in], first_ref[:depth_in, :])
+    out_ref[:, width:] = (
+        grad_ref[...]
+        + dot(block_ref[:, depth_in:cut], first_ref[depth_in:, :])
+        + dot(block_ref[:, cut:], second_ref[...])
+    )
+
+
+def finish_dots(block, panels, act, grad, depth_in):
+    rows, width = act.shape
+    vmem = pl.BlockSpec(memory_space=pltpu.VMEM)
+    return pl.pallas_call(
+        functools.partial(finish_dots_kernel, depth_in),
+        out_shape=jax.ShapeDtypeStruct((rows, 2 * width), jnp.float32),
+        in_specs=[vmem] * 5,
+        out_specs=vmem,
+        compiler_params=pltpu.CompilerParams(vmem_limit_bytes=16 * 2**20),
+        cost_estimate=pl.CostEstimate(flops=1, bytes_accessed=1, transcendentals=0),
+    )(block, *[pltpu.with_memory_space_constraint(x, pltpu.VMEM) for x in panels], act, grad)
+
+
 def last_kernel(scale, rows, me_ref, *refs):
     pieces, (corrected_ref, score_ref, squares, held) = refs[:-4], refs[-4:]
     me = me_ref[0]
@@ -143,15 +235,16 @@
     wanted = lax.broadcasted_iota(jnp.int32, (balanced, rows), 0)
     at, picks = 0, []
     for piece in pieces:
-        count = min(piece.shape[0], rows)
-        if at % rows:
-            count = rows - at % rows
-        squares[at : at + count, :] = piece[:count, :]
-        at += count
-        if at % rows == 0:
-            tag = piece[count : count + 16, :][:1].astype(jnp.float32).astype(jnp.int32)
-            owner, place = tag[:, :rows], tag[:, rows : 2 * rows]
-            picks.append(((owner == me) & (place == wanted)).astype(jnp.float32))
+        start = 0
+        while start < piece.shape[0]:
+            count = min(rows - at % rows, piece.shape[0] - start)
+            squares[at : at + count, :] = piece[start : start + count, :]
+            at, start = at + count, start + count
+            if at % rows == 0:
+                tag = piece[start : start + 16, :][:1].astype(jnp.float32).astype(jnp.int32)
+                owner, place = tag[:, :rows], tag[:, rows : 2 * rows]
+                picks.append(((owner == me) & (place == wanted)).astype(jnp.float32))
+                start += 16
     pick = jnp.concatenate(picks, axis=1).astype(jnp.bfloat16)
     act, grad = squares[:, :in_panel], squares[:, in_panel:]
     corrected = lax.dot_general(
@@ -232,8 +325,8 @@
     ) * 2 + own_index % 2
 
     cut = (depth_in + depth_out) // 2
-    first = {0: jnp.concatenate([basis_in, basis_out[: cut - depth_in]], axis=0)}
-    second = {0: basis_out[cut - depth_in :]}
+    first, second = halves(basis_in, basis_out, cut)
+    first, second = {0: first}, {0: second}
 
     def hop(ahead, behind, s):
         ahead[s] = send(ahead[s - 1], forward)
@@ -272,25 +365,36 @@
             grad = after(first, [s + 1], after(second, [-s - 1], grad))
     swapped_act = send(activations, swap)
     act = add((0,), pieces(first, distances[:-1]), [zero, zero])
-    mine, theirs = add((0, 1), pieces(first, [half]) + pieces(second, [half]), act + grad)
+    tokens = (activations, out_grads, swapped_act, swapped_grad)
+    block, *act = fetch(owners, chips - 1, tokens, depth_in, depth_out, act)
+    panels = (first[half], second[half])
+    theirs = finish_dots(block[1], panels, act[1], grad[1], depth_in)
+    block[0], swapped = lax.optimization_barrier((block[0], theirs))
+    swapped = send(swapped, swap)
+    mine = finish_dots(block[0], panels, act[0], grad[0], depth_in)
 
     is_valid = slot_of_row >= 0
     owner = jnp.where(is_valid, slot_of_row // balanced, -1)
     tag = jnp.concatenate([owner, slot_of_row % balanced]).astype(jnp.bfloat16)
     tag = jnp.broadcast_to(jnp.pad(tag, (0, 2 * width - 2 * rows))[None, :], (16, 2 * width))
-    rotated = mine + send(theirs, swap)
+    rotated = mine + swapped
     counts = is_valid[:, None] | (jnp.arange(2 * width) < width)[None, :]
     squares = jnp.where(counts, rotated * rotated, 0.0).astype(jnp.bfloat16)
 
     held = {0: jnp.concatenate([squares, tag], axis=0)}
-    middle = (rows + 16) // 32 * 16
     for s in range(1, half):
-        held[s], held[-s] = send(held[s - 1], forward), send(held[1 - s], backward)
-    gathered_pieces = [held[d] for d in distances[:-1]]
-    gathered_pieces.append(send(held[half - 1][:middle], forward))
-    gathered_pieces.append(send(held[1 - half][middle:], backward))
-    gathered_pieces += [send(x, swap) for x in gathered_pieces]
-    return last(own_index[None], gathered_pieces, rows, width, devices, balanced)
+        hop(held, held, s)
+    near = jnp.concatenate([held[d] for d in distances[:-3]], axis=0)
+    near, held[half - 1], held[1 - half] = lax.optimization_barrier(
+        (near, held[half - 1], held[1 - half])
+    )
+    core = own_index % 2
+    farthest = jnp.where(core == 0, held[half - 1], held[1 - half])
+    opposite = send(farthest, forward[0::2] + backward[1::2])
+    far = jnp.concatenate([held[half - 1], held[1 - half]], axis=0)
+    swapped = [send(x, swap) for x in (near, far, opposite)]
+    own = [near, far, opposite]
+    return last(own_index[None], own + swapped, rows, width, devices, balanced)
 
 
 def body(*arrays):

time: 129 us -> 127 us (0.984)
  starting transfers between devices: 26.4 us -> 24.5 us
  Pallas kernels: 22.2 us -> 24 us
    pallas_call x0 -> x4, Pallas kernels: none -> 4.61 us  [the longest x1 2.08 us: halves(): pl.pallas_call(halves_kernel, out_shape=(jax.ShapeDtypeStruct((cut, width...]
    pallas_call x8 -> x7, Pallas kernels: 20.7 us -> 17.9 us  [project(): pl.pallas_call(functools.partial(project_kernel, kinds, [p[:2] for p in p...]
    ppermute x34 -> x27, starting transfers between devices: 26.4 us -> 24.5 us  [send(): return lax.ppermute(x, 'dp', pairs)]
    ppermute x34 -> x27, waiting for transfers between devices: 77.2 us -> 76.2 us  [send(): return lax.ppermute(x, 'dp', pairs)]
  transfers between devices with their start and end apart: 34 -> 27, of which waited for: 20 -> 19; matrix products, arithmetic and copies ran while one was open for 2% -> 1% of each run, Pallas kernels for 14% -> 18%
where the time goes in v4:
time: 127 us; the launch traced here: 126 us
  waiting for transfers between devices  76.2 us (60%)
  starting transfers between devices  24.5 us (19%)
  Pallas kernels  24 us (19%)
    ppermute x27, waiting for transfers between devices, send(): return lax.ppermute(x, 'dp', pairs)  76.2 us
    ppermute x27, starting transfers between devices, send(): return lax.ppermute(x, 'dp', pairs)  24.5 us
    pallas_call x7, Pallas kernels, project(): pl.pallas_call(functools.partial(project_kernel, kinds, [p[:2] for p in p...  17.9 us
  transfers between devices with their start and end apart: 27, of which 19 were waited for; matrix products, arithmetic and copies ran while one was open for 1% of the time, Pallas kernels for 18%

profile of v4, /device:TPU:0, one launch (start us, length us, event | category | flops | bytes accessed | tf_op | source)
XLA Modules:
  0.0 126.5 jit_solution(9675606077001243492)
XLA Ops:
  0.6 0.5 collective-permute-start.1
  1.1 2.1 %shard_map.78 = (bf16[1152,256]{1,0:T(8,128)(2,1)S(1)}, bf16[1152,256]{1,0:T(8,128)(2,1)}) custom-call(bf16[512,256]{1,0:T(8,128)(2,1)} %upper_ref.1, bf16[1792,256]{1,0:T(8,128)(2,1)} %lower_ref.1), custom_call_target="tpu_custom_call" | custom-call | tf_op jit(solution)/shard_map/pallas_call | solution.py:160
  3.2 2.6 %collective-permute-start.2 = (bf16[1152,256]{1,0:T(8,128)(2,1)S(1)}, bf16[1152,256]{1,0:T(8,128)(2,1)S(1)}, u32[]{:S(2)}, u32[]{:S(2)}) collective-permute-start(bf16[1152,256]{1,0:T(8,128)(2,1)S(1)} %get-tuple-element.59.refs_2_), channel_id=1, source_target_pairs={{0,4},{1,5},{4,8},{5,9},{8,12},{9,13},{12,14},{13,15},{14,10},{15,... | collective-permute-start | bytes 1769480 | tf_op jit(solution)/shard_map/ppermute | solution.py:312
  6.1 1.8 %collective-permute-start.7 = (bf16[1152,256]{1,0:T(8,128)(2,1)S(1)}, bf16[1152,256]{1,0:T(8,128)(2,1)S(1)}, u32[]{:S(2)}, u32[]{:S(2)}) collective-permute-start(bf16[1152,256]{1,0:T(8,128)(2,1)S(1)} %get-tuple-element.59.refs_2_), channel_id=1, source_target_pairs={{0,2},{1,3},{4,0},{5,1},{8,4},{9,5},{12,8},{13,9},{14,12},{15,13},... | collective-permute-start | bytes 1769480 | tf_op jit(solution)/shard_map/ppermute | solution.py:312
  7.9 12.0 %collective-permute-done.2.refs_4_.refs_3_ = bf16[1152,256]{1,0:T(8,128)(2,1)S(1)} collective-permute-done((bf16[1152,256]{1,0:T(8,128)(2,1)S(1)}, bf16[1152,256]{1,0:T(8,128)(2,1)S(1)}, u32[]{:S(2)}, u32[]{:S(2)}) %collective-permute-start.2) | collective-permute-done | bytes 589856 | tf_op jit(solution)/shard_map/ppermute | solution.py:312
  19.8 1.8 %collective-permute-start.6 = (bf16[1152,256]{1,0:T(8,128)(2,1)}, bf16[1152,256]{1,0:T(8,128)(2,1)S(1)}, u32[]{:S(2)}, u32[]{:S(2)}) collective-permute-start(bf16[1152,256]{1,0:T(8,128)(2,1)} %get-tuple-element.60.refs_3_), channel_id=1, source_target_pairs={{0,4},{1,5},{4,8},{5,9},{8,12},{9,13},{12,14},{13,15},{14,10},{15,... | collective-permute-start | bytes 1769480 | tf_op jit(solution)/shard_map/ppermute | solution.py:312
  21.6 0.8 collective-permute-done.4.refs_5_
  22.4 2.0 %collective-permute-start.3 = (bf16[1152,256]{1,0:T(8,128)(2,1)S(1)}, bf16[1152,256]{1,0:T(8,128)(2,1)S(1)}, u32[]{:S(2)}, u32[]{:S(2)}) collective-permute-start(bf16[1152,256]{1,0:T(8,128)(2,1)S(1)} %collective-permute-done.2.refs_4_.refs_3_), channel_id=1, source_target_pairs={{0,4},{1,5},{4,8},{5,9},{8,12},{9,13},{12,14},{13,15},{14,10},{15,... | collective-permute-start | bytes 1769480 | tf_op jit(solution)/shard_map/ppermute | solution.py:312
  24.4 0.7 fusion.6.owners_ref
  25.1 3.8 %shard_map.79 = (f32[128,256]{1,0:T(8,128)S(1)}, f32[128,256]{1,0:T(8,128)S(1)}) custom-call(s32[8]{0:T(128)S(1)} %fusion.6.owners_ref, bf16[128,28672]{1,0:T(8,128)(2,1)} %refs_0_.15, bf16[128,28672]{1,0:T(8,128)(2,1)} %collective-permute-done.1.refs_3_.refs_1_, bf16[1152,256]{1,0:T(8,128)(2,1)S(1)} %get-tuple-element.59.refs_2_, ...), custom_call_target="tpu_custom_call" | custom-call | flops 1 | bytes 1 | tf_op jit(solution)/shard_map/pallas_call | solution.py:116
  28.9 6.0 %collective-permute-done.7.refs_3_.refs_4_ = bf16[1152,256]{1,0:T(8,128)(2,1)S(1)} collective-permute-done((bf16[1152,256]{1,0:T(8,128)(2,1)S(1)}, bf16[1152,256]{1,0:T(8,128)(2,1)S(1)}, u32[]{:S(2)}, u32[]{:S(2)}) %collective-permute-start.7) | collective-permute-done | bytes 589856 | tf_op jit(solution)/shard_map/ppermute | solution.py:312
  34.9 1.3 %collective-permute-done.6.refs_2_ = bf16[1152,256]{1,0:T(8,128)(2,1)S(1)} collective-permute-done((bf16[1152,256]{1,0:T(8,128)(2,1)}, bf16[1152,256]{1,0:T(8,128)(2,1)S(1)}, u32[]{:S(2)}, u32[]{:S(2)}) %collective-permute-start.6) | collective-permute-done | bytes 589856 | tf_op jit(solution)/shard_map/ppermute | solution.py:312
  36.2 1.8 %collective-permute-start.10 = (bf16[1152,256]{1,0:T(8,128)(2,1)S(1)}, bf16[1152,256]{1,0:T(8,128)(2,1)S(1)}, u32[]{:S(2)}, u32[]{:S(2)}) collective-permute-start(bf16[1152,256]{1,0:T(8,128)(2,1)S(1)} %collective-permute-done.6.refs_2_), channel_id=1, source_target_pairs={{0,4},{1,5},{4,8},{5,9},{8,12},{9,13},{12,14},{13,15},{14,10},{15,... | collective-permute-start | bytes 1769480 | tf_op jit(solution)/shard_map/ppermute | solution.py:312
  38.0 2.2 %shard_map.80 = (f32[128,256]{1,0:T(8,128)S(1)}, f32[128,256]{1,0:T(8,128)S(1)}) custom-call(s32[8]{0:T(128)S(1)} %fusion.6.owners_ref, bf16[128,28672]{1,0:T(8,128)(2,1)} %refs_0_.15, bf16[128,28672]{1,0:T(8,128)(2,1)} %collective-permute-done.1.refs_3_.refs_1_, bf16[1152,256]{1,0:T(8,128)(2,1)S(1)} %collective-permute-done.6.refs_2_, ...), custom_call_target="tpu_custom_call" | custom-call | flops 1 | bytes 1 | tf_op jit(solution)/shard_map/pallas_call | solution.py:116
  40.2 7.3 %collective-permute-done.5.refs_3_ = bf16[1152,256]{1,0:T(8,128)(2,1)S(1)} collective-permute-done((bf16[1152,256]{1,0:T(8,128)(2,1)}, bf16[1152,256]{1,0:T(8,128)(2,1)S(1)}, u32[]{:S(2)}, u32[]{:S(2)}) %collective-permute-start.5) | collective-permute-done | bytes 589856 | tf_op jit(solution)/shard_map/ppermute | solution.py:312
  47.5 1.3 %collective-permute-done.3.refs_2_.refs_5_ = bf16[1152,256]{1,0:T(8,128)(2,1)S(1)} collective-permute-done((bf16[1152,256]{1,0:T(8,128)(2,1)S(1)}, bf16[1152,256]{1,0:T(8,128)(2,1)S(1)}, u32[]{:S(2)}, u32[]{:S(2)}) %collective-permute-start.3) | collective-permute-done | bytes 589856 | tf_op jit(solution)/shard_map/ppermute | solution.py:312
  48.8 1.8 %collective-permute-start.8 = (bf16[1152,256]{1,0:T(8,128)(2,1)S(1)}, bf16[1152,256]{1,0:T(8,128)(2,1)S(1)}, u32[]{:S(2)}, u32[]{:S(2)}) collective-permute-start(bf16[1152,256]{1,0:T(8,128)(2,1)S(1)} %collective-permute-done.3.refs_2_.refs_5_), channel_id=1, source_target_pairs={{0,4},{1,5},{4,8},{5,9},{8,12},{9,13},{12,14},{13,15},{14,10},{15,... | collective-permute-start | bytes 1769480 | tf_op jit(solution)/shard_map/ppermute | solution.py:312
  50.7 2.2 %shard_map.81 = (f32[128,256]{1,0:T(8,128)S(1)}, f32[128,256]{1,0:T(8,128)S(1)}) custom-call(s32[8]{0:T(128)S(1)} %fusion.6.owners_ref, bf16[128,28672]{1,0:T(8,128)(2,1)} %refs_0_.15, bf16[128,28672]{1,0:T(8,128)(2,1)} %collective-permute-done.1.refs_3_.refs_1_, bf16[1152,256]{1,0:T(8,128)(2,1)S(1)} %collective-permute-done.3.refs_2_.refs_5_, ...), custom_call_target="tpu_custom_call" | custom-call | flops 1 | bytes 1 | tf_op jit(solution)/shard_map/pallas_call | solution.py:116
  52.9 7.3 %collective-permute-done.11.refs_3_.refs_6_ = bf16[1152,256]{1,0:T(8,128)(2,1)S(1)} collective-permute-done((bf16[1152,256]{1,0:T(8,128)(2,1)S(1)}, bf16[1152,256]{1,0:T(8,128)(2,1)S(1)}, u32[]{:S(2)}, u32[]{:S(2)}) %collective-permute-start.11) | collective-permute-done | bytes 589856 | tf_op jit(solution)/shard_map/ppermute | solution.py:312
  60.2 1.3 %collective-permute-done.10.refs_2_ = bf16[1152,256]{1,0:T(8,128)(2,1)S(1)} collective-permute-done((bf16[1152,256]{1,0:T(8,128)(2,1)S(1)}, bf16[1152,256]{1,0:T(8,128)(2,1)S(1)}, u32[]{:S(2)}, u32[]{:S(2)}) %collective-permute-start.10) | collective-permute-done | bytes 589856 | tf_op jit(solution)/shard_map/ppermute | solution.py:312
  61.5 1.8 %collective-permute-start.14 = (bf16[1152,256]{1,0:T(8,128)(2,1)S(1)}, bf16[1152,256]{1,0:T(8,128)(2,1)S(1)}, u32[]{:S(2)}, u32[]{:S(2)}) collective-permute-start(bf16[1152,256]{1,0:T(8,128)(2,1)S(1)} %collective-permute-done.11.refs_3_.refs_6_), channel_id=1, source_target_pairs={{0,2},{1,3},{4,0},{5,1},{8,4},{9,5},{12,8},{13,9},{14,12},{15,13},... | collective-permute-start | bytes 1769480 | tf_op jit(solution)/shard_map/ppermute | solution.py:312
  63.5 2.2 %shard_map.82 = (f32[128,256]{1,0:T(8,128)S(1)}, f32[128,256]{1,0:T(8,128)S(1)}) custom-call(s32[8]{0:T(128)S(1)} %fusion.6.owners_ref, bf16[128,28672]{1,0:T(8,128)(2,1)} %refs_0_.15, bf16[128,28672]{1,0:T(8,128)(2,1)} %collective-permute-done.1.refs_3_.refs_1_, bf16[1152,256]{1,0:T(8,128)(2,1)S(1)} %collective-permute-done.10.refs_2_, ...), custom_call_target="tpu_custom_call" | custom-call | flops 1 | bytes 1 | tf_op jit(solution)/shard_map/pallas_call | solution.py:116
  65.7 7.1 %collective-permute-done.9.refs_3_ = bf16[1152,256]{1,0:T(8,128)(2,1)S(1)} collective-permute-done((bf16[1152,256]{1,0:T(8,128)(2,1)S(1)}, bf16[1152,256]{1,0:T(8,128)(2,1)S(1)}, u32[]{:S(2)}, u32[]{:S(2)}) %collective-permute-start.9) | collective-permute-done | bytes 589856 | tf_op jit(solution)/shard_map/ppermute | solution.py:312
  72.8 1.3 %collective-permute-done.8.refs_2_.refs_7_ = bf16[1152,256]{1,0:T(8,128)(2,1)S(1)} collective-permute-done((bf16[1152,256]{1,0:T(8,128)(2,1)S(1)}, bf16[1152,256]{1,0:T(8,128)(2,1)S(1)}, u32[]{:S(2)}, u32[]{:S(2)}) %collective-permute-start.8) | collective-permute-done | bytes 589856 | tf_op jit(solution)/shard_map/ppermute | solution.py:312
  74.1 1.8 %collective-permute-start.12 = (bf16[1152,256]{1,0:T(8,128)(2,1)S(1)}, bf16[1152,256]{1,0:T(8,128)(2,1)S(1)}, u32[]{:S(2)}, u32[]{:S(2)}) collective-permute-start(bf16[1152,256]{1,0:T(8,128)(2,1)S(1)} %collective-permute-done.8.refs_2_.refs_7_), channel_id=1, source_target_pairs={{0,4},{1,5},{4,8},{5,9},{8,12},{9,13},{12,14},{13,15},{14,10},{15,... | collective-permute-start | bytes 1769480 | tf_op jit(solution)/shard_map/ppermute | solution.py:312
  76.2 1.9 %shard_map.77 = (bf16[128,2304]{1,0:T(8,128)(2,1)S(1)}, bf16[128,2304]{1,0:T(8,128)(2,1)S(1)}) custom-call(s32[8]{0:T(128)S(1)} %fusion.6.owners_ref, bf16[128,8192]{1,0:T(8,128)(2,1)} %refs_0_.14, bf16[128,28672]{1,0:T(8,128)(2,1)} %refs_0_.15, bf16[128,8192]{1,0:T(8,128)(2,1)} %collective-permute-done.refs_2_.refs_1_, ...), custom_call_target="tpu_custom_call" | custom-call | flops 1 | bytes 1 | tf_op jit(solution)/shard_map/pallas_call | solution.py:194
  78.1 2.2 %shard_map.83 = (f32[128,256]{1,0:T(8,128)S(1)}, f32[128,256]{1,0:T(8,128)S(1)}) custom-call(s32[8]{0:T(128)S(1)} %fusion.6.owners_ref, bf16[128,28672]{1,0:T(8,128)(2,1)} %refs_0_.15, bf16[128,28672]{1,0:T(8,128)(2,1)} %collective-permute-done.1.refs_3_.refs_1_, bf16[1152,256]{1,0:T(8,128)(2,1)S(1)} %collective-permute-done.8.refs_2_.refs_7_, ...), custom_call_target="tpu_custom_call" | custom-call | flops 1 | bytes 1 | tf_op jit(solution)/shard_map/pallas_call | solution.py:116
  80.3 5.1 %collective-permute-done.14.refs_8_.refs_3_ = bf16[1152,256]{1,0:T(8,128)(2,1)S(1)} collective-permute-done((bf16[1152,256]{1,0:T(8,128)(2,1)S(1)}, bf16[1152,256]{1,0:T(8,128)(2,1)S(1)}, u32[]{:S(2)}, u32[]{:S(2)}) %collective-permute-start.14) | collective-permute-done | bytes 589856 | tf_op jit(solution)/shard_map/ppermute | solution.py:312
  85.5 3.1 %shard_map.84 = (f32[128,256]{1,0:T(8,128)S(1)}, f32[128,256]{1,0:T(8,128)S(1)}) custom-call(s32[8]{0:T(128)S(1)} %fusion.6.owners_ref, bf16[128,8192]{1,0:T(8,128)(2,1)} %refs_0_.14, bf16[128,8192]{1,0:T(8,128)(2,1)} %collective-permute-done.refs_2_.refs_1_, bf16[1152,256]{1,0:T(8,128)(2,1)S(1)} %get-tuple-element.59.refs_2_, ...), custom_call_target="tpu_custom_call" | custom-call | flops 1 | bytes 1 | tf_op jit(solution)/shard_map/pallas_call | solution.py:116
  88.6 2.2 %shard_map.85 = (f32[128,256]{1,0:T(8,128)S(1)}, f32[128,256]{1,0:T(8,128)S(1)}) custom-call(s32[8]{0:T(128)S(1)} %fusion.6.owners_ref, bf16[128,28672]{1,0:T(8,128)(2,1)} %refs_0_.15, bf16[128,28672]{1,0:T(8,128)(2,1)} %collective-permute-done.1.refs_3_.refs_1_, bf16[1152,256]{1,0:T(8,128)(2,1)S(1)} %collective-permute-done.15.refs_2_, ...), custom_call_target="tpu_custom_call" | custom-call | flops 1 | bytes 1 | tf_op jit(solution)/shard_map/pallas_call | solution.py:116
  90.7 7.7 %collective-permute-done.12.first_ref = bf16[1152,256]{1,0:T(8,128)(2,1)S(1)} collective-permute-done((bf16[1152,256]{1,0:T(8,128)(2,1)S(1)}, bf16[1152,256]{1,0:T(8,128)(2,1)S(1)}, u32[]{:S(2)}, u32[]{:S(2)}) %collective-permute-start.12) | collective-permute-done | bytes 589856 | tf_op jit(solution)/shard_map/ppermute | solution.py:312
  98.5 0.3 shard_map.86
  98.9 0.3 shard_map.87
  99.2 1.2 collective-permute-done.16
  100.5 1.6 %collective-permute-start.17 = (bf16[144,512]{1,0:T(8,128)(2,1)S(1)}, bf16[144,512]{1,0:T(8,128)(2,1)S(1)}, u32[]{:S(2)}, u32[]{:S(2)}) collective-permute-start(bf16[144,512]{1,0:T(8,128)(2,1)S(1)} %pad_maximum_fusion), channel_id=1, source_target_pairs={{0,4},{1,5},{4,8},{5,9},{8,12},{9,13},{12,14},{13,15},{14,10},{15,... | collective-permute-start | bytes 442376 | tf_op jit(solution)/shard_map/ppermute | solution.py:312
  102.2 0.4 collective-permute-start.18
  102.6 3.9 %collective-permute-done.17 = bf16[144,512]{1,0:T(8,128)(2,1)S(1)} collective-permute-done((bf16[144,512]{1,0:T(8,128)(2,1)S(1)}, bf16[144,512]{1,0:T(8,128)(2,1)S(1)}, u32[]{:S(2)}, u32[]{:S(2)}) %collective-permute-start.17) | collective-permute-done | bytes 147488 | tf_op jit(solution)/shard_map/ppermute | solution.py:312
  106.5 1.6 %collective-permute-start.19 = (bf16[144,512]{1,0:T(8,128)(2,1)S(1)}, bf16[144,512]{1,0:T(8,128)(2,1)S(1)}, u32[]{:S(2)}, u32[]{:S(2)}) collective-permute-start(bf16[144,512]{1,0:T(8,128)(2,1)S(1)} %collective-permute-done.17), channel_id=1, source_target_pairs={{0,4},{1,5},{4,8},{5,9},{8,12},{9,13},{12,14},{13,15},{14,10},{15,... | collective-permute-start | bytes 442376 | tf_op jit(solution)/shard_map/ppermute | solution.py:312
  108.1 0.4 collective-permute-start.20
  108.5 3.1 %collective-permute-done.19 = bf16[144,512]{1,0:T(8,128)(2,1)S(1)} collective-permute-done((bf16[144,512]{1,0:T(8,128)(2,1)S(1)}, bf16[144,512]{1,0:T(8,128)(2,1)S(1)}, u32[]{:S(2)}, u32[]{:S(2)}) %collective-permute-start.19) | collective-permute-done | bytes 147488 | tf_op jit(solution)/shard_map/ppermute | solution.py:312
  111.6 1.6 %collective-permute-start.21 = (bf16[144,512]{1,0:T(8,128)(2,1)S(1)}, bf16[144,512]{1,0:T(8,128)(2,1)S(1)}, u32[]{:S(2)}, u32[]{:S(2)}) collective-permute-start(bf16[144,512]{1,0:T(8,128)(2,1)S(1)} %collective-permute-done.19), channel_id=1, source_target_pairs={{0,4},{1,5},{4,8},{5,9},{8,12},{9,13},{12,14},{13,15},{14,10},{15,... | collective-permute-start | bytes 442376 | tf_op jit(solution)/shard_map/ppermute | solution.py:312
  113.2 0.4 collective-permute-start.22
  113.7 3.1 %collective-permute-done.21 = bf16[144,512]{1,0:T(8,128)(2,1)S(1)} collective-permute-done((bf16[144,512]{1,0:T(8,128)(2,1)S(1)}, bf16[144,512]{1,0:T(8,128)(2,1)S(1)}, u32[]{:S(2)}, u32[]{:S(2)}) %collective-permute-start.21) | collective-permute-done | bytes 147488 | tf_op jit(solution)/shard_map/ppermute | solution.py:312
  116.8 1.6 %collective-permute-done.22 = bf16[144,512]{1,0:T(8,128)(2,1)S(1)} collective-permute-done((bf16[144,512]{1,0:T(8,128)(2,1)S(1)}, bf16[144,512]{1,0:T(8,128)(2,1)S(1)}, u32[]{:S(2)}, u32[]{:S(2)}) %collective-permute-start.22) | collective-permute-done | bytes 147488 | tf_op jit(solution)/shard_map/ppermute | solution.py:312
  118.4 1.6 %collective-permute-start.23 = (bf16[144,512]{1,0:T(8,128)(2,1)S(1)}, bf16[144,512]{1,0:T(8,128)(2,1)S(1)}, u32[]{:S(2)}, u32[]{:S(2)}) collective-permute-start(bf16[144,512]{1,0:T(8,128)(2,1)S(1)} %get-tuple-element.114), channel_id=1, source_target_pairs={{0,4},{4,8},{8,12},{12,14},{14,10},{10,6},{6,2},{2,0},{1,3},{5,1},... | collective-permute-start | bytes 442376 | tf_op jit(solution)/shard_map/ppermute | solution.py:312
  120.1 3.6 %collective-permute-done.23.refs_2_ = bf16[144,512]{1,0:T(8,128)(2,1)S(1)} collective-permute-done((bf16[144,512]{1,0:T(8,128)(2,1)S(1)}, bf16[144,512]{1,0:T(8,128)(2,1)S(1)}, u32[]{:S(2)}, u32[]{:S(2)}) %collective-permute-start.23) | collective-permute-done | bytes 147488 | tf_op jit(solution)/shard_map/ppermute | solution.py:312
  123.6 1.4 %collective-permute-done.26.refs_5_ = bf16[144,512]{1,0:T(8,128)(2,1)S(1)} collective-permute-done((bf16[144,512]{1,0:T(8,128)(2,1)S(1)}, bf16[144,512]{1,0:T(8,128)(2,1)S(1)}, u32[]{:S(2)}, u32[]{:S(2)}) %collective-permute-start.26) | collective-permute-done | bytes 147488 | tf_op jit(solution)/shard_map/ppermute | solution.py:312
  125.0 1.5 %shard_map.88 = (f32[16,256]{1,0:T(8,128)}, f32[1,64]{1,0:T(1,128)}) custom-call(s32[1]{0:T(128)} %bitcast.me_ref, bf16[720,512]{1,0:T(8,128)(2,1)S(1)} %constant_dynamic-update-slice_fusion.refs_0_, bf16[288,512]{1,0:T(8,128)(2,1)S(1)} %get-tuple-element.115.refs_1_, bf16[144,512]{1,0:T(8,128)(2,1)S(1)} %collective-permute-done.23.refs_2_, ...), custom_call_target="tpu_custom_call" | custom-call | tf_op jit(solution)/shard_map/pallas_call | solution.py:273
  (36 shorter events, 1.0 us)
Async XLA Ops:
  0.6 21.7 %collective-permute-start.1 = (bf16[128,28672]{1,0:T(8,128)(2,1)}, bf16[128,28672]{1,0:T(8,128)(2,1)}, u32[]{:S(2)}, u32[]{:S(2)}) collective-permute-start(bf16[128,28672]{1,0:T(8,128)(2,1)} %refs_0_.15), channel_id=1, source_target_pairs={{0,1},{1,0},{2,3},{3,2},{4,5},{5,4},{6,7},{7,6},{8,9},{9,8},{10,11... | collective-permute-start | bytes 22020104 | tf_op jit(solution)/shard_map/ppermute | solution.py:312
  3.2 16.6 %collective-permute-start.2 = (bf16[1152,256]{1,0:T(8,128)(2,1)S(1)}, bf16[1152,256]{1,0:T(8,128)(2,1)S(1)}, u32[]{:S(2)}, u32[]{:S(2)}) collective-permute-start(bf16[1152,256]{1,0:T(8,128)(2,1)S(1)} %get-tuple-element.59.refs_2_), channel_id=1, source_target_pairs={{0,4},{1,5},{4,8},{5,9},{8,12},{9,13},{12,14},{13,15},{14,10},{15,... | collective-permute-start | bytes 1769480 | tf_op jit(solution)/shard_map/ppermute | solution.py:312
  5.9 16.5 %collective-permute-start.4 = (bf16[1152,256]{1,0:T(8,128)(2,1)}, bf16[1152,256]{1,0:T(8,128)(2,1)}, u32[]{:S(2)}, u32[]{:S(2)}) collective-permute-start(bf16[1152,256]{1,0:T(8,128)(2,1)} %get-tuple-element.60.refs_3_), channel_id=1, source_target_pairs={{0,2},{1,3},{4,0},{5,1},{8,4},{9,5},{12,8},{13,9},{14,12},{15,13},... | collective-permute-start | bytes 1769480 | tf_op jit(solution)/shard_map/ppermute | solution.py:312
  5.9 70.3 %collective-permute-start = (bf16[128,8192]{1,0:T(8,128)(2,1)}, bf16[128,8192]{1,0:T(8,128)(2,1)}, u32[]{:S(2)}, u32[]{:S(2)}) collective-permute-start(bf16[128,8192]{1,0:T(8,128)(2,1)} %refs_0_.14), channel_id=1, source_target_pairs={{0,1},{1,0},{2,3},{3,2},{4,5},{5,4},{6,7},{7,6},{8,9},{9,8},{10,11... | collective-permute-start | bytes 6291464 | tf_op jit(solution)/shard_map/ppermute | solution.py:312
  6.1 28.8 %collective-permute-start.7 = (bf16[1152,256]{1,0:T(8,128)(2,1)S(1)}, bf16[1152,256]{1,0:T(8,128)(2,1)S(1)}, u32[]{:S(2)}, u32[]{:S(2)}) collective-permute-start(bf16[1152,256]{1,0:T(8,128)(2,1)S(1)} %get-tuple-element.59.refs_2_), channel_id=1, source_target_pairs={{0,2},{1,3},{4,0},{5,1},{8,4},{9,5},{12,8},{13,9},{14,12},{15,13},... | collective-permute-start | bytes 1769480 | tf_op jit(solution)/shard_map/ppermute | solution.py:312
  19.8 16.4 %collective-permute-start.6 = (bf16[1152,256]{1,0:T(8,128)(2,1)}, bf16[1152,256]{1,0:T(8,128)(2,1)S(1)}, u32[]{:S(2)}, u32[]{:S(2)}) collective-permute-start(bf16[1152,256]{1,0:T(8,128)(2,1)} %get-tuple-element.60.refs_3_), channel_id=1, source_target_pairs={{0,4},{1,5},{4,8},{5,9},{8,12},{9,13},{12,14},{13,15},{14,10},{15,... | collective-permute-start | bytes 1769480 | tf_op jit(solution)/shard_map/ppermute | solution.py:312
  22.4 25.2 %collective-permute-start.5 = (bf16[1152,256]{1,0:T(8,128)(2,1)}, bf16[1152,256]{1,0:T(8,128)(2,1)S(1)}, u32[]{:S(2)}, u32[]{:S(2)}) collective-permute-start(bf16[1152,256]{1,0:T(8,128)(2,1)} %collective-permute-done.4.refs_5_), channel_id=1, source_target_pairs={{0,2},{1,3},{4,0},{5,1},{8,4},{9,5},{12,8},{13,9},{14,12},{15,13},... | collective-permute-start | bytes 1769480 | tf_op jit(solution)/shard_map/ppermute | solution.py:312
  22.4 26.5 %collective-permute-start.3 = (bf16[1152,256]{1,0:T(8,128)(2,1)S(1)}, bf16[1152,256]{1,0:T(8,128)(2,1)S(1)}, u32[]{:S(2)}, u32[]{:S(2)}) collective-permute-start(bf16[1152,256]{1,0:T(8,128)(2,1)S(1)} %collective-permute-done.2.refs_4_.refs_3_), channel_id=1, source_target_pairs={{0,4},{1,5},{4,8},{5,9},{8,12},{9,13},{12,14},{13,15},{14,10},{15,... | collective-permute-start | bytes 1769480 | tf_op jit(solution)/shard_map/ppermute | solution.py:312
  34.9 25.3 %collective-permute-start.11 = (bf16[1152,256]{1,0:T(8,128)(2,1)S(1)}, bf16[1152,256]{1,0:T(8,128)(2,1)S(1)}, u32[]{:S(2)}, u32[]{:S(2)}) collective-permute-start(bf16[1152,256]{1,0:T(8,128)(2,1)S(1)} %collective-permute-done.7.refs_3_.refs_4_), channel_id=1, source_target_pairs={{0,2},{1,3},{4,0},{5,1},{8,4},{9,5},{12,8},{13,9},{14,12},{15,13},... | collective-permute-start | bytes 1769480 | tf_op jit(solution)/shard_map/ppermute | solution.py:312
  36.2 25.3 %collective-permute-start.10 = (bf16[1152,256]{1,0:T(8,128)(2,1)S(1)}, bf16[1152,256]{1,0:T(8,128)(2,1)S(1)}, u32[]{:S(2)}, u32[]{:S(2)}) collective-permute-start(bf16[1152,256]{1,0:T(8,128)(2,1)S(1)} %collective-permute-done.6.refs_2_), channel_id=1, source_target_pairs={{0,4},{1,5},{4,8},{5,9},{8,12},{9,13},{12,14},{13,15},{14,10},{15,... | collective-permute-start | bytes 1769480 | tf_op jit(solution)/shard_map/ppermute | solution.py:312
  47.5 25.3 %collective-permute-start.9 = (bf16[1152,256]{1,0:T(8,128)(2,1)S(1)}, bf16[1152,256]{1,0:T(8,128)(2,1)S(1)}, u32[]{:S(2)}, u32[]{:S(2)}) collective-permute-start(bf16[1152,256]{1,0:T(8,128)(2,1)S(1)} %collective-permute-done.5.refs_3_), channel_id=1, source_target_pairs={{0,2},{1,3},{4,0},{5,1},{8,4},{9,5},{12,8},{13,9},{14,12},{15,13},... | collective-permute-start | bytes 1769480 | tf_op jit(solution)/shard_map/ppermute | solution.py:312
  48.8 25.3 %collective-permute-start.8 = (bf16[1152,256]{1,0:T(8,128)(2,1)S(1)}, bf16[1152,256]{1,0:T(8,128)(2,1)S(1)}, u32[]{:S(2)}, u32[]{:S(2)}) collective-permute-start(bf16[1152,256]{1,0:T(8,128)(2,1)S(1)} %collective-permute-done.3.refs_2_.refs_5_), channel_id=1, source_target_pairs={{0,4},{1,5},{4,8},{5,9},{8,12},{9,13},{12,14},{13,15},{14,10},{15,... | collective-permute-start | bytes 1769480 | tf_op jit(solution)/shard_map/ppermute | solution.py:312
  60.2 16.0 %copy-start = (s32[128]{0:T(128)S(1)}, s32[128]{0:T(128)}, u32[]{:S(2)}) copy-start(s32[128]{0:T(128)} %param.8) | copy-start | bytes 1540
  61.5 24.0 %collective-permute-start.14 = (bf16[1152,256]{1,0:T(8,128)(2,1)S(1)}, bf16[1152,256]{1,0:T(8,128)(2,1)S(1)}, u32[]{:S(2)}, u32[]{:S(2)}) collective-permute-start(bf16[1152,256]{1,0:T(8,128)(2,1)S(1)} %collective-permute-done.11.refs_3_.refs_6_), channel_id=1, source_target_pairs={{0,2},{1,3},{4,0},{5,1},{8,4},{9,5},{12,8},{13,9},{14,12},{15,13},... | collective-permute-start | bytes 1769480 | tf_op jit(solution)/shard_map/ppermute | solution.py:312
  63.3 25.3 %collective-permute-start.15 = (bf16[1152,256]{1,0:T(8,128)(2,1)S(1)}, bf16[1152,256]{1,0:T(8,128)(2,1)S(1)}, u32[]{:S(2)}, u32[]{:S(2)}) collective-permute-start(bf16[1152,256]{1,0:T(8,128)(2,1)S(1)} %collective-permute-done.10.refs_2_), channel_id=1, source_target_pairs={{0,4},{1,5},{4,8},{5,9},{8,12},{9,13},{12,14},{13,15},{14,10},{15,... | collective-permute-start | bytes 1769480 | tf_op jit(solution)/shard_map/ppermute | solution.py:312
  74.1 24.3 %collective-permute-start.12 = (bf16[1152,256]{1,0:T(8,128)(2,1)S(1)}, bf16[1152,256]{1,0:T(8,128)(2,1)S(1)}, u32[]{:S(2)}, u32[]{:S(2)}) collective-permute-start(bf16[1152,256]{1,0:T(8,128)(2,1)S(1)} %collective-permute-done.8.refs_2_.refs_7_), channel_id=1, source_target_pairs={{0,4},{1,5},{4,8},{5,9},{8,12},{9,13},{12,14},{13,15},{14,10},{15,... | collective-permute-start | bytes 1769480 | tf_op jit(solution)/shard_map/ppermute | solution.py:312
  76.0 22.5 %collective-permute-start.13 = (bf16[1152,256]{1,0:T(8,128)(2,1)S(1)}, bf16[1152,256]{1,0:T(8,128)(2,1)S(1)}, u32[]{:S(2)}, u32[]{:S(2)}) collective-permute-start(bf16[1152,256]{1,0:T(8,128)(2,1)S(1)} %collective-permute-done.9.refs_3_), channel_id=1, source_target_pairs={{0,2},{1,3},{4,0},{5,1},{8,4},{9,5},{12,8},{13,9},{14,12},{15,13},... | collective-permute-start | bytes 1769480 | tf_op jit(solution)/shard_map/ppermute | solution.py:312
  98.8 1.6 %collective-permute-start.16 = (f32[128,512]{1,0:T(8,128)S(1)}, f32[128,512]{1,0:T(8,128)S(1)}, u32[]{:S(2)}, u32[]{:S(2)}) collective-permute-start(f32[128,512]{1,0:T(8,128)S(1)} %shard_map.86), channel_id=1, source_target_pairs={{0,1},{1,0},{2,3},{3,2},{4,5},{5,4},{6,7},{7,6},{8,9},{9,8},{10,11... | collective-permute-start | bytes 786440 | tf_op jit(solution)/shard_map/ppermute | solution.py:312
  100.5 5.9 %collective-permute-start.17 = (bf16[144,512]{1,0:T(8,128)(2,1)S(1)}, bf16[144,512]{1,0:T(8,128)(2,1)S(1)}, u32[]{:S(2)}, u32[]{:S(2)}) collective-permute-start(bf16[144,512]{1,0:T(8,128)(2,1)S(1)} %pad_maximum_fusion), channel_id=1, source_target_pairs={{0,4},{1,5},{4,8},{5,9},{8,12},{9,13},{12,14},{13,15},{14,10},{15,... | collective-permute-start | bytes 442376 | tf_op jit(solution)/shard_map/ppermute | solution.py:312
  102.2 5.9 %collective-permute-start.18 = (bf16[144,512]{1,0:T(8,128)(2,1)S(1)}, bf16[144,512]{1,0:T(8,128)(2,1)S(1)}, u32[]{:S(2)}, u32[]{:S(2)}) collective-permute-start(bf16[144,512]{1,0:T(8,128)(2,1)S(1)} %pad_maximum_fusion), channel_id=1, source_target_pairs={{0,2},{1,3},{4,0},{5,1},{8,4},{9,5},{12,8},{13,9},{14,12},{15,13},... | collective-permute-start | bytes 442376 | tf_op jit(solution)/shard_map/ppermute | solution.py:312
  106.5 5.1 %collective-permute-start.19 = (bf16[144,512]{1,0:T(8,128)(2,1)S(1)}, bf16[144,512]{1,0:T(8,128)(2,1)S(1)}, u32[]{:S(2)}, u32[]{:S(2)}) collective-permute-start(bf16[144,512]{1,0:T(8,128)(2,1)S(1)} %collective-permute-done.17), channel_id=1, source_target_pairs={{0,4},{1,5},{4,8},{5,9},{8,12},{9,13},{12,14},{13,15},{14,10},{15,... | collective-permute-start | bytes 442376 | tf_op jit(solution)/shard_map/ppermute | solution.py:312
  108.1 5.1 %collective-permute-start.20 = (bf16[144,512]{1,0:T(8,128)(2,1)S(1)}, bf16[144,512]{1,0:T(8,128)(2,1)S(1)}, u32[]{:S(2)}, u32[]{:S(2)}) collective-permute-start(bf16[144,512]{1,0:T(8,128)(2,1)S(1)} %collective-permute-done.18), channel_id=1, source_target_pairs={{0,2},{1,3},{4,0},{5,1},{8,4},{9,5},{12,8},{13,9},{14,12},{15,13},... | collective-permute-start | bytes 442376 | tf_op jit(solution)/shard_map/ppermute | solution.py:312
  111.6 5.1 %collective-permute-start.21 = (bf16[144,512]{1,0:T(8,128)(2,1)S(1)}, bf16[144,512]{1,0:T(8,128)(2,1)S(1)}, u32[]{:S(2)}, u32[]{:S(2)}) collective-permute-start(bf16[144,512]{1,0:T(8,128)(2,1)S(1)} %collective-permute-done.19), channel_id=1, source_target_pairs={{0,4},{1,5},{4,8},{5,9},{8,12},{9,13},{12,14},{13,15},{14,10},{15,... | collective-permute-start | bytes 442376 | tf_op jit(solution)/shard_map/ppermute | solution.py:312
  113.2 5.1 %collective-permute-start.22 = (bf16[144,512]{1,0:T(8,128)(2,1)S(1)}, bf16[144,512]{1,0:T(8,128)(2,1)S(1)}, u32[]{:S(2)}, u32[]{:S(2)}) collective-permute-start(bf16[144,512]{1,0:T(8,128)(2,1)S(1)} %collective-permute-done.20), channel_id=1, source_target_pairs={{0,2},{1,3},{4,0},{5,1},{8,4},{9,5},{12,8},{13,9},{14,12},{15,13},... | collective-permute-start | bytes 442376 | tf_op jit(solution)/shard_map/ppermute | solution.py:312
  118.4 6.6 %collective-permute-start.24 = (bf16[720,512]{1,0:T(8,128)(2,1)S(1)}, bf16[720,512]{1,0:T(8,128)(2,1)S(1)}, u32[]{:S(2)}, u32[]{:S(2)}) collective-permute-start(bf16[720,512]{1,0:T(8,128)(2,1)S(1)} %constant_dynamic-update-slice_fusion.refs_0_), channel_id=1, source_target_pairs={{0,1},{1,0},{2,3},{3,2},{4,5},{5,4},{6,7},{7,6},{8,9},{9,8},{10,11... | collective-permute-start | bytes 2211848 | tf_op jit(solution)/shard_map/ppermute | solution.py:312
  118.4 5.2 %collective-permute-start.23 = (bf16[144,512]{1,0:T(8,128)(2,1)S(1)}, bf16[144,512]{1,0:T(8,128)(2,1)S(1)}, u32[]{:S(2)}, u32[]{:S(2)}) collective-permute-start(bf16[144,512]{1,0:T(8,128)(2,1)S(1)} %get-tuple-element.114), channel_id=1, source_target_pairs={{0,4},{4,8},{8,12},{12,14},{14,10},{10,6},{6,2},{2,0},{1,3},{5,1},... | collective-permute-start | bytes 442376 | tf_op jit(solution)/shard_map/ppermute | solution.py:312
  120.1 4.9 %collective-permute-start.25 = (bf16[288,512]{1,0:T(8,128)(2,1)S(1)}, bf16[288,512]{1,0:T(8,128)(2,1)S(1)}, u32[]{:S(2)}, u32[]{:S(2)}) collective-permute-start(bf16[288,512]{1,0:T(8,128)(2,1)S(1)} %get-tuple-element.115.refs_1_), channel_id=1, source_target_pairs={{0,1},{1,0},{2,3},{3,2},{4,5},{5,4},{6,7},{7,6},{8,9},{9,8},{10,11... | collective-permute-start | bytes 884744 | tf_op jit(solution)/shard_map/ppermute | solution.py:312
  123.6 1.4 %collective-permute-start.26 = (bf16[144,512]{1,0:T(8,128)(2,1)S(1)}, bf16[144,512]{1,0:T(8,128)(2,1)S(1)}, u32[]{:S(2)}, u32[]{:S(2)}) collective-permute-start(bf16[144,512]{1,0:T(8,128)(2,1)S(1)} %collective-permute-done.23.refs_2_), channel_id=1, source_target_pairs={{0,1},{1,0},{2,3},{3,2},{4,5},{5,4},{6,7},{7,6},{8,9},{9,8},{10,11... | collective-permute-start | bytes 442376 | tf_op jit(solution)/shard_map/ppermute | solution.py:312

commit v5 on v4

--- a/solution.py
+++ b/solution.py
@@ -345,9 +345,11 @@
             held[d] = x
         return list(got[len(at) :])
 
+    swapped_act, swapped_grad = send(activations, swap), send(out_grads, swap)
     hop(first, second, 1)
-    hop(second, first, 1)
-    swapped_grad, swapped_act = send(out_grads, swap), None
+    second[1] = send(second[0], forward)
+    ready, swapped_act = lax.optimization_barrier((first[0], swapped_act))
+    first[-1] = send(ready, backward)
     zero = jnp.zeros((rows, width), jnp.float32)
     grad = [zero, zero]
     for s in range(1, half):
@@ -363,7 +365,6 @@
         grad = add((1,), pieces(second, [s]) + pieces(first, [-s]), grad)
         if s + 1 < half:
             grad = after(first, [s + 1], after(second, [-s - 1], grad))
-    swapped_act = send(activations, swap)
     act = add((0,), pieces(first, distances[:-1]), [zero, zero])
     tokens = (activations, out_grads, swapped_act, swapped_grad)
     block, *act = fetch(owners, chips - 1, tokens, depth_in, depth_out, act)

time: 127 us -> 125 us (0.984)
  waiting for transfers between devices: 76.2 us -> 73.3 us
    ppermute x27, waiting for transfers between devices: 76.2 us -> 73.3 us  [send(): return lax.ppermute(x, 'dp', pairs)]
  transfers between devices with their start and end apart: 27 -> 27, of which waited for: 19 -> 17; matrix products, arithmetic and copies ran while one was open for 1% -> 1% of each run, Pallas kernels for 18% -> 18%
where the time goes in v5:
time: 125 us; the launch traced here: 124 us
  waiting for transfers between devices  73.3 us (59%)
  starting transfers between devices  25.1 us (20%)
  Pallas kernels  24 us (19%)
    ppermute x27, waiting for transfers between devices, send(): return lax.ppermute(x, 'dp', pairs)  73.3 us
    ppermute x27, starting transfers between devices, send(): return lax.ppermute(x, 'dp', pairs)  25.1 us
    pallas_call x7, Pallas kernels, project(): pl.pallas_call(functools.partial(project_kernel, kinds, [p[:2] for p in p...  17.9 us
  transfers between devices with their start and end apart: 27, of which 17 were waited for; matrix products, arithmetic and copies ran while one was open for 1% of the time, Pallas kernels for 18%

profile of v5, /device:TPU:0, one launch (start us, length us, event | category | flops | bytes accessed | tf_op | source)
XLA Modules:
  0.0 124.2 jit_solution(9005705142425426176)
XLA Ops:
  0.6 0.5 collective-permute-start.1
  1.2 2.1 %shard_map.77 = (bf16[1152,256]{1,0:T(8,128)(2,1)S(1)}, bf16[1152,256]{1,0:T(8,128)(2,1)}) custom-call(bf16[512,256]{1,0:T(8,128)(2,1)} %upper_ref.1, bf16[1792,256]{1,0:T(8,128)(2,1)} %lower_ref.1), custom_call_target="tpu_custom_call" | custom-call | tf_op jit(solution)/shard_map/pallas_call | solution.py:160
  3.3 3.0 %collective-permute-start.4 = (bf16[1152,256]{1,0:T(8,128)(2,1)}, bf16[1152,256]{1,0:T(8,128)(2,1)}, u32[]{:S(2)}, u32[]{:S(2)}) collective-permute-start(bf16[1152,256]{1,0:T(8,128)(2,1)} %get-tuple-element.63.refs_3_), channel_id=1, source_target_pairs={{0,2},{1,3},{4,0},{5,1},{8,4},{9,5},{12,8},{13,9},{14,12},{15,13},... | collective-permute-start | bytes 1769480 | tf_op jit(solution)/shard_map/ppermute | solution.py:312
  6.4 6.2 %collective-permute-done.refs_2_.refs_1_ = bf16[128,8192]{1,0:T(8,128)(2,1)S(1)} collective-permute-done((bf16[128,8192]{1,0:T(8,128)(2,1)}, bf16[128,8192]{1,0:T(8,128)(2,1)S(1)}, u32[]{:S(2)}, u32[]{:S(2)}) %collective-permute-start) | collective-permute-done | bytes 2097184 | tf_op jit(solution)/shard_map/ppermute | solution.py:312
  12.6 3.1 %collective-permute-start.7 = (bf16[1152,256]{1,0:T(8,128)(2,1)S(1)}, bf16[1152,256]{1,0:T(8,128)(2,1)S(1)}, u32[]{:S(2)}, u32[]{:S(2)}) collective-permute-start(bf16[1152,256]{1,0:T(8,128)(2,1)S(1)} %get-tuple-element.64.refs_2_), channel_id=1, source_target_pairs={{0,2},{1,3},{4,0},{5,1},{8,4},{9,5},{12,8},{13,9},{14,12},{15,13},... | collective-permute-start | bytes 1769480 | tf_op jit(solution)/shard_map/ppermute | solution.py:312
  15.8 5.0 %collective-permute-done.4.refs_5_ = bf16[1152,256]{1,0:T(8,128)(2,1)} collective-permute-done((bf16[1152,256]{1,0:T(8,128)(2,1)}, bf16[1152,256]{1,0:T(8,128)(2,1)}, u32[]{:S(2)}, u32[]{:S(2)}) %collective-permute-start.4) | collective-permute-done | bytes 589856 | tf_op jit(solution)/shard_map/ppermute | solution.py:312
  20.8 2.0 %collective-permute-start.5 = (bf16[1152,256]{1,0:T(8,128)(2,1)}, bf16[1152,256]{1,0:T(8,128)(2,1)S(1)}, u32[]{:S(2)}, u32[]{:S(2)}) collective-permute-start(bf16[1152,256]{1,0:T(8,128)(2,1)} %collective-permute-done.4.refs_5_), channel_id=1, source_target_pairs={{0,2},{1,3},{4,0},{5,1},{8,4},{9,5},{12,8},{13,9},{14,12},{15,13},... | collective-permute-start | bytes 1769480 | tf_op jit(solution)/shard_map/ppermute | solution.py:312
  22.9 0.7 fusion.6.owners_ref
  23.6 3.8 %shard_map.79 = (f32[128,256]{1,0:T(8,128)S(1)}, f32[128,256]{1,0:T(8,128)S(1)}) custom-call(s32[8]{0:T(128)S(1)} %fusion.6.owners_ref, bf16[128,28672]{1,0:T(8,128)(2,1)} %refs_0_.15, bf16[128,28672]{1,0:T(8,128)(2,1)} %collective-permute-done.1.refs_3_.refs_1_, bf16[1152,256]{1,0:T(8,128)(2,1)S(1)} %get-tuple-element.64.refs_2_, ...), custom_call_target="tpu_custom_call" | custom-call | flops 1 | bytes 1 | tf_op jit(solution)/shard_map/pallas_call | solution.py:116
  27.5 5.9 %collective-permute-done.7.refs_3_.refs_4_ = bf16[1152,256]{1,0:T(8,128)(2,1)S(1)} collective-permute-done((bf16[1152,256]{1,0:T(8,128)(2,1)S(1)}, bf16[1152,256]{1,0:T(8,128)(2,1)S(1)}, u32[]{:S(2)}, u32[]{:S(2)}) %collective-permute-start.7) | collective-permute-done | bytes 589856 | tf_op jit(solution)/shard_map/ppermute | solution.py:312
  33.3 2.0 %collective-permute-start.11 = (bf16[1152,256]{1,0:T(8,128)(2,1)S(1)}, bf16[1152,256]{1,0:T(8,128)(2,1)S(1)}, u32[]{:S(2)}, u32[]{:S(2)}) collective-permute-start(bf16[1152,256]{1,0:T(8,128)(2,1)S(1)} %collective-permute-done.7.refs_3_.refs_4_), channel_id=1, source_target_pairs={{0,2},{1,3},{4,0},{5,1},{8,4},{9,5},{12,8},{13,9},{14,12},{15,13},... | collective-permute-start | bytes 1769480 | tf_op jit(solution)/shard_map/ppermute | solution.py:312
  35.4 2.2 %shard_map.80 = (f32[128,256]{1,0:T(8,128)S(1)}, f32[128,256]{1,0:T(8,128)S(1)}) custom-call(s32[8]{0:T(128)S(1)} %fusion.6.owners_ref, bf16[128,28672]{1,0:T(8,128)(2,1)} %refs_0_.15, bf16[128,28672]{1,0:T(8,128)(2,1)} %collective-permute-done.1.refs_3_.refs_1_, bf16[1152,256]{1,0:T(8,128)(2,1)S(1)} %collective-permute-done.6.refs_2_, ...), custom_call_target="tpu_custom_call" | custom-call | flops 1 | bytes 1 | tf_op jit(solution)/shard_map/pallas_call | solution.py:116
  37.6 8.4 %collective-permute-done.5.refs_3_ = bf16[1152,256]{1,0:T(8,128)(2,1)S(1)} collective-permute-done((bf16[1152,256]{1,0:T(8,128)(2,1)}, bf16[1152,256]{1,0:T(8,128)(2,1)S(1)}, u32[]{:S(2)}, u32[]{:S(2)}) %collective-permute-start.5) | collective-permute-done | bytes 589856 | tf_op jit(solution)/shard_map/ppermute | solution.py:312
  46.0 2.0 %collective-permute-start.9 = (bf16[1152,256]{1,0:T(8,128)(2,1)S(1)}, bf16[1152,256]{1,0:T(8,128)(2,1)S(1)}, u32[]{:S(2)}, u32[]{:S(2)}) collective-permute-start(bf16[1152,256]{1,0:T(8,128)(2,1)S(1)} %collective-permute-done.5.refs_3_), channel_id=1, source_target_pairs={{0,2},{1,3},{4,0},{5,1},{8,4},{9,5},{12,8},{13,9},{14,12},{15,13},... | collective-permute-start | bytes 1769480 | tf_op jit(solution)/shard_map/ppermute | solution.py:312
  48.0 2.2 %shard_map.81 = (f32[128,256]{1,0:T(8,128)S(1)}, f32[128,256]{1,0:T(8,128)S(1)}) custom-call(s32[8]{0:T(128)S(1)} %fusion.6.owners_ref, bf16[128,28672]{1,0:T(8,128)(2,1)} %refs_0_.15, bf16[128,28672]{1,0:T(8,128)(2,1)} %collective-permute-done.1.refs_3_.refs_1_, bf16[1152,256]{1,0:T(8,128)(2,1)S(1)} %collective-permute-done.3.refs_2_.refs_5_, ...), custom_call_target="tpu_custom_call" | custom-call | flops 1 | bytes 1 | tf_op jit(solution)/shard_map/pallas_call | solution.py:116
  50.3 8.3 %collective-permute-done.11.refs_3_.refs_6_ = bf16[1152,256]{1,0:T(8,128)(2,1)S(1)} collective-permute-done((bf16[1152,256]{1,0:T(8,128)(2,1)S(1)}, bf16[1152,256]{1,0:T(8,128)(2,1)S(1)}, u32[]{:S(2)}, u32[]{:S(2)}) %collective-permute-start.11) | collective-permute-done | bytes 589856 | tf_op jit(solution)/shard_map/ppermute | solution.py:312
  58.6 1.8 %collective-permute-done.10.refs_2_ = bf16[1152,256]{1,0:T(8,128)(2,1)S(1)} collective-permute-done((bf16[1152,256]{1,0:T(8,128)(2,1)S(1)}, bf16[1152,256]{1,0:T(8,128)(2,1)S(1)}, u32[]{:S(2)}, u32[]{:S(2)}) %collective-permute-start.10) | collective-permute-done | bytes 589856 | tf_op jit(solution)/shard_map/ppermute | solution.py:312
  60.4 1.6 %collective-permute-start.14 = (bf16[1152,256]{1,0:T(8,128)(2,1)S(1)}, bf16[1152,256]{1,0:T(8,128)(2,1)S(1)}, u32[]{:S(2)}, u32[]{:S(2)}) collective-permute-start(bf16[1152,256]{1,0:T(8,128)(2,1)S(1)} %collective-permute-done.11.refs_3_.refs_6_), channel_id=1, source_target_pairs={{0,2},{1,3},{4,0},{5,1},{8,4},{9,5},{12,8},{13,9},{14,12},{15,13},... | collective-permute-start | bytes 1769480 | tf_op jit(solution)/shard_map/ppermute | solution.py:312
  62.0 0.4 collective-permute-start.15
  62.5 2.2 %shard_map.82 = (f32[128,256]{1,0:T(8,128)S(1)}, f32[128,256]{1,0:T(8,128)S(1)}) custom-call(s32[8]{0:T(128)S(1)} %fusion.6.owners_ref, bf16[128,28672]{1,0:T(8,128)(2,1)} %refs_0_.15, bf16[128,28672]{1,0:T(8,128)(2,1)} %collective-permute-done.1.refs_3_.refs_1_, bf16[1152,256]{1,0:T(8,128)(2,1)S(1)} %collective-permute-done.10.refs_2_, ...), custom_call_target="tpu_custom_call" | custom-call | flops 1 | bytes 1 | tf_op jit(solution)/shard_map/pallas_call | solution.py:116
  64.6 6.6 %collective-permute-done.9.refs_3_ = bf16[1152,256]{1,0:T(8,128)(2,1)S(1)} collective-permute-done((bf16[1152,256]{1,0:T(8,128)(2,1)S(1)}, bf16[1152,256]{1,0:T(8,128)(2,1)S(1)}, u32[]{:S(2)}, u32[]{:S(2)}) %collective-permute-start.9) | collective-permute-done | bytes 589856 | tf_op jit(solution)/shard_map/ppermute | solution.py:312
  71.3 1.8 %collective-permute-done.8.refs_2_.refs_7_ = bf16[1152,256]{1,0:T(8,128)(2,1)S(1)} collective-permute-done((bf16[1152,256]{1,0:T(8,128)(2,1)S(1)}, bf16[1152,256]{1,0:T(8,128)(2,1)S(1)}, u32[]{:S(2)}, u32[]{:S(2)}) %collective-permute-start.8) | collective-permute-done | bytes 589856 | tf_op jit(solution)/shard_map/ppermute | solution.py:312
  73.1 0.2 collective-permute-start.12
  73.3 1.8 %collective-permute-start.13 = (bf16[1152,256]{1,0:T(8,128)(2,1)S(1)}, bf16[1152,256]{1,0:T(8,128)(2,1)S(1)}, u32[]{:S(2)}, u32[]{:S(2)}) collective-permute-start(bf16[1152,256]{1,0:T(8,128)(2,1)S(1)} %collective-permute-done.9.refs_3_), channel_id=1, source_target_pairs={{0,2},{1,3},{4,0},{5,1},{8,4},{9,5},{12,8},{13,9},{14,12},{15,13},... | collective-permute-start | bytes 1769480 | tf_op jit(solution)/shard_map/ppermute | solution.py:312
  75.1 1.9 %shard_map.78 = (bf16[128,2304]{1,0:T(8,128)(2,1)S(1)}, bf16[128,2304]{1,0:T(8,128)(2,1)S(1)}) custom-call(s32[8]{0:T(128)S(1)} %fusion.6.owners_ref, bf16[128,8192]{1,0:T(8,128)(2,1)} %refs_0_.14, bf16[128,28672]{1,0:T(8,128)(2,1)} %refs_0_.15, bf16[128,8192]{1,0:T(8,128)(2,1)} %copy-done, bf16[128,28672]{1,0:T(8,128)(2,1)} %collective-permute-done.1.refs_3_.refs_1_), custom_call_target="tpu_custom_call" | custom-call | flops 1 | bytes 1 | tf_op jit(solution)/shard_map/pallas_call | solution.py:194
  77.0 2.2 %shard_map.83 = (f32[128,256]{1,0:T(8,128)S(1)}, f32[128,256]{1,0:T(8,128)S(1)}) custom-call(s32[8]{0:T(128)S(1)} %fusion.6.owners_ref, bf16[128,28672]{1,0:T(8,128)(2,1)} %refs_0_.15, bf16[128,28672]{1,0:T(8,128)(2,1)} %collective-permute-done.1.refs_3_.refs_1_, bf16[1152,256]{1,0:T(8,128)(2,1)S(1)} %collective-permute-done.8.refs_2_.refs_7_, ...), custom_call_target="tpu_custom_call" | custom-call | flops 1 | bytes 1 | tf_op jit(solution)/shard_map/pallas_call | solution.py:116
  79.3 4.6 %collective-permute-done.14.refs_8_.refs_3_ = bf16[1152,256]{1,0:T(8,128)(2,1)S(1)} collective-permute-done((bf16[1152,256]{1,0:T(8,128)(2,1)S(1)}, bf16[1152,256]{1,0:T(8,128)(2,1)S(1)}, u32[]{:S(2)}, u32[]{:S(2)}) %collective-permute-start.14) | collective-permute-done | bytes 589856 | tf_op jit(solution)/shard_map/ppermute | solution.py:312
  83.9 3.1 %shard_map.84 = (f32[128,256]{1,0:T(8,128)S(1)}, f32[128,256]{1,0:T(8,128)S(1)}) custom-call(s32[8]{0:T(128)S(1)} %fusion.6.owners_ref, bf16[128,8192]{1,0:T(8,128)(2,1)} %refs_0_.14, bf16[128,8192]{1,0:T(8,128)(2,1)} %copy-done, bf16[1152,256]{1,0:T(8,128)(2,1)S(1)} %get-tuple-element.64.refs_2_, ...), custom_call_target="tpu_custom_call" | custom-call | flops 1 | bytes 1 | tf_op jit(solution)/shard_map/pallas_call | solution.py:116
  87.0 2.2 %shard_map.85 = (f32[128,256]{1,0:T(8,128)S(1)}, f32[128,256]{1,0:T(8,128)S(1)}) custom-call(s32[8]{0:T(128)S(1)} %fusion.6.owners_ref, bf16[128,28672]{1,0:T(8,128)(2,1)} %refs_0_.15, bf16[128,28672]{1,0:T(8,128)(2,1)} %collective-permute-done.1.refs_3_.refs_1_, bf16[1152,256]{1,0:T(8,128)(2,1)S(1)} %collective-permute-done.15.refs_2_, ...), custom_call_target="tpu_custom_call" | custom-call | flops 1 | bytes 1 | tf_op jit(solution)/shard_map/pallas_call | solution.py:116
  89.2 8.0 %collective-permute-done.12.first_ref = bf16[1152,256]{1,0:T(8,128)(2,1)S(1)} collective-permute-done((bf16[1152,256]{1,0:T(8,128)(2,1)S(1)}, bf16[1152,256]{1,0:T(8,128)(2,1)S(1)}, u32[]{:S(2)}, u32[]{:S(2)}) %collective-permute-start.12) | collective-permute-done | bytes 589856 | tf_op jit(solution)/shard_map/ppermute | solution.py:312
  97.2 0.3 shard_map.86
  97.6 0.3 shard_map.87
  98.0 1.2 collective-permute-done.16
  99.3 0.6 collective-permute-start.17
  99.9 1.5 %collective-permute-start.18 = (bf16[144,512]{1,0:T(8,128)(2,1)S(1)}, bf16[144,512]{1,0:T(8,128)(2,1)S(1)}, u32[]{:S(2)}, u32[]{:S(2)}) collective-permute-start(bf16[144,512]{1,0:T(8,128)(2,1)S(1)} %pad_maximum_fusion), channel_id=1, source_target_pairs={{0,2},{1,3},{4,0},{5,1},{8,4},{9,5},{12,8},{13,9},{14,12},{15,13},... | collective-permute-start | bytes 442376 | tf_op jit(solution)/shard_map/ppermute | solution.py:312
  101.3 3.9 %collective-permute-done.17 = bf16[144,512]{1,0:T(8,128)(2,1)S(1)} collective-permute-done((bf16[144,512]{1,0:T(8,128)(2,1)S(1)}, bf16[144,512]{1,0:T(8,128)(2,1)S(1)}, u32[]{:S(2)}, u32[]{:S(2)}) %collective-permute-start.17) | collective-permute-done | bytes 147488 | tf_op jit(solution)/shard_map/ppermute | solution.py:312
  105.2 0.5 collective-permute-start.19
  105.7 1.5 %collective-permute-start.20 = (bf16[144,512]{1,0:T(8,128)(2,1)S(1)}, bf16[144,512]{1,0:T(8,128)(2,1)S(1)}, u32[]{:S(2)}, u32[]{:S(2)}) collective-permute-start(bf16[144,512]{1,0:T(8,128)(2,1)S(1)} %collective-permute-done.18), channel_id=1, source_target_pairs={{0,2},{1,3},{4,0},{5,1},{8,4},{9,5},{12,8},{13,9},{14,12},{15,13},... | collective-permute-start | bytes 442376 | tf_op jit(solution)/shard_map/ppermute | solution.py:312
  107.3 3.1 %collective-permute-done.19 = bf16[144,512]{1,0:T(8,128)(2,1)S(1)} collective-permute-done((bf16[144,512]{1,0:T(8,128)(2,1)S(1)}, bf16[144,512]{1,0:T(8,128)(2,1)S(1)}, u32[]{:S(2)}, u32[]{:S(2)}) %collective-permute-start.19) | collective-permute-done | bytes 147488 | tf_op jit(solution)/shard_map/ppermute | solution.py:312
  110.3 0.5 collective-permute-start.21
  110.9 1.5 %collective-permute-start.22 = (bf16[144,512]{1,0:T(8,128)(2,1)S(1)}, bf16[144,512]{1,0:T(8,128)(2,1)S(1)}, u32[]{:S(2)}, u32[]{:S(2)}) collective-permute-start(bf16[144,512]{1,0:T(8,128)(2,1)S(1)} %collective-permute-done.20), channel_id=1, source_target_pairs={{0,2},{1,3},{4,0},{5,1},{8,4},{9,5},{12,8},{13,9},{14,12},{15,13},... | collective-permute-start | bytes 442376 | tf_op jit(solution)/shard_map/ppermute | solution.py:312
  112.4 3.1 %collective-permute-done.21 = bf16[144,512]{1,0:T(8,128)(2,1)S(1)} collective-permute-done((bf16[144,512]{1,0:T(8,128)(2,1)S(1)}, bf16[144,512]{1,0:T(8,128)(2,1)S(1)}, u32[]{:S(2)}, u32[]{:S(2)}) %collective-permute-start.21) | collective-permute-done | bytes 147488 | tf_op jit(solution)/shard_map/ppermute | solution.py:312
  115.5 0.5 collective-permute-done.22
  116.1 1.6 %collective-permute-start.23 = (bf16[144,512]{1,0:T(8,128)(2,1)S(1)}, bf16[144,512]{1,0:T(8,128)(2,1)S(1)}, u32[]{:S(2)}, u32[]{:S(2)}) collective-permute-start(bf16[144,512]{1,0:T(8,128)(2,1)S(1)} %get-tuple-element.118), channel_id=1, source_target_pairs={{0,4},{4,8},{8,12},{12,14},{14,10},{10,6},{6,2},{2,0},{1,3},{5,1},... | collective-permute-start | bytes 442376 | tf_op jit(solution)/shard_map/ppermute | solution.py:312
  117.7 0.1 collective-permute-start.25
  117.9 3.4 %collective-permute-done.23.refs_2_ = bf16[144,512]{1,0:T(8,128)(2,1)S(1)} collective-permute-done((bf16[144,512]{1,0:T(8,128)(2,1)S(1)}, bf16[144,512]{1,0:T(8,128)(2,1)S(1)}, u32[]{:S(2)}, u32[]{:S(2)}) %collective-permute-start.23) | collective-permute-done | bytes 147488 | tf_op jit(solution)/shard_map/ppermute | solution.py:312
  121.3 1.4 %collective-permute-done.26.refs_5_ = bf16[144,512]{1,0:T(8,128)(2,1)S(1)} collective-permute-done((bf16[144,512]{1,0:T(8,128)(2,1)S(1)}, bf16[144,512]{1,0:T(8,128)(2,1)S(1)}, u32[]{:S(2)}, u32[]{:S(2)}) %collective-permute-start.26) | collective-permute-done | bytes 147488 | tf_op jit(solution)/shard_map/ppermute | solution.py:312
  122.7 1.5 %shard_map.88 = (f32[16,256]{1,0:T(8,128)}, f32[1,64]{1,0:T(1,128)}) custom-call(s32[1]{0:T(128)} %bitcast.me_ref, bf16[720,512]{1,0:T(8,128)(2,1)S(1)} %constant_dynamic-update-slice_fusion.refs_0_, bf16[288,512]{1,0:T(8,128)(2,1)S(1)} %get-tuple-element.119.refs_1_, bf16[144,512]{1,0:T(8,128)(2,1)S(1)} %collective-permute-done.23.refs_2_, ...), custom_call_target="tpu_custom_call" | custom-call | tf_op jit(solution)/shard_map/pallas_call | solution.py:273
  (38 shorter events, 0.9 us)
Async XLA Ops:
  0.6 23.0 %collective-permute-start.1 = (bf16[128,28672]{1,0:T(8,128)(2,1)}, bf16[128,28672]{1,0:T(8,128)(2,1)}, u32[]{:S(2)}, u32[]{:S(2)}) collective-permute-start(bf16[128,28672]{1,0:T(8,128)(2,1)} %refs_0_.15), channel_id=1, source_target_pairs={{0,1},{1,0},{2,3},{3,2},{4,5},{5,4},{6,7},{7,6},{8,9},{9,8},{10,11... | collective-permute-start | bytes 22020104 | tf_op jit(solution)/shard_map/ppermute | solution.py:312
  1.1 11.4 %collective-permute-start = (bf16[128,8192]{1,0:T(8,128)(2,1)}, bf16[128,8192]{1,0:T(8,128)(2,1)S(1)}, u32[]{:S(2)}, u32[]{:S(2)}) collective-permute-start(bf16[128,8192]{1,0:T(8,128)(2,1)} %refs_0_.14), channel_id=1, source_target_pairs={{0,1},{1,0},{2,3},{3,2},{4,5},{5,4},{6,7},{7,6},{8,9},{9,8},{10,11... | collective-permute-start | bytes 6291464 | tf_op jit(solution)/shard_map/ppermute | solution.py:312
  3.3 17.5 %collective-permute-start.4 = (bf16[1152,256]{1,0:T(8,128)(2,1)}, bf16[1152,256]{1,0:T(8,128)(2,1)}, u32[]{:S(2)}, u32[]{:S(2)}) collective-permute-start(bf16[1152,256]{1,0:T(8,128)(2,1)} %get-tuple-element.63.refs_3_), channel_id=1, source_target_pairs={{0,2},{1,3},{4,0},{5,1},{8,4},{9,5},{12,8},{13,9},{14,12},{15,13},... | collective-permute-start | bytes 1769480 | tf_op jit(solution)/shard_map/ppermute | solution.py:312
  6.3 16.5 %collective-permute-start.2 = (bf16[1152,256]{1,0:T(8,128)(2,1)S(1)}, bf16[1152,256]{1,0:T(8,128)(2,1)S(1)}, u32[]{:S(2)}, u32[]{:S(2)}) collective-permute-start(bf16[1152,256]{1,0:T(8,128)(2,1)S(1)} %get-tuple-element.64.refs_2_), channel_id=1, source_target_pairs={{0,4},{1,5},{4,8},{5,9},{8,12},{9,13},{12,14},{13,15},{14,10},{15,... | collective-permute-start | bytes 1769480 | tf_op jit(solution)/shard_map/ppermute | solution.py:312
  12.6 10.2 %copy-start = (bf16[128,8192]{1,0:T(8,128)(2,1)}, bf16[128,8192]{1,0:T(8,128)(2,1)S(1)}, u32[]{:S(2)}) copy-start(bf16[128,8192]{1,0:T(8,128)(2,1)S(1)} %collective-permute-done.refs_2_.refs_1_) | copy-start | bytes 6291460
  12.6 20.7 %collective-permute-start.7 = (bf16[1152,256]{1,0:T(8,128)(2,1)S(1)}, bf16[1152,256]{1,0:T(8,128)(2,1)S(1)}, u32[]{:S(2)}, u32[]{:S(2)}) collective-permute-start(bf16[1152,256]{1,0:T(8,128)(2,1)S(1)} %get-tuple-element.64.refs_2_), channel_id=1, source_target_pairs={{0,2},{1,3},{4,0},{5,1},{8,4},{9,5},{12,8},{13,9},{14,12},{15,13},... | collective-permute-start | bytes 1769480 | tf_op jit(solution)/shard_map/ppermute | solution.py:312
  15.7 19.6 %collective-permute-start.6 = (bf16[1152,256]{1,0:T(8,128)(2,1)}, bf16[1152,256]{1,0:T(8,128)(2,1)S(1)}, u32[]{:S(2)}, u32[]{:S(2)}) collective-permute-start(bf16[1152,256]{1,0:T(8,128)(2,1)} %get-tuple-element.63.refs_3_), channel_id=1, source_target_pairs={{0,4},{1,5},{4,8},{5,9},{8,12},{9,13},{12,14},{13,15},{14,10},{15,... | collective-permute-start | bytes 1769480 | tf_op jit(solution)/shard_map/ppermute | solution.py:312
  20.8 25.2 %collective-permute-start.5 = (bf16[1152,256]{1,0:T(8,128)(2,1)}, bf16[1152,256]{1,0:T(8,128)(2,1)S(1)}, u32[]{:S(2)}, u32[]{:S(2)}) collective-permute-start(bf16[1152,256]{1,0:T(8,128)(2,1)} %collective-permute-done.4.refs_5_), channel_id=1, source_target_pairs={{0,2},{1,3},{4,0},{5,1},{8,4},{9,5},{12,8},{13,9},{14,12},{15,13},... | collective-permute-start | bytes 1769480 | tf_op jit(solution)/shard_map/ppermute | solution.py:312
  22.8 25.2 %collective-permute-start.3 = (bf16[1152,256]{1,0:T(8,128)(2,1)S(1)}, bf16[1152,256]{1,0:T(8,128)(2,1)S(1)}, u32[]{:S(2)}, u32[]{:S(2)}) collective-permute-start(bf16[1152,256]{1,0:T(8,128)(2,1)S(1)} %collective-permute-done.2.refs_4_.refs_3_), channel_id=1, source_target_pairs={{0,4},{1,5},{4,8},{5,9},{8,12},{9,13},{12,14},{13,15},{14,10},{15,... | collective-permute-start | bytes 1769480 | tf_op jit(solution)/shard_map/ppermute | solution.py:312
  33.3 25.3 %collective-permute-start.11 = (bf16[1152,256]{1,0:T(8,128)(2,1)S(1)}, bf16[1152,256]{1,0:T(8,128)(2,1)S(1)}, u32[]{:S(2)}, u32[]{:S(2)}) collective-permute-start(bf16[1152,256]{1,0:T(8,128)(2,1)S(1)} %collective-permute-done.7.refs_3_.refs_4_), channel_id=1, source_target_pairs={{0,2},{1,3},{4,0},{5,1},{8,4},{9,5},{12,8},{13,9},{14,12},{15,13},... | collective-permute-start | bytes 1769480 | tf_op jit(solution)/shard_map/ppermute | solution.py:312
  35.3 25.1 %collective-permute-start.10 = (bf16[1152,256]{1,0:T(8,128)(2,1)S(1)}, bf16[1152,256]{1,0:T(8,128)(2,1)S(1)}, u32[]{:S(2)}, u32[]{:S(2)}) collective-permute-start(bf16[1152,256]{1,0:T(8,128)(2,1)S(1)} %collective-permute-done.6.refs_2_), channel_id=1, source_target_pairs={{0,4},{1,5},{4,8},{5,9},{8,12},{9,13},{12,14},{13,15},{14,10},{15,... | collective-permute-start | bytes 1769480 | tf_op jit(solution)/shard_map/ppermute | solution.py:312
  46.0 25.3 %collective-permute-start.9 = (bf16[1152,256]{1,0:T(8,128)(2,1)S(1)}, bf16[1152,256]{1,0:T(8,128)(2,1)S(1)}, u32[]{:S(2)}, u32[]{:S(2)}) collective-permute-start(bf16[1152,256]{1,0:T(8,128)(2,1)S(1)} %collective-permute-done.5.refs_3_), channel_id=1, source_target_pairs={{0,2},{1,3},{4,0},{5,1},{8,4},{9,5},{12,8},{13,9},{14,12},{15,13},... | collective-permute-start | bytes 1769480 | tf_op jit(solution)/shard_map/ppermute | solution.py:312
  48.0 25.1 %collective-permute-start.8 = (bf16[1152,256]{1,0:T(8,128)(2,1)S(1)}, bf16[1152,256]{1,0:T(8,128)(2,1)S(1)}, u32[]{:S(2)}, u32[]{:S(2)}) collective-permute-start(bf16[1152,256]{1,0:T(8,128)(2,1)S(1)} %collective-permute-done.3.refs_2_.refs_5_), channel_id=1, source_target_pairs={{0,4},{1,5},{4,8},{5,9},{8,12},{9,13},{12,14},{13,15},{14,10},{15,... | collective-permute-start | bytes 1769480 | tf_op jit(solution)/shard_map/ppermute | solution.py:312
  58.6 16.5 %copy-start.1 = (s32[128]{0:T(128)S(1)}, s32[128]{0:T(128)}, u32[]{:S(2)}) copy-start(s32[128]{0:T(128)} %param.8) | copy-start | bytes 1540
  60.4 23.5 %collective-permute-start.14 = (bf16[1152,256]{1,0:T(8,128)(2,1)S(1)}, bf16[1152,256]{1,0:T(8,128)(2,1)S(1)}, u32[]{:S(2)}, u32[]{:S(2)}) collective-permute-start(bf16[1152,256]{1,0:T(8,128)(2,1)S(1)} %collective-permute-done.11.refs_3_.refs_6_), channel_id=1, source_target_pairs={{0,2},{1,3},{4,0},{5,1},{8,4},{9,5},{12,8},{13,9},{14,12},{15,13},... | collective-permute-start | bytes 1769480 | tf_op jit(solution)/shard_map/ppermute | solution.py:312
  62.0 25.0 %collective-permute-start.15 = (bf16[1152,256]{1,0:T(8,128)(2,1)S(1)}, bf16[1152,256]{1,0:T(8,128)(2,1)S(1)}, u32[]{:S(2)}, u32[]{:S(2)}) collective-permute-start(bf16[1152,256]{1,0:T(8,128)(2,1)S(1)} %collective-permute-done.10.refs_2_), channel_id=1, source_target_pairs={{0,4},{1,5},{4,8},{5,9},{8,12},{9,13},{12,14},{13,15},{14,10},{15,... | collective-permute-start | bytes 1769480 | tf_op jit(solution)/shard_map/ppermute | solution.py:312
  73.1 24.1 %collective-permute-start.12 = (bf16[1152,256]{1,0:T(8,128)(2,1)S(1)}, bf16[1152,256]{1,0:T(8,128)(2,1)S(1)}, u32[]{:S(2)}, u32[]{:S(2)}) collective-permute-start(bf16[1152,256]{1,0:T(8,128)(2,1)S(1)} %collective-permute-done.8.refs_2_.refs_7_), channel_id=1, source_target_pairs={{0,4},{1,5},{4,8},{5,9},{8,12},{9,13},{12,14},{13,15},{14,10},{15,... | collective-permute-start | bytes 1769480 | tf_op jit(solution)/shard_map/ppermute | solution.py:312
  73.3 23.9 %collective-permute-start.13 = (bf16[1152,256]{1,0:T(8,128)(2,1)S(1)}, bf16[1152,256]{1,0:T(8,128)(2,1)S(1)}, u32[]{:S(2)}, u32[]{:S(2)}) collective-permute-start(bf16[1152,256]{1,0:T(8,128)(2,1)S(1)} %collective-permute-done.9.refs_3_), channel_id=1, source_target_pairs={{0,2},{1,3},{4,0},{5,1},{8,4},{9,5},{12,8},{13,9},{14,12},{15,13},... | collective-permute-start | bytes 1769480 | tf_op jit(solution)/shard_map/ppermute | solution.py:312
  97.5 1.6 %collective-permute-start.16 = (f32[128,512]{1,0:T(8,128)S(1)}, f32[128,512]{1,0:T(8,128)S(1)}, u32[]{:S(2)}, u32[]{:S(2)}) collective-permute-start(f32[128,512]{1,0:T(8,128)S(1)} %shard_map.86), channel_id=1, source_target_pairs={{0,1},{1,0},{2,3},{3,2},{4,5},{5,4},{6,7},{7,6},{8,9},{9,8},{10,11... | collective-permute-start | bytes 786440 | tf_op jit(solution)/shard_map/ppermute | solution.py:312
  99.3 5.9 %collective-permute-start.17 = (bf16[144,512]{1,0:T(8,128)(2,1)S(1)}, bf16[144,512]{1,0:T(8,128)(2,1)S(1)}, u32[]{:S(2)}, u32[]{:S(2)}) collective-permute-start(bf16[144,512]{1,0:T(8,128)(2,1)S(1)} %pad_maximum_fusion), channel_id=1, source_target_pairs={{0,4},{1,5},{4,8},{5,9},{8,12},{9,13},{12,14},{13,15},{14,10},{15,... | collective-permute-start | bytes 442376 | tf_op jit(solution)/shard_map/ppermute | solution.py:312
  99.9 5.9 %collective-permute-start.18 = (bf16[144,512]{1,0:T(8,128)(2,1)S(1)}, bf16[144,512]{1,0:T(8,128)(2,1)S(1)}, u32[]{:S(2)}, u32[]{:S(2)}) collective-permute-start(bf16[144,512]{1,0:T(8,128)(2,1)S(1)} %pad_maximum_fusion), channel_id=1, source_target_pairs={{0,2},{1,3},{4,0},{5,1},{8,4},{9,5},{12,8},{13,9},{14,12},{15,13},... | collective-permute-start | bytes 442376 | tf_op jit(solution)/shard_map/ppermute | solution.py:312
  105.2 5.1 %collective-permute-start.19 = (bf16[144,512]{1,0:T(8,128)(2,1)S(1)}, bf16[144,512]{1,0:T(8,128)(2,1)S(1)}, u32[]{:S(2)}, u32[]{:S(2)}) collective-permute-start(bf16[144,512]{1,0:T(8,128)(2,1)S(1)} %collective-permute-done.17), channel_id=1, source_target_pairs={{0,4},{1,5},{4,8},{5,9},{8,12},{9,13},{12,14},{13,15},{14,10},{15,... | collective-permute-start | bytes 442376 | tf_op jit(solution)/shard_map/ppermute | solution.py:312
  105.7 5.1 %collective-permute-start.20 = (bf16[144,512]{1,0:T(8,128)(2,1)S(1)}, bf16[144,512]{1,0:T(8,128)(2,1)S(1)}, u32[]{:S(2)}, u32[]{:S(2)}) collective-permute-start(bf16[144,512]{1,0:T(8,128)(2,1)S(1)} %collective-permute-done.18), channel_id=1, source_target_pairs={{0,2},{1,3},{4,0},{5,1},{8,4},{9,5},{12,8},{13,9},{14,12},{15,13},... | collective-permute-start | bytes 442376 | tf_op jit(solution)/shard_map/ppermute | solution.py:312
  110.3 5.1 %collective-permute-start.21 = (bf16[144,512]{1,0:T(8,128)(2,1)S(1)}, bf16[144,512]{1,0:T(8,128)(2,1)S(1)}, u32[]{:S(2)}, u32[]{:S(2)}) collective-permute-start(bf16[144,512]{1,0:T(8,128)(2,1)S(1)} %collective-permute-done.19), channel_id=1, source_target_pairs={{0,4},{1,5},{4,8},{5,9},{8,12},{9,13},{12,14},{13,15},{14,10},{15,... | collective-permute-start | bytes 442376 | tf_op jit(solution)/shard_map/ppermute | solution.py:312
  110.9 5.1 %collective-permute-start.22 = (bf16[144,512]{1,0:T(8,128)(2,1)S(1)}, bf16[144,512]{1,0:T(8,128)(2,1)S(1)}, u32[]{:S(2)}, u32[]{:S(2)}) collective-permute-start(bf16[144,512]{1,0:T(8,128)(2,1)S(1)} %collective-permute-done.20), channel_id=1, source_target_pairs={{0,2},{1,3},{4,0},{5,1},{8,4},{9,5},{12,8},{13,9},{14,12},{15,13},... | collective-permute-start | bytes 442376 | tf_op jit(solution)/shard_map/ppermute | solution.py:312
  116.0 6.6 %collective-permute-start.24 = (bf16[720,512]{1,0:T(8,128)(2,1)S(1)}, bf16[720,512]{1,0:T(8,128)(2,1)S(1)}, u32[]{:S(2)}, u32[]{:S(2)}) collective-permute-start(bf16[720,512]{1,0:T(8,128)(2,1)S(1)} %constant_dynamic-update-slice_fusion.refs_0_), channel_id=1, source_target_pairs={{0,1},{1,0},{2,3},{3,2},{4,5},{5,4},{6,7},{7,6},{8,9},{9,8},{10,11... | collective-permute-start | bytes 2211848 | tf_op jit(solution)/shard_map/ppermute | solution.py:312
  116.1 5.2 %collective-permute-start.23 = (bf16[144,512]{1,0:T(8,128)(2,1)S(1)}, bf16[144,512]{1,0:T(8,128)(2,1)S(1)}, u32[]{:S(2)}, u32[]{:S(2)}) collective-permute-start(bf16[144,512]{1,0:T(8,128)(2,1)S(1)} %get-tuple-element.118), channel_id=1, source_target_pairs={{0,4},{4,8},{8,12},{12,14},{14,10},{10,6},{6,2},{2,0},{1,3},{5,1},... | collective-permute-start | bytes 442376 | tf_op jit(solution)/shard_map/ppermute | solution.py:312
  117.7 4.9 %collective-permute-start.25 = (bf16[288,512]{1,0:T(8,128)(2,1)S(1)}, bf16[288,512]{1,0:T(8,128)(2,1)S(1)}, u32[]{:S(2)}, u32[]{:S(2)}) collective-permute-start(bf16[288,512]{1,0:T(8,128)(2,1)S(1)} %get-tuple-element.119.refs_1_), channel_id=1, source_target_pairs={{0,1},{1,0},{2,3},{3,2},{4,5},{5,4},{6,7},{7,6},{8,9},{9,8},{10,11... | collective-permute-start | bytes 884744 | tf_op jit(solution)/shard_map/ppermute | solution.py:312
  121.3 1.4 %collective-permute-start.26 = (bf16[144,512]{1,0:T(8,128)(2,1)S(1)}, bf16[144,512]{1,0:T(8,128)(2,1)S(1)}, u32[]{:S(2)}, u32[]{:S(2)}) collective-permute-start(bf16[144,512]{1,0:T(8,128)(2,1)S(1)} %collective-permute-done.23.refs_2_), channel_id=1, source_target_pairs={{0,1},{1,0},{2,3},{3,2},{4,5},{5,4},{6,7},{7,6},{8,9},{9,8},{10,11... | collective-permute-start | bytes 442376 | tf_op jit(solution)/shard_map/ppermute | solution.py:312

commit v6 on v5

--- a/solution.py
+++ b/solution.py
@@ -325,7 +325,9 @@
     ) * 2 + own_index % 2
 
     cut = (depth_in + depth_out) // 2
-    first, second = halves(basis_in, basis_out, cut)
+    second = basis_out[cut - depth_in :]
+    first = lax.pad(basis_out, basis_out.dtype.type(0), ((depth_in, -second.shape[0], 0), (0, 0, 0)))
+    first = lax.dynamic_update_slice(first, basis_in, (0, 0))
     first, second = {0: first}, {0: second}
 
     def hop(ahead, behind, s):
@@ -385,16 +387,16 @@
     held = {0: jnp.concatenate([squares, tag], axis=0)}
     for s in range(1, half):
         hop(held, held, s)
+    middle = (rows + 16) // 32 * 16
+    upper = send(held[half - 2][:middle], ring(2))
+    lower = send(held[2 - half][middle:], ring(-2))
+    held[half - 1], held[1 - half], upper, lower = lax.optimization_barrier(
+        (held[half - 1], held[1 - half], upper, lower)
+    )
     near = jnp.concatenate([held[d] for d in distances[:-3]], axis=0)
-    near, held[half - 1], held[1 - half] = lax.optimization_barrier(
-        (near, held[half - 1], held[1 - half])
-    )
-    core = own_index % 2
-    farthest = jnp.where(core == 0, held[half - 1], held[1 - half])
-    opposite = send(farthest, forward[0::2] + backward[1::2])
-    far = jnp.concatenate([held[half - 1], held[1 - half]], axis=0)
-    swapped = [send(x, swap) for x in (near, far, opposite)]
-    own = [near, far, opposite]
+    far = jnp.concatenate([held[half - 1], held[1 - half], upper, lower], axis=0)
+    own = [near, far]
+    swapped = [send(x, swap) for x in own]
     return last(own_index[None], own + swapped, rows, width, devices, balanced)
 
 

time: 125 us -> 122 us (0.976)
  waiting for transfers between devices: 73.3 us -> 70.7 us
  Pallas kernels: 24 us -> 22.3 us
  starting transfers between devices: 25.1 us -> 26.5 us
  local copies, waits for them, and re-layouts: 0.08 us -> 1.38 us
    ppermute x27, waiting for transfers between devices: 73.3 us -> 70.7 us  [send(): return lax.ppermute(x, 'dp', pairs)]
    pallas_call x1 -> x0, Pallas kernels: 2.07 us -> none  [halves(): pl.pallas_call(halves_kernel, out_shape=(jax.ShapeDtypeStruct((cut, width...]
    ppermute x27, starting transfers between devices: 25.1 us -> 26.5 us  [send(): return lax.ppermute(x, 'dp', pairs)]
  transfers between devices with their start and end apart: 27 -> 27, of which waited for: 17 -> 18; matrix products, arithmetic and copies ran while one was open for 1% -> 1% of each run, Pallas kernels for 18% -> 17%
where the time goes in v6:
time: 122 us
  waiting for transfers between devices  70.7 us (58%)
  starting transfers between devices  26.5 us (22%)
  Pallas kernels  22.3 us (18%)
  local copies, waits for them, and re-layouts  1.38 us (1%)
    ppermute x27, waiting for transfers between devices, send(): return lax.ppermute(x, 'dp', pairs)  70.7 us
    ppermute x27, starting transfers between devices, send(): return lax.ppermute(x, 'dp', pairs)  26.5 us
    pallas_call x7, Pallas kernels, project(): pl.pallas_call(functools.partial(project_kernel, kinds, [p[:2] for p in p...  18.3 us
  transfers between devices with their start and end apart: 27, of which 18 were waited for; matrix products, arithmetic and copies ran while one was open for 1% of the time, Pallas kernels for 17%

profile of v6, /device:TPU:0, one launch (start us, length us, event | category | flops | bytes accessed | tf_op | source)
XLA Modules:
  0.0 121.8 jit_solution(283769989532412807)
XLA Ops:
  0.7 0.5 collective-permute-start.1
  1.3 1.2 %fusion.7 = (bf16[1152,256]{1,0:T(8,128)(2,1)S(1)}, bf16[1152,256]{1,0:T(8,128)(2,1)S(1)}) fusion(bf16[1792,256]{1,0:T(8,128)(2,1)} %param.10), kind=kLoop, calls=%fused_computation.34 | loop fusion | bytes 2686976 | tf_op jit(solution)/shard_map/slice | solution.py:328
  2.5 3.0 %collective-permute-start.4 = (bf16[1152,256]{1,0:T(8,128)(2,1)S(1)}, bf16[1152,256]{1,0:T(8,128)(2,1)}, u32[]{:S(2)}, u32[]{:S(2)}) collective-permute-start(bf16[1152,256]{1,0:T(8,128)(2,1)S(1)} %get-tuple-element.116.refs_3_), channel_id=1, source_target_pairs={{0,2},{1,3},{4,0},{5,1},{8,4},{9,5},{12,8},{13,9},{14,12},{15,13},... | collective-permute-start | bytes 1769480 | tf_op jit(solution)/shard_map/ppermute | solution.py:312
  5.5 0.1 collective-permute-start.2
  5.6 7.0 %collective-permute-done.refs_2_.refs_1_ = bf16[128,8192]{1,0:T(8,128)(2,1)S(1)} collective-permute-done((bf16[128,8192]{1,0:T(8,128)(2,1)}, bf16[128,8192]{1,0:T(8,128)(2,1)S(1)}, u32[]{:S(2)}, u32[]{:S(2)}) %collective-permute-start) | collective-permute-done | bytes 2097184 | tf_op jit(solution)/shard_map/ppermute | solution.py:312
  12.6 3.1 %collective-permute-start.7 = (bf16[1152,256]{1,0:T(8,128)(2,1)S(1)}, bf16[1152,256]{1,0:T(8,128)(2,1)S(1)}, u32[]{:S(2)}, u32[]{:S(2)}) collective-permute-start(bf16[1152,256]{1,0:T(8,128)(2,1)S(1)} %constant_dynamic-update-slice_fusion.10.refs_2_), channel_id=1, source_target_pairs={{0,2},{1,3},{4,0},{5,1},{8,4},{9,5},{12,8},{13,9},{14,12},{15,13},... | collective-permute-start | bytes 1769480 | tf_op jit(solution)/shard_map/ppermute | solution.py:312
  15.8 4.0 %collective-permute-done.4.refs_5_ = bf16[1152,256]{1,0:T(8,128)(2,1)} collective-permute-done((bf16[1152,256]{1,0:T(8,128)(2,1)S(1)}, bf16[1152,256]{1,0:T(8,128)(2,1)}, u32[]{:S(2)}, u32[]{:S(2)}) %collective-permute-start.4) | collective-permute-done | bytes 589856 | tf_op jit(solution)/shard_map/ppermute | solution.py:312
  19.8 2.0 %collective-permute-start.5 = (bf16[1152,256]{1,0:T(8,128)(2,1)}, bf16[1152,256]{1,0:T(8,128)(2,1)S(1)}, u32[]{:S(2)}, u32[]{:S(2)}) collective-permute-start(bf16[1152,256]{1,0:T(8,128)(2,1)} %collective-permute-done.4.refs_5_), channel_id=1, source_target_pairs={{0,2},{1,3},{4,0},{5,1},{8,4},{9,5},{12,8},{13,9},{14,12},{15,13},... | collective-permute-start | bytes 1769480 | tf_op jit(solution)/shard_map/ppermute | solution.py:312
  21.9 3.7 %shard_map.78 = (f32[128,256]{1,0:T(8,128)S(1)}, f32[128,256]{1,0:T(8,128)S(1)}) custom-call(s32[8]{0:T(128)S(1)} %fusion.6.owners_ref, bf16[128,28672]{1,0:T(8,128)(2,1)} %refs_0_.15, bf16[128,28672]{1,0:T(8,128)(2,1)} %collective-permute-done.1.refs_3_.refs_1_, bf16[1152,256]{1,0:T(8,128)(2,1)S(1)} %constant_dynamic-update-slice_fusion.10.refs_2_, ...), custom_call_target="tpu_custom_call" | custom-call | flops 1 | bytes 1 | tf_op jit(solution)/shard_map/pallas_call | solution.py:116
  25.6 6.7 %collective-permute-done.7.refs_3_.refs_4_ = bf16[1152,256]{1,0:T(8,128)(2,1)S(1)} collective-permute-done((bf16[1152,256]{1,0:T(8,128)(2,1)S(1)}, bf16[1152,256]{1,0:T(8,128)(2,1)S(1)}, u32[]{:S(2)}, u32[]{:S(2)}) %collective-permute-start.7) | collective-permute-done | bytes 589856 | tf_op jit(solution)/shard_map/ppermute | solution.py:312
  32.3 2.0 %collective-permute-start.11 = (bf16[1152,256]{1,0:T(8,128)(2,1)S(1)}, bf16[1152,256]{1,0:T(8,128)(2,1)S(1)}, u32[]{:S(2)}, u32[]{:S(2)}) collective-permute-start(bf16[1152,256]{1,0:T(8,128)(2,1)S(1)} %collective-permute-done.7.refs_3_.refs_4_), channel_id=1, source_target_pairs={{0,2},{1,3},{4,0},{5,1},{8,4},{9,5},{12,8},{13,9},{14,12},{15,13},... | collective-permute-start | bytes 1769480 | tf_op jit(solution)/shard_map/ppermute | solution.py:312
  34.3 0.2 collective-permute-done.6.refs_2_
  34.6 2.7 %shard_map.79 = (f32[128,256]{1,0:T(8,128)S(1)}, f32[128,256]{1,0:T(8,128)S(1)}) custom-call(s32[8]{0:T(128)S(1)} %fusion.6.owners_ref, bf16[128,28672]{1,0:T(8,128)(2,1)} %refs_0_.15, bf16[128,28672]{1,0:T(8,128)(2,1)} %collective-permute-done.1.refs_3_.refs_1_, bf16[1152,256]{1,0:T(8,128)(2,1)} %collective-permute-done.6.refs_2_, ...), custom_call_target="tpu_custom_call" | custom-call | flops 1 | bytes 1 | tf_op jit(solution)/shard_map/pallas_call | solution.py:116
  37.3 7.6 %collective-permute-done.5.refs_3_ = bf16[1152,256]{1,0:T(8,128)(2,1)S(1)} collective-permute-done((bf16[1152,256]{1,0:T(8,128)(2,1)}, bf16[1152,256]{1,0:T(8,128)(2,1)S(1)}, u32[]{:S(2)}, u32[]{:S(2)}) %collective-permute-start.5) | collective-permute-done | bytes 589856 | tf_op jit(solution)/shard_map/ppermute | solution.py:312
  44.9 2.0 %collective-permute-start.9 = (bf16[1152,256]{1,0:T(8,128)(2,1)S(1)}, bf16[1152,256]{1,0:T(8,128)(2,1)S(1)}, u32[]{:S(2)}, u32[]{:S(2)}) collective-permute-start(bf16[1152,256]{1,0:T(8,128)(2,1)S(1)} %collective-permute-done.5.refs_3_), channel_id=1, source_target_pairs={{0,2},{1,3},{4,0},{5,1},{8,4},{9,5},{12,8},{13,9},{14,12},{15,13},... | collective-permute-start | bytes 1769480 | tf_op jit(solution)/shard_map/ppermute | solution.py:312
  46.9 0.1 collective-permute-done.3.refs_2_.refs_5_
  47.1 2.2 %shard_map.80 = (f32[128,256]{1,0:T(8,128)S(1)}, f32[128,256]{1,0:T(8,128)S(1)}) custom-call(s32[8]{0:T(128)S(1)} %fusion.6.owners_ref, bf16[128,28672]{1,0:T(8,128)(2,1)} %refs_0_.15, bf16[128,28672]{1,0:T(8,128)(2,1)} %collective-permute-done.1.refs_3_.refs_1_, bf16[1152,256]{1,0:T(8,128)(2,1)S(1)} %collective-permute-done.3.refs_2_.refs_5_, ...), custom_call_target="tpu_custom_call" | custom-call | flops 1 | bytes 1 | tf_op jit(solution)/shard_map/pallas_call | solution.py:116
  49.3 8.2 %collective-permute-done.11.refs_3_.refs_6_ = bf16[1152,256]{1,0:T(8,128)(2,1)S(1)} collective-permute-done((bf16[1152,256]{1,0:T(8,128)(2,1)S(1)}, bf16[1152,256]{1,0:T(8,128)(2,1)S(1)}, u32[]{:S(2)}, u32[]{:S(2)}) %collective-permute-start.11) | collective-permute-done | bytes 589856 | tf_op jit(solution)/shard_map/ppermute | solution.py:312
  57.6 2.1 %collective-permute-done.10.refs_2_ = bf16[1152,256]{1,0:T(8,128)(2,1)S(1)} collective-permute-done((bf16[1152,256]{1,0:T(8,128)(2,1)}, bf16[1152,256]{1,0:T(8,128)(2,1)S(1)}, u32[]{:S(2)}, u32[]{:S(2)}) %collective-permute-start.10) | collective-permute-done | bytes 589856 | tf_op jit(solution)/shard_map/ppermute | solution.py:312
  59.7 1.6 %collective-permute-start.14 = (bf16[1152,256]{1,0:T(8,128)(2,1)S(1)}, bf16[1152,256]{1,0:T(8,128)(2,1)S(1)}, u32[]{:S(2)}, u32[]{:S(2)}) collective-permute-start(bf16[1152,256]{1,0:T(8,128)(2,1)S(1)} %collective-permute-done.11.refs_3_.refs_6_), channel_id=1, source_target_pairs={{0,2},{1,3},{4,0},{5,1},{8,4},{9,5},{12,8},{13,9},{14,12},{15,13},... | collective-permute-start | bytes 1769480 | tf_op jit(solution)/shard_map/ppermute | solution.py:312
  61.3 0.4 collective-permute-start.15
  61.7 2.2 %shard_map.81 = (f32[128,256]{1,0:T(8,128)S(1)}, f32[128,256]{1,0:T(8,128)S(1)}) custom-call(s32[8]{0:T(128)S(1)} %fusion.6.owners_ref, bf16[128,28672]{1,0:T(8,128)(2,1)} %refs_0_.15, bf16[128,28672]{1,0:T(8,128)(2,1)} %collective-permute-done.1.refs_3_.refs_1_, bf16[1152,256]{1,0:T(8,128)(2,1)S(1)} %collective-permute-done.10.refs_2_, ...), custom_call_target="tpu_custom_call" | custom-call | flops 1 | bytes 1 | tf_op jit(solution)/shard_map/pallas_call | solution.py:116
  63.9 6.3 %collective-permute-done.9.refs_3_ = bf16[1152,256]{1,0:T(8,128)(2,1)S(1)} collective-permute-done((bf16[1152,256]{1,0:T(8,128)(2,1)S(1)}, bf16[1152,256]{1,0:T(8,128)(2,1)S(1)}, u32[]{:S(2)}, u32[]{:S(2)}) %collective-permute-start.9) | collective-permute-done | bytes 589856 | tf_op jit(solution)/shard_map/ppermute | solution.py:312
  70.2 2.1 %collective-permute-done.8.refs_2_.refs_7_ = bf16[1152,256]{1,0:T(8,128)(2,1)S(1)} collective-permute-done((bf16[1152,256]{1,0:T(8,128)(2,1)S(1)}, bf16[1152,256]{1,0:T(8,128)(2,1)S(1)}, u32[]{:S(2)}, u32[]{:S(2)}) %collective-permute-start.8) | collective-permute-done | bytes 589856 | tf_op jit(solution)/shard_map/ppermute | solution.py:312
  72.4 2.0 %collective-permute-start.13 = (bf16[1152,256]{1,0:T(8,128)(2,1)S(1)}, bf16[1152,256]{1,0:T(8,128)(2,1)S(1)}, u32[]{:S(2)}, u32[]{:S(2)}) collective-permute-start(bf16[1152,256]{1,0:T(8,128)(2,1)S(1)} %collective-permute-done.9.refs_3_), channel_id=1, source_target_pairs={{0,2},{1,3},{4,0},{5,1},{8,4},{9,5},{12,8},{13,9},{14,12},{15,13},... | collective-permute-start | bytes 1769480 | tf_op jit(solution)/shard_map/ppermute | solution.py:312
  74.4 1.9 %shard_map.77 = (bf16[128,2304]{1,0:T(8,128)(2,1)S(1)}, bf16[128,2304]{1,0:T(8,128)(2,1)S(1)}) custom-call(s32[8]{0:T(128)S(1)} %fusion.6.owners_ref, bf16[128,8192]{1,0:T(8,128)(2,1)} %refs_0_.14, bf16[128,28672]{1,0:T(8,128)(2,1)} %refs_0_.15, bf16[128,8192]{1,0:T(8,128)(2,1)} %copy-done, bf16[128,28672]{1,0:T(8,128)(2,1)} %collective-permute-done.1.refs_3_.refs_1_), custom_call_target="tpu_custom_call" | custom-call | flops 1 | bytes 1 | tf_op jit(solution)/shard_map/pallas_call | solution.py:194
  76.3 2.2 %shard_map.82 = (f32[128,256]{1,0:T(8,128)S(1)}, f32[128,256]{1,0:T(8,128)S(1)}) custom-call(s32[8]{0:T(128)S(1)} %fusion.6.owners_ref, bf16[128,28672]{1,0:T(8,128)(2,1)} %refs_0_.15, bf16[128,28672]{1,0:T(8,128)(2,1)} %collective-permute-done.1.refs_3_.refs_1_, bf16[1152,256]{1,0:T(8,128)(2,1)S(1)} %collective-permute-done.8.refs_2_.refs_7_, ...), custom_call_target="tpu_custom_call" | custom-call | flops 1 | bytes 1 | tf_op jit(solution)/shard_map/pallas_call | solution.py:116
  78.5 4.3 %collective-permute-done.14.refs_8_.refs_3_ = bf16[1152,256]{1,0:T(8,128)(2,1)S(1)} collective-permute-done((bf16[1152,256]{1,0:T(8,128)(2,1)S(1)}, bf16[1152,256]{1,0:T(8,128)(2,1)S(1)}, u32[]{:S(2)}, u32[]{:S(2)}) %collective-permute-start.14) | collective-permute-done | bytes 589856 | tf_op jit(solution)/shard_map/ppermute | solution.py:312
  82.9 3.1 %shard_map.83 = (f32[128,256]{1,0:T(8,128)S(1)}, f32[128,256]{1,0:T(8,128)S(1)}) custom-call(s32[8]{0:T(128)S(1)} %fusion.6.owners_ref, bf16[128,8192]{1,0:T(8,128)(2,1)} %refs_0_.14, bf16[128,8192]{1,0:T(8,128)(2,1)} %copy-done, bf16[1152,256]{1,0:T(8,128)(2,1)S(1)} %constant_dynamic-update-slice_fusion.10.refs_2_, ...), custom_call_target="tpu_custom_call" | custom-call | flops 1 | bytes 1 | tf_op jit(solution)/shard_map/pallas_call | solution.py:116
  86.0 2.2 %shard_map.84 = (f32[128,256]{1,0:T(8,128)S(1)}, f32[128,256]{1,0:T(8,128)S(1)}) custom-call(s32[8]{0:T(128)S(1)} %fusion.6.owners_ref, bf16[128,28672]{1,0:T(8,128)(2,1)} %refs_0_.15, bf16[128,28672]{1,0:T(8,128)(2,1)} %collective-permute-done.1.refs_3_.refs_1_, bf16[1152,256]{1,0:T(8,128)(2,1)S(1)} %collective-permute-done.15.refs_2_, ...), custom_call_target="tpu_custom_call" | custom-call | flops 1 | bytes 1 | tf_op jit(solution)/shard_map/pallas_call | solution.py:116
  88.1 8.3 %collective-permute-done.12.first_ref = bf16[1152,256]{1,0:T(8,128)(2,1)S(1)} collective-permute-done((bf16[1152,256]{1,0:T(8,128)(2,1)S(1)}, bf16[1152,256]{1,0:T(8,128)(2,1)S(1)}, u32[]{:S(2)}, u32[]{:S(2)}) %collective-permute-start.12) | collective-permute-done | bytes 589856 | tf_op jit(solution)/shard_map/ppermute | solution.py:312
  96.4 0.3 shard_map.85
  96.9 0.3 shard_map.86
  97.2 1.2 collective-permute-done.16
  98.5 1.6 %collective-permute-start.18 = (bf16[144,512]{1,0:T(8,128)(2,1)S(1)}, bf16[144,512]{1,0:T(8,128)(2,1)S(1)}, u32[]{:S(2)}, u32[]{:S(2)}) collective-permute-start(bf16[144,512]{1,0:T(8,128)(2,1)S(1)} %pad_maximum_fusion), channel_id=1, source_target_pairs={{0,2},{1,3},{4,0},{5,1},{8,4},{9,5},{12,8},{13,9},{14,12},{15,13},... | collective-permute-start | bytes 442376 | tf_op jit(solution)/shard_map/ppermute | solution.py:312
  100.1 0.5 collective-permute-start.17
  100.6 3.9 %collective-permute-done.18 = bf16[144,512]{1,0:T(8,128)(2,1)S(1)} collective-permute-done((bf16[144,512]{1,0:T(8,128)(2,1)S(1)}, bf16[144,512]{1,0:T(8,128)(2,1)S(1)}, u32[]{:S(2)}, u32[]{:S(2)}) %collective-permute-start.18) | collective-permute-done | bytes 147488 | tf_op jit(solution)/shard_map/ppermute | solution.py:312
  104.4 1.6 %collective-permute-start.20 = (bf16[144,512]{1,0:T(8,128)(2,1)S(1)}, bf16[144,512]{1,0:T(8,128)(2,1)S(1)}, u32[]{:S(2)}, u32[]{:S(2)}) collective-permute-start(bf16[144,512]{1,0:T(8,128)(2,1)S(1)} %collective-permute-done.18), channel_id=1, source_target_pairs={{0,2},{1,3},{4,0},{5,1},{8,4},{9,5},{12,8},{13,9},{14,12},{15,13},... | collective-permute-start | bytes 442376 | tf_op jit(solution)/shard_map/ppermute | solution.py:312
  106.0 0.5 collective-permute-start.19
  106.5 3.1 %collective-permute-done.20 = bf16[144,512]{1,0:T(8,128)(2,1)S(1)} collective-permute-done((bf16[144,512]{1,0:T(8,128)(2,1)S(1)}, bf16[144,512]{1,0:T(8,128)(2,1)S(1)}, u32[]{:S(2)}, u32[]{:S(2)}) %collective-permute-start.20) | collective-permute-done | bytes 147488 | tf_op jit(solution)/shard_map/ppermute | solution.py:312
  109.6 2.6 %collective-permute-start.24 = (bf16[80,512]{1,0:T(8,128)(2,1)S(1)}, bf16[80,512]{1,0:T(8,128)(2,1)S(1)}, u32[]{:S(2)}, u32[]{:S(2)}) collective-permute-start(bf16[80,512]{1,0:T(8,128)(2,1)S(1)} %slice.14), channel_id=1, source_target_pairs={{0,6},{1,7},{4,2},{5,3},{8,0},{9,1},{12,4},{13,5},{14,8},{15,9},{1... | collective-permute-start | bytes 245768 | tf_op jit(solution)/shard_map/ppermute | solution.py:312
  112.2 0.4 collective-permute-start.23
  112.6 0.6 collective-permute-start.21
  113.1 1.5 %collective-permute-start.22 = (bf16[144,512]{1,0:T(8,128)(2,1)S(1)}, bf16[144,512]{1,0:T(8,128)(2,1)S(1)}, u32[]{:S(2)}, u32[]{:S(2)}) collective-permute-start(bf16[144,512]{1,0:T(8,128)(2,1)S(1)} %collective-permute-done.20), channel_id=1, source_target_pairs={{0,2},{1,3},{4,0},{5,1},{8,4},{9,5},{12,8},{13,9},{14,12},{15,13},... | collective-permute-start | bytes 442376 | tf_op jit(solution)/shard_map/ppermute | solution.py:312
  114.7 2.8 %collective-permute-done.23 = bf16[64,512]{1,0:T(8,128)(2,1)S(1)} collective-permute-done((bf16[64,512]{1,0:T(8,128)(2,1)S(1)}, bf16[64,512]{1,0:T(8,128)(2,1)S(1)}, u32[]{:S(2)}, u32[]{:S(2)}) %collective-permute-start.23) | collective-permute-done | bytes 65568 | tf_op jit(solution)/shard_map/ppermute | solution.py:312
  117.5 0.9 collective-permute-done.21
  118.6 1.8 %collective-permute-done.26.refs_3_ = bf16[432,512]{1,0:T(8,128)(2,1)S(1)} collective-permute-done((bf16[432,512]{1,0:T(8,128)(2,1)S(1)}, bf16[432,512]{1,0:T(8,128)(2,1)S(1)}, u32[]{:S(2)}, u32[]{:S(2)}) %collective-permute-start.26) | collective-permute-done | bytes 442400 | tf_op jit(solution)/shard_map/ppermute | solution.py:312
  120.4 1.5 %shard_map.87 = (f32[16,256]{1,0:T(8,128)}, f32[1,64]{1,0:T(1,128)}) custom-call(s32[1]{0:T(128)} %bitcast.me_ref, bf16[720,512]{1,0:T(8,128)(2,1)S(1)} %constant_dynamic-update-slice_fusion.refs_0_, bf16[432,512]{1,0:T(8,128)(2,1)S(1)} %constant_dynamic-update-slice_fusion.6.refs_1_, bf16[720,512]{1,0:T(8,128)(2,1)S(1)} %collective-permute-done.25.refs_2_, ...), custom_call_target="tpu_custom_call" | custom-call | tf_op jit(solution)/shard_map/pallas_call | solution.py:273
  (47 shorter events, 0.9 us)
Async XLA Ops:
  0.6 21.3 %copy-start.2 = (s32[8]{0:T(128)S(1)}, s32[8]{0:T(128)}, u32[]{:S(2)}) copy-start(s32[8]{0:T(128)} %constant.104) | copy-start | bytes 100
  0.6 4.8 %copy-start.1 = (bf16[512,256]{1,0:T(8,128)(2,1)S(1)}, bf16[512,256]{1,0:T(8,128)(2,1)}, u32[]{:S(2)}) copy-start(bf16[512,256]{1,0:T(8,128)(2,1)} %param.9) | copy-start | bytes 786436
  0.7 21.3 %collective-permute-start.1 = (bf16[128,28672]{1,0:T(8,128)(2,1)}, bf16[128,28672]{1,0:T(8,128)(2,1)}, u32[]{:S(2)}, u32[]{:S(2)}) collective-permute-start(bf16[128,28672]{1,0:T(8,128)(2,1)} %refs_0_.15), channel_id=1, source_target_pairs={{0,1},{1,0},{2,3},{3,2},{4,5},{5,4},{6,7},{7,6},{8,9},{9,8},{10,11... | collective-permute-start | bytes 22020104 | tf_op jit(solution)/shard_map/ppermute | solution.py:312
  1.2 11.4 %collective-permute-start = (bf16[128,8192]{1,0:T(8,128)(2,1)}, bf16[128,8192]{1,0:T(8,128)(2,1)S(1)}, u32[]{:S(2)}, u32[]{:S(2)}) collective-permute-start(bf16[128,8192]{1,0:T(8,128)(2,1)} %refs_0_.14), channel_id=1, source_target_pairs={{0,1},{1,0},{2,3},{3,2},{4,5},{5,4},{6,7},{7,6},{8,9},{9,8},{10,11... | collective-permute-start | bytes 6291464 | tf_op jit(solution)/shard_map/ppermute | solution.py:312
  2.5 17.3 %collective-permute-start.4 = (bf16[1152,256]{1,0:T(8,128)(2,1)S(1)}, bf16[1152,256]{1,0:T(8,128)(2,1)}, u32[]{:S(2)}, u32[]{:S(2)}) collective-permute-start(bf16[1152,256]{1,0:T(8,128)(2,1)S(1)} %get-tuple-element.116.refs_3_), channel_id=1, source_target_pairs={{0,2},{1,3},{4,0},{5,1},{8,4},{9,5},{12,8},{13,9},{14,12},{15,13},... | collective-permute-start | bytes 1769480 | tf_op jit(solution)/shard_map/ppermute | solution.py:312
  5.5 16.3 %collective-permute-start.2 = (bf16[1152,256]{1,0:T(8,128)(2,1)S(1)}, bf16[1152,256]{1,0:T(8,128)(2,1)S(1)}, u32[]{:S(2)}, u32[]{:S(2)}) collective-permute-start(bf16[1152,256]{1,0:T(8,128)(2,1)S(1)} %constant_dynamic-update-slice_fusion.10.refs_2_), channel_id=1, source_target_pairs={{0,4},{1,5},{4,8},{5,9},{8,12},{9,13},{12,14},{13,15},{14,10},{15,... | collective-permute-start | bytes 1769480 | tf_op jit(solution)/shard_map/ppermute | solution.py:312
  12.6 9.2 %copy-start = (bf16[128,8192]{1,0:T(8,128)(2,1)}, bf16[128,8192]{1,0:T(8,128)(2,1)S(1)}, u32[]{:S(2)}) copy-start(bf16[128,8192]{1,0:T(8,128)(2,1)S(1)} %collective-permute-done.refs_2_.refs_1_) | copy-start | bytes 6291460
  12.6 19.7 %collective-permute-start.7 = (bf16[1152,256]{1,0:T(8,128)(2,1)S(1)}, bf16[1152,256]{1,0:T(8,128)(2,1)S(1)}, u32[]{:S(2)}, u32[]{:S(2)}) collective-permute-start(bf16[1152,256]{1,0:T(8,128)(2,1)S(1)} %constant_dynamic-update-slice_fusion.10.refs_2_), channel_id=1, source_target_pairs={{0,2},{1,3},{4,0},{5,1},{8,4},{9,5},{12,8},{13,9},{14,12},{15,13},... | collective-permute-start | bytes 1769480 | tf_op jit(solution)/shard_map/ppermute | solution.py:312
  15.7 18.8 %collective-permute-start.6 = (bf16[1152,256]{1,0:T(8,128)(2,1)S(1)}, bf16[1152,256]{1,0:T(8,128)(2,1)}, u32[]{:S(2)}, u32[]{:S(2)}) collective-permute-start(bf16[1152,256]{1,0:T(8,128)(2,1)S(1)} %get-tuple-element.116.refs_3_), channel_id=1, source_target_pairs={{0,4},{1,5},{4,8},{5,9},{8,12},{9,13},{12,14},{13,15},{14,10},{15,... | collective-permute-start | bytes 1769480 | tf_op jit(solution)/shard_map/ppermute | solution.py:312
  19.8 25.2 %collective-permute-start.5 = (bf16[1152,256]{1,0:T(8,128)(2,1)}, bf16[1152,256]{1,0:T(8,128)(2,1)S(1)}, u32[]{:S(2)}, u32[]{:S(2)}) collective-permute-start(bf16[1152,256]{1,0:T(8,128)(2,1)} %collective-permute-done.4.refs_5_), channel_id=1, source_target_pairs={{0,2},{1,3},{4,0},{5,1},{8,4},{9,5},{12,8},{13,9},{14,12},{15,13},... | collective-permute-start | bytes 1769480 | tf_op jit(solution)/shard_map/ppermute | solution.py:312
  21.8 25.3 %collective-permute-start.3 = (bf16[1152,256]{1,0:T(8,128)(2,1)S(1)}, bf16[1152,256]{1,0:T(8,128)(2,1)S(1)}, u32[]{:S(2)}, u32[]{:S(2)}) collective-permute-start(bf16[1152,256]{1,0:T(8,128)(2,1)S(1)} %collective-permute-done.2.refs_4_.refs_3_), channel_id=1, source_target_pairs={{0,4},{1,5},{4,8},{5,9},{8,12},{9,13},{12,14},{13,15},{14,10},{15,... | collective-permute-start | bytes 1769480 | tf_op jit(solution)/shard_map/ppermute | solution.py:312
  32.3 25.3 %collective-permute-start.11 = (bf16[1152,256]{1,0:T(8,128)(2,1)S(1)}, bf16[1152,256]{1,0:T(8,128)(2,1)S(1)}, u32[]{:S(2)}, u32[]{:S(2)}) collective-permute-start(bf16[1152,256]{1,0:T(8,128)(2,1)S(1)} %collective-permute-done.7.refs_3_.refs_4_), channel_id=1, source_target_pairs={{0,2},{1,3},{4,0},{5,1},{8,4},{9,5},{12,8},{13,9},{14,12},{15,13},... | collective-permute-start | bytes 1769480 | tf_op jit(solution)/shard_map/ppermute | solution.py:312
  34.5 25.2 %collective-permute-start.10 = (bf16[1152,256]{1,0:T(8,128)(2,1)}, bf16[1152,256]{1,0:T(8,128)(2,1)S(1)}, u32[]{:S(2)}, u32[]{:S(2)}) collective-permute-start(bf16[1152,256]{1,0:T(8,128)(2,1)} %collective-permute-done.6.refs_2_), channel_id=1, source_target_pairs={{0,4},{1,5},{4,8},{5,9},{8,12},{9,13},{12,14},{13,15},{14,10},{15,... | collective-permute-start | bytes 1769480 | tf_op jit(solution)/shard_map/ppermute | solution.py:312
  44.9 25.3 %collective-permute-start.9 = (bf16[1152,256]{1,0:T(8,128)(2,1)S(1)}, bf16[1152,256]{1,0:T(8,128)(2,1)S(1)}, u32[]{:S(2)}, u32[]{:S(2)}) collective-permute-start(bf16[1152,256]{1,0:T(8,128)(2,1)S(1)} %collective-permute-done.5.refs_3_), channel_id=1, source_target_pairs={{0,2},{1,3},{4,0},{5,1},{8,4},{9,5},{12,8},{13,9},{14,12},{15,13},... | collective-permute-start | bytes 1769480 | tf_op jit(solution)/shard_map/ppermute | solution.py:312
  47.1 25.3 %collective-permute-start.8 = (bf16[1152,256]{1,0:T(8,128)(2,1)S(1)}, bf16[1152,256]{1,0:T(8,128)(2,1)S(1)}, u32[]{:S(2)}, u32[]{:S(2)}) collective-permute-start(bf16[1152,256]{1,0:T(8,128)(2,1)S(1)} %collective-permute-done.3.refs_2_.refs_5_), channel_id=1, source_target_pairs={{0,4},{1,5},{4,8},{5,9},{8,12},{9,13},{12,14},{13,15},{14,10},{15,... | collective-permute-start | bytes 1769480 | tf_op jit(solution)/shard_map/ppermute | solution.py:312
  57.6 16.8 %copy-start.3 = (s32[128]{0:T(128)S(1)}, s32[128]{0:T(128)}, u32[]{:S(2)}) copy-start(s32[128]{0:T(128)} %param.8) | copy-start | bytes 1540
  59.7 23.2 %collective-permute-start.14 = (bf16[1152,256]{1,0:T(8,128)(2,1)S(1)}, bf16[1152,256]{1,0:T(8,128)(2,1)S(1)}, u32[]{:S(2)}, u32[]{:S(2)}) collective-permute-start(bf16[1152,256]{1,0:T(8,128)(2,1)S(1)} %collective-permute-done.11.refs_3_.refs_6_), channel_id=1, source_target_pairs={{0,2},{1,3},{4,0},{5,1},{8,4},{9,5},{12,8},{13,9},{14,12},{15,13},... | collective-permute-start | bytes 1769480 | tf_op jit(solution)/shard_map/ppermute | solution.py:312
  61.3 24.7 %collective-permute-start.15 = (bf16[1152,256]{1,0:T(8,128)(2,1)S(1)}, bf16[1152,256]{1,0:T(8,128)(2,1)S(1)}, u32[]{:S(2)}, u32[]{:S(2)}) collective-permute-start(bf16[1152,256]{1,0:T(8,128)(2,1)S(1)} %collective-permute-done.10.refs_2_), channel_id=1, source_target_pairs={{0,4},{1,5},{4,8},{5,9},{8,12},{9,13},{12,14},{13,15},{14,10},{15,... | collective-permute-start | bytes 1769480 | tf_op jit(solution)/shard_map/ppermute | solution.py:312
  72.3 24.1 %collective-permute-start.12 = (bf16[1152,256]{1,0:T(8,128)(2,1)S(1)}, bf16[1152,256]{1,0:T(8,128)(2,1)S(1)}, u32[]{:S(2)}, u32[]{:S(2)}) collective-permute-start(bf16[1152,256]{1,0:T(8,128)(2,1)S(1)} %collective-permute-done.8.refs_2_.refs_7_), channel_id=1, source_target_pairs={{0,4},{1,5},{4,8},{5,9},{8,12},{9,13},{12,14},{13,15},{14,10},{15,... | collective-permute-start | bytes 1769480 | tf_op jit(solution)/shard_map/ppermute | solution.py:312
  72.4 24.1 %collective-permute-start.13 = (bf16[1152,256]{1,0:T(8,128)(2,1)S(1)}, bf16[1152,256]{1,0:T(8,128)(2,1)S(1)}, u32[]{:S(2)}, u32[]{:S(2)}) collective-permute-start(bf16[1152,256]{1,0:T(8,128)(2,1)S(1)} %collective-permute-done.9.refs_3_), channel_id=1, source_target_pairs={{0,2},{1,3},{4,0},{5,1},{8,4},{9,5},{12,8},{13,9},{14,12},{15,13},... | collective-permute-start | bytes 1769480 | tf_op jit(solution)/shard_map/ppermute | solution.py:312
  96.8 1.6 %collective-permute-start.16 = (f32[128,512]{1,0:T(8,128)S(1)}, f32[128,512]{1,0:T(8,128)S(1)}, u32[]{:S(2)}, u32[]{:S(2)}) collective-permute-start(f32[128,512]{1,0:T(8,128)S(1)} %shard_map.85), channel_id=1, source_target_pairs={{0,1},{1,0},{2,3},{3,2},{4,5},{5,4},{6,7},{7,6},{8,9},{9,8},{10,11... | collective-permute-start | bytes 786440 | tf_op jit(solution)/shard_map/ppermute | solution.py:312
  98.5 5.9 %collective-permute-start.18 = (bf16[144,512]{1,0:T(8,128)(2,1)S(1)}, bf16[144,512]{1,0:T(8,128)(2,1)S(1)}, u32[]{:S(2)}, u32[]{:S(2)}) collective-permute-start(bf16[144,512]{1,0:T(8,128)(2,1)S(1)} %pad_maximum_fusion), channel_id=1, source_target_pairs={{0,2},{1,3},{4,0},{5,1},{8,4},{9,5},{12,8},{13,9},{14,12},{15,13},... | collective-permute-start | bytes 442376 | tf_op jit(solution)/shard_map/ppermute | solution.py:312
  100.1 5.9 %collective-permute-start.17 = (bf16[144,512]{1,0:T(8,128)(2,1)S(1)}, bf16[144,512]{1,0:T(8,128)(2,1)S(1)}, u32[]{:S(2)}, u32[]{:S(2)}) collective-permute-start(bf16[144,512]{1,0:T(8,128)(2,1)S(1)} %pad_maximum_fusion), channel_id=1, source_target_pairs={{0,4},{1,5},{4,8},{5,9},{8,12},{9,13},{12,14},{13,15},{14,10},{15,... | collective-permute-start | bytes 442376 | tf_op jit(solution)/shard_map/ppermute | solution.py:312
  104.4 5.1 %collective-permute-start.20 = (bf16[144,512]{1,0:T(8,128)(2,1)S(1)}, bf16[144,512]{1,0:T(8,128)(2,1)S(1)}, u32[]{:S(2)}, u32[]{:S(2)}) collective-permute-start(bf16[144,512]{1,0:T(8,128)(2,1)S(1)} %collective-permute-done.18), channel_id=1, source_target_pairs={{0,2},{1,3},{4,0},{5,1},{8,4},{9,5},{12,8},{13,9},{14,12},{15,13},... | collective-permute-start | bytes 442376 | tf_op jit(solution)/shard_map/ppermute | solution.py:312
  106.0 6.2 %collective-permute-start.19 = (bf16[144,512]{1,0:T(8,128)(2,1)S(1)}, bf16[144,512]{1,0:T(8,128)(2,1)S(1)}, u32[]{:S(2)}, u32[]{:S(2)}) collective-permute-start(bf16[144,512]{1,0:T(8,128)(2,1)S(1)} %collective-permute-done.17), channel_id=1, source_target_pairs={{0,4},{1,5},{4,8},{5,9},{8,12},{9,13},{12,14},{13,15},{14,10},{15,... | collective-permute-start | bytes 442376 | tf_op jit(solution)/shard_map/ppermute | solution.py:312
  109.6 7.9 %collective-permute-start.24 = (bf16[80,512]{1,0:T(8,128)(2,1)S(1)}, bf16[80,512]{1,0:T(8,128)(2,1)S(1)}, u32[]{:S(2)}, u32[]{:S(2)}) collective-permute-start(bf16[80,512]{1,0:T(8,128)(2,1)S(1)} %slice.14), channel_id=1, source_target_pairs={{0,6},{1,7},{4,2},{5,3},{8,0},{9,1},{12,4},{13,5},{14,8},{15,9},{1... | collective-permute-start | bytes 245768 | tf_op jit(solution)/shard_map/ppermute | solution.py:312
  112.2 5.3 %collective-permute-start.23 = (bf16[64,512]{1,0:T(8,128)(2,1)S(1)}, bf16[64,512]{1,0:T(8,128)(2,1)S(1)}, u32[]{:S(2)}, u32[]{:S(2)}) collective-permute-start(bf16[64,512]{1,0:T(8,128)(2,1)S(1)} %slice.13), channel_id=1, source_target_pairs={{0,8},{1,9},{4,12},{5,13},{8,14},{9,15},{12,10},{13,11},{14,6},{15... | collective-permute-start | bytes 196616 | tf_op jit(solution)/shard_map/ppermute | solution.py:312
  112.6 5.8 %collective-permute-start.21 = (bf16[144,512]{1,0:T(8,128)(2,1)S(1)}, bf16[144,512]{1,0:T(8,128)(2,1)S(1)}, u32[]{:S(2)}, u32[]{:S(2)}) collective-permute-start(bf16[144,512]{1,0:T(8,128)(2,1)S(1)} %collective-permute-done.19), channel_id=1, source_target_pairs={{0,4},{1,5},{4,8},{5,9},{8,12},{9,13},{12,14},{13,15},{14,10},{15,... | collective-permute-start | bytes 442376 | tf_op jit(solution)/shard_map/ppermute | solution.py:312
  113.1 5.3 %collective-permute-start.22 = (bf16[144,512]{1,0:T(8,128)(2,1)S(1)}, bf16[144,512]{1,0:T(8,128)(2,1)S(1)}, u32[]{:S(2)}, u32[]{:S(2)}) collective-permute-start(bf16[144,512]{1,0:T(8,128)(2,1)S(1)} %collective-permute-done.20), channel_id=1, source_target_pairs={{0,2},{1,3},{4,0},{5,1},{8,4},{9,5},{12,8},{13,9},{14,12},{15,13},... | collective-permute-start | bytes 442376 | tf_op jit(solution)/shard_map/ppermute | solution.py:312
  114.6 5.7 %collective-permute-start.25 = (bf16[720,512]{1,0:T(8,128)(2,1)S(1)}, bf16[720,512]{1,0:T(8,128)(2,1)S(1)}, u32[]{:S(2)}, u32[]{:S(2)}) collective-permute-start(bf16[720,512]{1,0:T(8,128)(2,1)S(1)} %constant_dynamic-update-slice_fusion.refs_0_), channel_id=1, source_target_pairs={{0,1},{1,0},{2,3},{3,2},{4,5},{5,4},{6,7},{7,6},{8,9},{9,8},{10,11... | collective-permute-start | bytes 2211848 | tf_op jit(solution)/shard_map/ppermute | solution.py:312
  118.5 1.9 %collective-permute-start.26 = (bf16[432,512]{1,0:T(8,128)(2,1)S(1)}, bf16[432,512]{1,0:T(8,128)(2,1)S(1)}, u32[]{:S(2)}, u32[]{:S(2)}) collective-permute-start(bf16[432,512]{1,0:T(8,128)(2,1)S(1)} %constant_dynamic-update-slice_fusion.6.refs_1_), channel_id=1, source_target_pairs={{0,1},{1,0},{2,3},{3,2},{4,5},{5,4},{6,7},{7,6},{8,9},{9,8},{10,11... | collective-permute-start | bytes 1327112 | tf_op jit(solution)/shard_map/ppermute | solution.py:312

commit v7 on v6

--- a/solution.py
+++ b/solution.py
@@ -226,64 +226,93 @@
     )(block, *[pltpu.with_memory_space_constraint(x, pltpu.VMEM) for x in panels], act, grad)
 
 
-def last_kernel(scale, rows, me_ref, *refs):
-    pieces, (corrected_ref, score_ref, squares, held) = refs[:-4], refs[-4:]
-    me = me_ref[0]
-    panel_rows, in_panel = corrected_ref.shape
-    out_panel = squares.shape[1] - in_panel
-    balanced = score_ref.shape[1]
+def add_up(me, pieces, squares, rows, width, balanced):
     wanted = lax.broadcasted_iota(jnp.int32, (balanced, rows), 0)
     at, picks = 0, []
     for piece in pieces:
-        start = 0
-        while start < piece.shape[0]:
-            count = min(rows - at % rows, piece.shape[0] - start)
-            squares[at : at + count, :] = piece[start : start + count, :]
-            at, start = at + count, start + count
-            if at % rows == 0:
-                tag = piece[start : start + 16, :][:1].astype(jnp.float32).astype(jnp.int32)
-                owner, place = tag[:, :rows], tag[:, rows : 2 * rows]
-                picks.append(((owner == me) & (place == wanted)).astype(jnp.float32))
-                start += 16
+        for start in range(0, piece.shape[0], rows + 16):
+            squares[at : at + rows, :] = piece[start : start + rows, :]
+            tag = piece[start + rows : start + rows + 16, :][:1].astype(jnp.float32).astype(jnp.int32)
+            owner, place = tag[:, :rows], tag[:, rows : 2 * rows]
+            picks.append(((owner == me) & (place == wanted)).astype(jnp.float32))
+            at += rows
     pick = jnp.concatenate(picks, axis=1).astype(jnp.bfloat16)
-    act, grad = squares[:, :in_panel], squares[:, in_panel:]
-    corrected = lax.dot_general(
-        grad, act, (((0,), (0,)), ((), ())), preferred_element_type=jnp.float32
-    ) * scale
+    act, grad = squares[:, :width], squares[:, width:]
+    return (
+        lax.dot_general(grad, act, (((0,), (0,)), ((), ())), preferred_element_type=jnp.float32),
+        dot(pick, act),
+        lax.dot_general(grad, pick, (((0,), (1,)), ((), ())), preferred_element_type=jnp.float32),
+    )
+
+
+def some_sums_kernel(rows, me_ref, *refs):
+    pieces, (total_ref, act_ref, grad_ref, squares) = refs[:-4], refs[-4:]
+    balanced, width = act_ref.shape
+    total_ref[...], act_ref[...], grad_ref[...] = add_up(
+        me_ref[0], pieces, squares, rows, width, balanced
+    )
+
+
+def some_sums(me, pieces, rows, width, balanced):
+    vmem = pl.BlockSpec(memory_space=pltpu.VMEM)
+    tokens = sum(piece.shape[0] for piece in pieces) // (rows + 16) * rows
+    out_panel = pieces[0].shape[1] - width
+    return pl.pallas_call(
+        functools.partial(some_sums_kernel, rows),
+        out_shape=(
+            jax.ShapeDtypeStruct((out_panel, width), jnp.float32),
+            jax.ShapeDtypeStruct((balanced, width), jnp.float32),
+            jax.ShapeDtypeStruct((out_panel, balanced), jnp.float32),
+        ),
+        in_specs=[pl.BlockSpec(memory_space=pltpu.SMEM)] + [vmem] * len(pieces),
+        out_specs=(vmem, vmem, vmem),
+        scratch_shapes=[pltpu.VMEM((tokens, pieces[0].shape[1]), jnp.bfloat16)],
+        compiler_params=pltpu.CompilerParams(vmem_limit_bytes=16 * 2**20),
+        cost_estimate=pl.CostEstimate(flops=1, bytes_accessed=1, transcendentals=0),
+    )(me, *pieces)
+
+
+def last_kernel(rows, scale, me_ref, first_ref, second_ref, total_ref, act_ref, grad_ref, *refs):
+    corrected_ref, score_ref, squares, held = refs
+    me = me_ref[0]
+    panel_rows, in_panel = corrected_ref.shape
+    out_panel = total_ref.shape[0]
+    total, own_act, own_grad = add_up(
+        me, (first_ref, second_ref), squares, rows, in_panel, act_ref.shape[0]
+    )
+    corrected = (total + total_ref[...]) * scale
     held[...] = corrected
     corrected_ref[...] = held[pl.ds(pl.multiple_of(me * panel_rows, panel_rows), panel_rows), :]
     inverse = 1.0 / (corrected + damping)
     high = inverse.astype(jnp.bfloat16)
     low = (inverse - high.astype(jnp.float32)).astype(jnp.bfloat16)
-    own_act = dot(pick, act).astype(jnp.bfloat16)
-    own_grad = lax.dot_general(
-        grad, pick, (((0,), (1,)), ((), ())), preferred_element_type=jnp.float32
-    )
+    own_act = (own_act + act_ref[...]).astype(jnp.bfloat16)
     weighted = sum(
         lax.dot_general(part, own_act, (((1,), (1,)), ((), ())), preferred_element_type=jnp.float32)
         for part in (high, low)
     )
-    score_ref[...] = jnp.sum(own_grad * weighted, axis=0, keepdims=True) / (out_panel * in_panel)
-
-
-def last(me, pieces, rows, out_panel, devices, balanced):
-    vmem = pl.BlockSpec(memory_space=pltpu.VMEM)
-    width = pieces[0].shape[1]
-    in_panel = width - out_panel
+    score = jnp.sum((own_grad + grad_ref[...]) * weighted, axis=0, keepdims=True)
+    score_ref[...] = score / (out_panel * in_panel)
+
+
+def last(me, pieces, sums, rows, devices):
+    vmem = pl.BlockSpec(memory_space=pltpu.VMEM)
+    (out_panel, in_panel), balanced = sums[0].shape, sums[1].shape[0]
+    tokens = sum(piece.shape[0] for piece in pieces) // (rows + 16) * rows
     corrected, score = pl.pallas_call(
-        functools.partial(last_kernel, 1.0 / (devices * balanced), rows),
+        functools.partial(last_kernel, rows, 1.0 / (devices * balanced)),
         out_shape=(
             jax.ShapeDtypeStruct((out_panel // devices, in_panel), jnp.float32),
             jax.ShapeDtypeStruct((1, balanced), jnp.float32),
         ),
-        in_specs=[pl.BlockSpec(memory_space=pltpu.SMEM)] + [vmem] * len(pieces),
+        in_specs=[pl.BlockSpec(memory_space=pltpu.SMEM)] + [vmem] * 5,
         out_specs=(vmem, vmem),
         scratch_shapes=[
-            pltpu.VMEM((devices * rows, width), jnp.bfloat16),
+            pltpu.VMEM((tokens, out_panel + in_panel), jnp.bfloat16),
             pltpu.VMEM((out_panel, in_panel), jnp.float32),
         ],
         compiler_params=pltpu.CompilerParams(vmem_limit_bytes=16 * 2**20),
-    )(me, *pieces)
+    )(me, *pieces, *sums)
     return corrected, score.reshape(balanced)
 
 
@@ -393,11 +422,14 @@
     held[half - 1], held[1 - half], upper, lower = lax.optimization_barrier(
         (held[half - 1], held[1 - half], upper, lower)
     )
-    near = jnp.concatenate([held[d] for d in distances[:-3]], axis=0)
+    near = jnp.concatenate([held[-d] for d in distances[:-3]], axis=0)
     far = jnp.concatenate([held[half - 1], held[1 - half], upper, lower], axis=0)
     own = [near, far]
     swapped = [send(x, swap) for x in own]
-    return last(own_index[None], own + swapped, rows, width, devices, balanced)
+    me = own_index[None]
+    near_both = lax.optimization_barrier((near, swapped[0], far))[:2]
+    sums = some_sums(me, list(near_both), rows, width, balanced)
+    return last(me, [far, swapped[1]], sums, rows, devices)
 
 
 def body(*arrays):

time: 122 us -> 122 us (level)
  no operation moved by 1% of the time
where the time goes in v7:
time: 122 us
  waiting for transfers between devices  70 us (57%)
  starting transfers between devices  26.5 us (22%)
  Pallas kernels  22.6 us (19%)
  local copies, waits for them, and re-layouts  1.38 us (1%)
    ppermute x27, waiting for transfers between devices, send(): return lax.ppermute(x, 'dp', pairs)  70 us
    ppermute x27, starting transfers between devices, send(): return lax.ppermute(x, 'dp', pairs)  26.5 us
    pallas_call x7, Pallas kernels, project(): pl.pallas_call(functools.partial(project_kernel, kinds, [p[:2] for p in p...  18.3 us
  transfers between devices with their start and end apart: 27, of which 18 were waited for; matrix products, arithmetic and copies ran while one was open for 1% of the time, Pallas kernels for 17%

profile of v7, /device:TPU:0, one launch (start us, length us, event | category | flops | bytes accessed | tf_op | source)
XLA Modules:
  0.0 121.5 jit_solution(15849287784271880542)
XLA Ops:
  0.7 0.5 collective-permute-start.1
  1.3 1.2 %fusion.7 = (bf16[1152,256]{1,0:T(8,128)(2,1)S(1)}, bf16[1152,256]{1,0:T(8,128)(2,1)S(1)}) fusion(bf16[1792,256]{1,0:T(8,128)(2,1)} %param.10), kind=kLoop, calls=%fused_computation.34 | loop fusion | bytes 2686976 | tf_op jit(solution)/shard_map/slice | solution.py:357
  2.5 3.0 %collective-permute-start.4 = (bf16[1152,256]{1,0:T(8,128)(2,1)S(1)}, bf16[1152,256]{1,0:T(8,128)(2,1)}, u32[]{:S(2)}, u32[]{:S(2)}) collective-permute-start(bf16[1152,256]{1,0:T(8,128)(2,1)S(1)} %get-tuple-element.126.refs_3_), channel_id=1, source_target_pairs={{0,2},{1,3},{4,0},{5,1},{8,4},{9,5},{12,8},{13,9},{14,12},{15,13},... | collective-permute-start | bytes 1769480 | tf_op jit(solution)/shard_map/ppermute | solution.py:341
  5.5 0.1 collective-permute-start.2
  5.6 7.0 %collective-permute-done.refs_2_.refs_1_ = bf16[128,8192]{1,0:T(8,128)(2,1)S(1)} collective-permute-done((bf16[128,8192]{1,0:T(8,128)(2,1)}, bf16[128,8192]{1,0:T(8,128)(2,1)S(1)}, u32[]{:S(2)}, u32[]{:S(2)}) %collective-permute-start) | collective-permute-done | bytes 2097184 | tf_op jit(solution)/shard_map/ppermute | solution.py:341
  12.6 3.1 %collective-permute-start.7 = (bf16[1152,256]{1,0:T(8,128)(2,1)S(1)}, bf16[1152,256]{1,0:T(8,128)(2,1)S(1)}, u32[]{:S(2)}, u32[]{:S(2)}) collective-permute-start(bf16[1152,256]{1,0:T(8,128)(2,1)S(1)} %constant_dynamic-update-slice_fusion.10.refs_2_), channel_id=1, source_target_pairs={{0,2},{1,3},{4,0},{5,1},{8,4},{9,5},{12,8},{13,9},{14,12},{15,13},... | collective-permute-start | bytes 1769480 | tf_op jit(solution)/shard_map/ppermute | solution.py:341
  15.8 4.0 %collective-permute-done.4.refs_5_ = bf16[1152,256]{1,0:T(8,128)(2,1)} collective-permute-done((bf16[1152,256]{1,0:T(8,128)(2,1)S(1)}, bf16[1152,256]{1,0:T(8,128)(2,1)}, u32[]{:S(2)}, u32[]{:S(2)}) %collective-permute-start.4) | collective-permute-done | bytes 589856 | tf_op jit(solution)/shard_map/ppermute | solution.py:341
  19.8 2.0 %collective-permute-start.5 = (bf16[1152,256]{1,0:T(8,128)(2,1)}, bf16[1152,256]{1,0:T(8,128)(2,1)S(1)}, u32[]{:S(2)}, u32[]{:S(2)}) collective-permute-start(bf16[1152,256]{1,0:T(8,128)(2,1)} %collective-permute-done.4.refs_5_), channel_id=1, source_target_pairs={{0,2},{1,3},{4,0},{5,1},{8,4},{9,5},{12,8},{13,9},{14,12},{15,13},... | collective-permute-start | bytes 1769480 | tf_op jit(solution)/shard_map/ppermute | solution.py:341
  21.9 3.7 %shard_map.78 = (f32[128,256]{1,0:T(8,128)S(1)}, f32[128,256]{1,0:T(8,128)S(1)}) custom-call(s32[8]{0:T(128)S(1)} %fusion.6.owners_ref, bf16[128,28672]{1,0:T(8,128)(2,1)} %refs_0_.15, bf16[128,28672]{1,0:T(8,128)(2,1)} %collective-permute-done.1.refs_3_.refs_1_, bf16[1152,256]{1,0:T(8,128)(2,1)S(1)} %constant_dynamic-update-slice_fusion.10.refs_2_, ...), custom_call_target="tpu_custom_call" | custom-call | flops 1 | bytes 1 | tf_op jit(solution)/shard_map/pallas_call | solution.py:116
  25.6 6.7 %collective-permute-done.7.refs_3_.refs_4_ = bf16[1152,256]{1,0:T(8,128)(2,1)S(1)} collective-permute-done((bf16[1152,256]{1,0:T(8,128)(2,1)S(1)}, bf16[1152,256]{1,0:T(8,128)(2,1)S(1)}, u32[]{:S(2)}, u32[]{:S(2)}) %collective-permute-start.7) | collective-permute-done | bytes 589856 | tf_op jit(solution)/shard_map/ppermute | solution.py:341
  32.3 2.0 %collective-permute-start.11 = (bf16[1152,256]{1,0:T(8,128)(2,1)S(1)}, bf16[1152,256]{1,0:T(8,128)(2,1)S(1)}, u32[]{:S(2)}, u32[]{:S(2)}) collective-permute-start(bf16[1152,256]{1,0:T(8,128)(2,1)S(1)} %collective-permute-done.7.refs_3_.refs_4_), channel_id=1, source_target_pairs={{0,2},{1,3},{4,0},{5,1},{8,4},{9,5},{12,8},{13,9},{14,12},{15,13},... | collective-permute-start | bytes 1769480 | tf_op jit(solution)/shard_map/ppermute | solution.py:341
  34.3 0.2 collective-permute-done.6.refs_2_
  34.6 2.7 %shard_map.79 = (f32[128,256]{1,0:T(8,128)S(1)}, f32[128,256]{1,0:T(8,128)S(1)}) custom-call(s32[8]{0:T(128)S(1)} %fusion.6.owners_ref, bf16[128,28672]{1,0:T(8,128)(2,1)} %refs_0_.15, bf16[128,28672]{1,0:T(8,128)(2,1)} %collective-permute-done.1.refs_3_.refs_1_, bf16[1152,256]{1,0:T(8,128)(2,1)} %collective-permute-done.6.refs_2_, ...), custom_call_target="tpu_custom_call" | custom-call | flops 1 | bytes 1 | tf_op jit(solution)/shard_map/pallas_call | solution.py:116
  37.3 7.6 %collective-permute-done.5.refs_3_ = bf16[1152,256]{1,0:T(8,128)(2,1)S(1)} collective-permute-done((bf16[1152,256]{1,0:T(8,128)(2,1)}, bf16[1152,256]{1,0:T(8,128)(2,1)S(1)}, u32[]{:S(2)}, u32[]{:S(2)}) %collective-permute-start.5) | collective-permute-done | bytes 589856 | tf_op jit(solution)/shard_map/ppermute | solution.py:341
  44.9 2.0 %collective-permute-start.9 = (bf16[1152,256]{1,0:T(8,128)(2,1)S(1)}, bf16[1152,256]{1,0:T(8,128)(2,1)S(1)}, u32[]{:S(2)}, u32[]{:S(2)}) collective-permute-start(bf16[1152,256]{1,0:T(8,128)(2,1)S(1)} %collective-permute-done.5.refs_3_), channel_id=1, source_target_pairs={{0,2},{1,3},{4,0},{5,1},{8,4},{9,5},{12,8},{13,9},{14,12},{15,13},... | collective-permute-start | bytes 1769480 | tf_op jit(solution)/shard_map/ppermute | solution.py:341
  47.1 2.2 %shard_map.80 = (f32[128,256]{1,0:T(8,128)S(1)}, f32[128,256]{1,0:T(8,128)S(1)}) custom-call(s32[8]{0:T(128)S(1)} %fusion.6.owners_ref, bf16[128,28672]{1,0:T(8,128)(2,1)} %refs_0_.15, bf16[128,28672]{1,0:T(8,128)(2,1)} %collective-permute-done.1.refs_3_.refs_1_, bf16[1152,256]{1,0:T(8,128)(2,1)S(1)} %collective-permute-done.3.refs_2_.refs_5_, ...), custom_call_target="tpu_custom_call" | custom-call | flops 1 | bytes 1 | tf_op jit(solution)/shard_map/pallas_call | solution.py:116
  49.3 8.2 %collective-permute-done.11.refs_3_.refs_6_ = bf16[1152,256]{1,0:T(8,128)(2,1)S(1)} collective-permute-done((bf16[1152,256]{1,0:T(8,128)(2,1)S(1)}, bf16[1152,256]{1,0:T(8,128)(2,1)S(1)}, u32[]{:S(2)}, u32[]{:S(2)}) %collective-permute-start.11) | collective-permute-done | bytes 589856 | tf_op jit(solution)/shard_map/ppermute | solution.py:341
  57.6 2.1 %collective-permute-done.10.refs_2_ = bf16[1152,256]{1,0:T(8,128)(2,1)S(1)} collective-permute-done((bf16[1152,256]{1,0:T(8,128)(2,1)}, bf16[1152,256]{1,0:T(8,128)(2,1)S(1)}, u32[]{:S(2)}, u32[]{:S(2)}) %collective-permute-start.10) | collective-permute-done | bytes 589856 | tf_op jit(solution)/shard_map/ppermute | solution.py:341
  59.7 1.6 %collective-permute-start.14 = (bf16[1152,256]{1,0:T(8,128)(2,1)S(1)}, bf16[1152,256]{1,0:T(8,128)(2,1)S(1)}, u32[]{:S(2)}, u32[]{:S(2)}) collective-permute-start(bf16[1152,256]{1,0:T(8,128)(2,1)S(1)} %collective-permute-done.11.refs_3_.refs_6_), channel_id=1, source_target_pairs={{0,2},{1,3},{4,0},{5,1},{8,4},{9,5},{12,8},{13,9},{14,12},{15,13},... | collective-permute-start | bytes 1769480 | tf_op jit(solution)/shard_map/ppermute | solution.py:341
  61.3 0.4 collective-permute-start.15
  61.7 2.2 %shard_map.81 = (f32[128,256]{1,0:T(8,128)S(1)}, f32[128,256]{1,0:T(8,128)S(1)}) custom-call(s32[8]{0:T(128)S(1)} %fusion.6.owners_ref, bf16[128,28672]{1,0:T(8,128)(2,1)} %refs_0_.15, bf16[128,28672]{1,0:T(8,128)(2,1)} %collective-permute-done.1.refs_3_.refs_1_, bf16[1152,256]{1,0:T(8,128)(2,1)S(1)} %collective-permute-done.10.refs_2_, ...), custom_call_target="tpu_custom_call" | custom-call | flops 1 | bytes 1 | tf_op jit(solution)/shard_map/pallas_call | solution.py:116
  63.9 6.3 %collective-permute-done.9.refs_3_ = bf16[1152,256]{1,0:T(8,128)(2,1)S(1)} collective-permute-done((bf16[1152,256]{1,0:T(8,128)(2,1)S(1)}, bf16[1152,256]{1,0:T(8,128)(2,1)S(1)}, u32[]{:S(2)}, u32[]{:S(2)}) %collective-permute-start.9) | collective-permute-done | bytes 589856 | tf_op jit(solution)/shard_map/ppermute | solution.py:341
  70.2 2.1 %collective-permute-done.8.refs_2_.refs_7_ = bf16[1152,256]{1,0:T(8,128)(2,1)S(1)} collective-permute-done((bf16[1152,256]{1,0:T(8,128)(2,1)S(1)}, bf16[1152,256]{1,0:T(8,128)(2,1)S(1)}, u32[]{:S(2)}, u32[]{:S(2)}) %collective-permute-start.8) | collective-permute-done | bytes 589856 | tf_op jit(solution)/shard_map/ppermute | solution.py:341
  72.4 2.0 %collective-permute-start.13 = (bf16[1152,256]{1,0:T(8,128)(2,1)S(1)}, bf16[1152,256]{1,0:T(8,128)(2,1)S(1)}, u32[]{:S(2)}, u32[]{:S(2)}) collective-permute-start(bf16[1152,256]{1,0:T(8,128)(2,1)S(1)} %collective-permute-done.9.refs_3_), channel_id=1, source_target_pairs={{0,2},{1,3},{4,0},{5,1},{8,4},{9,5},{12,8},{13,9},{14,12},{15,13},... | collective-permute-start | bytes 1769480 | tf_op jit(solution)/shard_map/ppermute | solution.py:341
  74.4 1.9 %shard_map.77 = (bf16[128,2304]{1,0:T(8,128)(2,1)S(1)}, bf16[128,2304]{1,0:T(8,128)(2,1)S(1)}) custom-call(s32[8]{0:T(128)S(1)} %fusion.6.owners_ref, bf16[128,8192]{1,0:T(8,128)(2,1)} %refs_0_.14, bf16[128,28672]{1,0:T(8,128)(2,1)} %refs_0_.15, bf16[128,8192]{1,0:T(8,128)(2,1)} %copy-done, bf16[128,28672]{1,0:T(8,128)(2,1)} %collective-permute-done.1.refs_3_.refs_1_), custom_call_target="tpu_custom_call" | custom-call | flops 1 | bytes 1 | tf_op jit(solution)/shard_map/pallas_call | solution.py:194
  76.3 2.2 %shard_map.82 = (f32[128,256]{1,0:T(8,128)S(1)}, f32[128,256]{1,0:T(8,128)S(1)}) custom-call(s32[8]{0:T(128)S(1)} %fusion.6.owners_ref, bf16[128,28672]{1,0:T(8,128)(2,1)} %refs_0_.15, bf16[128,28672]{1,0:T(8,128)(2,1)} %collective-permute-done.1.refs_3_.refs_1_, bf16[1152,256]{1,0:T(8,128)(2,1)S(1)} %collective-permute-done.8.refs_2_.refs_7_, ...), custom_call_target="tpu_custom_call" | custom-call | flops 1 | bytes 1 | tf_op jit(solution)/shard_map/pallas_call | solution.py:116
  78.5 4.3 %collective-permute-done.14.refs_8_.refs_3_ = bf16[1152,256]{1,0:T(8,128)(2,1)S(1)} collective-permute-done((bf16[1152,256]{1,0:T(8,128)(2,1)S(1)}, bf16[1152,256]{1,0:T(8,128)(2,1)S(1)}, u32[]{:S(2)}, u32[]{:S(2)}) %collective-permute-start.14) | collective-permute-done | bytes 589856 | tf_op jit(solution)/shard_map/ppermute | solution.py:341
  82.9 3.1 %shard_map.83 = (f32[128,256]{1,0:T(8,128)S(1)}, f32[128,256]{1,0:T(8,128)S(1)}) custom-call(s32[8]{0:T(128)S(1)} %fusion.6.owners_ref, bf16[128,8192]{1,0:T(8,128)(2,1)} %refs_0_.14, bf16[128,8192]{1,0:T(8,128)(2,1)} %copy-done, bf16[1152,256]{1,0:T(8,128)(2,1)S(1)} %constant_dynamic-update-slice_fusion.10.refs_2_, ...), custom_call_target="tpu_custom_call" | custom-call | flops 1 | bytes 1 | tf_op jit(solution)/shard_map/pallas_call | solution.py:116
  86.0 2.2 %shard_map.84 = (f32[128,256]{1,0:T(8,128)S(1)}, f32[128,256]{1,0:T(8,128)S(1)}) custom-call(s32[8]{0:T(128)S(1)} %fusion.6.owners_ref, bf16[128,28672]{1,0:T(8,128)(2,1)} %refs_0_.15, bf16[128,28672]{1,0:T(8,128)(2,1)} %collective-permute-done.1.refs_3_.refs_1_, bf16[1152,256]{1,0:T(8,128)(2,1)S(1)} %collective-permute-done.15.refs_2_, ...), custom_call_target="tpu_custom_call" | custom-call | flops 1 | bytes 1 | tf_op jit(solution)/shard_map/pallas_call | solution.py:116
  88.1 8.3 %collective-permute-done.12.first_ref = bf16[1152,256]{1,0:T(8,128)(2,1)S(1)} collective-permute-done((bf16[1152,256]{1,0:T(8,128)(2,1)S(1)}, bf16[1152,256]{1,0:T(8,128)(2,1)S(1)}, u32[]{:S(2)}, u32[]{:S(2)}) %collective-permute-start.12) | collective-permute-done | bytes 589856 | tf_op jit(solution)/shard_map/ppermute | solution.py:341
  96.4 0.3 shard_map.85
  96.9 0.3 shard_map.86
  97.2 1.2 collective-permute-done.16
  98.5 1.6 %collective-permute-start.20 = (bf16[144,512]{1,0:T(8,128)(2,1)S(1)}, bf16[144,512]{1,0:T(8,128)(2,1)S(1)}, u32[]{:S(2)}, u32[]{:S(2)}) collective-permute-start(bf16[144,512]{1,0:T(8,128)(2,1)S(1)} %pad_maximum_fusion), channel_id=1, source_target_pairs={{0,2},{1,3},{4,0},{5,1},{8,4},{9,5},{12,8},{13,9},{14,12},{15,13},... | collective-permute-start | bytes 442376 | tf_op jit(solution)/shard_map/ppermute | solution.py:341
  100.1 0.5 collective-permute-start.17
  100.6 3.9 %collective-permute-done.20 = bf16[144,512]{1,0:T(8,128)(2,1)S(1)} collective-permute-done((bf16[144,512]{1,0:T(8,128)(2,1)S(1)}, bf16[144,512]{1,0:T(8,128)(2,1)S(1)}, u32[]{:S(2)}, u32[]{:S(2)}) %collective-permute-start.20) | collective-permute-done | bytes 147488 | tf_op jit(solution)/shard_map/ppermute | solution.py:341
  104.4 1.6 %collective-permute-start.21 = (bf16[144,512]{1,0:T(8,128)(2,1)S(1)}, bf16[144,512]{1,0:T(8,128)(2,1)S(1)}, u32[]{:S(2)}, u32[]{:S(2)}) collective-permute-start(bf16[144,512]{1,0:T(8,128)(2,1)S(1)} %collective-permute-done.20), channel_id=1, source_target_pairs={{0,2},{1,3},{4,0},{5,1},{8,4},{9,5},{12,8},{13,9},{14,12},{15,13},... | collective-permute-start | bytes 442376 | tf_op jit(solution)/shard_map/ppermute | solution.py:341
  106.0 0.5 collective-permute-start.18
  106.5 3.1 %collective-permute-done.21 = bf16[144,512]{1,0:T(8,128)(2,1)S(1)} collective-permute-done((bf16[144,512]{1,0:T(8,128)(2,1)S(1)}, bf16[144,512]{1,0:T(8,128)(2,1)S(1)}, u32[]{:S(2)}, u32[]{:S(2)}) %collective-permute-start.21) | collective-permute-done | bytes 147488 | tf_op jit(solution)/shard_map/ppermute | solution.py:341
  109.6 2.6 %collective-permute-start.24 = (bf16[80,512]{1,0:T(8,128)(2,1)S(1)}, bf16[80,512]{1,0:T(8,128)(2,1)S(1)}, u32[]{:S(2)}, u32[]{:S(2)}) collective-permute-start(bf16[80,512]{1,0:T(8,128)(2,1)S(1)} %slice.14), channel_id=1, source_target_pairs={{0,6},{1,7},{4,2},{5,3},{8,0},{9,1},{12,4},{13,5},{14,8},{15,9},{1... | collective-permute-start | bytes 245768 | tf_op jit(solution)/shard_map/ppermute | solution.py:341
  112.2 0.4 collective-permute-start.23
  112.6 0.6 collective-permute-start.19
  113.1 1.5 %collective-permute-start.22 = (bf16[144,512]{1,0:T(8,128)(2,1)S(1)}, bf16[144,512]{1,0:T(8,128)(2,1)S(1)}, u32[]{:S(2)}, u32[]{:S(2)}) collective-permute-start(bf16[144,512]{1,0:T(8,128)(2,1)S(1)} %collective-permute-done.21), channel_id=1, source_target_pairs={{0,2},{1,3},{4,0},{5,1},{8,4},{9,5},{12,8},{13,9},{14,12},{15,13},... | collective-permute-start | bytes 442376 | tf_op jit(solution)/shard_map/ppermute | solution.py:341
  114.7 2.8 %collective-permute-done.23 = bf16[64,512]{1,0:T(8,128)(2,1)S(1)} collective-permute-done((bf16[64,512]{1,0:T(8,128)(2,1)S(1)}, bf16[64,512]{1,0:T(8,128)(2,1)S(1)}, u32[]{:S(2)}, u32[]{:S(2)}) %collective-permute-start.23) | collective-permute-done | bytes 65568 | tf_op jit(solution)/shard_map/ppermute | solution.py:341
  117.5 0.9 collective-permute-done.19
  118.6 0.6 shard_map.87
  119.2 1.2 collective-permute-done.25.second_ref
  120.4 1.2 shard_map.88
  (48 shorter events, 1.1 us)
Async XLA Ops:
  0.6 21.3 %copy-start.2 = (s32[8]{0:T(128)S(1)}, s32[8]{0:T(128)}, u32[]{:S(2)}) copy-start(s32[8]{0:T(128)} %constant.104) | copy-start | bytes 100
  0.6 4.8 %copy-start.1 = (bf16[512,256]{1,0:T(8,128)(2,1)S(1)}, bf16[512,256]{1,0:T(8,128)(2,1)}, u32[]{:S(2)}) copy-start(bf16[512,256]{1,0:T(8,128)(2,1)} %param.9) | copy-start | bytes 786436
  0.7 21.3 %collective-permute-start.1 = (bf16[128,28672]{1,0:T(8,128)(2,1)}, bf16[128,28672]{1,0:T(8,128)(2,1)}, u32[]{:S(2)}, u32[]{:S(2)}) collective-permute-start(bf16[128,28672]{1,0:T(8,128)(2,1)} %refs_0_.15), channel_id=1, source_target_pairs={{0,1},{1,0},{2,3},{3,2},{4,5},{5,4},{6,7},{7,6},{8,9},{9,8},{10,11... | collective-permute-start | bytes 22020104 | tf_op jit(solution)/shard_map/ppermute | solution.py:341
  1.2 11.4 %collective-permute-start = (bf16[128,8192]{1,0:T(8,128)(2,1)}, bf16[128,8192]{1,0:T(8,128)(2,1)S(1)}, u32[]{:S(2)}, u32[]{:S(2)}) collective-permute-start(bf16[128,8192]{1,0:T(8,128)(2,1)} %refs_0_.14), channel_id=1, source_target_pairs={{0,1},{1,0},{2,3},{3,2},{4,5},{5,4},{6,7},{7,6},{8,9},{9,8},{10,11... | collective-permute-start | bytes 6291464 | tf_op jit(solution)/shard_map/ppermute | solution.py:341
  2.5 17.3 %collective-permute-start.4 = (bf16[1152,256]{1,0:T(8,128)(2,1)S(1)}, bf16[1152,256]{1,0:T(8,128)(2,1)}, u32[]{:S(2)}, u32[]{:S(2)}) collective-permute-start(bf16[1152,256]{1,0:T(8,128)(2,1)S(1)} %get-tuple-element.126.refs_3_), channel_id=1, source_target_pairs={{0,2},{1,3},{4,0},{5,1},{8,4},{9,5},{12,8},{13,9},{14,12},{15,13},... | collective-permute-start | bytes 1769480 | tf_op jit(solution)/shard_map/ppermute | solution.py:341
  5.5 16.3 %collective-permute-start.2 = (bf16[1152,256]{1,0:T(8,128)(2,1)S(1)}, bf16[1152,256]{1,0:T(8,128)(2,1)S(1)}, u32[]{:S(2)}, u32[]{:S(2)}) collective-permute-start(bf16[1152,256]{1,0:T(8,128)(2,1)S(1)} %constant_dynamic-update-slice_fusion.10.refs_2_), channel_id=1, source_target_pairs={{0,4},{1,5},{4,8},{5,9},{8,12},{9,13},{12,14},{13,15},{14,10},{15,... | collective-permute-start | bytes 1769480 | tf_op jit(solution)/shard_map/ppermute | solution.py:341
  12.6 9.2 %copy-start = (bf16[128,8192]{1,0:T(8,128)(2,1)}, bf16[128,8192]{1,0:T(8,128)(2,1)S(1)}, u32[]{:S(2)}) copy-start(bf16[128,8192]{1,0:T(8,128)(2,1)S(1)} %collective-permute-done.refs_2_.refs_1_) | copy-start | bytes 6291460
  12.6 19.7 %collective-permute-start.7 = (bf16[1152,256]{1,0:T(8,128)(2,1)S(1)}, bf16[1152,256]{1,0:T(8,128)(2,1)S(1)}, u32[]{:S(2)}, u32[]{:S(2)}) collective-permute-start(bf16[1152,256]{1,0:T(8,128)(2,1)S(1)} %constant_dynamic-update-slice_fusion.10.refs_2_), channel_id=1, source_target_pairs={{0,2},{1,3},{4,0},{5,1},{8,4},{9,5},{12,8},{13,9},{14,12},{15,13},... | collective-permute-start | bytes 1769480 | tf_op jit(solution)/shard_map/ppermute | solution.py:341
  15.7 18.8 %collective-permute-start.6 = (bf16[1152,256]{1,0:T(8,128)(2,1)S(1)}, bf16[1152,256]{1,0:T(8,128)(2,1)}, u32[]{:S(2)}, u32[]{:S(2)}) collective-permute-start(bf16[1152,256]{1,0:T(8,128)(2,1)S(1)} %get-tuple-element.126.refs_3_), channel_id=1, source_target_pairs={{0,4},{1,5},{4,8},{5,9},{8,12},{9,13},{12,14},{13,15},{14,10},{15,... | collective-permute-start | bytes 1769480 | tf_op jit(solution)/shard_map/ppermute | solution.py:341
  19.8 25.2 %collective-permute-start.5 = (bf16[1152,256]{1,0:T(8,128)(2,1)}, bf16[1152,256]{1,0:T(8,128)(2,1)S(1)}, u32[]{:S(2)}, u32[]{:S(2)}) collective-permute-start(bf16[1152,256]{1,0:T(8,128)(2,1)} %collective-permute-done.4.refs_5_), channel_id=1, source_target_pairs={{0,2},{1,3},{4,0},{5,1},{8,4},{9,5},{12,8},{13,9},{14,12},{15,13},... | collective-permute-start | bytes 1769480 | tf_op jit(solution)/shard_map/ppermute | solution.py:341
  21.8 25.3 %collective-permute-start.3 = (bf16[1152,256]{1,0:T(8,128)(2,1)S(1)}, bf16[1152,256]{1,0:T(8,128)(2,1)S(1)}, u32[]{:S(2)}, u32[]{:S(2)}) collective-permute-start(bf16[1152,256]{1,0:T(8,128)(2,1)S(1)} %collective-permute-done.2.refs_4_.refs_3_), channel_id=1, source_target_pairs={{0,4},{1,5},{4,8},{5,9},{8,12},{9,13},{12,14},{13,15},{14,10},{15,... | collective-permute-start | bytes 1769480 | tf_op jit(solution)/shard_map/ppermute | solution.py:341
  32.3 25.3 %collective-permute-start.11 = (bf16[1152,256]{1,0:T(8,128)(2,1)S(1)}, bf16[1152,256]{1,0:T(8,128)(2,1)S(1)}, u32[]{:S(2)}, u32[]{:S(2)}) collective-permute-start(bf16[1152,256]{1,0:T(8,128)(2,1)S(1)} %collective-permute-done.7.refs_3_.refs_4_), channel_id=1, source_target_pairs={{0,2},{1,3},{4,0},{5,1},{8,4},{9,5},{12,8},{13,9},{14,12},{15,13},... | collective-permute-start | bytes 1769480 | tf_op jit(solution)/shard_map/ppermute | solution.py:341
  34.5 25.2 %collective-permute-start.10 = (bf16[1152,256]{1,0:T(8,128)(2,1)}, bf16[1152,256]{1,0:T(8,128)(2,1)S(1)}, u32[]{:S(2)}, u32[]{:S(2)}) collective-permute-start(bf16[1152,256]{1,0:T(8,128)(2,1)} %collective-permute-done.6.refs_2_), channel_id=1, source_target_pairs={{0,4},{1,5},{4,8},{5,9},{8,12},{9,13},{12,14},{13,15},{14,10},{15,... | collective-permute-start | bytes 1769480 | tf_op jit(solution)/shard_map/ppermute | solution.py:341
  44.9 25.3 %collective-permute-start.9 = (bf16[1152,256]{1,0:T(8,128)(2,1)S(1)}, bf16[1152,256]{1,0:T(8,128)(2,1)S(1)}, u32[]{:S(2)}, u32[]{:S(2)}) collective-permute-start(bf16[1152,256]{1,0:T(8,128)(2,1)S(1)} %collective-permute-done.5.refs_3_), channel_id=1, source_target_pairs={{0,2},{1,3},{4,0},{5,1},{8,4},{9,5},{12,8},{13,9},{14,12},{15,13},... | collective-permute-start | bytes 1769480 | tf_op jit(solution)/shard_map/ppermute | solution.py:341
  47.1 25.3 %collective-permute-start.8 = (bf16[1152,256]{1,0:T(8,128)(2,1)S(1)}, bf16[1152,256]{1,0:T(8,128)(2,1)S(1)}, u32[]{:S(2)}, u32[]{:S(2)}) collective-permute-start(bf16[1152,256]{1,0:T(8,128)(2,1)S(1)} %collective-permute-done.3.refs_2_.refs_5_), channel_id=1, source_target_pairs={{0,4},{1,5},{4,8},{5,9},{8,12},{9,13},{12,14},{13,15},{14,10},{15,... | collective-permute-start | bytes 1769480 | tf_op jit(solution)/shard_map/ppermute | solution.py:341
  57.6 16.8 %copy-start.3 = (s32[128]{0:T(128)S(1)}, s32[128]{0:T(128)}, u32[]{:S(2)}) copy-start(s32[128]{0:T(128)} %param.8) | copy-start | bytes 1540
  59.7 23.2 %collective-permute-start.14 = (bf16[1152,256]{1,0:T(8,128)(2,1)S(1)}, bf16[1152,256]{1,0:T(8,128)(2,1)S(1)}, u32[]{:S(2)}, u32[]{:S(2)}) collective-permute-start(bf16[1152,256]{1,0:T(8,128)(2,1)S(1)} %collective-permute-done.11.refs_3_.refs_6_), channel_id=1, source_target_pairs={{0,2},{1,3},{4,0},{5,1},{8,4},{9,5},{12,8},{13,9},{14,12},{15,13},... | collective-permute-start | bytes 1769480 | tf_op jit(solution)/shard_map/ppermute | solution.py:341
  61.3 24.7 %collective-permute-start.15 = (bf16[1152,256]{1,0:T(8,128)(2,1)S(1)}, bf16[1152,256]{1,0:T(8,128)(2,1)S(1)}, u32[]{:S(2)}, u32[]{:S(2)}) collective-permute-start(bf16[1152,256]{1,0:T(8,128)(2,1)S(1)} %collective-permute-done.10.refs_2_), channel_id=1, source_target_pairs={{0,4},{1,5},{4,8},{5,9},{8,12},{9,13},{12,14},{13,15},{14,10},{15,... | collective-permute-start | bytes 1769480 | tf_op jit(solution)/shard_map/ppermute | solution.py:341
  72.3 24.1 %collective-permute-start.12 = (bf16[1152,256]{1,0:T(8,128)(2,1)S(1)}, bf16[1152,256]{1,0:T(8,128)(2,1)S(1)}, u32[]{:S(2)}, u32[]{:S(2)}) collective-permute-start(bf16[1152,256]{1,0:T(8,128)(2,1)S(1)} %collective-permute-done.8.refs_2_.refs_7_), channel_id=1, source_target_pairs={{0,4},{1,5},{4,8},{5,9},{8,12},{9,13},{12,14},{13,15},{14,10},{15,... | collective-permute-start | bytes 1769480 | tf_op jit(solution)/shard_map/ppermute | solution.py:341
  72.4 24.1 %collective-permute-start.13 = (bf16[1152,256]{1,0:T(8,128)(2,1)S(1)}, bf16[1152,256]{1,0:T(8,128)(2,1)S(1)}, u32[]{:S(2)}, u32[]{:S(2)}) collective-permute-start(bf16[1152,256]{1,0:T(8,128)(2,1)S(1)} %collective-permute-done.9.refs_3_), channel_id=1, source_target_pairs={{0,2},{1,3},{4,0},{5,1},{8,4},{9,5},{12,8},{13,9},{14,12},{15,13},... | collective-permute-start | bytes 1769480 | tf_op jit(solution)/shard_map/ppermute | solution.py:341
  96.8 1.6 %collective-permute-start.16 = (f32[128,512]{1,0:T(8,128)S(1)}, f32[128,512]{1,0:T(8,128)S(1)}, u32[]{:S(2)}, u32[]{:S(2)}) collective-permute-start(f32[128,512]{1,0:T(8,128)S(1)} %shard_map.85), channel_id=1, source_target_pairs={{0,1},{1,0},{2,3},{3,2},{4,5},{5,4},{6,7},{7,6},{8,9},{9,8},{10,11... | collective-permute-start | bytes 786440 | tf_op jit(solution)/shard_map/ppermute | solution.py:341
  98.5 5.9 %collective-permute-start.20 = (bf16[144,512]{1,0:T(8,128)(2,1)S(1)}, bf16[144,512]{1,0:T(8,128)(2,1)S(1)}, u32[]{:S(2)}, u32[]{:S(2)}) collective-permute-start(bf16[144,512]{1,0:T(8,128)(2,1)S(1)} %pad_maximum_fusion), channel_id=1, source_target_pairs={{0,2},{1,3},{4,0},{5,1},{8,4},{9,5},{12,8},{13,9},{14,12},{15,13},... | collective-permute-start | bytes 442376 | tf_op jit(solution)/shard_map/ppermute | solution.py:341
  100.1 5.9 %collective-permute-start.17 = (bf16[144,512]{1,0:T(8,128)(2,1)S(1)}, bf16[144,512]{1,0:T(8,128)(2,1)S(1)}, u32[]{:S(2)}, u32[]{:S(2)}) collective-permute-start(bf16[144,512]{1,0:T(8,128)(2,1)S(1)} %pad_maximum_fusion), channel_id=1, source_target_pairs={{0,4},{1,5},{4,8},{5,9},{8,12},{9,13},{12,14},{13,15},{14,10},{15,... | collective-permute-start | bytes 442376 | tf_op jit(solution)/shard_map/ppermute | solution.py:341
  104.4 5.1 %collective-permute-start.21 = (bf16[144,512]{1,0:T(8,128)(2,1)S(1)}, bf16[144,512]{1,0:T(8,128)(2,1)S(1)}, u32[]{:S(2)}, u32[]{:S(2)}) collective-permute-start(bf16[144,512]{1,0:T(8,128)(2,1)S(1)} %collective-permute-done.20), channel_id=1, source_target_pairs={{0,2},{1,3},{4,0},{5,1},{8,4},{9,5},{12,8},{13,9},{14,12},{15,13},... | collective-permute-start | bytes 442376 | tf_op jit(solution)/shard_map/ppermute | solution.py:341
  106.0 6.2 %collective-permute-start.18 = (bf16[144,512]{1,0:T(8,128)(2,1)S(1)}, bf16[144,512]{1,0:T(8,128)(2,1)S(1)}, u32[]{:S(2)}, u32[]{:S(2)}) collective-permute-start(bf16[144,512]{1,0:T(8,128)(2,1)S(1)} %collective-permute-done.17), channel_id=1, source_target_pairs={{0,4},{1,5},{4,8},{5,9},{8,12},{9,13},{12,14},{13,15},{14,10},{15,... | collective-permute-start | bytes 442376 | tf_op jit(solution)/shard_map/ppermute | solution.py:341
  109.6 7.9 %collective-permute-start.24 = (bf16[80,512]{1,0:T(8,128)(2,1)S(1)}, bf16[80,512]{1,0:T(8,128)(2,1)S(1)}, u32[]{:S(2)}, u32[]{:S(2)}) collective-permute-start(bf16[80,512]{1,0:T(8,128)(2,1)S(1)} %slice.14), channel_id=1, source_target_pairs={{0,6},{1,7},{4,2},{5,3},{8,0},{9,1},{12,4},{13,5},{14,8},{15,9},{1... | collective-permute-start | bytes 245768 | tf_op jit(solution)/shard_map/ppermute | solution.py:341
  112.2 5.3 %collective-permute-start.23 = (bf16[64,512]{1,0:T(8,128)(2,1)S(1)}, bf16[64,512]{1,0:T(8,128)(2,1)S(1)}, u32[]{:S(2)}, u32[]{:S(2)}) collective-permute-start(bf16[64,512]{1,0:T(8,128)(2,1)S(1)} %slice.13), channel_id=1, source_target_pairs={{0,8},{1,9},{4,12},{5,13},{8,14},{9,15},{12,10},{13,11},{14,6},{15... | collective-permute-start | bytes 196616 | tf_op jit(solution)/shard_map/ppermute | solution.py:341
  112.6 5.8 %collective-permute-start.19 = (bf16[144,512]{1,0:T(8,128)(2,1)S(1)}, bf16[144,512]{1,0:T(8,128)(2,1)S(1)}, u32[]{:S(2)}, u32[]{:S(2)}) collective-permute-start(bf16[144,512]{1,0:T(8,128)(2,1)S(1)} %collective-permute-done.18), channel_id=1, source_target_pairs={{0,4},{1,5},{4,8},{5,9},{8,12},{9,13},{12,14},{13,15},{14,10},{15,... | collective-permute-start | bytes 442376 | tf_op jit(solution)/shard_map/ppermute | solution.py:341
  113.1 5.3 %collective-permute-start.22 = (bf16[144,512]{1,0:T(8,128)(2,1)S(1)}, bf16[144,512]{1,0:T(8,128)(2,1)S(1)}, u32[]{:S(2)}, u32[]{:S(2)}) collective-permute-start(bf16[144,512]{1,0:T(8,128)(2,1)S(1)} %collective-permute-done.21), channel_id=1, source_target_pairs={{0,2},{1,3},{4,0},{5,1},{8,4},{9,5},{12,8},{13,9},{14,12},{15,13},... | collective-permute-start | bytes 442376 | tf_op jit(solution)/shard_map/ppermute | solution.py:341
  114.6 3.9 %collective-permute-start.26 = (bf16[720,512]{1,0:T(8,128)(2,1)S(1)}, bf16[720,512]{1,0:T(8,128)(2,1)S(1)}, u32[]{:S(2)}, u32[]{:S(2)}) collective-permute-start(bf16[720,512]{1,0:T(8,128)(2,1)S(1)} %constant_dynamic-update-slice_fusion.4.refs_0_), channel_id=1, source_target_pairs={{0,1},{1,0},{2,3},{3,2},{4,5},{5,4},{6,7},{7,6},{8,9},{9,8},{10,11... | collective-permute-start | bytes 2211848 | tf_op jit(solution)/shard_map/ppermute | solution.py:341
  118.5 1.9 %collective-permute-start.25 = (bf16[432,512]{1,0:T(8,128)(2,1)S(1)}, bf16[432,512]{1,0:T(8,128)(2,1)S(1)}, u32[]{:S(2)}, u32[]{:S(2)}) collective-permute-start(bf16[432,512]{1,0:T(8,128)(2,1)S(1)} %constant_dynamic-update-slice_fusion.first_ref), channel_id=1, source_target_pairs={{0,1},{1,0},{2,3},{3,2},{4,5},{5,4},{6,7},{7,6},{8,9},{9,8},{10,11... | collective-permute-start | bytes 1327112 | tf_op jit(solution)/shard_map/ppermute | solution.py:341

commit v8 on v7

--- a/solution.py
+++ b/solution.py
@@ -272,13 +272,13 @@
     )(me, *pieces)
 
 
-def last_kernel(rows, scale, me_ref, first_ref, second_ref, total_ref, act_ref, grad_ref, *refs):
+def last_kernel(rows, scale, me_ref, piece_ref, total_ref, act_ref, grad_ref, *refs):
     corrected_ref, score_ref, squares, held = refs
     me = me_ref[0]
     panel_rows, in_panel = corrected_ref.shape
     out_panel = total_ref.shape[0]
     total, own_act, own_grad = add_up(
-        me, (first_ref, second_ref), squares, rows, in_panel, act_ref.shape[0]
+        me, (piece_ref,), squares, rows, in_panel, act_ref.shape[0]
     )
     corrected = (total + total_ref[...]) * scale
     held[...] = corrected
@@ -305,7 +305,7 @@
             jax.ShapeDtypeStruct((out_panel // devices, in_panel), jnp.float32),
             jax.ShapeDtypeStruct((1, balanced), jnp.float32),
         ),
-        in_specs=[pl.BlockSpec(memory_space=pltpu.SMEM)] + [vmem] * 5,
+        in_specs=[pl.BlockSpec(memory_space=pltpu.SMEM)] + [vmem] * (len(pieces) + 3),
         out_specs=(vmem, vmem),
         scratch_shapes=[
             pltpu.VMEM((tokens, out_panel + in_panel), jnp.bfloat16),
@@ -389,11 +389,11 @@
             hop(first, second, s + 1)
         else:
             first[half], second[half] = send(first[s], forward), send(second[-s], backward)
-        grad = add((1,), own + pieces(first, [s]) + pieces(second, [-s]), grad)
+        grad = add((1,), own + pieces(second, [-s]) + pieces(first, [s]), grad)
         grad = after(second, [s], after(first, [-s], grad))
         if s + 1 < half:
             hop(second, first, s + 1)
-        grad = add((1,), pieces(second, [s]) + pieces(first, [-s]), grad)
+        grad = add((1,), pieces(first, [-s]) + pieces(second, [s]), grad)
         if s + 1 < half:
             grad = after(first, [s + 1], after(second, [-s - 1], grad))
     act = add((0,), pieces(first, distances[:-1]), [zero, zero])
@@ -427,9 +427,9 @@
     own = [near, far]
     swapped = [send(x, swap) for x in own]
     me = own_index[None]
-    near_both = lax.optimization_barrier((near, swapped[0], far))[:2]
-    sums = some_sums(me, list(near_both), rows, width, balanced)
-    return last(me, [far, swapped[1]], sums, rows, devices)
+    gathered_rows = lax.optimization_barrier((near, swapped[0], far))
+    sums = some_sums(me, list(gathered_rows), rows, width, balanced)
+    return last(me, [swapped[1]], sums, rows, devices)
 
 
 def body(*arrays):

time: 122 us -> 122 us (level)
  transfers between devices with their start and end apart: 27 -> 27, of which waited for: 18 -> 18; matrix products, arithmetic and copies ran while one was open for 1% -> 1% of each run, Pallas kernels for 17% -> 18%
where the time goes in v8:
time: 122 us; the launch traced here: 121 us
  waiting for transfers between devices  69.8 us (57%)
  starting transfers between devices  26.5 us (22%)
  Pallas kernels  22.7 us (19%)
  local copies, waits for them, and re-layouts  1.38 us (1%)
    ppermute x27, waiting for transfers between devices, send(): return lax.ppermute(x, 'dp', pairs)  69.8 us
    ppermute x27, starting transfers between devices, send(): return lax.ppermute(x, 'dp', pairs)  26.5 us
    pallas_call x7, Pallas kernels, project(): pl.pallas_call(functools.partial(project_kernel, kinds, [p[:2] for p in p...  18.4 us
  transfers between devices with their start and end apart: 27, of which 18 were waited for; matrix products, arithmetic and copies ran while one was open for 1% of the time, Pallas kernels for 18%

profile of v8, /device:TPU:0, one launch (start us, length us, event | category | flops | bytes accessed | tf_op | source)
XLA Modules:
  0.0 121.4 jit_solution(8756155000760323017)
XLA Ops:
  0.7 0.5 collective-permute-start.1
  1.3 1.2 %fusion.7 = (bf16[1152,256]{1,0:T(8,128)(2,1)S(1)}, bf16[1152,256]{1,0:T(8,128)(2,1)S(1)}) fusion(bf16[1792,256]{1,0:T(8,128)(2,1)} %param.10), kind=kLoop, calls=%fused_computation.34 | loop fusion | bytes 2686976 | tf_op jit(solution)/shard_map/slice | solution.py:357
  2.5 3.0 %collective-permute-start.4 = (bf16[1152,256]{1,0:T(8,128)(2,1)S(1)}, bf16[1152,256]{1,0:T(8,128)(2,1)}, u32[]{:S(2)}, u32[]{:S(2)}) collective-permute-start(bf16[1152,256]{1,0:T(8,128)(2,1)S(1)} %get-tuple-element.128.refs_3_), channel_id=1, source_target_pairs={{0,2},{1,3},{4,0},{5,1},{8,4},{9,5},{12,8},{13,9},{14,12},{15,13},... | collective-permute-start | bytes 1769480 | tf_op jit(solution)/shard_map/ppermute | solution.py:341
  5.5 0.1 collective-permute-start.2
  5.6 7.0 %collective-permute-done.refs_2_.refs_1_ = bf16[128,8192]{1,0:T(8,128)(2,1)S(1)} collective-permute-done((bf16[128,8192]{1,0:T(8,128)(2,1)}, bf16[128,8192]{1,0:T(8,128)(2,1)S(1)}, u32[]{:S(2)}, u32[]{:S(2)}) %collective-permute-start) | collective-permute-done | bytes 2097184 | tf_op jit(solution)/shard_map/ppermute | solution.py:341
  12.6 3.1 %collective-permute-start.6 = (bf16[1152,256]{1,0:T(8,128)(2,1)S(1)}, bf16[1152,256]{1,0:T(8,128)(2,1)S(1)}, u32[]{:S(2)}, u32[]{:S(2)}) collective-permute-start(bf16[1152,256]{1,0:T(8,128)(2,1)S(1)} %constant_dynamic-update-slice_fusion.10.refs_2_), channel_id=1, source_target_pairs={{0,2},{1,3},{4,0},{5,1},{8,4},{9,5},{12,8},{13,9},{14,12},{15,13},... | collective-permute-start | bytes 1769480 | tf_op jit(solution)/shard_map/ppermute | solution.py:341
  15.8 4.0 %collective-permute-done.4.refs_4_ = bf16[1152,256]{1,0:T(8,128)(2,1)} collective-permute-done((bf16[1152,256]{1,0:T(8,128)(2,1)S(1)}, bf16[1152,256]{1,0:T(8,128)(2,1)}, u32[]{:S(2)}, u32[]{:S(2)}) %collective-permute-start.4) | collective-permute-done | bytes 589856 | tf_op jit(solution)/shard_map/ppermute | solution.py:341
  19.8 2.0 %collective-permute-start.5 = (bf16[1152,256]{1,0:T(8,128)(2,1)}, bf16[1152,256]{1,0:T(8,128)(2,1)S(1)}, u32[]{:S(2)}, u32[]{:S(2)}) collective-permute-start(bf16[1152,256]{1,0:T(8,128)(2,1)} %collective-permute-done.4.refs_4_), channel_id=1, source_target_pairs={{0,2},{1,3},{4,0},{5,1},{8,4},{9,5},{12,8},{13,9},{14,12},{15,13},... | collective-permute-start | bytes 1769480 | tf_op jit(solution)/shard_map/ppermute | solution.py:341
  21.9 3.7 %shard_map.78 = (f32[128,256]{1,0:T(8,128)S(1)}, f32[128,256]{1,0:T(8,128)S(1)}) custom-call(s32[8]{0:T(128)S(1)} %fusion.6.owners_ref, bf16[128,28672]{1,0:T(8,128)(2,1)} %refs_0_.15, bf16[128,28672]{1,0:T(8,128)(2,1)} %collective-permute-done.1.refs_3_.refs_1_, bf16[1152,256]{1,0:T(8,128)(2,1)S(1)} %constant_dynamic-update-slice_fusion.10.refs_2_, ...), custom_call_target="tpu_custom_call" | custom-call | flops 1 | bytes 1 | tf_op jit(solution)/shard_map/pallas_call | solution.py:116
  25.6 6.7 %collective-permute-done.6.refs_2_.refs_4_ = bf16[1152,256]{1,0:T(8,128)(2,1)S(1)} collective-permute-done((bf16[1152,256]{1,0:T(8,128)(2,1)S(1)}, bf16[1152,256]{1,0:T(8,128)(2,1)S(1)}, u32[]{:S(2)}, u32[]{:S(2)}) %collective-permute-start.6) | collective-permute-done | bytes 589856 | tf_op jit(solution)/shard_map/ppermute | solution.py:341
  32.3 2.0 %collective-permute-start.10 = (bf16[1152,256]{1,0:T(8,128)(2,1)S(1)}, bf16[1152,256]{1,0:T(8,128)(2,1)S(1)}, u32[]{:S(2)}, u32[]{:S(2)}) collective-permute-start(bf16[1152,256]{1,0:T(8,128)(2,1)S(1)} %collective-permute-done.6.refs_2_.refs_4_), channel_id=1, source_target_pairs={{0,2},{1,3},{4,0},{5,1},{8,4},{9,5},{12,8},{13,9},{14,12},{15,13},... | collective-permute-start | bytes 1769480 | tf_op jit(solution)/shard_map/ppermute | solution.py:341
  34.3 0.2 collective-permute-done.7.refs_3_
  34.6 2.8 %shard_map.79 = (f32[128,256]{1,0:T(8,128)S(1)}, f32[128,256]{1,0:T(8,128)S(1)}) custom-call(s32[8]{0:T(128)S(1)} %fusion.6.owners_ref, bf16[128,28672]{1,0:T(8,128)(2,1)} %refs_0_.15, bf16[128,28672]{1,0:T(8,128)(2,1)} %collective-permute-done.1.refs_3_.refs_1_, bf16[1152,256]{1,0:T(8,128)(2,1)S(1)} %collective-permute-done.6.refs_2_.refs_4_, ...), custom_call_target="tpu_custom_call" | custom-call | flops 1 | bytes 1 | tf_op jit(solution)/shard_map/pallas_call | solution.py:116
  37.4 7.6 %collective-permute-done.5.refs_2_ = bf16[1152,256]{1,0:T(8,128)(2,1)S(1)} collective-permute-done((bf16[1152,256]{1,0:T(8,128)(2,1)}, bf16[1152,256]{1,0:T(8,128)(2,1)S(1)}, u32[]{:S(2)}, u32[]{:S(2)}) %collective-permute-start.5) | collective-permute-done | bytes 589856 | tf_op jit(solution)/shard_map/ppermute | solution.py:341
  44.9 2.0 %collective-permute-start.9 = (bf16[1152,256]{1,0:T(8,128)(2,1)S(1)}, bf16[1152,256]{1,0:T(8,128)(2,1)S(1)}, u32[]{:S(2)}, u32[]{:S(2)}) collective-permute-start(bf16[1152,256]{1,0:T(8,128)(2,1)S(1)} %collective-permute-done.5.refs_2_), channel_id=1, source_target_pairs={{0,2},{1,3},{4,0},{5,1},{8,4},{9,5},{12,8},{13,9},{14,12},{15,13},... | collective-permute-start | bytes 1769480 | tf_op jit(solution)/shard_map/ppermute | solution.py:341
  47.1 2.2 %shard_map.80 = (f32[128,256]{1,0:T(8,128)S(1)}, f32[128,256]{1,0:T(8,128)S(1)}) custom-call(s32[8]{0:T(128)S(1)} %fusion.6.owners_ref, bf16[128,28672]{1,0:T(8,128)(2,1)} %refs_0_.15, bf16[128,28672]{1,0:T(8,128)(2,1)} %collective-permute-done.1.refs_3_.refs_1_, bf16[1152,256]{1,0:T(8,128)(2,1)S(1)} %collective-permute-done.5.refs_2_, ...), custom_call_target="tpu_custom_call" | custom-call | flops 1 | bytes 1 | tf_op jit(solution)/shard_map/pallas_call | solution.py:116
  49.3 8.3 %collective-permute-done.10.refs_2_.refs_6_ = bf16[1152,256]{1,0:T(8,128)(2,1)S(1)} collective-permute-done((bf16[1152,256]{1,0:T(8,128)(2,1)S(1)}, bf16[1152,256]{1,0:T(8,128)(2,1)S(1)}, u32[]{:S(2)}, u32[]{:S(2)}) %collective-permute-start.10) | collective-permute-done | bytes 589856 | tf_op jit(solution)/shard_map/ppermute | solution.py:341
  57.6 2.1 %collective-permute-done.11.refs_3_ = bf16[1152,256]{1,0:T(8,128)(2,1)S(1)} collective-permute-done((bf16[1152,256]{1,0:T(8,128)(2,1)}, bf16[1152,256]{1,0:T(8,128)(2,1)S(1)}, u32[]{:S(2)}, u32[]{:S(2)}) %collective-permute-start.11) | collective-permute-done | bytes 589856 | tf_op jit(solution)/shard_map/ppermute | solution.py:341
  59.7 1.6 %collective-permute-start.14 = (bf16[1152,256]{1,0:T(8,128)(2,1)S(1)}, bf16[1152,256]{1,0:T(8,128)(2,1)S(1)}, u32[]{:S(2)}, u32[]{:S(2)}) collective-permute-start(bf16[1152,256]{1,0:T(8,128)(2,1)S(1)} %collective-permute-done.10.refs_2_.refs_6_), channel_id=1, source_target_pairs={{0,2},{1,3},{4,0},{5,1},{8,4},{9,5},{12,8},{13,9},{14,12},{15,13},... | collective-permute-start | bytes 1769480 | tf_op jit(solution)/shard_map/ppermute | solution.py:341
  61.3 0.4 collective-permute-start.15
  61.7 2.2 %shard_map.81 = (f32[128,256]{1,0:T(8,128)S(1)}, f32[128,256]{1,0:T(8,128)S(1)}) custom-call(s32[8]{0:T(128)S(1)} %fusion.6.owners_ref, bf16[128,28672]{1,0:T(8,128)(2,1)} %refs_0_.15, bf16[128,28672]{1,0:T(8,128)(2,1)} %collective-permute-done.1.refs_3_.refs_1_, bf16[1152,256]{1,0:T(8,128)(2,1)S(1)} %collective-permute-done.10.refs_2_.refs_6_, ...), custom_call_target="tpu_custom_call" | custom-call | flops 1 | bytes 1 | tf_op jit(solution)/shard_map/pallas_call | solution.py:116
  64.0 6.3 %collective-permute-done.9.refs_2_ = bf16[1152,256]{1,0:T(8,128)(2,1)S(1)} collective-permute-done((bf16[1152,256]{1,0:T(8,128)(2,1)S(1)}, bf16[1152,256]{1,0:T(8,128)(2,1)S(1)}, u32[]{:S(2)}, u32[]{:S(2)}) %collective-permute-start.9) | collective-permute-done | bytes 589856 | tf_op jit(solution)/shard_map/ppermute | solution.py:341
  70.2 2.1 %collective-permute-done.8.refs_3_.refs_7_ = bf16[1152,256]{1,0:T(8,128)(2,1)S(1)} collective-permute-done((bf16[1152,256]{1,0:T(8,128)(2,1)S(1)}, bf16[1152,256]{1,0:T(8,128)(2,1)S(1)}, u32[]{:S(2)}, u32[]{:S(2)}) %collective-permute-start.8) | collective-permute-done | bytes 589856 | tf_op jit(solution)/shard_map/ppermute | solution.py:341
  72.4 2.0 %collective-permute-start.13 = (bf16[1152,256]{1,0:T(8,128)(2,1)S(1)}, bf16[1152,256]{1,0:T(8,128)(2,1)S(1)}, u32[]{:S(2)}, u32[]{:S(2)}) collective-permute-start(bf16[1152,256]{1,0:T(8,128)(2,1)S(1)} %collective-permute-done.9.refs_2_), channel_id=1, source_target_pairs={{0,2},{1,3},{4,0},{5,1},{8,4},{9,5},{12,8},{13,9},{14,12},{15,13},... | collective-permute-start | bytes 1769480 | tf_op jit(solution)/shard_map/ppermute | solution.py:341
  74.4 1.9 %shard_map.77 = (bf16[128,2304]{1,0:T(8,128)(2,1)S(1)}, bf16[128,2304]{1,0:T(8,128)(2,1)S(1)}) custom-call(s32[8]{0:T(128)S(1)} %fusion.6.owners_ref, bf16[128,8192]{1,0:T(8,128)(2,1)} %refs_0_.14, bf16[128,28672]{1,0:T(8,128)(2,1)} %refs_0_.15, bf16[128,8192]{1,0:T(8,128)(2,1)} %copy-done, bf16[128,28672]{1,0:T(8,128)(2,1)} %collective-permute-done.1.refs_3_.refs_1_), custom_call_target="tpu_custom_call" | custom-call | flops 1 | bytes 1 | tf_op jit(solution)/shard_map/pallas_call | solution.py:194
  76.3 2.2 %shard_map.82 = (f32[128,256]{1,0:T(8,128)S(1)}, f32[128,256]{1,0:T(8,128)S(1)}) custom-call(s32[8]{0:T(128)S(1)} %fusion.6.owners_ref, bf16[128,28672]{1,0:T(8,128)(2,1)} %refs_0_.15, bf16[128,28672]{1,0:T(8,128)(2,1)} %collective-permute-done.1.refs_3_.refs_1_, bf16[1152,256]{1,0:T(8,128)(2,1)S(1)} %collective-permute-done.9.refs_2_, ...), custom_call_target="tpu_custom_call" | custom-call | flops 1 | bytes 1 | tf_op jit(solution)/shard_map/pallas_call | solution.py:116
  78.4 4.4 %collective-permute-done.14.refs_8_.refs_2_ = bf16[1152,256]{1,0:T(8,128)(2,1)S(1)} collective-permute-done((bf16[1152,256]{1,0:T(8,128)(2,1)S(1)}, bf16[1152,256]{1,0:T(8,128)(2,1)S(1)}, u32[]{:S(2)}, u32[]{:S(2)}) %collective-permute-start.14) | collective-permute-done | bytes 589856 | tf_op jit(solution)/shard_map/ppermute | solution.py:341
  82.9 3.1 %shard_map.83 = (f32[128,256]{1,0:T(8,128)S(1)}, f32[128,256]{1,0:T(8,128)S(1)}) custom-call(s32[8]{0:T(128)S(1)} %fusion.6.owners_ref, bf16[128,8192]{1,0:T(8,128)(2,1)} %refs_0_.14, bf16[128,8192]{1,0:T(8,128)(2,1)} %copy-done, bf16[1152,256]{1,0:T(8,128)(2,1)S(1)} %constant_dynamic-update-slice_fusion.10.refs_2_, ...), custom_call_target="tpu_custom_call" | custom-call | flops 1 | bytes 1 | tf_op jit(solution)/shard_map/pallas_call | solution.py:116
  86.0 2.2 %shard_map.84 = (f32[128,256]{1,0:T(8,128)S(1)}, f32[128,256]{1,0:T(8,128)S(1)}) custom-call(s32[8]{0:T(128)S(1)} %fusion.6.owners_ref, bf16[128,28672]{1,0:T(8,128)(2,1)} %refs_0_.15, bf16[128,28672]{1,0:T(8,128)(2,1)} %collective-permute-done.1.refs_3_.refs_1_, bf16[1152,256]{1,0:T(8,128)(2,1)S(1)} %collective-permute-done.14.refs_8_.refs_2_, ...), custom_call_target="tpu_custom_call" | custom-call | flops 1 | bytes 1 | tf_op jit(solution)/shard_map/pallas_call | solution.py:116
  88.2 8.2 %collective-permute-done.12.first_ref = bf16[1152,256]{1,0:T(8,128)(2,1)S(1)} collective-permute-done((bf16[1152,256]{1,0:T(8,128)(2,1)S(1)}, bf16[1152,256]{1,0:T(8,128)(2,1)S(1)}, u32[]{:S(2)}, u32[]{:S(2)}) %collective-permute-start.12) | collective-permute-done | bytes 589856 | tf_op jit(solution)/shard_map/ppermute | solution.py:341
  96.4 0.3 shard_map.85
  96.9 0.3 shard_map.86
  97.2 1.2 collective-permute-done.16
  98.5 1.6 %collective-permute-start.20 = (bf16[144,512]{1,0:T(8,128)(2,1)S(1)}, bf16[144,512]{1,0:T(8,128)(2,1)S(1)}, u32[]{:S(2)}, u32[]{:S(2)}) collective-permute-start(bf16[144,512]{1,0:T(8,128)(2,1)S(1)} %pad_maximum_fusion), channel_id=1, source_target_pairs={{0,2},{1,3},{4,0},{5,1},{8,4},{9,5},{12,8},{13,9},{14,12},{15,13},... | collective-permute-start | bytes 442376 | tf_op jit(solution)/shard_map/ppermute | solution.py:341
  100.1 0.5 collective-permute-start.17
  100.6 3.9 %collective-permute-done.20 = bf16[144,512]{1,0:T(8,128)(2,1)S(1)} collective-permute-done((bf16[144,512]{1,0:T(8,128)(2,1)S(1)}, bf16[144,512]{1,0:T(8,128)(2,1)S(1)}, u32[]{:S(2)}, u32[]{:S(2)}) %collective-permute-start.20) | collective-permute-done | bytes 147488 | tf_op jit(solution)/shard_map/ppermute | solution.py:341
  104.4 1.6 %collective-permute-start.21 = (bf16[144,512]{1,0:T(8,128)(2,1)S(1)}, bf16[144,512]{1,0:T(8,128)(2,1)S(1)}, u32[]{:S(2)}, u32[]{:S(2)}) collective-permute-start(bf16[144,512]{1,0:T(8,128)(2,1)S(1)} %collective-permute-done.20), channel_id=1, source_target_pairs={{0,2},{1,3},{4,0},{5,1},{8,4},{9,5},{12,8},{13,9},{14,12},{15,13},... | collective-permute-start | bytes 442376 | tf_op jit(solution)/shard_map/ppermute | solution.py:341
  106.0 0.5 collective-permute-start.18
  106.5 3.1 %collective-permute-done.21 = bf16[144,512]{1,0:T(8,128)(2,1)S(1)} collective-permute-done((bf16[144,512]{1,0:T(8,128)(2,1)S(1)}, bf16[144,512]{1,0:T(8,128)(2,1)S(1)}, u32[]{:S(2)}, u32[]{:S(2)}) %collective-permute-start.21) | collective-permute-done | bytes 147488 | tf_op jit(solution)/shard_map/ppermute | solution.py:341
  109.6 2.6 %collective-permute-start.24 = (bf16[80,512]{1,0:T(8,128)(2,1)S(1)}, bf16[80,512]{1,0:T(8,128)(2,1)S(1)}, u32[]{:S(2)}, u32[]{:S(2)}) collective-permute-start(bf16[80,512]{1,0:T(8,128)(2,1)S(1)} %slice.14), channel_id=1, source_target_pairs={{0,6},{1,7},{4,2},{5,3},{8,0},{9,1},{12,4},{13,5},{14,8},{15,9},{1... | collective-permute-start | bytes 245768 | tf_op jit(solution)/shard_map/ppermute | solution.py:341
  112.2 0.4 collective-permute-start.23
  112.6 0.6 collective-permute-start.19
  113.1 1.5 %collective-permute-start.22 = (bf16[144,512]{1,0:T(8,128)(2,1)S(1)}, bf16[144,512]{1,0:T(8,128)(2,1)S(1)}, u32[]{:S(2)}, u32[]{:S(2)}) collective-permute-start(bf16[144,512]{1,0:T(8,128)(2,1)S(1)} %collective-permute-done.21), channel_id=1, source_target_pairs={{0,2},{1,3},{4,0},{5,1},{8,4},{9,5},{12,8},{13,9},{14,12},{15,13},... | collective-permute-start | bytes 442376 | tf_op jit(solution)/shard_map/ppermute | solution.py:341
  114.7 2.8 %collective-permute-done.23 = bf16[64,512]{1,0:T(8,128)(2,1)S(1)} collective-permute-done((bf16[64,512]{1,0:T(8,128)(2,1)S(1)}, bf16[64,512]{1,0:T(8,128)(2,1)S(1)}, u32[]{:S(2)}, u32[]{:S(2)}) %collective-permute-start.23) | collective-permute-done | bytes 65568 | tf_op jit(solution)/shard_map/ppermute | solution.py:341
  117.5 0.9 collective-permute-done.19
  118.6 0.8 shard_map.87
  119.4 1.0 collective-permute-done.25.piece_ref
  120.4 1.1 shard_map.88
  (48 shorter events, 1.1 us)
Async XLA Ops:
  0.6 21.3 %copy-start.2 = (s32[8]{0:T(128)S(1)}, s32[8]{0:T(128)}, u32[]{:S(2)}) copy-start(s32[8]{0:T(128)} %constant.104) | copy-start | bytes 100
  0.6 4.8 %copy-start.1 = (bf16[512,256]{1,0:T(8,128)(2,1)S(1)}, bf16[512,256]{1,0:T(8,128)(2,1)}, u32[]{:S(2)}) copy-start(bf16[512,256]{1,0:T(8,128)(2,1)} %param.9) | copy-start | bytes 786436
  0.7 21.3 %collective-permute-start.1 = (bf16[128,28672]{1,0:T(8,128)(2,1)}, bf16[128,28672]{1,0:T(8,128)(2,1)}, u32[]{:S(2)}, u32[]{:S(2)}) collective-permute-start(bf16[128,28672]{1,0:T(8,128)(2,1)} %refs_0_.15), channel_id=1, source_target_pairs={{0,1},{1,0},{2,3},{3,2},{4,5},{5,4},{6,7},{7,6},{8,9},{9,8},{10,11... | collective-permute-start | bytes 22020104 | tf_op jit(solution)/shard_map/ppermute | solution.py:341
  1.2 11.4 %collective-permute-start = (bf16[128,8192]{1,0:T(8,128)(2,1)}, bf16[128,8192]{1,0:T(8,128)(2,1)S(1)}, u32[]{:S(2)}, u32[]{:S(2)}) collective-permute-start(bf16[128,8192]{1,0:T(8,128)(2,1)} %refs_0_.14), channel_id=1, source_target_pairs={{0,1},{1,0},{2,3},{3,2},{4,5},{5,4},{6,7},{7,6},{8,9},{9,8},{10,11... | collective-permute-start | bytes 6291464 | tf_op jit(solution)/shard_map/ppermute | solution.py:341
  2.5 17.3 %collective-permute-start.4 = (bf16[1152,256]{1,0:T(8,128)(2,1)S(1)}, bf16[1152,256]{1,0:T(8,128)(2,1)}, u32[]{:S(2)}, u32[]{:S(2)}) collective-permute-start(bf16[1152,256]{1,0:T(8,128)(2,1)S(1)} %get-tuple-element.128.refs_3_), channel_id=1, source_target_pairs={{0,2},{1,3},{4,0},{5,1},{8,4},{9,5},{12,8},{13,9},{14,12},{15,13},... | collective-permute-start | bytes 1769480 | tf_op jit(solution)/shard_map/ppermute | solution.py:341
  5.5 16.3 %collective-permute-start.2 = (bf16[1152,256]{1,0:T(8,128)(2,1)S(1)}, bf16[1152,256]{1,0:T(8,128)(2,1)S(1)}, u32[]{:S(2)}, u32[]{:S(2)}) collective-permute-start(bf16[1152,256]{1,0:T(8,128)(2,1)S(1)} %constant_dynamic-update-slice_fusion.10.refs_2_), channel_id=1, source_target_pairs={{0,4},{1,5},{4,8},{5,9},{8,12},{9,13},{12,14},{13,15},{14,10},{15,... | collective-permute-start | bytes 1769480 | tf_op jit(solution)/shard_map/ppermute | solution.py:341
  12.6 9.2 %copy-start = (bf16[128,8192]{1,0:T(8,128)(2,1)}, bf16[128,8192]{1,0:T(8,128)(2,1)S(1)}, u32[]{:S(2)}) copy-start(bf16[128,8192]{1,0:T(8,128)(2,1)S(1)} %collective-permute-done.refs_2_.refs_1_) | copy-start | bytes 6291460
  12.6 19.7 %collective-permute-start.6 = (bf16[1152,256]{1,0:T(8,128)(2,1)S(1)}, bf16[1152,256]{1,0:T(8,128)(2,1)S(1)}, u32[]{:S(2)}, u32[]{:S(2)}) collective-permute-start(bf16[1152,256]{1,0:T(8,128)(2,1)S(1)} %constant_dynamic-update-slice_fusion.10.refs_2_), channel_id=1, source_target_pairs={{0,2},{1,3},{4,0},{5,1},{8,4},{9,5},{12,8},{13,9},{14,12},{15,13},... | collective-permute-start | bytes 1769480 | tf_op jit(solution)/shard_map/ppermute | solution.py:341
  15.7 18.8 %collective-permute-start.7 = (bf16[1152,256]{1,0:T(8,128)(2,1)S(1)}, bf16[1152,256]{1,0:T(8,128)(2,1)}, u32[]{:S(2)}, u32[]{:S(2)}) collective-permute-start(bf16[1152,256]{1,0:T(8,128)(2,1)S(1)} %get-tuple-element.128.refs_3_), channel_id=1, source_target_pairs={{0,4},{1,5},{4,8},{5,9},{8,12},{9,13},{12,14},{13,15},{14,10},{15,... | collective-permute-start | bytes 1769480 | tf_op jit(solution)/shard_map/ppermute | solution.py:341
  19.8 25.2 %collective-permute-start.5 = (bf16[1152,256]{1,0:T(8,128)(2,1)}, bf16[1152,256]{1,0:T(8,128)(2,1)S(1)}, u32[]{:S(2)}, u32[]{:S(2)}) collective-permute-start(bf16[1152,256]{1,0:T(8,128)(2,1)} %collective-permute-done.4.refs_4_), channel_id=1, source_target_pairs={{0,2},{1,3},{4,0},{5,1},{8,4},{9,5},{12,8},{13,9},{14,12},{15,13},... | collective-permute-start | bytes 1769480 | tf_op jit(solution)/shard_map/ppermute | solution.py:341
  21.8 25.3 %collective-permute-start.3 = (bf16[1152,256]{1,0:T(8,128)(2,1)S(1)}, bf16[1152,256]{1,0:T(8,128)(2,1)S(1)}, u32[]{:S(2)}, u32[]{:S(2)}) collective-permute-start(bf16[1152,256]{1,0:T(8,128)(2,1)S(1)} %collective-permute-done.2.refs_5_.refs_3_), channel_id=1, source_target_pairs={{0,4},{1,5},{4,8},{5,9},{8,12},{9,13},{12,14},{13,15},{14,10},{15,... | collective-permute-start | bytes 1769480 | tf_op jit(solution)/shard_map/ppermute | solution.py:341
  32.3 25.3 %collective-permute-start.10 = (bf16[1152,256]{1,0:T(8,128)(2,1)S(1)}, bf16[1152,256]{1,0:T(8,128)(2,1)S(1)}, u32[]{:S(2)}, u32[]{:S(2)}) collective-permute-start(bf16[1152,256]{1,0:T(8,128)(2,1)S(1)} %collective-permute-done.6.refs_2_.refs_4_), channel_id=1, source_target_pairs={{0,2},{1,3},{4,0},{5,1},{8,4},{9,5},{12,8},{13,9},{14,12},{15,13},... | collective-permute-start | bytes 1769480 | tf_op jit(solution)/shard_map/ppermute | solution.py:341
  34.5 25.2 %collective-permute-start.11 = (bf16[1152,256]{1,0:T(8,128)(2,1)}, bf16[1152,256]{1,0:T(8,128)(2,1)S(1)}, u32[]{:S(2)}, u32[]{:S(2)}) collective-permute-start(bf16[1152,256]{1,0:T(8,128)(2,1)} %collective-permute-done.7.refs_3_), channel_id=1, source_target_pairs={{0,4},{1,5},{4,8},{5,9},{8,12},{9,13},{12,14},{13,15},{14,10},{15,... | collective-permute-start | bytes 1769480 | tf_op jit(solution)/shard_map/ppermute | solution.py:341
  44.9 25.3 %collective-permute-start.9 = (bf16[1152,256]{1,0:T(8,128)(2,1)S(1)}, bf16[1152,256]{1,0:T(8,128)(2,1)S(1)}, u32[]{:S(2)}, u32[]{:S(2)}) collective-permute-start(bf16[1152,256]{1,0:T(8,128)(2,1)S(1)} %collective-permute-done.5.refs_2_), channel_id=1, source_target_pairs={{0,2},{1,3},{4,0},{5,1},{8,4},{9,5},{12,8},{13,9},{14,12},{15,13},... | collective-permute-start | bytes 1769480 | tf_op jit(solution)/shard_map/ppermute | solution.py:341
  47.1 25.3 %collective-permute-start.8 = (bf16[1152,256]{1,0:T(8,128)(2,1)S(1)}, bf16[1152,256]{1,0:T(8,128)(2,1)S(1)}, u32[]{:S(2)}, u32[]{:S(2)}) collective-permute-start(bf16[1152,256]{1,0:T(8,128)(2,1)S(1)} %collective-permute-done.3.refs_3_.refs_5_), channel_id=1, source_target_pairs={{0,4},{1,5},{4,8},{5,9},{8,12},{9,13},{12,14},{13,15},{14,10},{15,... | collective-permute-start | bytes 1769480 | tf_op jit(solution)/shard_map/ppermute | solution.py:341
  57.6 16.8 %copy-start.3 = (s32[128]{0:T(128)S(1)}, s32[128]{0:T(128)}, u32[]{:S(2)}) copy-start(s32[128]{0:T(128)} %param.8) | copy-start | bytes 1540
  59.7 23.2 %collective-permute-start.14 = (bf16[1152,256]{1,0:T(8,128)(2,1)S(1)}, bf16[1152,256]{1,0:T(8,128)(2,1)S(1)}, u32[]{:S(2)}, u32[]{:S(2)}) collective-permute-start(bf16[1152,256]{1,0:T(8,128)(2,1)S(1)} %collective-permute-done.10.refs_2_.refs_6_), channel_id=1, source_target_pairs={{0,2},{1,3},{4,0},{5,1},{8,4},{9,5},{12,8},{13,9},{14,12},{15,13},... | collective-permute-start | bytes 1769480 | tf_op jit(solution)/shard_map/ppermute | solution.py:341
  61.3 24.7 %collective-permute-start.15 = (bf16[1152,256]{1,0:T(8,128)(2,1)S(1)}, bf16[1152,256]{1,0:T(8,128)(2,1)S(1)}, u32[]{:S(2)}, u32[]{:S(2)}) collective-permute-start(bf16[1152,256]{1,0:T(8,128)(2,1)S(1)} %collective-permute-done.11.refs_3_), channel_id=1, source_target_pairs={{0,4},{1,5},{4,8},{5,9},{8,12},{9,13},{12,14},{13,15},{14,10},{15,... | collective-permute-start | bytes 1769480 | tf_op jit(solution)/shard_map/ppermute | solution.py:341
  72.3 24.1 %collective-permute-start.12 = (bf16[1152,256]{1,0:T(8,128)(2,1)S(1)}, bf16[1152,256]{1,0:T(8,128)(2,1)S(1)}, u32[]{:S(2)}, u32[]{:S(2)}) collective-permute-start(bf16[1152,256]{1,0:T(8,128)(2,1)S(1)} %collective-permute-done.8.refs_3_.refs_7_), channel_id=1, source_target_pairs={{0,4},{1,5},{4,8},{5,9},{8,12},{9,13},{12,14},{13,15},{14,10},{15,... | collective-permute-start | bytes 1769480 | tf_op jit(solution)/shard_map/ppermute | solution.py:341
  72.4 24.1 %collective-permute-start.13 = (bf16[1152,256]{1,0:T(8,128)(2,1)S(1)}, bf16[1152,256]{1,0:T(8,128)(2,1)S(1)}, u32[]{:S(2)}, u32[]{:S(2)}) collective-permute-start(bf16[1152,256]{1,0:T(8,128)(2,1)S(1)} %collective-permute-done.9.refs_2_), channel_id=1, source_target_pairs={{0,2},{1,3},{4,0},{5,1},{8,4},{9,5},{12,8},{13,9},{14,12},{15,13},... | collective-permute-start | bytes 1769480 | tf_op jit(solution)/shard_map/ppermute | solution.py:341
  96.8 1.6 %collective-permute-start.16 = (f32[128,512]{1,0:T(8,128)S(1)}, f32[128,512]{1,0:T(8,128)S(1)}, u32[]{:S(2)}, u32[]{:S(2)}) collective-permute-start(f32[128,512]{1,0:T(8,128)S(1)} %shard_map.85), channel_id=1, source_target_pairs={{0,1},{1,0},{2,3},{3,2},{4,5},{5,4},{6,7},{7,6},{8,9},{9,8},{10,11... | collective-permute-start | bytes 786440 | tf_op jit(solution)/shard_map/ppermute | solution.py:341
  98.5 5.9 %collective-permute-start.20 = (bf16[144,512]{1,0:T(8,128)(2,1)S(1)}, bf16[144,512]{1,0:T(8,128)(2,1)S(1)}, u32[]{:S(2)}, u32[]{:S(2)}) collective-permute-start(bf16[144,512]{1,0:T(8,128)(2,1)S(1)} %pad_maximum_fusion), channel_id=1, source_target_pairs={{0,2},{1,3},{4,0},{5,1},{8,4},{9,5},{12,8},{13,9},{14,12},{15,13},... | collective-permute-start | bytes 442376 | tf_op jit(solution)/shard_map/ppermute | solution.py:341
  100.1 5.9 %collective-permute-start.17 = (bf16[144,512]{1,0:T(8,128)(2,1)S(1)}, bf16[144,512]{1,0:T(8,128)(2,1)S(1)}, u32[]{:S(2)}, u32[]{:S(2)}) collective-permute-start(bf16[144,512]{1,0:T(8,128)(2,1)S(1)} %pad_maximum_fusion), channel_id=1, source_target_pairs={{0,4},{1,5},{4,8},{5,9},{8,12},{9,13},{12,14},{13,15},{14,10},{15,... | collective-permute-start | bytes 442376 | tf_op jit(solution)/shard_map/ppermute | solution.py:341
  104.4 5.1 %collective-permute-start.21 = (bf16[144,512]{1,0:T(8,128)(2,1)S(1)}, bf16[144,512]{1,0:T(8,128)(2,1)S(1)}, u32[]{:S(2)}, u32[]{:S(2)}) collective-permute-start(bf16[144,512]{1,0:T(8,128)(2,1)S(1)} %collective-permute-done.20), channel_id=1, source_target_pairs={{0,2},{1,3},{4,0},{5,1},{8,4},{9,5},{12,8},{13,9},{14,12},{15,13},... | collective-permute-start | bytes 442376 | tf_op jit(solution)/shard_map/ppermute | solution.py:341
  106.0 6.2 %collective-permute-start.18 = (bf16[144,512]{1,0:T(8,128)(2,1)S(1)}, bf16[144,512]{1,0:T(8,128)(2,1)S(1)}, u32[]{:S(2)}, u32[]{:S(2)}) collective-permute-start(bf16[144,512]{1,0:T(8,128)(2,1)S(1)} %collective-permute-done.17), channel_id=1, source_target_pairs={{0,4},{1,5},{4,8},{5,9},{8,12},{9,13},{12,14},{13,15},{14,10},{15,... | collective-permute-start | bytes 442376 | tf_op jit(solution)/shard_map/ppermute | solution.py:341
  109.6 7.9 %collective-permute-start.24 = (bf16[80,512]{1,0:T(8,128)(2,1)S(1)}, bf16[80,512]{1,0:T(8,128)(2,1)S(1)}, u32[]{:S(2)}, u32[]{:S(2)}) collective-permute-start(bf16[80,512]{1,0:T(8,128)(2,1)S(1)} %slice.14), channel_id=1, source_target_pairs={{0,6},{1,7},{4,2},{5,3},{8,0},{9,1},{12,4},{13,5},{14,8},{15,9},{1... | collective-permute-start | bytes 245768 | tf_op jit(solution)/shard_map/ppermute | solution.py:341
  112.2 5.3 %collective-permute-start.23 = (bf16[64,512]{1,0:T(8,128)(2,1)S(1)}, bf16[64,512]{1,0:T(8,128)(2,1)S(1)}, u32[]{:S(2)}, u32[]{:S(2)}) collective-permute-start(bf16[64,512]{1,0:T(8,128)(2,1)S(1)} %slice.13), channel_id=1, source_target_pairs={{0,8},{1,9},{4,12},{5,13},{8,14},{9,15},{12,10},{13,11},{14,6},{15... | collective-permute-start | bytes 196616 | tf_op jit(solution)/shard_map/ppermute | solution.py:341
  112.6 5.8 %collective-permute-start.19 = (bf16[144,512]{1,0:T(8,128)(2,1)S(1)}, bf16[144,512]{1,0:T(8,128)(2,1)S(1)}, u32[]{:S(2)}, u32[]{:S(2)}) collective-permute-start(bf16[144,512]{1,0:T(8,128)(2,1)S(1)} %collective-permute-done.18), channel_id=1, source_target_pairs={{0,4},{1,5},{4,8},{5,9},{8,12},{9,13},{12,14},{13,15},{14,10},{15,... | collective-permute-start | bytes 442376 | tf_op jit(solution)/shard_map/ppermute | solution.py:341
  113.1 5.3 %collective-permute-start.22 = (bf16[144,512]{1,0:T(8,128)(2,1)S(1)}, bf16[144,512]{1,0:T(8,128)(2,1)S(1)}, u32[]{:S(2)}, u32[]{:S(2)}) collective-permute-start(bf16[144,512]{1,0:T(8,128)(2,1)S(1)} %collective-permute-done.21), channel_id=1, source_target_pairs={{0,2},{1,3},{4,0},{5,1},{8,4},{9,5},{12,8},{13,9},{14,12},{15,13},... | collective-permute-start | bytes 442376 | tf_op jit(solution)/shard_map/ppermute | solution.py:341
  114.6 3.9 %collective-permute-start.26 = (bf16[720,512]{1,0:T(8,128)(2,1)S(1)}, bf16[720,512]{1,0:T(8,128)(2,1)S(1)}, u32[]{:S(2)}, u32[]{:S(2)}) collective-permute-start(bf16[720,512]{1,0:T(8,128)(2,1)S(1)} %constant_dynamic-update-slice_fusion.4.refs_0_), channel_id=1, source_target_pairs={{0,1},{1,0},{2,3},{3,2},{4,5},{5,4},{6,7},{7,6},{8,9},{9,8},{10,11... | collective-permute-start | bytes 2211848 | tf_op jit(solution)/shard_map/ppermute | solution.py:341
  118.5 1.9 %collective-permute-start.25 = (bf16[432,512]{1,0:T(8,128)(2,1)S(1)}, bf16[432,512]{1,0:T(8,128)(2,1)S(1)}, u32[]{:S(2)}, u32[]{:S(2)}) collective-permute-start(bf16[432,512]{1,0:T(8,128)(2,1)S(1)} %constant_dynamic-update-slice_fusion.refs_2_), channel_id=1, source_target_pairs={{0,1},{1,0},{2,3},{3,2},{4,5},{5,4},{6,7},{7,6},{8,9},{9,8},{10,11... | collective-permute-start | bytes 1327112 | tf_op jit(solution)/shard_map/ppermute | solution.py:341

commit v9 on v7

--- a/solution.py
+++ b/solution.py
@@ -427,7 +427,7 @@
     own = [near, far]
     swapped = [send(x, swap) for x in own]
     me = own_index[None]
-    near_both = lax.optimization_barrier((near, swapped[0], far))[:2]
+    near_both = (near, swapped[0])
     sums = some_sums(me, list(near_both), rows, width, balanced)
     return last(me, [far, swapped[1]], sums, rows, devices)
 

time: 122 us -> 122 us (level)
  no operation moved by 1% of the time
where the time goes in v9:
time: 122 us
  waiting for transfers between devices  70 us (57%)
  starting transfers between devices  26.5 us (22%)
  Pallas kernels  22.6 us (19%)
  local copies, waits for them, and re-layouts  1.38 us (1%)
    ppermute x27, waiting for transfers between devices, send(): return lax.ppermute(x, 'dp', pairs)  70 us
    ppermute x27, starting transfers between devices, send(): return lax.ppermute(x, 'dp', pairs)  26.5 us
    pallas_call x7, Pallas kernels, project(): pl.pallas_call(functools.partial(project_kernel, kinds, [p[:2] for p in p...  18.3 us
  transfers between devices with their start and end apart: 27, of which 18 were waited for; matrix products, arithmetic and copies ran while one was open for 1% of the time, Pallas kernels for 17%

profile of v9, /device:TPU:0, one launch (start us, length us, event | category | flops | bytes accessed | tf_op | source)
XLA Modules:
  0.0 121.5 jit_solution(15849287784271880542)
XLA Ops:
  0.7 0.5 collective-permute-start.1
  1.3 1.2 %fusion.7 = (bf16[1152,256]{1,0:T(8,128)(2,1)S(1)}, bf16[1152,256]{1,0:T(8,128)(2,1)S(1)}) fusion(bf16[1792,256]{1,0:T(8,128)(2,1)} %param.10), kind=kLoop, calls=%fused_computation.34 | loop fusion | bytes 2686976 | tf_op jit(solution)/shard_map/slice | solution.py:357
  2.5 3.0 %collective-permute-start.4 = (bf16[1152,256]{1,0:T(8,128)(2,1)S(1)}, bf16[1152,256]{1,0:T(8,128)(2,1)}, u32[]{:S(2)}, u32[]{:S(2)}) collective-permute-start(bf16[1152,256]{1,0:T(8,128)(2,1)S(1)} %get-tuple-element.122.refs_3_), channel_id=1, source_target_pairs={{0,2},{1,3},{4,0},{5,1},{8,4},{9,5},{12,8},{13,9},{14,12},{15,13},... | collective-permute-start | bytes 1769480 | tf_op jit(solution)/shard_map/ppermute | solution.py:341
  5.5 0.1 collective-permute-start.2
  5.6 7.0 %collective-permute-done.refs_2_.refs_1_ = bf16[128,8192]{1,0:T(8,128)(2,1)S(1)} collective-permute-done((bf16[128,8192]{1,0:T(8,128)(2,1)}, bf16[128,8192]{1,0:T(8,128)(2,1)S(1)}, u32[]{:S(2)}, u32[]{:S(2)}) %collective-permute-start) | collective-permute-done | bytes 2097184 | tf_op jit(solution)/shard_map/ppermute | solution.py:341
  12.6 3.1 %collective-permute-start.7 = (bf16[1152,256]{1,0:T(8,128)(2,1)S(1)}, bf16[1152,256]{1,0:T(8,128)(2,1)S(1)}, u32[]{:S(2)}, u32[]{:S(2)}) collective-permute-start(bf16[1152,256]{1,0:T(8,128)(2,1)S(1)} %constant_dynamic-update-slice_fusion.10.refs_2_), channel_id=1, source_target_pairs={{0,2},{1,3},{4,0},{5,1},{8,4},{9,5},{12,8},{13,9},{14,12},{15,13},... | collective-permute-start | bytes 1769480 | tf_op jit(solution)/shard_map/ppermute | solution.py:341
  15.8 4.0 %collective-permute-done.4.refs_5_ = bf16[1152,256]{1,0:T(8,128)(2,1)} collective-permute-done((bf16[1152,256]{1,0:T(8,128)(2,1)S(1)}, bf16[1152,256]{1,0:T(8,128)(2,1)}, u32[]{:S(2)}, u32[]{:S(2)}) %collective-permute-start.4) | collective-permute-done | bytes 589856 | tf_op jit(solution)/shard_map/ppermute | solution.py:341
  19.8 2.0 %collective-permute-start.5 = (bf16[1152,256]{1,0:T(8,128)(2,1)}, bf16[1152,256]{1,0:T(8,128)(2,1)S(1)}, u32[]{:S(2)}, u32[]{:S(2)}) collective-permute-start(bf16[1152,256]{1,0:T(8,128)(2,1)} %collective-permute-done.4.refs_5_), channel_id=1, source_target_pairs={{0,2},{1,3},{4,0},{5,1},{8,4},{9,5},{12,8},{13,9},{14,12},{15,13},... | collective-permute-start | bytes 1769480 | tf_op jit(solution)/shard_map/ppermute | solution.py:341
  21.9 3.7 %shard_map.78 = (f32[128,256]{1,0:T(8,128)S(1)}, f32[128,256]{1,0:T(8,128)S(1)}) custom-call(s32[8]{0:T(128)S(1)} %fusion.6.owners_ref, bf16[128,28672]{1,0:T(8,128)(2,1)} %refs_0_.15, bf16[128,28672]{1,0:T(8,128)(2,1)} %collective-permute-done.1.refs_3_.refs_1_, bf16[1152,256]{1,0:T(8,128)(2,1)S(1)} %constant_dynamic-update-slice_fusion.10.refs_2_, ...), custom_call_target="tpu_custom_call" | custom-call | flops 1 | bytes 1 | tf_op jit(solution)/shard_map/pallas_call | solution.py:116
  25.6 6.7 %collective-permute-done.7.refs_3_.refs_4_ = bf16[1152,256]{1,0:T(8,128)(2,1)S(1)} collective-permute-done((bf16[1152,256]{1,0:T(8,128)(2,1)S(1)}, bf16[1152,256]{1,0:T(8,128)(2,1)S(1)}, u32[]{:S(2)}, u32[]{:S(2)}) %collective-permute-start.7) | collective-permute-done | bytes 589856 | tf_op jit(solution)/shard_map/ppermute | solution.py:341
  32.3 2.0 %collective-permute-start.11 = (bf16[1152,256]{1,0:T(8,128)(2,1)S(1)}, bf16[1152,256]{1,0:T(8,128)(2,1)S(1)}, u32[]{:S(2)}, u32[]{:S(2)}) collective-permute-start(bf16[1152,256]{1,0:T(8,128)(2,1)S(1)} %collective-permute-done.7.refs_3_.refs_4_), channel_id=1, source_target_pairs={{0,2},{1,3},{4,0},{5,1},{8,4},{9,5},{12,8},{13,9},{14,12},{15,13},... | collective-permute-start | bytes 1769480 | tf_op jit(solution)/shard_map/ppermute | solution.py:341
  34.3 0.2 collective-permute-done.6.refs_2_
  34.6 2.7 %shard_map.79 = (f32[128,256]{1,0:T(8,128)S(1)}, f32[128,256]{1,0:T(8,128)S(1)}) custom-call(s32[8]{0:T(128)S(1)} %fusion.6.owners_ref, bf16[128,28672]{1,0:T(8,128)(2,1)} %refs_0_.15, bf16[128,28672]{1,0:T(8,128)(2,1)} %collective-permute-done.1.refs_3_.refs_1_, bf16[1152,256]{1,0:T(8,128)(2,1)} %collective-permute-done.6.refs_2_, ...), custom_call_target="tpu_custom_call" | custom-call | flops 1 | bytes 1 | tf_op jit(solution)/shard_map/pallas_call | solution.py:116
  37.3 7.6 %collective-permute-done.5.refs_3_ = bf16[1152,256]{1,0:T(8,128)(2,1)S(1)} collective-permute-done((bf16[1152,256]{1,0:T(8,128)(2,1)}, bf16[1152,256]{1,0:T(8,128)(2,1)S(1)}, u32[]{:S(2)}, u32[]{:S(2)}) %collective-permute-start.5) | collective-permute-done | bytes 589856 | tf_op jit(solution)/shard_map/ppermute | solution.py:341
  44.9 2.0 %collective-permute-start.9 = (bf16[1152,256]{1,0:T(8,128)(2,1)S(1)}, bf16[1152,256]{1,0:T(8,128)(2,1)S(1)}, u32[]{:S(2)}, u32[]{:S(2)}) collective-permute-start(bf16[1152,256]{1,0:T(8,128)(2,1)S(1)} %collective-permute-done.5.refs_3_), channel_id=1, source_target_pairs={{0,2},{1,3},{4,0},{5,1},{8,4},{9,5},{12,8},{13,9},{14,12},{15,13},... | collective-permute-start | bytes 1769480 | tf_op jit(solution)/shard_map/ppermute | solution.py:341
  47.1 2.2 %shard_map.80 = (f32[128,256]{1,0:T(8,128)S(1)}, f32[128,256]{1,0:T(8,128)S(1)}) custom-call(s32[8]{0:T(128)S(1)} %fusion.6.owners_ref, bf16[128,28672]{1,0:T(8,128)(2,1)} %refs_0_.15, bf16[128,28672]{1,0:T(8,128)(2,1)} %collective-permute-done.1.refs_3_.refs_1_, bf16[1152,256]{1,0:T(8,128)(2,1)S(1)} %collective-permute-done.3.refs_2_.refs_5_, ...), custom_call_target="tpu_custom_call" | custom-call | flops 1 | bytes 1 | tf_op jit(solution)/shard_map/pallas_call | solution.py:116
  49.3 8.2 %collective-permute-done.11.refs_3_.refs_6_ = bf16[1152,256]{1,0:T(8,128)(2,1)S(1)} collective-permute-done((bf16[1152,256]{1,0:T(8,128)(2,1)S(1)}, bf16[1152,256]{1,0:T(8,128)(2,1)S(1)}, u32[]{:S(2)}, u32[]{:S(2)}) %collective-permute-start.11) | collective-permute-done | bytes 589856 | tf_op jit(solution)/shard_map/ppermute | solution.py:341
  57.6 2.1 %collective-permute-done.10.refs_2_ = bf16[1152,256]{1,0:T(8,128)(2,1)S(1)} collective-permute-done((bf16[1152,256]{1,0:T(8,128)(2,1)}, bf16[1152,256]{1,0:T(8,128)(2,1)S(1)}, u32[]{:S(2)}, u32[]{:S(2)}) %collective-permute-start.10) | collective-permute-done | bytes 589856 | tf_op jit(solution)/shard_map/ppermute | solution.py:341
  59.7 1.6 %collective-permute-start.14 = (bf16[1152,256]{1,0:T(8,128)(2,1)S(1)}, bf16[1152,256]{1,0:T(8,128)(2,1)S(1)}, u32[]{:S(2)}, u32[]{:S(2)}) collective-permute-start(bf16[1152,256]{1,0:T(8,128)(2,1)S(1)} %collective-permute-done.11.refs_3_.refs_6_), channel_id=1, source_target_pairs={{0,2},{1,3},{4,0},{5,1},{8,4},{9,5},{12,8},{13,9},{14,12},{15,13},... | collective-permute-start | bytes 1769480 | tf_op jit(solution)/shard_map/ppermute | solution.py:341
  61.3 0.4 collective-permute-start.15
  61.7 2.2 %shard_map.81 = (f32[128,256]{1,0:T(8,128)S(1)}, f32[128,256]{1,0:T(8,128)S(1)}) custom-call(s32[8]{0:T(128)S(1)} %fusion.6.owners_ref, bf16[128,28672]{1,0:T(8,128)(2,1)} %refs_0_.15, bf16[128,28672]{1,0:T(8,128)(2,1)} %collective-permute-done.1.refs_3_.refs_1_, bf16[1152,256]{1,0:T(8,128)(2,1)S(1)} %collective-permute-done.10.refs_2_, ...), custom_call_target="tpu_custom_call" | custom-call | flops 1 | bytes 1 | tf_op jit(solution)/shard_map/pallas_call | solution.py:116
  63.9 6.3 %collective-permute-done.9.refs_3_ = bf16[1152,256]{1,0:T(8,128)(2,1)S(1)} collective-permute-done((bf16[1152,256]{1,0:T(8,128)(2,1)S(1)}, bf16[1152,256]{1,0:T(8,128)(2,1)S(1)}, u32[]{:S(2)}, u32[]{:S(2)}) %collective-permute-start.9) | collective-permute-done | bytes 589856 | tf_op jit(solution)/shard_map/ppermute | solution.py:341
  70.2 2.1 %collective-permute-done.8.refs_2_.refs_7_ = bf16[1152,256]{1,0:T(8,128)(2,1)S(1)} collective-permute-done((bf16[1152,256]{1,0:T(8,128)(2,1)S(1)}, bf16[1152,256]{1,0:T(8,128)(2,1)S(1)}, u32[]{:S(2)}, u32[]{:S(2)}) %collective-permute-start.8) | collective-permute-done | bytes 589856 | tf_op jit(solution)/shard_map/ppermute | solution.py:341
  72.4 2.0 %collective-permute-start.13 = (bf16[1152,256]{1,0:T(8,128)(2,1)S(1)}, bf16[1152,256]{1,0:T(8,128)(2,1)S(1)}, u32[]{:S(2)}, u32[]{:S(2)}) collective-permute-start(bf16[1152,256]{1,0:T(8,128)(2,1)S(1)} %collective-permute-done.9.refs_3_), channel_id=1, source_target_pairs={{0,2},{1,3},{4,0},{5,1},{8,4},{9,5},{12,8},{13,9},{14,12},{15,13},... | collective-permute-start | bytes 1769480 | tf_op jit(solution)/shard_map/ppermute | solution.py:341
  74.4 1.9 %shard_map.77 = (bf16[128,2304]{1,0:T(8,128)(2,1)S(1)}, bf16[128,2304]{1,0:T(8,128)(2,1)S(1)}) custom-call(s32[8]{0:T(128)S(1)} %fusion.6.owners_ref, bf16[128,8192]{1,0:T(8,128)(2,1)} %refs_0_.14, bf16[128,28672]{1,0:T(8,128)(2,1)} %refs_0_.15, bf16[128,8192]{1,0:T(8,128)(2,1)} %copy-done, bf16[128,28672]{1,0:T(8,128)(2,1)} %collective-permute-done.1.refs_3_.refs_1_), custom_call_target="tpu_custom_call" | custom-call | flops 1 | bytes 1 | tf_op jit(solution)/shard_map/pallas_call | solution.py:194
  76.3 2.2 %shard_map.82 = (f32[128,256]{1,0:T(8,128)S(1)}, f32[128,256]{1,0:T(8,128)S(1)}) custom-call(s32[8]{0:T(128)S(1)} %fusion.6.owners_ref, bf16[128,28672]{1,0:T(8,128)(2,1)} %refs_0_.15, bf16[128,28672]{1,0:T(8,128)(2,1)} %collective-permute-done.1.refs_3_.refs_1_, bf16[1152,256]{1,0:T(8,128)(2,1)S(1)} %collective-permute-done.8.refs_2_.refs_7_, ...), custom_call_target="tpu_custom_call" | custom-call | flops 1 | bytes 1 | tf_op jit(solution)/shard_map/pallas_call | solution.py:116
  78.5 4.3 %collective-permute-done.14.refs_8_.refs_3_ = bf16[1152,256]{1,0:T(8,128)(2,1)S(1)} collective-permute-done((bf16[1152,256]{1,0:T(8,128)(2,1)S(1)}, bf16[1152,256]{1,0:T(8,128)(2,1)S(1)}, u32[]{:S(2)}, u32[]{:S(2)}) %collective-permute-start.14) | collective-permute-done | bytes 589856 | tf_op jit(solution)/shard_map/ppermute | solution.py:341
  82.9 3.1 %shard_map.83 = (f32[128,256]{1,0:T(8,128)S(1)}, f32[128,256]{1,0:T(8,128)S(1)}) custom-call(s32[8]{0:T(128)S(1)} %fusion.6.owners_ref, bf16[128,8192]{1,0:T(8,128)(2,1)} %refs_0_.14, bf16[128,8192]{1,0:T(8,128)(2,1)} %copy-done, bf16[1152,256]{1,0:T(8,128)(2,1)S(1)} %constant_dynamic-update-slice_fusion.10.refs_2_, ...), custom_call_target="tpu_custom_call" | custom-call | flops 1 | bytes 1 | tf_op jit(solution)/shard_map/pallas_call | solution.py:116
  86.0 2.2 %shard_map.84 = (f32[128,256]{1,0:T(8,128)S(1)}, f32[128,256]{1,0:T(8,128)S(1)}) custom-call(s32[8]{0:T(128)S(1)} %fusion.6.owners_ref, bf16[128,28672]{1,0:T(8,128)(2,1)} %refs_0_.15, bf16[128,28672]{1,0:T(8,128)(2,1)} %collective-permute-done.1.refs_3_.refs_1_, bf16[1152,256]{1,0:T(8,128)(2,1)S(1)} %collective-permute-done.15.refs_2_, ...), custom_call_target="tpu_custom_call" | custom-call | flops 1 | bytes 1 | tf_op jit(solution)/shard_map/pallas_call | solution.py:116
  88.1 8.3 %collective-permute-done.12.first_ref = bf16[1152,256]{1,0:T(8,128)(2,1)S(1)} collective-permute-done((bf16[1152,256]{1,0:T(8,128)(2,1)S(1)}, bf16[1152,256]{1,0:T(8,128)(2,1)S(1)}, u32[]{:S(2)}, u32[]{:S(2)}) %collective-permute-start.12) | collective-permute-done | bytes 589856 | tf_op jit(solution)/shard_map/ppermute | solution.py:341
  96.4 0.3 shard_map.85
  96.9 0.3 shard_map.86
  97.2 1.2 collective-permute-done.16
  98.5 1.6 %collective-permute-start.20 = (bf16[144,512]{1,0:T(8,128)(2,1)S(1)}, bf16[144,512]{1,0:T(8,128)(2,1)S(1)}, u32[]{:S(2)}, u32[]{:S(2)}) collective-permute-start(bf16[144,512]{1,0:T(8,128)(2,1)S(1)} %pad_maximum_fusion), channel_id=1, source_target_pairs={{0,2},{1,3},{4,0},{5,1},{8,4},{9,5},{12,8},{13,9},{14,12},{15,13},... | collective-permute-start | bytes 442376 | tf_op jit(solution)/shard_map/ppermute | solution.py:341
  100.1 0.5 collective-permute-start.17
  100.6 3.9 %collective-permute-done.20 = bf16[144,512]{1,0:T(8,128)(2,1)S(1)} collective-permute-done((bf16[144,512]{1,0:T(8,128)(2,1)S(1)}, bf16[144,512]{1,0:T(8,128)(2,1)S(1)}, u32[]{:S(2)}, u32[]{:S(2)}) %collective-permute-start.20) | collective-permute-done | bytes 147488 | tf_op jit(solution)/shard_map/ppermute | solution.py:341
  104.4 1.6 %collective-permute-start.21 = (bf16[144,512]{1,0:T(8,128)(2,1)S(1)}, bf16[144,512]{1,0:T(8,128)(2,1)S(1)}, u32[]{:S(2)}, u32[]{:S(2)}) collective-permute-start(bf16[144,512]{1,0:T(8,128)(2,1)S(1)} %collective-permute-done.20), channel_id=1, source_target_pairs={{0,2},{1,3},{4,0},{5,1},{8,4},{9,5},{12,8},{13,9},{14,12},{15,13},... | collective-permute-start | bytes 442376 | tf_op jit(solution)/shard_map/ppermute | solution.py:341
  106.0 0.5 collective-permute-start.18
  106.5 3.1 %collective-permute-done.21 = bf16[144,512]{1,0:T(8,128)(2,1)S(1)} collective-permute-done((bf16[144,512]{1,0:T(8,128)(2,1)S(1)}, bf16[144,512]{1,0:T(8,128)(2,1)S(1)}, u32[]{:S(2)}, u32[]{:S(2)}) %collective-permute-start.21) | collective-permute-done | bytes 147488 | tf_op jit(solution)/shard_map/ppermute | solution.py:341
  109.6 2.6 %collective-permute-start.24 = (bf16[80,512]{1,0:T(8,128)(2,1)S(1)}, bf16[80,512]{1,0:T(8,128)(2,1)S(1)}, u32[]{:S(2)}, u32[]{:S(2)}) collective-permute-start(bf16[80,512]{1,0:T(8,128)(2,1)S(1)} %slice.14), channel_id=1, source_target_pairs={{0,6},{1,7},{4,2},{5,3},{8,0},{9,1},{12,4},{13,5},{14,8},{15,9},{1... | collective-permute-start | bytes 245768 | tf_op jit(solution)/shard_map/ppermute | solution.py:341
  112.2 0.4 collective-permute-start.23
  112.6 0.6 collective-permute-start.19
  113.1 1.5 %collective-permute-start.22 = (bf16[144,512]{1,0:T(8,128)(2,1)S(1)}, bf16[144,512]{1,0:T(8,128)(2,1)S(1)}, u32[]{:S(2)}, u32[]{:S(2)}) collective-permute-start(bf16[144,512]{1,0:T(8,128)(2,1)S(1)} %collective-permute-done.21), channel_id=1, source_target_pairs={{0,2},{1,3},{4,0},{5,1},{8,4},{9,5},{12,8},{13,9},{14,12},{15,13},... | collective-permute-start | bytes 442376 | tf_op jit(solution)/shard_map/ppermute | solution.py:341
  114.7 2.8 %collective-permute-done.23 = bf16[64,512]{1,0:T(8,128)(2,1)S(1)} collective-permute-done((bf16[64,512]{1,0:T(8,128)(2,1)S(1)}, bf16[64,512]{1,0:T(8,128)(2,1)S(1)}, u32[]{:S(2)}, u32[]{:S(2)}) %collective-permute-start.23) | collective-permute-done | bytes 65568 | tf_op jit(solution)/shard_map/ppermute | solution.py:341
  117.5 0.9 collective-permute-done.19
  118.6 0.6 shard_map.87
  119.2 1.2 collective-permute-done.25.second_ref
  120.4 1.2 shard_map.88
  (48 shorter events, 1.1 us)
Async XLA Ops:
  0.6 21.3 %copy-start.2 = (s32[8]{0:T(128)S(1)}, s32[8]{0:T(128)}, u32[]{:S(2)}) copy-start(s32[8]{0:T(128)} %constant.104) | copy-start | bytes 100
  0.6 4.8 %copy-start.1 = (bf16[512,256]{1,0:T(8,128)(2,1)S(1)}, bf16[512,256]{1,0:T(8,128)(2,1)}, u32[]{:S(2)}) copy-start(bf16[512,256]{1,0:T(8,128)(2,1)} %param.9) | copy-start | bytes 786436
  0.7 21.3 %collective-permute-start.1 = (bf16[128,28672]{1,0:T(8,128)(2,1)}, bf16[128,28672]{1,0:T(8,128)(2,1)}, u32[]{:S(2)}, u32[]{:S(2)}) collective-permute-start(bf16[128,28672]{1,0:T(8,128)(2,1)} %refs_0_.15), channel_id=1, source_target_pairs={{0,1},{1,0},{2,3},{3,2},{4,5},{5,4},{6,7},{7,6},{8,9},{9,8},{10,11... | collective-permute-start | bytes 22020104 | tf_op jit(solution)/shard_map/ppermute | solution.py:341
  1.2 11.4 %collective-permute-start = (bf16[128,8192]{1,0:T(8,128)(2,1)}, bf16[128,8192]{1,0:T(8,128)(2,1)S(1)}, u32[]{:S(2)}, u32[]{:S(2)}) collective-permute-start(bf16[128,8192]{1,0:T(8,128)(2,1)} %refs_0_.14), channel_id=1, source_target_pairs={{0,1},{1,0},{2,3},{3,2},{4,5},{5,4},{6,7},{7,6},{8,9},{9,8},{10,11... | collective-permute-start | bytes 6291464 | tf_op jit(solution)/shard_map/ppermute | solution.py:341
  2.5 17.3 %collective-permute-start.4 = (bf16[1152,256]{1,0:T(8,128)(2,1)S(1)}, bf16[1152,256]{1,0:T(8,128)(2,1)}, u32[]{:S(2)}, u32[]{:S(2)}) collective-permute-start(bf16[1152,256]{1,0:T(8,128)(2,1)S(1)} %get-tuple-element.122.refs_3_), channel_id=1, source_target_pairs={{0,2},{1,3},{4,0},{5,1},{8,4},{9,5},{12,8},{13,9},{14,12},{15,13},... | collective-permute-start | bytes 1769480 | tf_op jit(solution)/shard_map/ppermute | solution.py:341
  5.5 16.3 %collective-permute-start.2 = (bf16[1152,256]{1,0:T(8,128)(2,1)S(1)}, bf16[1152,256]{1,0:T(8,128)(2,1)S(1)}, u32[]{:S(2)}, u32[]{:S(2)}) collective-permute-start(bf16[1152,256]{1,0:T(8,128)(2,1)S(1)} %constant_dynamic-update-slice_fusion.10.refs_2_), channel_id=1, source_target_pairs={{0,4},{1,5},{4,8},{5,9},{8,12},{9,13},{12,14},{13,15},{14,10},{15,... | collective-permute-start | bytes 1769480 | tf_op jit(solution)/shard_map/ppermute | solution.py:341
  12.6 9.2 %copy-start = (bf16[128,8192]{1,0:T(8,128)(2,1)}, bf16[128,8192]{1,0:T(8,128)(2,1)S(1)}, u32[]{:S(2)}) copy-start(bf16[128,8192]{1,0:T(8,128)(2,1)S(1)} %collective-permute-done.refs_2_.refs_1_) | copy-start | bytes 6291460
  12.6 19.7 %collective-permute-start.7 = (bf16[1152,256]{1,0:T(8,128)(2,1)S(1)}, bf16[1152,256]{1,0:T(8,128)(2,1)S(1)}, u32[]{:S(2)}, u32[]{:S(2)}) collective-permute-start(bf16[1152,256]{1,0:T(8,128)(2,1)S(1)} %constant_dynamic-update-slice_fusion.10.refs_2_), channel_id=1, source_target_pairs={{0,2},{1,3},{4,0},{5,1},{8,4},{9,5},{12,8},{13,9},{14,12},{15,13},... | collective-permute-start | bytes 1769480 | tf_op jit(solution)/shard_map/ppermute | solution.py:341
  15.7 18.8 %collective-permute-start.6 = (bf16[1152,256]{1,0:T(8,128)(2,1)S(1)}, bf16[1152,256]{1,0:T(8,128)(2,1)}, u32[]{:S(2)}, u32[]{:S(2)}) collective-permute-start(bf16[1152,256]{1,0:T(8,128)(2,1)S(1)} %get-tuple-element.122.refs_3_), channel_id=1, source_target_pairs={{0,4},{1,5},{4,8},{5,9},{8,12},{9,13},{12,14},{13,15},{14,10},{15,... | collective-permute-start | bytes 1769480 | tf_op jit(solution)/shard_map/ppermute | solution.py:341
  19.8 25.2 %collective-permute-start.5 = (bf16[1152,256]{1,0:T(8,128)(2,1)}, bf16[1152,256]{1,0:T(8,128)(2,1)S(1)}, u32[]{:S(2)}, u32[]{:S(2)}) collective-permute-start(bf16[1152,256]{1,0:T(8,128)(2,1)} %collective-permute-done.4.refs_5_), channel_id=1, source_target_pairs={{0,2},{1,3},{4,0},{5,1},{8,4},{9,5},{12,8},{13,9},{14,12},{15,13},... | collective-permute-start | bytes 1769480 | tf_op jit(solution)/shard_map/ppermute | solution.py:341
  21.8 25.3 %collective-permute-start.3 = (bf16[1152,256]{1,0:T(8,128)(2,1)S(1)}, bf16[1152,256]{1,0:T(8,128)(2,1)S(1)}, u32[]{:S(2)}, u32[]{:S(2)}) collective-permute-start(bf16[1152,256]{1,0:T(8,128)(2,1)S(1)} %collective-permute-done.2.refs_4_.refs_3_), channel_id=1, source_target_pairs={{0,4},{1,5},{4,8},{5,9},{8,12},{9,13},{12,14},{13,15},{14,10},{15,... | collective-permute-start | bytes 1769480 | tf_op jit(solution)/shard_map/ppermute | solution.py:341
  32.3 25.3 %collective-permute-start.11 = (bf16[1152,256]{1,0:T(8,128)(2,1)S(1)}, bf16[1152,256]{1,0:T(8,128)(2,1)S(1)}, u32[]{:S(2)}, u32[]{:S(2)}) collective-permute-start(bf16[1152,256]{1,0:T(8,128)(2,1)S(1)} %collective-permute-done.7.refs_3_.refs_4_), channel_id=1, source_target_pairs={{0,2},{1,3},{4,0},{5,1},{8,4},{9,5},{12,8},{13,9},{14,12},{15,13},... | collective-permute-start | bytes 1769480 | tf_op jit(solution)/shard_map/ppermute | solution.py:341
  34.5 25.2 %collective-permute-start.10 = (bf16[1152,256]{1,0:T(8,128)(2,1)}, bf16[1152,256]{1,0:T(8,128)(2,1)S(1)}, u32[]{:S(2)}, u32[]{:S(2)}) collective-permute-start(bf16[1152,256]{1,0:T(8,128)(2,1)} %collective-permute-done.6.refs_2_), channel_id=1, source_target_pairs={{0,4},{1,5},{4,8},{5,9},{8,12},{9,13},{12,14},{13,15},{14,10},{15,... | collective-permute-start | bytes 1769480 | tf_op jit(solution)/shard_map/ppermute | solution.py:341
  44.9 25.3 %collective-permute-start.9 = (bf16[1152,256]{1,0:T(8,128)(2,1)S(1)}, bf16[1152,256]{1,0:T(8,128)(2,1)S(1)}, u32[]{:S(2)}, u32[]{:S(2)}) collective-permute-start(bf16[1152,256]{1,0:T(8,128)(2,1)S(1)} %collective-permute-done.5.refs_3_), channel_id=1, source_target_pairs={{0,2},{1,3},{4,0},{5,1},{8,4},{9,5},{12,8},{13,9},{14,12},{15,13},... | collective-permute-start | bytes 1769480 | tf_op jit(solution)/shard_map/ppermute | solution.py:341
  47.1 25.3 %collective-permute-start.8 = (bf16[1152,256]{1,0:T(8,128)(2,1)S(1)}, bf16[1152,256]{1,0:T(8,128)(2,1)S(1)}, u32[]{:S(2)}, u32[]{:S(2)}) collective-permute-start(bf16[1152,256]{1,0:T(8,128)(2,1)S(1)} %collective-permute-done.3.refs_2_.refs_5_), channel_id=1, source_target_pairs={{0,4},{1,5},{4,8},{5,9},{8,12},{9,13},{12,14},{13,15},{14,10},{15,... | collective-permute-start | bytes 1769480 | tf_op jit(solution)/shard_map/ppermute | solution.py:341
  57.6 16.8 %copy-start.3 = (s32[128]{0:T(128)S(1)}, s32[128]{0:T(128)}, u32[]{:S(2)}) copy-start(s32[128]{0:T(128)} %param.8) | copy-start | bytes 1540
  59.7 23.2 %collective-permute-start.14 = (bf16[1152,256]{1,0:T(8,128)(2,1)S(1)}, bf16[1152,256]{1,0:T(8,128)(2,1)S(1)}, u32[]{:S(2)}, u32[]{:S(2)}) collective-permute-start(bf16[1152,256]{1,0:T(8,128)(2,1)S(1)} %collective-permute-done.11.refs_3_.refs_6_), channel_id=1, source_target_pairs={{0,2},{1,3},{4,0},{5,1},{8,4},{9,5},{12,8},{13,9},{14,12},{15,13},... | collective-permute-start | bytes 1769480 | tf_op jit(solution)/shard_map/ppermute | solution.py:341
  61.3 24.7 %collective-permute-start.15 = (bf16[1152,256]{1,0:T(8,128)(2,1)S(1)}, bf16[1152,256]{1,0:T(8,128)(2,1)S(1)}, u32[]{:S(2)}, u32[]{:S(2)}) collective-permute-start(bf16[1152,256]{1,0:T(8,128)(2,1)S(1)} %collective-permute-done.10.refs_2_), channel_id=1, source_target_pairs={{0,4},{1,5},{4,8},{5,9},{8,12},{9,13},{12,14},{13,15},{14,10},{15,... | collective-permute-start | bytes 1769480 | tf_op jit(solution)/shard_map/ppermute | solution.py:341
  72.3 24.1 %collective-permute-start.12 = (bf16[1152,256]{1,0:T(8,128)(2,1)S(1)}, bf16[1152,256]{1,0:T(8,128)(2,1)S(1)}, u32[]{:S(2)}, u32[]{:S(2)}) collective-permute-start(bf16[1152,256]{1,0:T(8,128)(2,1)S(1)} %collective-permute-done.8.refs_2_.refs_7_), channel_id=1, source_target_pairs={{0,4},{1,5},{4,8},{5,9},{8,12},{9,13},{12,14},{13,15},{14,10},{15,... | collective-permute-start | bytes 1769480 | tf_op jit(solution)/shard_map/ppermute | solution.py:341
  72.4 24.1 %collective-permute-start.13 = (bf16[1152,256]{1,0:T(8,128)(2,1)S(1)}, bf16[1152,256]{1,0:T(8,128)(2,1)S(1)}, u32[]{:S(2)}, u32[]{:S(2)}) collective-permute-start(bf16[1152,256]{1,0:T(8,128)(2,1)S(1)} %collective-permute-done.9.refs_3_), channel_id=1, source_target_pairs={{0,2},{1,3},{4,0},{5,1},{8,4},{9,5},{12,8},{13,9},{14,12},{15,13},... | collective-permute-start | bytes 1769480 | tf_op jit(solution)/shard_map/ppermute | solution.py:341
  96.8 1.6 %collective-permute-start.16 = (f32[128,512]{1,0:T(8,128)S(1)}, f32[128,512]{1,0:T(8,128)S(1)}, u32[]{:S(2)}, u32[]{:S(2)}) collective-permute-start(f32[128,512]{1,0:T(8,128)S(1)} %shard_map.85), channel_id=1, source_target_pairs={{0,1},{1,0},{2,3},{3,2},{4,5},{5,4},{6,7},{7,6},{8,9},{9,8},{10,11... | collective-permute-start | bytes 786440 | tf_op jit(solution)/shard_map/ppermute | solution.py:341
  98.5 5.9 %collective-permute-start.20 = (bf16[144,512]{1,0:T(8,128)(2,1)S(1)}, bf16[144,512]{1,0:T(8,128)(2,1)S(1)}, u32[]{:S(2)}, u32[]{:S(2)}) collective-permute-start(bf16[144,512]{1,0:T(8,128)(2,1)S(1)} %pad_maximum_fusion), channel_id=1, source_target_pairs={{0,2},{1,3},{4,0},{5,1},{8,4},{9,5},{12,8},{13,9},{14,12},{15,13},... | collective-permute-start | bytes 442376 | tf_op jit(solution)/shard_map/ppermute | solution.py:341
  100.1 5.9 %collective-permute-start.17 = (bf16[144,512]{1,0:T(8,128)(2,1)S(1)}, bf16[144,512]{1,0:T(8,128)(2,1)S(1)}, u32[]{:S(2)}, u32[]{:S(2)}) collective-permute-start(bf16[144,512]{1,0:T(8,128)(2,1)S(1)} %pad_maximum_fusion), channel_id=1, source_target_pairs={{0,4},{1,5},{4,8},{5,9},{8,12},{9,13},{12,14},{13,15},{14,10},{15,... | collective-permute-start | bytes 442376 | tf_op jit(solution)/shard_map/ppermute | solution.py:341
  104.4 5.1 %collective-permute-start.21 = (bf16[144,512]{1,0:T(8,128)(2,1)S(1)}, bf16[144,512]{1,0:T(8,128)(2,1)S(1)}, u32[]{:S(2)}, u32[]{:S(2)}) collective-permute-start(bf16[144,512]{1,0:T(8,128)(2,1)S(1)} %collective-permute-done.20), channel_id=1, source_target_pairs={{0,2},{1,3},{4,0},{5,1},{8,4},{9,5},{12,8},{13,9},{14,12},{15,13},... | collective-permute-start | bytes 442376 | tf_op jit(solution)/shard_map/ppermute | solution.py:341
  106.0 6.2 %collective-permute-start.18 = (bf16[144,512]{1,0:T(8,128)(2,1)S(1)}, bf16[144,512]{1,0:T(8,128)(2,1)S(1)}, u32[]{:S(2)}, u32[]{:S(2)}) collective-permute-start(bf16[144,512]{1,0:T(8,128)(2,1)S(1)} %collective-permute-done.17), channel_id=1, source_target_pairs={{0,4},{1,5},{4,8},{5,9},{8,12},{9,13},{12,14},{13,15},{14,10},{15,... | collective-permute-start | bytes 442376 | tf_op jit(solution)/shard_map/ppermute | solution.py:341
  109.6 7.9 %collective-permute-start.24 = (bf16[80,512]{1,0:T(8,128)(2,1)S(1)}, bf16[80,512]{1,0:T(8,128)(2,1)S(1)}, u32[]{:S(2)}, u32[]{:S(2)}) collective-permute-start(bf16[80,512]{1,0:T(8,128)(2,1)S(1)} %slice.14), channel_id=1, source_target_pairs={{0,6},{1,7},{4,2},{5,3},{8,0},{9,1},{12,4},{13,5},{14,8},{15,9},{1... | collective-permute-start | bytes 245768 | tf_op jit(solution)/shard_map/ppermute | solution.py:341
  112.2 5.3 %collective-permute-start.23 = (bf16[64,512]{1,0:T(8,128)(2,1)S(1)}, bf16[64,512]{1,0:T(8,128)(2,1)S(1)}, u32[]{:S(2)}, u32[]{:S(2)}) collective-permute-start(bf16[64,512]{1,0:T(8,128)(2,1)S(1)} %slice.13), channel_id=1, source_target_pairs={{0,8},{1,9},{4,12},{5,13},{8,14},{9,15},{12,10},{13,11},{14,6},{15... | collective-permute-start | bytes 196616 | tf_op jit(solution)/shard_map/ppermute | solution.py:341
  112.6 5.8 %collective-permute-start.19 = (bf16[144,512]{1,0:T(8,128)(2,1)S(1)}, bf16[144,512]{1,0:T(8,128)(2,1)S(1)}, u32[]{:S(2)}, u32[]{:S(2)}) collective-permute-start(bf16[144,512]{1,0:T(8,128)(2,1)S(1)} %collective-permute-done.18), channel_id=1, source_target_pairs={{0,4},{1,5},{4,8},{5,9},{8,12},{9,13},{12,14},{13,15},{14,10},{15,... | collective-permute-start | bytes 442376 | tf_op jit(solution)/shard_map/ppermute | solution.py:341
  113.1 5.3 %collective-permute-start.22 = (bf16[144,512]{1,0:T(8,128)(2,1)S(1)}, bf16[144,512]{1,0:T(8,128)(2,1)S(1)}, u32[]{:S(2)}, u32[]{:S(2)}) collective-permute-start(bf16[144,512]{1,0:T(8,128)(2,1)S(1)} %collective-permute-done.21), channel_id=1, source_target_pairs={{0,2},{1,3},{4,0},{5,1},{8,4},{9,5},{12,8},{13,9},{14,12},{15,13},... | collective-permute-start | bytes 442376 | tf_op jit(solution)/shard_map/ppermute | solution.py:341
  114.6 3.9 %collective-permute-start.26 = (bf16[720,512]{1,0:T(8,128)(2,1)S(1)}, bf16[720,512]{1,0:T(8,128)(2,1)S(1)}, u32[]{:S(2)}, u32[]{:S(2)}) collective-permute-start(bf16[720,512]{1,0:T(8,128)(2,1)S(1)} %constant_dynamic-update-slice_fusion.4.refs_0_), channel_id=1, source_target_pairs={{0,1},{1,0},{2,3},{3,2},{4,5},{5,4},{6,7},{7,6},{8,9},{9,8},{10,11... | collective-permute-start | bytes 2211848 | tf_op jit(solution)/shard_map/ppermute | solution.py:341
  118.5 1.9 %collective-permute-start.25 = (bf16[432,512]{1,0:T(8,128)(2,1)S(1)}, bf16[432,512]{1,0:T(8,128)(2,1)S(1)}, u32[]{:S(2)}, u32[]{:S(2)}) collective-permute-start(bf16[432,512]{1,0:T(8,128)(2,1)S(1)} %constant_dynamic-update-slice_fusion.first_ref), channel_id=1, source_target_pairs={{0,1},{1,0},{2,3},{3,2},{4,5},{5,4},{6,7},{7,6},{8,9},{9,8},{10,11... | collective-permute-start | bytes 1327112 | tf_op jit(solution)/shard_map/ppermute | solution.py:341
